TPU v7x, 256 devices: a whole 4x4x8 slice. The times are simulated.
256 devices in a mesh: row: 8 (over y_lo, x), col: 32 (over y_hi, z, core).
Axes of the slice: x: 4, y: 4 (y_hi: 2, y_lo: 2; y = y_hi * 2 + y_lo), z: 8, core: 2. Of those that a mesh axis runs over, the one named last changes fastest.
Arguments:
- gradient: bfloat16 [16384, 32768], P('row', 'col'), may hold values from -6 to 6
- in_panels: bfloat16 [3, 32768, 256], P(None, 'col'), may hold values from -0.03125 to 0.03125
- out_pool: bfloat16 [32, 16384, 256], P('col', 'row'), may hold values from -0.046875 to 0.046875
- eigenvalues: float32 [3, 256, 256], replicated, may hold values from 0.003 to 0.3
- owners: int32 [3], replicated, may hold values from 0 to 31, as said below
Outputs:
- preconditioned: bfloat16 [16384, 32768], P('row', 'col')
Inputs may be any that keep to these rules, and one draw needn't show every extreme that they name: `owners`: each entry names a column group; the last group is named in every draw; entries may repeat.
All inputs are finite; a program needn't handle non-finite values.
Results may differ from a plain program's by a relative error of at most 0.006.
Values may be sent and summed in bfloat16 or wider, within the bound.
No kernel may reach another device: no remote copies, remote signals or barrier semaphores. Data moves between devices by JAX's collectives and lax.ppermute only.
A program may use at most 128 MiB of HBM per device.

v0:
```python
import jax
import jax.numpy as jnp
from jax import lax
from jax.sharding import PartitionSpec as P


def from_root(x, axis, root):
    mine = lax.axis_index(axis) == root
    return lax.psum(jnp.where(mine, x, jnp.zeros_like(x)), axis)


def fetch(owned, root):
    return from_root(owned, "col", root)


def partial_term(grad_block, basis, fetched):
    projected = jnp.dot(grad_block, basis, preferred_element_type=jnp.float32)
    return jnp.dot(
        fetched.astype(jnp.float32).T,
        projected,
        precision=lax.Precision.HIGHEST,
        preferred_element_type=jnp.float32,
    )


def scaled_terms(parts, values):
    damping = 0.1 * jnp.mean(values, axis=(1, 2), keepdims=True)
    totals = lax.psum(parts, ("row", "col"))
    return (totals / (values + damping)).astype(jnp.bfloat16)


def body(gradient, in_panels, out_pool, eigenvalues, owners):
    owned = out_pool[0]
    count = in_panels.shape[0]
    total = jnp.zeros(gradient.shape, jnp.float32)
    for number in range(count):
        fetched = fetch(owned, owners[number])
        basis = in_panels[number]
        parts = partial_term(gradient, basis, fetched)[None]
        scaled = scaled_terms(parts, eigenvalues[number][None])[0]
        rotated = jnp.dot(fetched, scaled, preferred_element_type=jnp.float32).astype(jnp.bfloat16)
        total = total + jnp.dot(rotated, basis.T, preferred_element_type=jnp.float32)
    return total.astype(jnp.bfloat16)


def solution(mesh):
    return jax.shard_map(
        body,
        mesh=mesh,
        in_specs=(P("row", "col"), P(None, "col", None), P("col", "row", None), P(), P()),
        out_specs=P("row", "col"),
        check_vma=False,
    )
```

profile of v0, /device:TPU:1, one launch (start us, length us, event | category | flops | bytes accessed | tf_op | source)
XLA Modules:
  0.0 580.2 jit_solution(14170137619611259127)
XLA Ops:
  6.5 0.0 all-reduce.7.cloned.1.call-start
  6.5 1.4 fusion.23
  9.9 2.9 select_bitcast_fusion
  12.9 0.0 all-reduce.7.cloned.1.call-update
  12.9 0.0 all-reduce.5.cloned.1.call-start
  12.9 0.0 copy-start.6
  12.9 0.0 copy-start.9
  12.9 5.0 fusion.9
  18.0 0.0 copy-done.6
  18.0 0.0 copy-done.9
  18.0 1.3 fusion.3
  19.3 2.6 fusion.6
  21.9 270.4 %all-reduce.7.cloned.1.call-done = (bf16[2048,256]{1,0:T(8,128)(2,1)}, bf16[2048,256]{1,0:T(8,128)(2,1)}, bf16[2048,256]{1,0:T(8,128)(2,1)}) async-done(((bf16[2048,256]{1,0:T(8,128)(2,1)}, bf16[2048,256]{1,0:T(8,128)(2,1)}, bf16[2048,256]{1,0:T(8,128)(2,1)}), (bf16[2048,256]{1,0:T(8,128)(2,1)}, bf16[2048,256]{1,0:T(8,128)(2,1)}, bf16[2048,256]{1,0:T(8,128)(2,1)})) %all-reduce.7.cloned.1.call-update) | async-done | bytes 3145744 | tf_op jit(solution)/shard_map/psum | solution.py:9
  292.3 0.0 copy-start.1
  292.3 0.0 copy-start.5
  292.3 3.6 convolution_bitcast_fusion
  295.8 0.0 copy-start.2
  295.8 0.0 copy-start.4
  295.8 0.0 copy-done.1
  295.8 0.0 copy-done.5
  295.8 2.2 convolution_bitcast_fusion.1
  298.1 0.0 copy-done.2
  298.1 0.0 copy-done.4
  298.1 0.0 copy-start.3
  298.1 2.2 convolution_bitcast_fusion.2
  300.3 0.0 all-reduce.5.cloned.1.call-update
  300.3 0.0 copy-done.3
  300.3 0.7 slice_reduce_fusion
  302.7 249.8 %all-reduce.5.cloned.1.call-done = (f32[1,256,256]{2,1,0:T(8,128)}, f32[1,256,256]{2,1,0:T(8,128)}, f32[1,256,256]{2,1,0:T(8,128)}) async-done(((f32[1,256,256]{2,1,0:T(8,128)}, f32[1,256,256]{2,1,0:T(8,128)}, f32[1,256,256]{2,1,0:T(8,128)}), (f32[1,256,256]{2,1,0:T(8,128)}, f32[1,256,256]{2,1,0:T(8,128)}, f32[1,256,256]{2,1,0:T(8,128)})) %all-reduce.5.cloned.1.call-update) | async-done | bytes 786448 | tf_op jit(solution)/shard_map/psum | solution.py:28
  552.5 0.0 copy-start.8
  552.5 5.9 %fusion = f32[2048,1024]{1,0:T(8,128)} fusion(bf16[2048,256]{1,0:T(8,128)(2,1)S(1)} %copy-done.2, bf16[3,1024,256]{2,1,0:T(8,128)(2,1)} %param.6, f32[1,256,256]{2,1,0:T(8,128)} %get-tuple-element.8, f32[3,256,256]{2,1,0:T(8,128)S(1)} %copy-done.3, f32[]{:T(128)S(6)} %mul.12), kind=kOutput, calls=%fused_computation.4 | convolution fusion | flops 1342898176 | bytes 10485764 | tf_op jit(solution)/shard_map/dot_general | solution.py:42
  558.4 0.0 copy-done.8
  558.4 0.0 copy-start
  558.4 0.0 copy-start.7
  558.4 5.9 %fusion.1 = f32[2048,1024]{1,0:T(8,128)} fusion(bf16[2048,256]{1,0:T(8,128)(2,1)S(1)} %copy-done.1, bf16[3,1024,256]{2,1,0:T(8,128)(2,1)} %param.6, f32[1,256,256]{2,1,0:T(8,128)S(1)} %copy-done.8, f32[3,256,256]{2,1,0:T(8,128)S(1)} %copy-done.3, f32[]{:T(128)S(6)} %mul.13), kind=kOutput, calls=%fused_computation.5 | convolution fusion | flops 1342898176 | bytes 10485764 | tf_op jit(solution)/shard_map/dot_general | solution.py:42
  564.4 0.0 copy-done
  564.4 0.0 copy-done.7
  564.4 8.9 %add_convert_fusion = bf16[2048,1024]{1,0:T(8,128)(2,1)} fusion(f32[2048,1024]{1,0:T(8,128)} %fusion, f32[2048,1024]{1,0:T(8,128)} %fusion.1, bf16[2048,256]{1,0:T(8,128)(2,1)S(1)} %copy-done, bf16[3,1024,256]{2,1,0:T(8,128)(2,1)} %param.6, f32[1,256,256]{2,1,0:T(8,128)S(1)} %copy-done.7, f32[3,256,256]{2,1,0:T(8,128)S(1)} %copy-done.3, f32[]{:T(128)S(6)} %mul.14), kind=kOutput, calls=%fused_computation | convolution fusion | flops 1349189632 | bytes 23068676 | tf_op jit(solution)/shard_map/dot_general | solution.py:42
Async XLA Ops:
  6.5 285.7 %all-reduce.7.cloned.1.call-start = ((), (), s32[]{:S(2)}) async-start(), calls=%async_computation.1 | async-start | bytes 6291456 | tf_op jit(solution)/shard_map/psum | solution.py:9
  12.9 539.6 %all-reduce.5.cloned.1.call-start = ((), (), s32[]{:S(2)}) async-start(), calls=%async_computation | async-start | bytes 1572864 | tf_op jit(solution)/shard_map/psum | solution.py:28
  12.9 5.1 copy-start.6
  12.9 5.0 copy-start.9
  292.3 3.6 copy-start.1
  292.3 3.6 copy-start.5
  295.8 2.2 copy-start.2
  295.8 2.2 copy-start.4
  298.1 2.2 copy-start.3
  552.5 5.9 %copy-start.8 = (f32[1,256,256]{2,1,0:T(8,128)S(1)}, f32[1,256,256]{2,1,0:T(8,128)}, u32[]{:S(2)}) copy-start(f32[1,256,256]{2,1,0:T(8,128)} %get-tuple-element.9) | copy-start | bytes 786436
  558.4 5.9 %copy-start = (bf16[2048,256]{1,0:T(8,128)(2,1)S(1)}, bf16[2048,256]{1,0:T(8,128)(2,1)}, u32[]{:S(2)}) copy-start(bf16[2048,256]{1,0:T(8,128)(2,1)} %get-tuple-element.13) | copy-start | bytes 3145732
  558.4 5.9 %copy-start.7 = (f32[1,256,256]{2,1,0:T(8,128)S(1)}, f32[1,256,256]{2,1,0:T(8,128)}, u32[]{:S(2)}) copy-start(f32[1,256,256]{2,1,0:T(8,128)} %get-tuple-element.10) | copy-start | bytes 786436
Sparse Core Ops, SparseCore 0:
  13.0 279.2 all-reduce.6
  300.4 252.0 all-reduce.4
where the time goes:
time: 581 us; the launch traced here: 580 us
  waiting for transfers between devices  520 us (90%)
  matrix products  37.7 us (6%)
  between operations  17.2 us (3%)
    psum x1, waiting for transfers between devices, from_root(): return lax.psum(jnp.where(mine, x, jnp.zeros_like(x)), axis)  270 us
    psum x1, waiting for transfers between devices, scaled_terms(): totals = lax.psum(parts, ('row', 'col'))  250 us
    dot_general x3, matrix products, body(): jnp.dot(rotated, basis.T, preferred_element_type=jnp.float32)  20.8 us
  transfers between devices with their start and end apart: 2, of which 2 were waited for; matrix products, arithmetic and copies ran while one was open for 2% of the time, Pallas kernels for 0%

commit v1 on v0

v1 whole, which is shorter than its diff:
```python
import jax
import jax.numpy as jnp
from jax import lax
from jax.sharding import Mesh
from jax.sharding import PartitionSpec as P

ROW = ("yl", "x")
COL = ("yh", "z", "core")
SPREAD = ("core", "yh", "z")
F32 = jnp.float32
BF16 = jnp.bfloat16


def swap(x, axis):
    return lax.ppermute(x, axis, [(0, 1), (1, 0)])


def paired(x, axis, dim):
    other = swap(x, axis)
    first = lax.axis_index(axis) == 0
    return jnp.concatenate([jnp.where(first, x, other), jnp.where(first, other, x)], axis=dim)


def halved(x, axis):
    here = lax.axis_index(axis)
    half = x.shape[0] // 2
    other = swap(lax.dynamic_slice_in_dim(x, (1 - here) * half, half, 0), axis)
    return lax.dynamic_slice_in_dim(x, here * half, half, 0) + other


def ring(x, axis, size):
    here = lax.axis_index(axis)
    whole = jnp.zeros((size,) + x.shape, x.dtype)
    whole = lax.dynamic_update_index_in_dim(whole, x, here, 0)
    up = down = x
    for step in range(1, size // 2 + 1):
        up = lax.ppermute(up, axis, [(i, (i + 1) % size) for i in range(size)])
        whole = lax.dynamic_update_index_in_dim(whole, up, (here - step) % size, 0)
        if step < size - step:
            down = lax.ppermute(down, axis, [(i, (i - 1) % size) for i in range(size)])
            whole = lax.dynamic_update_index_in_dim(whole, down, (here + step) % size, 0)
    return whole


def everyones(x, axes, count):
    return lax.all_to_all(jnp.broadcast_to(x[None], (count,) + x.shape), axes, 0, 0, tiled=False)


def body(gradient, in_panels, out_pool, eigenvalues, owners):
    count = in_panels.shape[0]
    rows, vec = out_pool.shape[1:]

    with jax.named_scope("panels"):
        pieces = lax.all_to_all(out_pool[0].reshape(32, rows // 32, vec), SPREAD, 0, 0, tiled=False)
        where = (owners % 2) * 16 + owners // 2
        mine = jnp.stack([lax.dynamic_index_in_dim(pieces, where[k], 0, keepdims=False) for k in range(count)])
        both = paired(mine[None], "yh", 0)
        gathered = ring(both, "z", 8)
        half = gathered.transpose(2, 1, 0, 3, 4).reshape(count, rows // 2, vec)
        fetched = paired(half, "core", 1)

    with jax.named_scope("projection"):
        parts = []
        for k in range(count):
            projected = jnp.dot(gradient, in_panels[k], preferred_element_type=F32)
            high = lax.reduce_precision(projected, 8, 7)
            low = (projected - high).astype(BF16)
            split = jnp.concatenate([high.astype(BF16), low], axis=1)
            part = jnp.dot(fetched[k].T, split, preferred_element_type=F32)
            parts.append(part[:, :vec] + part[:, vec:])
        part = jnp.concatenate(parts, axis=0)

    with jax.named_scope("sum"):
        damping = 0.1 * jnp.mean(eigenvalues, axis=(1, 2), keepdims=True)
        below = (eigenvalues + damping).reshape(count * vec, vec)
        part = halved(part, "core")
        exchanged = lax.all_to_all(part.reshape(8, part.shape[0] // 8, vec), ROW, 0, 0, tiled=False)
        part = jnp.sum(exchanged, axis=0)
        part = halved(part, "yh")
        total = jnp.sum(everyones(part, "z", 8), axis=0)
        size = total.shape[0]
        at = (lax.axis_index("core") * 8 + lax.axis_index(ROW)) * 2 + lax.axis_index("yh")
        scaled = (total / lax.dynamic_slice_in_dim(below, at * size, size, 0)).astype(BF16)
        scaled = everyones(scaled, ("core",) + ROW + ("yh",), 32).reshape(count, vec, vec)

    with jax.named_scope("output"):
        out = jnp.zeros(gradient.shape, F32)
        for k in range(count):
            rotated = jnp.dot(fetched[k], scaled[k], preferred_element_type=F32).astype(BF16)
            out = out + lax.dot_general(rotated, in_panels[k], (((1,), (1,)), ((), ())), preferred_element_type=F32)
        return out.astype(BF16)


def solution(mesh):
    fine = Mesh(mesh.devices.reshape(2, 4, 2, 8, 2), ROW + COL)
    return jax.shard_map(
        body,
        mesh=fine,
        in_specs=(P(ROW, COL), P(None, COL, None), P(COL, ROW, None), P(), P()),
        out_specs=P(ROW, COL),
        check_vma=False,
    )
```

time: 581 us -> 166 us (0.29)
  waiting for transfers between devices: 520 us -> 64.2 us
  starting transfers between devices: 0.04 us -> 33.9 us
  blocking collectives: 0 us -> 16.5 us
  between operations: 17.2 us -> 6 us
  matrix products: 37.7 us -> 29.1 us
  other arithmetic: 3.64 us -> 9.94 us
    psum x2 -> x0, waiting for transfers between devices: 520 us -> none  [the longest x1 270 us: from_root(): return lax.psum(jnp.where(mine, x, jnp.zeros_like(x)), axis)]
    all_to_all x0 -> x3, waiting for transfers between devices: none -> 37.9 us  [the longest x1 22.6 us: body(): lax.all_to_all(out_pool[0].reshape(32, rows // 32, vec), SPREAD, 0, 0, ti...]
    ppermute x0 -> x11, waiting for transfers between devices: none -> 26.2 us  [the longest x4 16.3 us: ring(): up = lax.ppermute(up, axis, [(i, (i + 1) % size) for i in range(size)])]
    all_to_all x0 -> x3, starting transfers between devices: none -> 20.4 us  [the longest x1 12.9 us: body(): lax.all_to_all(out_pool[0].reshape(32, rows // 32, vec), SPREAD, 0, 0, ti...]
    all_to_all x0 -> x1, blocking collectives: none -> 16.5 us  [everyones(): lax.all_to_all(jnp.broadcast_to(x[None], (count,) + x.shape), axes, 0, 0,...]
    ppermute x0 -> x11, starting transfers between devices: none -> 13.5 us  [the longest x3 6.16 us: ring(): down = lax.ppermute(down, axis, [(i, (i - 1) % size) for i in range(size)])]
    dot_general x9, matrix products: 37.7 us -> 29.1 us  [the longest x3 20.5 us: body(): lax.dot_general(rotated, in_panels[k], (((1,), (1,)), ((), ())), preferre...]
  transfers between devices with their start and end apart: 2 -> 14, of which waited for: 2 -> 10; matrix products, arithmetic and copies ran while one was open for 2% -> 7% of each run, Pallas kernels for 0% -> 0%
where the time goes in v1:
time: 166 us; the launch traced here: 165 us
  waiting for transfers between devices  64.2 us (39%)
  starting transfers between devices  33.9 us (20%)
  matrix products  29.1 us (18%)
  blocking collectives  16.5 us (10%)
  other arithmetic  9.94 us (6%)
  between operations  6 us (4%)
  local copies, waits for them, and re-layouts  5.08 us (3%)
    all_to_all x1, waiting for transfers between devices, body(): lax.all_to_all(out_pool[0].reshape(32, rows // 32, vec), SPREAD, 0, 0, ti...  22.6 us
    dot_general x3, matrix products, body(): lax.dot_general(rotated, in_panels[k], (((1,), (1,)), ((), ())), preferre...  20.5 us
    all_to_all x1, blocking collectives, everyones(): lax.all_to_all(jnp.broadcast_to(x[None], (count,) + x.shape), axes, 0, 0,...  16.5 us
    ppermute x4, waiting for transfers between devices, ring(): up = lax.ppermute(up, axis, [(i, (i + 1) % size) for i in range(size)])  16.3 us
    all_to_all x1, starting transfers between devices, body(): lax.all_to_all(out_pool[0].reshape(32, rows // 32, vec), SPREAD, 0, 0, ti...  12.9 us
    ppermute x4, waiting for transfers between devices, swap(): return lax.ppermute(x, axis, [(0, 1), (1, 0)])  9.91 us
    all_to_all x1, waiting for transfers between devices, body(): lax.all_to_all(part.reshape(8, part.shape[0] // 8, vec), ROW, 0, 0, tiled...  8.86 us
    all_to_all x1, waiting for transfers between devices, everyones(): lax.all_to_all(jnp.broadcast_to(x[None], (count,) + x.shape), axes, 0, 0,...  6.47 us
  transfers between devices with their start and end apart: 14, of which 10 were waited for; matrix products, arithmetic and copies ran while one was open for 7% of the time, Pallas kernels for 0%

profile of v1, /device:TPU:1, one launch (start us, length us, event | category | flops | bytes accessed | tf_op | source)
XLA Modules:
  0.0 164.6 jit_solution(10220837770600361425)
XLA Ops:
  0.0 12.9 %all-to-all-start = ((bf16[32,64,256]{2,1,0:T(8,128)(2,1)}), bf16[32,64,256]{2,1,0:T(8,128)(2,1)S(1)}, u32[]{:S(2)}, u32[]{:S(2)}) async-start(bf16[32,64,256]{2,1,0:T(8,128)(2,1)} %bitcast.104), calls=%async_computation | async-start | bytes 2097152 | tf_op jit(solution)/shard_map/panels/all_to_all | solution.py:54
  12.9 0.7 fusion.51
  19.3 22.6 %all-to-all-done = bf16[32,64,256]{2,1,0:T(8,128)(2,1)S(1)} async-done(((bf16[32,64,256]{2,1,0:T(8,128)(2,1)}), bf16[32,64,256]{2,1,0:T(8,128)(2,1)S(1)}, u32[]{:S(2)}, u32[]{:S(2)}) %all-to-all-start) | async-done | bytes 1048608 | tf_op jit(solution)/shard_map/panels/all_to_all | solution.py:54
  41.9 0.1 collective-permute-start
  42.0 5.7 %collective-permute-done = bf16[1,3,64,256]{3,2,0,1:T(8,128)(2,1)S(1)} collective-permute-done((bf16[1,3,64,256]{3,2,0,1:T(8,128)(2,1)S(1)}, bf16[1,3,64,256]{3,2,0,1:T(8,128)(2,1)S(1)}, u32[]{:S(2)}, u32[]{:S(2)}) %collective-permute-start) | collective-permute-done | bytes 98336 | tf_op jit(solution)/shard_map/panels/ppermute | solution.py:15
  47.8 0.7 pad_maximum_fusion.2
  48.5 1.9 %collective-permute-start.1 = (bf16[2,3,64,256]{3,2,0,1:T(8,128)(2,1)}, bf16[2,3,64,256]{3,2,0,1:T(8,128)(2,1)}, u32[]{:S(2)}, u32[]{:S(2)}) collective-permute-start(bf16[2,3,64,256]{3,2,0,1:T(8,128)(2,1)} %pad_maximum_fusion.2), channel_id=1, source_target_pairs={{0,2},{2,4},{4,6},{6,8},{8,10},{10,12},{12,14},{14,0},{1,3},{3,5},... | collective-permute-start | bytes 589832 | tf_op jit(solution)/shard_map/panels/ppermute | solution.py:37
  50.3 0.8 collective-permute-start.2
  51.1 0.2 broadcast_in_dim.44
  51.3 4.7 %collective-permute-done.1 = bf16[2,3,64,256]{3,2,0,1:T(8,128)(2,1)} collective-permute-done((bf16[2,3,64,256]{3,2,0,1:T(8,128)(2,1)}, bf16[2,3,64,256]{3,2,0,1:T(8,128)(2,1)}, u32[]{:S(2)}, u32[]{:S(2)}) %collective-permute-start.1) | collective-permute-done | bytes 196640 | tf_op jit(solution)/shard_map/panels/ppermute | solution.py:37
  56.1 2.7 %collective-permute-start.4 = (bf16[2,3,64,256]{3,2,0,1:T(8,128)(2,1)S(1)}, bf16[2,3,64,256]{3,2,0,1:T(8,128)(2,1)S(1)}, u32[]{:S(2)}, u32[]{:S(2)}) collective-permute-start(bf16[2,3,64,256]{3,2,0,1:T(8,128)(2,1)S(1)} %collective-permute-done.2), channel_id=1, source_target_pairs={{0,14},{2,0},{4,2},{6,4},{8,6},{10,8},{12,10},{14,12},{1,15},{3,1}... | collective-permute-start | bytes 589832 | tf_op jit(solution)/shard_map/panels/ppermute | solution.py:40
  58.8 0.9 bitcast_dynamic-update-slice_fusion.5
  59.7 2.9 %collective-permute-done.3 = bf16[2,3,64,256]{3,2,0,1:T(8,128)(2,1)S(1)} collective-permute-done((bf16[2,3,64,256]{3,2,0,1:T(8,128)(2,1)}, bf16[2,3,64,256]{3,2,0,1:T(8,128)(2,1)S(1)}, u32[]{:S(2)}, u32[]{:S(2)}) %collective-permute-start.3) | collective-permute-done | bytes 196640 | tf_op jit(solution)/shard_map/panels/ppermute | solution.py:37
  62.7 2.7 %collective-permute-start.6 = (bf16[2,3,64,256]{3,2,0,1:T(8,128)(2,1)S(1)}, bf16[2,3,64,256]{3,2,0,1:T(8,128)(2,1)S(1)}, u32[]{:S(2)}, u32[]{:S(2)}) collective-permute-start(bf16[2,3,64,256]{3,2,0,1:T(8,128)(2,1)S(1)} %collective-permute-done.4), channel_id=1, source_target_pairs={{0,14},{2,0},{4,2},{6,4},{8,6},{10,8},{12,10},{14,12},{1,15},{3,1}... | collective-permute-start | bytes 589832 | tf_op jit(solution)/shard_map/panels/ppermute | solution.py:40
  65.4 3.0 %collective-permute-done.5 = bf16[2,3,64,256]{3,2,0,1:T(8,128)(2,1)S(1)} collective-permute-done((bf16[2,3,64,256]{3,2,0,1:T(8,128)(2,1)S(1)}, bf16[2,3,64,256]{3,2,0,1:T(8,128)(2,1)S(1)}, u32[]{:S(2)}, u32[]{:S(2)}) %collective-permute-start.5) | collective-permute-done | bytes 196640 | tf_op jit(solution)/shard_map/panels/ppermute | solution.py:37
  68.5 5.7 %collective-permute-done.7 = bf16[2,3,64,256]{3,2,0,1:T(8,128)(2,1)S(1)} collective-permute-done((bf16[2,3,64,256]{3,2,0,1:T(8,128)(2,1)S(1)}, bf16[2,3,64,256]{3,2,0,1:T(8,128)(2,1)S(1)}, u32[]{:S(2)}, u32[]{:S(2)}) %collective-permute-start.7) | collective-permute-done | bytes 196640 | tf_op jit(solution)/shard_map/panels/ppermute | solution.py:37
  74.2 4.7 %collective-permute-start.8 = (bf16[3,1024,256]{2,1,0:T(8,128)(2,1)S(1)}, bf16[3,1024,256]{2,1,0:T(8,128)(2,1)}, u32[]{:S(2)}, u32[]{:S(2)}) collective-permute-start(bf16[3,1024,256]{2,1,0:T(8,128)(2,1)S(1)} %bitcast.99), channel_id=1, source_target_pairs={{0,1},{1,0},{2,3},{3,2},{4,5},{5,4},{6,7},{7,6},{8,9},{9,8},{10,11... | collective-permute-start | bytes 4718600 | tf_op jit(solution)/shard_map/panels/ppermute | solution.py:15
  78.9 3.6 %reduce-precision_convert_fusion.2 = (bf16[2048,256]{0,1:T(8,128)(2,1)S(1)}, bf16[2048,256]{0,1:T(8,128)(2,1)S(1)}) fusion(bf16[2048,1024]{1,0:T(8,128)(2,1)} %param.5, bf16[3,1024,256]{2,1,0:T(8,128)(2,1)S(1)} %copy-done.3), kind=kOutput, calls=%fused_computation.10 | convolution fusion | flops 1075838976 | bytes 6815744 | tf_op jit(solution)/shard_map/projection/dot_general | solution.py:65
  82.6 1.3 reduce-precision_convert_fusion
  83.9 1.3 reduce-precision_convert_fusion.1
  85.2 0.1 copy-done.1
  85.3 1.6 broadcast_select_fusion.1
  86.9 0.8 fusion.3
  87.7 0.8 fusion.11
  88.5 0.8 fusion.7
  89.2 0.1 slice_add_fusion
  89.4 0.9 copy-done.2
  90.2 0.8 constant_dynamic-slice_fusion.1
  91.0 0.2 collective-permute-start.9
  91.2 1.8 %collective-permute-done.9 = f32[384,256]{1,0:T(8,128)S(1)} collective-permute-done((f32[384,256]{1,0:T(8,128)}, f32[384,256]{1,0:T(8,128)S(1)}, u32[]{:S(2)}, u32[]{:S(2)}) %collective-permute-start.9) | collective-permute-done | bytes 393248 | tf_op jit(solution)/shard_map/sum/ppermute | solution.py:15
  93.0 1.8 %dynamic-slice_add_fusion = f32[384,256]{1,0:T(8,128)} fusion(f32[384,256]{1,0:T(8,128)S(1)} %collective-permute-done.9, f32[768,256]{1,0:T(8,128)} %copy-done.2, s32[]{:T(128)S(6)} %select_n.142), kind=kLoop, calls=%fused_computation.56 | loop fusion | flops 98304 | bytes 1179652 | tf_op jit(solution)/shard_map/sum/add | solution.py:28
  94.7 4.1 %all-to-all-start.1 = ((f32[8,48,256]{2,1,0:T(8,128)}), f32[8,48,256]{2,1,0:T(8,128)S(1)}, u32[]{:S(2)}, u32[]{:S(2)}) async-start(f32[8,48,256]{2,1,0:T(8,128)} %bitcast.103), calls=%async_computation.1 | async-start | bytes 786432 | tf_op jit(solution)/shard_map/sum/all_to_all | solution.py:77
  98.9 8.9 %all-to-all-done.1 = f32[8,48,256]{2,1,0:T(8,128)S(1)} async-done(((f32[8,48,256]{2,1,0:T(8,128)}), f32[8,48,256]{2,1,0:T(8,128)S(1)}, u32[]{:S(2)}, u32[]{:S(2)}) %all-to-all-start.1) | async-done | bytes 393248 | tf_op jit(solution)/shard_map/sum/all_to_all | solution.py:77
  107.7 0.6 reduce_sum.27
  108.4 0.7 constant_dynamic-slice_fusion
  109.1 0.4 collective-permute-start.10
  109.6 1.3 reduce_sum.29
  110.9 2.4 %collective-permute-done.10 = f32[24,256]{1,0:T(8,128)S(1)} collective-permute-done((f32[24,256]{1,0:T(8,128)S(1)}, f32[24,256]{1,0:T(8,128)S(1)}, u32[]{:S(2)}, u32[]{:S(2)}) %collective-permute-start.10) | collective-permute-done | bytes 24608 | tf_op jit(solution)/shard_map/sum/ppermute | solution.py:15
  113.3 0.7 dynamic-slice_add_fusion.1
  114.0 0.7 broadcast_in_dim.54
  114.7 3.4 %all-to-all-start.2 = ((f32[8,24,256]{2,1,0:T(8,128)}), f32[8,24,256]{2,1,0:T(8,128)S(1)}, u32[]{:S(2)}, u32[]{:S(2)}) async-start(f32[8,24,256]{2,1,0:T(8,128)} %broadcast_in_dim.54), calls=%async_computation.2 | async-start | bytes 393216 | tf_op jit(solution)/shard_map/sum/all_to_all | solution.py:46
  118.2 2.1 %broadcast_add_fusion = f32[3,256,256]{2,1,0:T(8,128)} fusion(f32[3,256,256]{2,1,0:T(8,128)} %param.8, f32[3]{0:T(128)S(1)} %broadcast_multiply_fusion), kind=kLoop, calls=%fused_computation.55 | loop fusion | flops 196608 | bytes 1572876 | tf_op jit(solution)/shard_map/sum/add | solution.py:75
  120.3 6.5 %all-to-all-done.2 = f32[8,24,256]{2,1,0:T(8,128)S(1)} async-done(((f32[8,24,256]{2,1,0:T(8,128)}), f32[8,24,256]{2,1,0:T(8,128)S(1)}, u32[]{:S(2)}, u32[]{:S(2)}) %all-to-all-start.2) | async-done | bytes 196640 | tf_op jit(solution)/shard_map/sum/all_to_all | solution.py:46
  126.8 0.8 divide_convert_fusion
  127.6 16.5 %all_to_all.20 = bf16[32,24,256]{2,1,0:T(8,128)(2,1)S(1)} all-to-all(bf16[32,24,256]{2,1,0:T(8,128)(2,1)S(1)} %broadcast_in_dim.55), channel_id=1, replica_groups=mesh['yl'=2,'x'=4,'yh'=2,'z'=8,'core'=2] {'core','yl','x','yh'}, dimensions={0} | all-to-all | bytes 786432 | tf_op jit(solution)/shard_map/sum/all_to_all | solution.py:46
  144.1 5.8 %fusion.16 = f32[2048,1024]{1,0:T(8,128)} fusion(bf16[3,1024,256]{2,1,0:T(8,128)(2,1)} %param.6, bf16[3,256,256]{2,1,0:T(8,128)(2,1)S(1)} %bitcast.100, bf16[3,1024,256]{2,1,0:T(8,128)(2,1)S(1)} %get-tuple-element.5, bf16[3,1024,256]{2,1,0:T(8,128)(2,1)S(1)} %get-tuple-element.6), kind=kOutput, calls=%fused_computation.32 | convolution fusion | flops 1344798720 | bytes 12189696 | tf_op jit(solution)/shard_map/output/dot_general | solution.py:90
  149.9 5.8 %fusion.15 = f32[2048,1024]{1,0:T(8,128)} fusion(bf16[3,1024,256]{2,1,0:T(8,128)(2,1)} %param.6, bf16[3,256,256]{2,1,0:T(8,128)(2,1)S(1)} %bitcast.101, bf16[3,1024,256]{2,1,0:T(8,128)(2,1)S(1)} %get-tuple-element.5, bf16[3,1024,256]{2,1,0:T(8,128)(2,1)S(1)} %get-tuple-element.6), kind=kOutput, calls=%fused_computation.31 | convolution fusion | flops 1344798720 | bytes 12189696 | tf_op jit(solution)/shard_map/output/dot_general | solution.py:90
  155.7 8.9 %add_convert_fusion = bf16[2048,1024]{1,0:T(8,128)(2,1)} fusion(f32[2048,1024]{1,0:T(8,128)} %fusion.15, f32[2048,1024]{1,0:T(8,128)} %fusion.16, bf16[3,1024,256]{2,1,0:T(8,128)(2,1)} %param.6, bf16[3,256,256]{2,1,0:T(8,128)(2,1)S(1)} %bitcast.102, bf16[3,1024,256]{2,1,0:T(8,128)(2,1)S(1)} %get-tuple-element.6, bf16[3,1024,256]{2,1,0:T(8,128)(2,1)S(1)} %get-tuple-element.5), kind=kOutput, calls=%fused_computation | convolution fusion | flops 1351090176 | bytes 24772608 | tf_op jit(solution)/shard_map/output/dot_general | solution.py:90
  (33 shorter events, 0.4 us)
Async XLA Ops:
  0.0 12.9 %copy-start.5 = (s32[3]{0:T(128)S(1)}, s32[3]{0:T(128)}, u32[]{:S(2)}) copy-start(s32[3]{0:T(128)} %param.9) | copy-start | bytes 40
  0.0 41.9 %all-to-all-start = ((bf16[32,64,256]{2,1,0:T(8,128)(2,1)}), bf16[32,64,256]{2,1,0:T(8,128)(2,1)S(1)}, u32[]{:S(2)}, u32[]{:S(2)}) async-start(bf16[32,64,256]{2,1,0:T(8,128)(2,1)} %bitcast.104), calls=%async_computation | async-start | bytes 2097152 | tf_op jit(solution)/shard_map/panels/all_to_all | solution.py:54
  41.9 5.8 %collective-permute-start = (bf16[1,3,64,256]{3,2,0,1:T(8,128)(2,1)S(1)}, bf16[1,3,64,256]{3,2,0,1:T(8,128)(2,1)S(1)}, u32[]{:S(2)}, u32[]{:S(2)}) collective-permute-start(bf16[1,3,64,256]{3,2,0,1:T(8,128)(2,1)S(1)} %maximum_bitcast_fusion), channel_id=1, source_target_pairs={{0,16},{16,0},{1,17},{17,1},{2,18},{18,2},{3,19},{19,3},{4,20},{20... | collective-permute-start | bytes 294920 | tf_op jit(solution)/shard_map/panels/ppermute | solution.py:15
  48.5 7.6 %collective-permute-start.1 = (bf16[2,3,64,256]{3,2,0,1:T(8,128)(2,1)}, bf16[2,3,64,256]{3,2,0,1:T(8,128)(2,1)}, u32[]{:S(2)}, u32[]{:S(2)}) collective-permute-start(bf16[2,3,64,256]{3,2,0,1:T(8,128)(2,1)} %pad_maximum_fusion.2), channel_id=1, source_target_pairs={{0,2},{2,4},{4,6},{6,8},{8,10},{10,12},{12,14},{14,0},{1,3},{3,5},... | collective-permute-start | bytes 589832 | tf_op jit(solution)/shard_map/panels/ppermute | solution.py:37
  50.3 5.8 %collective-permute-start.2 = (bf16[2,3,64,256]{3,2,0,1:T(8,128)(2,1)}, bf16[2,3,64,256]{3,2,0,1:T(8,128)(2,1)S(1)}, u32[]{:S(2)}, u32[]{:S(2)}) collective-permute-start(bf16[2,3,64,256]{3,2,0,1:T(8,128)(2,1)} %pad_maximum_fusion.2), channel_id=1, source_target_pairs={{0,14},{2,0},{4,2},{6,4},{8,6},{10,8},{12,10},{14,12},{1,15},{3,1}... | collective-permute-start | bytes 589832 | tf_op jit(solution)/shard_map/panels/ppermute | solution.py:40
  51.1 27.7 %copy-start.3 = (bf16[3,1024,256]{2,1,0:T(8,128)(2,1)S(1)}, bf16[3,1024,256]{2,1,0:T(8,128)(2,1)}, u32[]{:S(2)}) copy-start(bf16[3,1024,256]{2,1,0:T(8,128)(2,1)} %param.6) | copy-start | bytes 4718596
  56.1 6.6 %collective-permute-start.3 = (bf16[2,3,64,256]{3,2,0,1:T(8,128)(2,1)}, bf16[2,3,64,256]{3,2,0,1:T(8,128)(2,1)S(1)}, u32[]{:S(2)}, u32[]{:S(2)}) collective-permute-start(bf16[2,3,64,256]{3,2,0,1:T(8,128)(2,1)} %collective-permute-done.1), channel_id=1, source_target_pairs={{0,2},{2,4},{4,6},{6,8},{8,10},{10,12},{12,14},{14,0},{1,3},{3,5},... | collective-permute-start | bytes 589832 | tf_op jit(solution)/shard_map/panels/ppermute | solution.py:37
  56.1 6.6 %collective-permute-start.4 = (bf16[2,3,64,256]{3,2,0,1:T(8,128)(2,1)S(1)}, bf16[2,3,64,256]{3,2,0,1:T(8,128)(2,1)S(1)}, u32[]{:S(2)}, u32[]{:S(2)}) collective-permute-start(bf16[2,3,64,256]{3,2,0,1:T(8,128)(2,1)S(1)} %collective-permute-done.2), channel_id=1, source_target_pairs={{0,14},{2,0},{4,2},{6,4},{8,6},{10,8},{12,10},{14,12},{1,15},{3,1}... | collective-permute-start | bytes 589832 | tf_op jit(solution)/shard_map/panels/ppermute | solution.py:40
  62.7 5.7 %collective-permute-start.5 = (bf16[2,3,64,256]{3,2,0,1:T(8,128)(2,1)S(1)}, bf16[2,3,64,256]{3,2,0,1:T(8,128)(2,1)S(1)}, u32[]{:S(2)}, u32[]{:S(2)}) collective-permute-start(bf16[2,3,64,256]{3,2,0,1:T(8,128)(2,1)S(1)} %collective-permute-done.3), channel_id=1, source_target_pairs={{0,2},{2,4},{4,6},{6,8},{8,10},{10,12},{12,14},{14,0},{1,3},{3,5},... | collective-permute-start | bytes 589832 | tf_op jit(solution)/shard_map/panels/ppermute | solution.py:37
  62.7 5.8 %collective-permute-start.6 = (bf16[2,3,64,256]{3,2,0,1:T(8,128)(2,1)S(1)}, bf16[2,3,64,256]{3,2,0,1:T(8,128)(2,1)S(1)}, u32[]{:S(2)}, u32[]{:S(2)}) collective-permute-start(bf16[2,3,64,256]{3,2,0,1:T(8,128)(2,1)S(1)} %collective-permute-done.4), channel_id=1, source_target_pairs={{0,14},{2,0},{4,2},{6,4},{8,6},{10,8},{12,10},{14,12},{1,15},{3,1}... | collective-permute-start | bytes 589832 | tf_op jit(solution)/shard_map/panels/ppermute | solution.py:40
  68.4 5.7 %collective-permute-start.7 = (bf16[2,3,64,256]{3,2,0,1:T(8,128)(2,1)S(1)}, bf16[2,3,64,256]{3,2,0,1:T(8,128)(2,1)S(1)}, u32[]{:S(2)}, u32[]{:S(2)}) collective-permute-start(bf16[2,3,64,256]{3,2,0,1:T(8,128)(2,1)S(1)} %collective-permute-done.5), channel_id=1, source_target_pairs={{0,2},{2,4},{4,6},{6,8},{8,10},{10,12},{12,14},{14,0},{1,3},{3,5},... | collective-permute-start | bytes 589832 | tf_op jit(solution)/shard_map/panels/ppermute | solution.py:37
  74.1 8.4 %copy-start = (bf16[8,2,3,64,256]{4,3,0,1,2:T(8,128)(2,1)}, bf16[8,2,3,64,256]{4,3,0,1,2:T(8,128)(2,1)S(1)}, u32[]{:S(2)}) copy-start(bf16[8,2,3,64,256]{4,3,0,1,2:T(8,128)(2,1)S(1)} %bitcast_dynamic-update-slice_fusion.7) | copy-start | bytes 4718596
  74.2 11.0 %collective-permute-start.8 = (bf16[3,1024,256]{2,1,0:T(8,128)(2,1)S(1)}, bf16[3,1024,256]{2,1,0:T(8,128)(2,1)}, u32[]{:S(2)}, u32[]{:S(2)}) collective-permute-start(bf16[3,1024,256]{2,1,0:T(8,128)(2,1)S(1)} %bitcast.99), channel_id=1, source_target_pairs={{0,1},{1,0},{2,3},{3,2},{4,5},{5,4},{6,7},{7,6},{8,9},{9,8},{10,11... | collective-permute-start | bytes 4718600 | tf_op jit(solution)/shard_map/panels/ppermute | solution.py:15
  78.9 3.7 %copy-start.4 = (bf16[2048,1024]{1,0:T(8,128)(2,1)S(1)}, bf16[2048,1024]{1,0:T(8,128)(2,1)}, u32[]{:S(2)}) copy-start(bf16[2048,1024]{1,0:T(8,128)(2,1)} %param.5) | copy-start | bytes 12582916
  83.9 1.4 copy-start.1
  89.4 0.9 copy-start.2
  91.0 1.9 %collective-permute-start.9 = (f32[384,256]{1,0:T(8,128)}, f32[384,256]{1,0:T(8,128)S(1)}, u32[]{:S(2)}, u32[]{:S(2)}) collective-permute-start(f32[384,256]{1,0:T(8,128)} %constant_dynamic-slice_fusion.1), channel_id=1, source_target_pairs={{0,1},{1,0},{2,3},{3,2},{4,5},{5,4},{6,7},{7,6},{8,9},{9,8},{10,11... | collective-permute-start | bytes 1179656 | tf_op jit(solution)/shard_map/sum/ppermute | solution.py:15
  94.7 13.0 %all-to-all-start.1 = ((f32[8,48,256]{2,1,0:T(8,128)}), f32[8,48,256]{2,1,0:T(8,128)S(1)}, u32[]{:S(2)}, u32[]{:S(2)}) async-start(f32[8,48,256]{2,1,0:T(8,128)} %bitcast.103), calls=%async_computation.1 | async-start | bytes 786432 | tf_op jit(solution)/shard_map/sum/all_to_all | solution.py:77
  109.1 4.2 %collective-permute-start.10 = (f32[24,256]{1,0:T(8,128)S(1)}, f32[24,256]{1,0:T(8,128)S(1)}, u32[]{:S(2)}, u32[]{:S(2)}) collective-permute-start(f32[24,256]{1,0:T(8,128)S(1)} %constant_dynamic-slice_fusion), channel_id=1, source_target_pairs={{0,16},{16,0},{1,17},{17,1},{2,18},{18,2},{3,19},{19,3},{4,20},{20... | collective-permute-start | bytes 73736 | tf_op jit(solution)/shard_map/sum/ppermute | solution.py:15
  114.7 12.0 %all-to-all-start.2 = ((f32[8,24,256]{2,1,0:T(8,128)}), f32[8,24,256]{2,1,0:T(8,128)S(1)}, u32[]{:S(2)}, u32[]{:S(2)}) async-start(f32[8,24,256]{2,1,0:T(8,128)} %broadcast_in_dim.54), calls=%async_computation.2 | async-start | bytes 393216 | tf_op jit(solution)/shard_map/sum/all_to_all | solution.py:46

commit v2 on v0

v2 whole, which is shorter than its diff:
```python
import functools

import jax
import jax.numpy as jnp
from jax import lax
from jax.experimental import pallas as pl
from jax.experimental.pallas import tpu as pltpu
from jax.sharding import Mesh
from jax.sharding import PartitionSpec as P

ROW = ("yl", "x")
COL = ("yh", "z", "core")
F32 = jnp.float32
BF16 = jnp.bfloat16
RING = 8
BLOCK = 256
LIMIT = 40 * 1024 * 1024


def swap(x, axis):
    return lax.ppermute(x, axis, [(0, 1), (1, 0)])


def shift(x, by):
    return lax.ppermute(x, "z", [(i, (i + by) % RING) for i in range(RING)])


def params():
    return pltpu.CompilerParams(vmem_limit_bytes=LIMIT)


def call(kernel, grid, in_specs, out_specs, out_shape, flops, moved):
    spec = pltpu.PrefetchScalarGridSpec(num_scalar_prefetch=1, grid=grid, in_specs=in_specs, out_specs=out_specs)
    return pl.pallas_call(
        kernel,
        grid_spec=spec,
        out_shape=out_shape,
        compiler_params=params(),
        cost_estimate=pl.CostEstimate(flops=flops, bytes_accessed=moved, transcendentals=0),
    )


def project_kernel(at_ref, gradient_ref, panels_ref, out_ref):
    for k in range(panels_ref.shape[0]):
        out_ref[k] = jnp.dot(gradient_ref[...], panels_ref[k], preferred_element_type=F32)


def project(gradient, panels, half):
    count, width, vec = panels.shape
    rows = gradient.shape[0] // 2
    steps = rows // BLOCK
    return call(
        project_kernel,
        (steps,),
        [
            pl.BlockSpec((BLOCK, width), lambda i, at: (at[0] * steps + i, 0)),
            pl.BlockSpec((count, width, vec), lambda i, at: (0, 0, 0)),
        ],
        pl.BlockSpec((count, BLOCK, vec), lambda i, at: (0, i, 0)),
        jax.ShapeDtypeStruct((count, rows, vec), F32),
        2 * rows * width * vec * count,
        2 * rows * width + 2 * count * width * vec + 4 * count * rows * vec,
    )(half[None], gradient, panels)


def split_kernel(own_ref, other_ref, out_ref):
    vec = own_ref.shape[2]
    total = (own_ref[0] + other_ref[0]).T
    high = total.astype(BF16)
    out_ref[0, :vec] = high
    out_ref[0, vec:] = (total - high.astype(F32)).astype(BF16)


def split(own, other):
    count, rows, vec = own.shape
    return pl.pallas_call(
        split_kernel,
        grid=(count,),
        in_specs=[pl.BlockSpec((1, rows, vec), lambda k: (k, 0, 0))] * 2,
        out_specs=pl.BlockSpec((1, 2 * vec, rows), lambda k: (k, 0, 0)),
        out_shape=jax.ShapeDtypeStruct((count, 2 * vec, rows), BF16),
        compiler_params=params(),
        cost_estimate=pl.CostEstimate(flops=3 * own.size, bytes_accessed=12 * own.size, transcendentals=0),
    )(own, other)


def couple_kernel(at_ref, terms_ref, fetched_ref, keep_ref, send_ref, total_ref):
    count, rows, vec = fetched_ref.shape
    for k in range(count):
        both = jnp.dot(terms_ref[k], fetched_ref[k], preferred_element_type=F32)
        total_ref[k * vec : (k + 1) * vec] = both[:vec] + both[vec:]
    size = keep_ref.shape[0]
    at = pl.multiple_of(at_ref[0] * size, size)
    other = pl.multiple_of((1 - at_ref[0]) * size, size)
    keep_ref[...] = total_ref[pl.ds(at, size)]
    send_ref[...] = total_ref[pl.ds(other, size)]


def couple(terms, fetched, here):
    count, rows, vec = fetched.shape
    size = count * vec // 2
    half = jax.ShapeDtypeStruct((size, vec), F32)
    whole = pl.BlockSpec(memory_space=pltpu.VMEM)
    return pl.pallas_call(
        couple_kernel,
        in_specs=[pl.BlockSpec(memory_space=pltpu.SMEM), whole, whole],
        out_specs=[whole, whole],
        out_shape=[half, half],
        scratch_shapes=[pltpu.VMEM((count * vec, vec), F32)],
        compiler_params=params(),
        cost_estimate=pl.CostEstimate(flops=4 * fetched.size * vec, bytes_accessed=8 * fetched.size, transcendentals=0),
    )(here[None], terms, fetched)


def apply_kernel(steps, at_ref, own_ref, other_ref, scaled_ref, panels_ref, out_ref):
    def run(fetched_ref):
        total = None
        for k in range(panels_ref.shape[0]):
            rotated = lax.dot_general(fetched_ref[k], scaled_ref[k], (((1,), (1,)), ((), ())), preferred_element_type=F32)
            term = lax.dot_general(rotated.astype(BF16), panels_ref[k], (((1,), (1,)), ((), ())), preferred_element_type=F32)
            total = term if total is None else total + term
        out_ref[...] = total.astype(BF16)

    own = pl.program_id(0) < steps
    pl.when(own)(lambda: run(own_ref))
    pl.when(jnp.logical_not(own))(lambda: run(other_ref))


def apply(own, other, scaled, panels, here):
    count, rows, vec = own.shape
    width = panels.shape[1]
    steps = rows // BLOCK
    return call(
        functools.partial(apply_kernel, steps),
        (2 * steps,),
        [
            pl.BlockSpec((count, BLOCK, vec), lambda i, at: (0, jnp.minimum(i, steps - 1), 0)),
            pl.BlockSpec((count, BLOCK, vec), lambda i, at: (0, jnp.maximum(i - steps, 0), 0)),
            pl.BlockSpec((count, vec, vec), lambda i, at: (0, 0, 0)),
            pl.BlockSpec((count, width, vec), lambda i, at: (0, 0, 0)),
        ],
        pl.BlockSpec((BLOCK, width), lambda i, at: (jnp.where(i < steps, at[0] * steps + i, (1 - at[0]) * steps + i - steps), 0)),
        jax.ShapeDtypeStruct((2 * rows, width), BF16),
        4 * count * rows * vec * (vec + width),
        4 * rows * width + 4 * count * rows * vec,
    )(here[None], own, other, scaled, panels)


def ring(x):
    here = lax.axis_index("z")
    whole = jnp.zeros(x.shape[:1] + (RING,) + x.shape[1:], x.dtype)
    whole = lax.dynamic_update_index_in_dim(whole, x, here, 1)
    up = down = x
    for step in range(1, RING // 2 + 1):
        up = shift(up, 1)
        whole = lax.dynamic_update_index_in_dim(whole, up, (here + RING - step) % RING, 1)
        if step < RING - step:
            down = shift(down, -1)
            whole = lax.dynamic_update_index_in_dim(whole, down, (here + step) % RING, 1)
    return whole


def fetch(panel, owners):
    core, high, here = (lax.axis_index(a) for a in ("core", "yh", "z"))
    rows, vec = panel.shape
    half = rows // 2
    own = lax.dynamic_slice_in_dim(panel, core * half, half, 0)
    other = swap(lax.dynamic_slice_in_dim(panel, (1 - core) * half, half, 0), "core")
    owners = owners[:, None, None]
    of_core, of_ring, of_high = owners % 2, owners // 2 % RING, owners // (2 * RING)
    slots = jnp.where((of_core == core)[..., None], own.reshape(1, RING, half // RING, vec), other.reshape(1, RING, half // RING, vec))
    owned = of_ring == here

    def piece(index):
        return lax.dynamic_index_in_dim(slots, (index + RING) % RING, 1, keepdims=False)

    reach = RING // 2
    up, down = piece(here + reach - 1), piece(here - reach)
    for step in range(1, reach + 1):
        down = jnp.where(owned, piece(here - reach + step), shift(down, -1))
        if step < reach:
            up = jnp.where(owned, piece(here + reach - 1 - step), shift(up, 1))
    mine = jnp.where((here - of_ring + RING) % RING < reach, up, down)
    mine = jnp.where(of_high == high, mine, swap(mine, "yh"))
    return ring(mine).reshape(owners.shape[0], half, vec)


def body(gradient, in_panels, out_pool, eigenvalues, owners):
    core = lax.axis_index("core")
    count, _, vec = in_panels.shape

    with jax.named_scope("panels"):
        own = fetch(out_pool[0], owners)
        other = swap(own, "core")

    with jax.named_scope("projection"):
        sent = swap(project(gradient, in_panels, 1 - core), "core")
        terms = split(project(gradient, in_panels, core), sent)

    with jax.named_scope("coupling"):
        damping = 0.1 * jnp.mean(eigenvalues, axis=(1, 2), keepdims=True)
        below = jnp.swapaxes(eigenvalues + damping, 1, 2).reshape(count * vec, vec)
        keep, send = couple(terms, own, core)
        part = keep + swap(send, "core")
        part = jnp.sum(lax.all_to_all(part.reshape(8, -1, vec), ROW, 0, 0), axis=0)
        copies = jnp.broadcast_to(part.reshape(2, 1, -1, vec), (2, RING, part.shape[0] // 2, vec))
        total = jnp.sum(lax.all_to_all(copies.reshape(2 * RING, -1, vec), ("yh", "z"), 0, 0), axis=0)
        size = total.shape[0]
        at = (core * 8 + lax.axis_index(ROW)) * 2 + lax.axis_index("yh")
        scaled = (total / lax.dynamic_slice_in_dim(below, at * size, size, 0)).astype(BF16)
        copies = jnp.broadcast_to(scaled[None], (32,) + scaled.shape)
        scaled = lax.all_to_all(copies, ("core",) + ROW + ("yh",), 0, 0).reshape(count, vec, vec)

    with jax.named_scope("output"):
        return apply(own, other, scaled, in_panels, core)


def solution(mesh):
    fine = Mesh(mesh.devices.reshape(2, 4, 2, 8, 2), ROW + COL)
    return jax.shard_map(
        body,
        mesh=fine,
        in_specs=(P(ROW, COL), P(None, COL, None), P(COL, ROW, None), P(), P()),
        out_specs=P(ROW, COL),
        check_vma=False,
    )
```

time: 581 us -> 165 us (0.28)
  waiting for transfers between devices: 520 us -> 63.9 us
  starting transfers between devices: 0.04 us -> 54.5 us
  matrix products: 37.7 us -> 0 us
  Pallas kernels: 0 us -> 19.9 us
  between operations: 17.2 us -> 0.2 us
  other arithmetic: 3.64 us -> 14.2 us
  local copies, waits for them, and re-layouts: 1.44 us -> 10.7 us
    psum x2 -> x0, waiting for transfers between devices: 520 us -> none  [the longest x1 270 us: from_root(): return lax.psum(jnp.where(mine, x, jnp.zeros_like(x)), axis)]
    ppermute x0 -> x19, waiting for transfers between devices: none -> 38.9 us  [the longest x14 33 us: shift(): return lax.ppermute(x, 'z', [(i, (i + by) % RING) for i in range(RING)])]
    ppermute x0 -> x19, starting transfers between devices: none -> 37.8 us  [the longest x14 21.5 us: shift(): return lax.ppermute(x, 'z', [(i, (i + by) % RING) for i in range(RING)])]
    dot_general x9 -> x0, matrix products: 37.7 us -> none  [the longest x3 20.8 us: body(): jnp.dot(rotated, basis.T, preferred_element_type=jnp.float32)]
    all_to_all x0 -> x3, waiting for transfers between devices: none -> 25 us  [the longest x1 10.3 us: body(): lax.all_to_all(copies, ('core',) + ROW + ('yh',), 0, 0)]
    pallas_call x0 -> x5, Pallas kernels: none -> 19.9 us  [the longest x1 9.73 us: apply(): call(functools.partial(apply_kernel, steps), (2 * steps,), [pl.BlockSpec(...]
    all_to_all x0 -> x3, starting transfers between devices: none -> 16.8 us  [the longest x1 6.46 us: body(): lax.all_to_all(copies, ('core',) + ROW + ('yh',), 0, 0)]
    unnamed x20 -> x11, local copies, waits for them, and re-layouts: 0.04 us -> 6.67 us
  transfers between devices with their start and end apart: 2 -> 22, of which waited for: 2 -> 13; matrix products, arithmetic and copies ran while one was open for 2% -> 11% of each run, Pallas kernels for 0% -> 4%
where the time goes in v2:
time: 165 us; the launch traced here: 164 us
  waiting for transfers between devices  63.9 us (39%)
  starting transfers between devices  54.5 us (33%)
  Pallas kernels  19.9 us (12%)
  other arithmetic  14.2 us (9%)
  local copies, waits for them, and re-layouts  10.7 us (6%)
    ppermute x14, waiting for transfers between devices, shift(): return lax.ppermute(x, 'z', [(i, (i + by) % RING) for i in range(RING)])  33 us
    ppermute x14, starting transfers between devices, shift(): return lax.ppermute(x, 'z', [(i, (i + by) % RING) for i in range(RING)])  21.5 us
    ppermute x5, starting transfers between devices, swap(): return lax.ppermute(x, axis, [(0, 1), (1, 0)])  16.3 us
    all_to_all x1, waiting for transfers between devices, body(): lax.all_to_all(copies, ('core',) + ROW + ('yh',), 0, 0)  10.3 us
    pallas_call x1, Pallas kernels, apply(): call(functools.partial(apply_kernel, steps), (2 * steps,), [pl.BlockSpec(...  9.73 us
    all_to_all x1, waiting for transfers between devices, body(): part = jnp.sum(lax.all_to_all(part.reshape(8, -1, vec), ROW, 0, 0), axis=0)  8.18 us
    unnamed x11, local copies, waits for them, and re-layouts  6.67 us
    all_to_all x1, waiting for transfers between devices, body(): lax.all_to_all(copies.reshape(2 * RING, -1, vec), ('yh', 'z'), 0, 0)  6.53 us
  transfers between devices with their start and end apart: 22, of which 13 were waited for; matrix products, arithmetic and copies ran while one was open for 11% of the time, Pallas kernels for 4%

profile of v2, /device:TPU:1, one launch (start us, length us, event | category | flops | bytes accessed | tf_op | source)
XLA Modules:
  0.0 163.5 jit_solution(18179248735764542208)
XLA Ops:
  0.0 1.3 constant_dynamic-slice_fusion
  1.3 3.3 %collective-permute-start = (bf16[1024,256]{1,0:T(8,128)(2,1)S(1)}, bf16[1024,256]{1,0:T(8,128)(2,1)S(1)}, u32[]{:S(2)}, u32[]{:S(2)}) collective-permute-start(bf16[1024,256]{1,0:T(8,128)(2,1)S(1)} %get-tuple-element.18), channel_id=1, source_target_pairs={{0,1},{1,0},{2,3},{3,2},{4,5},{5,4},{6,7},{7,6},{8,9},{9,8},{10,11... | collective-permute-start | bytes 1572872 | tf_op jit(solution)/shard_map/panels/ppermute | solution.py:21
  4.6 1.5 collective-permute-done
  6.4 3.9 %collective-permute-start.4 = (bf16[3,128,256]{2,1,0:T(8,128)(2,1)S(1)}, bf16[3,128,256]{2,1,0:T(8,128)(2,1)S(1)}, u32[]{:S(2)}, u32[]{:S(2)}) collective-permute-start(bf16[3,128,256]{2,1,0:T(8,128)(2,1)S(1)} %get-tuple-element.15), channel_id=1, source_target_pairs={{0,14},{2,0},{4,2},{6,4},{8,6},{10,8},{12,10},{14,12},{1,15},{3,1}... | collective-permute-start | bytes 589832 | tf_op jit(solution)/shard_map/panels/ppermute | solution.py:25
  10.3 3.9 %collective-permute-done.4 = bf16[3,128,256]{2,1,0:T(8,128)(2,1)S(1)} collective-permute-done((bf16[3,128,256]{2,1,0:T(8,128)(2,1)S(1)}, bf16[3,128,256]{2,1,0:T(8,128)(2,1)S(1)}, u32[]{:S(2)}, u32[]{:S(2)}) %collective-permute-start.4) | collective-permute-done | bytes 196640 | tf_op jit(solution)/shard_map/panels/ppermute | solution.py:25
  14.2 0.8 bitcast_select_fusion
  15.0 3.4 %collective-permute-start.5 = (bf16[3,128,256]{2,1,0:T(8,128)(2,1)}, bf16[3,128,256]{2,1,0:T(8,128)(2,1)}, u32[]{:S(2)}, u32[]{:S(2)}) collective-permute-start(bf16[3,128,256]{2,1,0:T(8,128)(2,1)} %bitcast_select_fusion), channel_id=1, source_target_pairs={{0,14},{2,0},{4,2},{6,4},{8,6},{10,8},{12,10},{14,12},{1,15},{3,1}... | collective-permute-start | bytes 589832 | tf_op jit(solution)/shard_map/panels/ppermute | solution.py:25
  18.4 3.3 %collective-permute-done.5 = bf16[3,128,256]{2,1,0:T(8,128)(2,1)} collective-permute-done((bf16[3,128,256]{2,1,0:T(8,128)(2,1)}, bf16[3,128,256]{2,1,0:T(8,128)(2,1)}, u32[]{:S(2)}, u32[]{:S(2)}) %collective-permute-start.5) | collective-permute-done | bytes 196640 | tf_op jit(solution)/shard_map/panels/ppermute | solution.py:25
  21.7 1.7 %bitcast_select_fusion.1 = bf16[3,128,256]{2,1,0:T(8,128)(2,1)} fusion(bf16[3,128,256]{2,1,0:T(8,128)(2,1)} %collective-permute-done.5, bf16[3,8,128,256]{3,2,0,1:T(8,128)(2,1)S(1)} %broadcast_select_fusion, s32[]{:T(128)S(6)} %select_n.190, pred[3]{0:T(512)(128)(4,1)S(1)} %broadcast_compare_fusion), kind=kLoop, calls=%fused_computation.12 | loop fusion | flops 98304 | bytes 589831 | tf_op jit(solution)/shard_map/panels/jit(_where)/select_n | solution.py:180
  23.4 3.4 %collective-permute-start.6 = (bf16[3,128,256]{2,1,0:T(8,128)(2,1)}, bf16[3,128,256]{2,1,0:T(8,128)(2,1)}, u32[]{:S(2)}, u32[]{:S(2)}) collective-permute-start(bf16[3,128,256]{2,1,0:T(8,128)(2,1)} %bitcast_select_fusion.1), channel_id=1, source_target_pairs={{0,14},{2,0},{4,2},{6,4},{8,6},{10,8},{12,10},{14,12},{1,15},{3,1}... | collective-permute-start | bytes 589832 | tf_op jit(solution)/shard_map/panels/ppermute | solution.py:25
  26.8 2.2 %copy-done = bf16[2048,1024]{1,0:T(8,128)(2,1)S(1)} copy-done((bf16[2048,1024]{1,0:T(8,128)(2,1)S(1)}, bf16[2048,1024]{1,0:T(8,128)(2,1)}, u32[]{:S(2)}) %copy-start) | copy-done | bytes 4194328
  29.0 3.5 %projection.4 = f32[3,1024,256]{2,1,0:T(8,128)} custom-call(s32[1]{0:T(128)} %bitcast.28.at_ref, bf16[2048,1024]{1,0:T(8,128)(2,1)S(1)} %copy-done, bf16[3,1024,256]{2,1,0:T(8,128)(2,1)S(1)} %copy-done.2), custom_call_target="tpu_custom_call" | custom-call | flops 1610612736 | bytes 6815744 | tf_op jit(solution)/shard_map/projection/pallas_call | solution.py:52
  32.5 2.4 %collective-permute-start.17 = (f32[3,1024,256]{2,1,0:T(8,128)}, f32[3,1024,256]{2,1,0:T(8,128)}, u32[]{:S(2)}, u32[]{:S(2)}) collective-permute-start(f32[3,1024,256]{2,1,0:T(8,128)} %projection.4), channel_id=1, source_target_pairs={{0,1},{1,0},{2,3},{3,2},{4,5},{5,4},{6,7},{7,6},{8,9},{9,8},{10,11... | collective-permute-start | bytes 9437192 | tf_op jit(solution)/shard_map/projection/ppermute | solution.py:21
  34.9 1.7 %bitcast_select_fusion.2 = (bf16[3,128,256]{2,1,0:T(8,128)(2,1)S(1)}, bf16[3,128,256]{2,1,0:T(8,128)(2,1)}) fusion(bf16[3,128,256]{2,1,0:T(8,128)(2,1)} %collective-permute-done.6, bf16[3,8,128,256]{3,2,0,1:T(8,128)(2,1)S(1)} %broadcast_select_fusion, s32[]{:T(128)S(6)} %select_n.188, pred[3]{0:T(512)(128)(4,1)S(1)} %broadcast_compare_fusion, ...), kind=kLoop, calls=%fused_computation.13 | loop fusion | flops 196608 | bytes 1179659 | tf_op jit(solution)/shard_map/panels/jit(_where)/select_n | solution.py:180
  36.6 2.7 %collective-permute-start.7 = (bf16[3,128,256]{2,1,0:T(8,128)(2,1)S(1)}, bf16[3,128,256]{2,1,0:T(8,128)(2,1)S(1)}, u32[]{:S(2)}, u32[]{:S(2)}) collective-permute-start(bf16[3,128,256]{2,1,0:T(8,128)(2,1)S(1)} %get-tuple-element.13), channel_id=1, source_target_pairs={{0,14},{2,0},{4,2},{6,4},{8,6},{10,8},{12,10},{14,12},{1,15},{3,1}... | collective-permute-start | bytes 589832 | tf_op jit(solution)/shard_map/panels/ppermute | solution.py:25
  39.3 5.4 %collective-permute-done.2 = bf16[3,128,256]{2,1,0:T(8,128)(2,1)} collective-permute-done((bf16[3,128,256]{2,1,0:T(8,128)(2,1)}, bf16[3,128,256]{2,1,0:T(8,128)(2,1)}, u32[]{:S(2)}, u32[]{:S(2)}) %collective-permute-start.2) | collective-permute-done | bytes 196640 | tf_op jit(solution)/shard_map/panels/ppermute | solution.py:25
  44.6 1.7 %bitcast_select_fusion.4 = bf16[3,128,256]{2,1,0:T(8,128)(2,1)} fusion(bf16[3,128,256]{2,1,0:T(8,128)(2,1)} %collective-permute-done.2, bf16[3,8,128,256]{3,2,0,1:T(8,128)(2,1)S(1)} %broadcast_select_fusion, s32[]{:T(128)S(6)} %select_n.179, pred[3]{0:T(512)(128)(4,1)S(1)} %broadcast_compare_fusion), kind=kLoop, calls=%fused_computation.15 | loop fusion | flops 98304 | bytes 589831 | tf_op jit(solution)/shard_map/panels/jit(_where)/select_n | solution.py:182
  46.3 7.2 %collective-permute-done.3 = bf16[3,128,256]{2,1,0:T(8,128)(2,1)} collective-permute-done((bf16[3,128,256]{2,1,0:T(8,128)(2,1)}, bf16[3,128,256]{2,1,0:T(8,128)(2,1)}, u32[]{:S(2)}, u32[]{:S(2)}) %collective-permute-start.3) | collective-permute-done | bytes 196640 | tf_op jit(solution)/shard_map/panels/ppermute | solution.py:25
  53.5 1.1 fusion
  54.6 3.0 %collective-permute-start.8 = (bf16[3,128,256]{2,1,0:T(8,128)(2,1)S(1)}, bf16[3,128,256]{2,1,0:T(8,128)(2,1)S(1)}, u32[]{:S(2)}, u32[]{:S(2)}) collective-permute-start(bf16[3,128,256]{2,1,0:T(8,128)(2,1)S(1)} %fusion), channel_id=1, source_target_pairs={{0,16},{16,0},{1,17},{17,1},{2,18},{18,2},{3,19},{19,3},{4,20},{20... | collective-permute-start | bytes 589832 | tf_op jit(solution)/shard_map/panels/ppermute | solution.py:21
  57.6 3.1 %collective-permute-done.8 = bf16[3,128,256]{2,1,0:T(8,128)(2,1)S(1)} collective-permute-done((bf16[3,128,256]{2,1,0:T(8,128)(2,1)S(1)}, bf16[3,128,256]{2,1,0:T(8,128)(2,1)S(1)}, u32[]{:S(2)}, u32[]{:S(2)}) %collective-permute-start.8) | collective-permute-done | bytes 196640 | tf_op jit(solution)/shard_map/panels/ppermute | solution.py:21
  60.9 0.8 bitcast_dynamic-update-slice_fusion.6
  61.7 2.7 %collective-permute-start.10 = (bf16[3,128,256]{2,1,0:T(8,128)(2,1)}, bf16[3,128,256]{2,1,0:T(8,128)(2,1)S(1)}, u32[]{:S(2)}, u32[]{:S(2)}) collective-permute-start(bf16[3,128,256]{2,1,0:T(8,128)(2,1)} %get-tuple-element.10), channel_id=1, source_target_pairs={{0,14},{2,0},{4,2},{6,4},{8,6},{10,8},{12,10},{14,12},{1,15},{3,1}... | collective-permute-start | bytes 589832 | tf_op jit(solution)/shard_map/panels/ppermute | solution.py:25
  64.4 2.2 %copy-done.1 = bf16[2048,1024]{1,0:T(8,128)(2,1)S(1)} copy-done((bf16[2048,1024]{1,0:T(8,128)(2,1)S(1)}, bf16[2048,1024]{1,0:T(8,128)(2,1)}, u32[]{:S(2)}) %copy-start.1) | copy-done | bytes 4194328
  66.6 2.5 %projection.3.own_ref = f32[3,1024,256]{2,1,0:T(8,128)S(1)} custom-call(s32[1]{0:T(128)} %bitcast.at_ref, bf16[2048,1024]{1,0:T(8,128)(2,1)S(1)} %copy-done.1, bf16[3,1024,256]{2,1,0:T(8,128)(2,1)S(1)} %copy-done.2), custom_call_target="tpu_custom_call" | custom-call | flops 1610612736 | bytes 6815744 | tf_op jit(solution)/shard_map/projection/pallas_call | solution.py:52
  69.2 2.7 %collective-permute-start.12 = (bf16[3,128,256]{2,1,0:T(8,128)(2,1)S(1)}, bf16[3,128,256]{2,1,0:T(8,128)(2,1)S(1)}, u32[]{:S(2)}, u32[]{:S(2)}) collective-permute-start(bf16[3,128,256]{2,1,0:T(8,128)(2,1)S(1)} %collective-permute-done.10), channel_id=1, source_target_pairs={{0,14},{2,0},{4,2},{6,4},{8,6},{10,8},{12,10},{14,12},{1,15},{3,1}... | collective-permute-start | bytes 589832 | tf_op jit(solution)/shard_map/panels/ppermute | solution.py:25
  71.9 3.0 %collective-permute-done.11 = bf16[3,128,256]{2,1,0:T(8,128)(2,1)S(1)} collective-permute-done((bf16[3,128,256]{2,1,0:T(8,128)(2,1)S(1)}, bf16[3,128,256]{2,1,0:T(8,128)(2,1)S(1)}, u32[]{:S(2)}, u32[]{:S(2)}) %collective-permute-start.11) | collective-permute-done | bytes 196640 | tf_op jit(solution)/shard_map/panels/ppermute | solution.py:25
  74.9 2.7 %collective-permute-start.14 = (bf16[3,128,256]{2,1,0:T(8,128)(2,1)S(1)}, bf16[3,128,256]{2,1,0:T(8,128)(2,1)S(1)}, u32[]{:S(2)}, u32[]{:S(2)}) collective-permute-start(bf16[3,128,256]{2,1,0:T(8,128)(2,1)S(1)} %collective-permute-done.12), channel_id=1, source_target_pairs={{0,14},{2,0},{4,2},{6,4},{8,6},{10,8},{12,10},{14,12},{1,15},{3,1}... | collective-permute-start | bytes 589832 | tf_op jit(solution)/shard_map/panels/ppermute | solution.py:25
  77.6 3.2 %collective-permute-done.13 = bf16[3,128,256]{2,1,0:T(8,128)(2,1)S(1)} collective-permute-done((bf16[3,128,256]{2,1,0:T(8,128)(2,1)S(1)}, bf16[3,128,256]{2,1,0:T(8,128)(2,1)S(1)}, u32[]{:S(2)}, u32[]{:S(2)}) %collective-permute-start.13) | collective-permute-done | bytes 196640 | tf_op jit(solution)/shard_map/panels/ppermute | solution.py:25
  80.9 7.0 %collective-permute-done.15 = bf16[3,128,256]{2,1,0:T(8,128)(2,1)S(1)} collective-permute-done((bf16[3,128,256]{2,1,0:T(8,128)(2,1)S(1)}, bf16[3,128,256]{2,1,0:T(8,128)(2,1)S(1)}, u32[]{:S(2)}, u32[]{:S(2)}) %collective-permute-start.15) | collective-permute-done | bytes 196640 | tf_op jit(solution)/shard_map/panels/ppermute | solution.py:25
  87.9 3.2 %projection.5.terms_ref = bf16[3,512,1024]{2,1,0:T(8,128)(2,1)S(1)} custom-call(f32[3,1024,256]{2,1,0:T(8,128)S(1)} %projection.3.own_ref, f32[3,1024,256]{2,1,0:T(8,128)} %collective-permute-done.17.other_ref), custom_call_target="tpu_custom_call" | custom-call | flops 2359296 | bytes 9437184 | tf_op jit(solution)/shard_map/projection/pallas_call | solution.py:76
  91.1 1.0 coupling.1
  92.2 6.9 %collective-permute-start.18 = (f32[384,256]{1,0:T(8,128)S(1)}, f32[384,256]{1,0:T(8,128)S(1)}, u32[]{:S(2)}, u32[]{:S(2)}) collective-permute-start(f32[384,256]{1,0:T(8,128)S(1)} %get-tuple-element.8), channel_id=1, source_target_pairs={{0,1},{1,0},{2,3},{3,2},{4,5},{5,4},{6,7},{7,6},{8,9},{9,8},{10,11... | collective-permute-start | bytes 1179656 | tf_op jit(solution)/shard_map/coupling/ppermute | solution.py:21
  99.0 1.3 collective-permute-done.18
  100.4 0.8 add.267
  101.2 5.0 %all-to-all-start = ((f32[8,48,256]{2,1,0:T(8,128)}), f32[8,48,256]{2,1,0:T(8,128)S(1)}, u32[]{:S(2)}, u32[]{:S(2)}) async-start(f32[8,48,256]{2,1,0:T(8,128)} %bitcast.71), calls=%async_computation | async-start | bytes 786432 | tf_op jit(solution)/shard_map/coupling/all_to_all | solution.py:205
  106.9 8.2 %all-to-all-done = f32[8,48,256]{2,1,0:T(8,128)S(1)} async-done(((f32[8,48,256]{2,1,0:T(8,128)}), f32[8,48,256]{2,1,0:T(8,128)S(1)}, u32[]{:S(2)}, u32[]{:S(2)}) %all-to-all-start) | async-done | bytes 393248 | tf_op jit(solution)/shard_map/coupling/all_to_all | solution.py:205
  115.7 1.6 broadcast_in_dim.136
  117.3 5.3 %all-to-all-start.1 = ((f32[16,24,256]{2,1,0:T(8,128)}), f32[16,24,256]{2,1,0:T(8,128)S(1)}, u32[]{:S(2)}, u32[]{:S(2)}) async-start(f32[16,24,256]{2,1,0:T(8,128)} %bitcast.70), calls=%async_computation.1 | async-start | bytes 786432 | tf_op jit(solution)/shard_map/coupling/all_to_all | solution.py:207
  122.6 2.3 %copy.28 = f32[3,256,256]{1,2,0:T(8,128)} copy(f32[3,256,256]{2,1,0:T(8,128)} %param.8) | data formatting | bytes 1572864 | tf_op args[3]
  124.9 1.3 reduce_sum.29
  126.2 2.1 %broadcast_add_fusion = f32[3,256,256]{1,2,0:T(8,128)} fusion(f32[3,256,256]{1,2,0:T(8,128)} %copy.28, f32[3]{0:T(128)S(1)} %broadcast_multiply_fusion), kind=kLoop, calls=%fused_computation.2 | loop fusion | flops 196608 | bytes 1572876 | tf_op jit(solution)/shard_map/coupling/add | solution.py:202
  128.3 6.5 %all-to-all-done.1 = f32[16,24,256]{2,1,0:T(8,128)S(1)} async-done(((f32[16,24,256]{2,1,0:T(8,128)}), f32[16,24,256]{2,1,0:T(8,128)S(1)}, u32[]{:S(2)}, u32[]{:S(2)}) %all-to-all-start.1) | async-done | bytes 393248 | tf_op jit(solution)/shard_map/coupling/all_to_all | solution.py:207
  135.5 0.8 divide_convert_fusion
  136.2 0.8 broadcast_in_dim.137
  137.0 6.5 %all-to-all-start.2 = ((bf16[32,24,256]{2,1,0:T(8,128)(2,1)}), bf16[32,24,256]{2,1,0:T(8,128)(2,1)S(1)}, u32[]{:S(2)}, u32[]{:S(2)}) async-start(bf16[32,24,256]{2,1,0:T(8,128)(2,1)} %broadcast_in_dim.137), calls=%async_computation.2 | async-start | bytes 786432 | tf_op jit(solution)/shard_map/coupling/all_to_all | solution.py:212
  143.5 10.3 %all-to-all-done.2 = bf16[32,24,256]{2,1,0:T(8,128)(2,1)S(1)} async-done(((bf16[32,24,256]{2,1,0:T(8,128)(2,1)}), bf16[32,24,256]{2,1,0:T(8,128)(2,1)S(1)}, u32[]{:S(2)}, u32[]{:S(2)}) %all-to-all-start.2) | async-done | bytes 393248 | tf_op jit(solution)/shard_map/coupling/all_to_all | solution.py:212
  153.8 9.7 %output.1 = bf16[2048,1024]{1,0:T(8,128)(2,1)} custom-call(s32[1]{0:T(128)} %bitcast.at_ref, bf16[3,1024,256]{2,1,0:T(8,128)(2,1)S(1)} %bitcast.67, bf16[3,1024,256]{2,1,0:T(8,128)(2,1)} %collective-permute-done.16.other_ref, bf16[3,256,256]{2,1,0:T(8,128)(2,1)S(1)} %bitcast.68, bf16[3,1024,256]{2,1,0:T(8,128)(2,1)S(1)} %copy-done.2), custom_call_target="tpu_custom_call" | custom-call | flops 4026531840 | bytes 7340032 | tf_op jit(solution)/shard_map/output/pallas_call | solution.py:133
  (40 shorter events, 2.6 us)
Async XLA Ops:
  0.0 4.6 %copy-start.4 = (s32[3]{0:T(128)S(1)}, s32[3]{0:T(128)}, u32[]{:S(2)}) copy-start(s32[3]{0:T(128)} %param.9) | copy-start | bytes 40
  1.3 4.9 %collective-permute-start = (bf16[1024,256]{1,0:T(8,128)(2,1)S(1)}, bf16[1024,256]{1,0:T(8,128)(2,1)S(1)}, u32[]{:S(2)}, u32[]{:S(2)}) collective-permute-start(bf16[1024,256]{1,0:T(8,128)(2,1)S(1)} %get-tuple-element.18), channel_id=1, source_target_pairs={{0,1},{1,0},{2,3},{3,2},{4,5},{5,4},{6,7},{7,6},{8,9},{9,8},{10,11... | collective-permute-start | bytes 1572872 | tf_op jit(solution)/shard_map/panels/ppermute | solution.py:21
  6.3 20.5 %copy-start.2 = (bf16[3,1024,256]{2,1,0:T(8,128)(2,1)S(1)}, bf16[3,1024,256]{2,1,0:T(8,128)(2,1)}, u32[]{:S(2)}) copy-start(bf16[3,1024,256]{2,1,0:T(8,128)(2,1)} %panels_ref.5) | copy-start | bytes 4718596
  6.4 7.8 %collective-permute-start.4 = (bf16[3,128,256]{2,1,0:T(8,128)(2,1)S(1)}, bf16[3,128,256]{2,1,0:T(8,128)(2,1)S(1)}, u32[]{:S(2)}, u32[]{:S(2)}) collective-permute-start(bf16[3,128,256]{2,1,0:T(8,128)(2,1)S(1)} %get-tuple-element.15), channel_id=1, source_target_pairs={{0,14},{2,0},{4,2},{6,4},{8,6},{10,8},{12,10},{14,12},{1,15},{3,1}... | collective-permute-start | bytes 589832 | tf_op jit(solution)/shard_map/panels/ppermute | solution.py:25
  15.0 6.7 %collective-permute-start.5 = (bf16[3,128,256]{2,1,0:T(8,128)(2,1)}, bf16[3,128,256]{2,1,0:T(8,128)(2,1)}, u32[]{:S(2)}, u32[]{:S(2)}) collective-permute-start(bf16[3,128,256]{2,1,0:T(8,128)(2,1)} %bitcast_select_fusion), channel_id=1, source_target_pairs={{0,14},{2,0},{4,2},{6,4},{8,6},{10,8},{12,10},{14,12},{1,15},{3,1}... | collective-permute-start | bytes 589832 | tf_op jit(solution)/shard_map/panels/ppermute | solution.py:25
  18.4 16.5 %collective-permute-start.1 = (bf16[3,128,256]{2,1,0:T(8,128)(2,1)S(1)}, bf16[3,128,256]{2,1,0:T(8,128)(2,1)S(1)}, u32[]{:S(2)}, u32[]{:S(2)}) collective-permute-start(bf16[3,128,256]{2,1,0:T(8,128)(2,1)S(1)} %get-tuple-element.16), channel_id=1, source_target_pairs={{0,2},{2,4},{4,6},{6,8},{8,10},{10,12},{12,14},{14,0},{1,3},{3,5},... | collective-permute-start | bytes 589832 | tf_op jit(solution)/shard_map/panels/ppermute | solution.py:25
  23.4 11.5 %collective-permute-start.6 = (bf16[3,128,256]{2,1,0:T(8,128)(2,1)}, bf16[3,128,256]{2,1,0:T(8,128)(2,1)}, u32[]{:S(2)}, u32[]{:S(2)}) collective-permute-start(bf16[3,128,256]{2,1,0:T(8,128)(2,1)} %bitcast_select_fusion.1), channel_id=1, source_target_pairs={{0,14},{2,0},{4,2},{6,4},{8,6},{10,8},{12,10},{14,12},{1,15},{3,1}... | collective-permute-start | bytes 589832 | tf_op jit(solution)/shard_map/panels/ppermute | solution.py:25
  26.8 2.2 %copy-start = (bf16[2048,1024]{1,0:T(8,128)(2,1)S(1)}, bf16[2048,1024]{1,0:T(8,128)(2,1)}, u32[]{:S(2)}) copy-start(bf16[2048,1024]{1,0:T(8,128)(2,1)} %gradient_ref.3) | copy-start | bytes 12582916
  32.5 55.4 %collective-permute-start.17 = (f32[3,1024,256]{2,1,0:T(8,128)}, f32[3,1024,256]{2,1,0:T(8,128)}, u32[]{:S(2)}, u32[]{:S(2)}) collective-permute-start(f32[3,1024,256]{2,1,0:T(8,128)} %projection.4), channel_id=1, source_target_pairs={{0,1},{1,0},{2,3},{3,2},{4,5},{5,4},{6,7},{7,6},{8,9},{9,8},{10,11... | collective-permute-start | bytes 9437192 | tf_op jit(solution)/shard_map/projection/ppermute | solution.py:21
  36.6 8.1 %collective-permute-start.2 = (bf16[3,128,256]{2,1,0:T(8,128)(2,1)}, bf16[3,128,256]{2,1,0:T(8,128)(2,1)}, u32[]{:S(2)}, u32[]{:S(2)}) collective-permute-start(bf16[3,128,256]{2,1,0:T(8,128)(2,1)} %get-tuple-element.14), channel_id=1, source_target_pairs={{0,2},{2,4},{4,6},{6,8},{8,10},{10,12},{12,14},{14,0},{1,3},{3,5},... | collective-permute-start | bytes 589832 | tf_op jit(solution)/shard_map/panels/ppermute | solution.py:25
  36.6 9.7 %collective-permute-start.7 = (bf16[3,128,256]{2,1,0:T(8,128)(2,1)S(1)}, bf16[3,128,256]{2,1,0:T(8,128)(2,1)S(1)}, u32[]{:S(2)}, u32[]{:S(2)}) collective-permute-start(bf16[3,128,256]{2,1,0:T(8,128)(2,1)S(1)} %get-tuple-element.13), channel_id=1, source_target_pairs={{0,14},{2,0},{4,2},{6,4},{8,6},{10,8},{12,10},{14,12},{1,15},{3,1}... | collective-permute-start | bytes 589832 | tf_op jit(solution)/shard_map/panels/ppermute | solution.py:25
  46.3 7.2 %collective-permute-start.3 = (bf16[3,128,256]{2,1,0:T(8,128)(2,1)}, bf16[3,128,256]{2,1,0:T(8,128)(2,1)}, u32[]{:S(2)}, u32[]{:S(2)}) collective-permute-start(bf16[3,128,256]{2,1,0:T(8,128)(2,1)} %bitcast_select_fusion.4), channel_id=1, source_target_pairs={{0,2},{2,4},{4,6},{6,8},{8,10},{10,12},{12,14},{14,0},{1,3},{3,5},... | collective-permute-start | bytes 589832 | tf_op jit(solution)/shard_map/panels/ppermute | solution.py:25
  46.3 7.2 %copy-start.3 = (bf16[3,128,256]{2,1,0:T(8,128)(2,1)}, bf16[3,128,256]{2,1,0:T(8,128)(2,1)S(1)}, u32[]{:S(2)}) copy-start(bf16[3,128,256]{2,1,0:T(8,128)(2,1)S(1)} %collective-permute-done.7) | copy-start | bytes 589828
  54.6 6.1 %collective-permute-start.8 = (bf16[3,128,256]{2,1,0:T(8,128)(2,1)S(1)}, bf16[3,128,256]{2,1,0:T(8,128)(2,1)S(1)}, u32[]{:S(2)}, u32[]{:S(2)}) collective-permute-start(bf16[3,128,256]{2,1,0:T(8,128)(2,1)S(1)} %fusion), channel_id=1, source_target_pairs={{0,16},{16,0},{1,17},{17,1},{2,18},{18,2},{3,19},{19,3},{4,20},{20... | collective-permute-start | bytes 589832 | tf_op jit(solution)/shard_map/panels/ppermute | solution.py:21
  61.7 7.4 %collective-permute-start.9 = (bf16[3,128,256]{2,1,0:T(8,128)(2,1)}, bf16[3,128,256]{2,1,0:T(8,128)(2,1)S(1)}, u32[]{:S(2)}, u32[]{:S(2)}) collective-permute-start(bf16[3,128,256]{2,1,0:T(8,128)(2,1)} %get-tuple-element.10), channel_id=1, source_target_pairs={{0,2},{2,4},{4,6},{6,8},{8,10},{10,12},{12,14},{14,0},{1,3},{3,5},... | collective-permute-start | bytes 589832 | tf_op jit(solution)/shard_map/panels/ppermute | solution.py:25
  61.7 7.4 %collective-permute-start.10 = (bf16[3,128,256]{2,1,0:T(8,128)(2,1)}, bf16[3,128,256]{2,1,0:T(8,128)(2,1)S(1)}, u32[]{:S(2)}, u32[]{:S(2)}) collective-permute-start(bf16[3,128,256]{2,1,0:T(8,128)(2,1)} %get-tuple-element.10), channel_id=1, source_target_pairs={{0,14},{2,0},{4,2},{6,4},{8,6},{10,8},{12,10},{14,12},{1,15},{3,1}... | collective-permute-start | bytes 589832 | tf_op jit(solution)/shard_map/panels/ppermute | solution.py:25
  64.4 2.2 %copy-start.1 = (bf16[2048,1024]{1,0:T(8,128)(2,1)S(1)}, bf16[2048,1024]{1,0:T(8,128)(2,1)}, u32[]{:S(2)}) copy-start(bf16[2048,1024]{1,0:T(8,128)(2,1)} %gradient_ref.3) | copy-start | bytes 12582916
  69.1 5.8 %collective-permute-start.11 = (bf16[3,128,256]{2,1,0:T(8,128)(2,1)S(1)}, bf16[3,128,256]{2,1,0:T(8,128)(2,1)S(1)}, u32[]{:S(2)}, u32[]{:S(2)}) collective-permute-start(bf16[3,128,256]{2,1,0:T(8,128)(2,1)S(1)} %collective-permute-done.9), channel_id=1, source_target_pairs={{0,2},{2,4},{4,6},{6,8},{8,10},{10,12},{12,14},{14,0},{1,3},{3,5},... | collective-permute-start | bytes 589832 | tf_op jit(solution)/shard_map/panels/ppermute | solution.py:25
  69.2 5.7 %collective-permute-start.12 = (bf16[3,128,256]{2,1,0:T(8,128)(2,1)S(1)}, bf16[3,128,256]{2,1,0:T(8,128)(2,1)S(1)}, u32[]{:S(2)}, u32[]{:S(2)}) collective-permute-start(bf16[3,128,256]{2,1,0:T(8,128)(2,1)S(1)} %collective-permute-done.10), channel_id=1, source_target_pairs={{0,14},{2,0},{4,2},{6,4},{8,6},{10,8},{12,10},{14,12},{1,15},{3,1}... | collective-permute-start | bytes 589832 | tf_op jit(solution)/shard_map/panels/ppermute | solution.py:25
  74.9 6.0 %collective-permute-start.13 = (bf16[3,128,256]{2,1,0:T(8,128)(2,1)S(1)}, bf16[3,128,256]{2,1,0:T(8,128)(2,1)S(1)}, u32[]{:S(2)}, u32[]{:S(2)}) collective-permute-start(bf16[3,128,256]{2,1,0:T(8,128)(2,1)S(1)} %collective-permute-done.11), channel_id=1, source_target_pairs={{0,2},{2,4},{4,6},{6,8},{8,10},{10,12},{12,14},{14,0},{1,3},{3,5},... | collective-permute-start | bytes 589832 | tf_op jit(solution)/shard_map/panels/ppermute | solution.py:25
  74.9 6.0 %collective-permute-start.14 = (bf16[3,128,256]{2,1,0:T(8,128)(2,1)S(1)}, bf16[3,128,256]{2,1,0:T(8,128)(2,1)S(1)}, u32[]{:S(2)}, u32[]{:S(2)}) collective-permute-start(bf16[3,128,256]{2,1,0:T(8,128)(2,1)S(1)} %collective-permute-done.12), channel_id=1, source_target_pairs={{0,14},{2,0},{4,2},{6,4},{8,6},{10,8},{12,10},{14,12},{1,15},{3,1}... | collective-permute-start | bytes 589832 | tf_op jit(solution)/shard_map/panels/ppermute | solution.py:25
  80.8 7.0 %collective-permute-start.15 = (bf16[3,128,256]{2,1,0:T(8,128)(2,1)S(1)}, bf16[3,128,256]{2,1,0:T(8,128)(2,1)S(1)}, u32[]{:S(2)}, u32[]{:S(2)}) collective-permute-start(bf16[3,128,256]{2,1,0:T(8,128)(2,1)S(1)} %collective-permute-done.13), channel_id=1, source_target_pairs={{0,2},{2,4},{4,6},{6,8},{8,10},{10,12},{12,14},{14,0},{1,3},{3,5},... | collective-permute-start | bytes 589832 | tf_op jit(solution)/shard_map/panels/ppermute | solution.py:25
  92.2 8.2 %collective-permute-start.18 = (f32[384,256]{1,0:T(8,128)S(1)}, f32[384,256]{1,0:T(8,128)S(1)}, u32[]{:S(2)}, u32[]{:S(2)}) collective-permute-start(f32[384,256]{1,0:T(8,128)S(1)} %get-tuple-element.8), channel_id=1, source_target_pairs={{0,1},{1,0},{2,3},{3,2},{4,5},{5,4},{6,7},{7,6},{8,9},{9,8},{10,11... | collective-permute-start | bytes 1179656 | tf_op jit(solution)/shard_map/coupling/ppermute | solution.py:21
  101.2 13.9 %all-to-all-start = ((f32[8,48,256]{2,1,0:T(8,128)}), f32[8,48,256]{2,1,0:T(8,128)S(1)}, u32[]{:S(2)}, u32[]{:S(2)}) async-start(f32[8,48,256]{2,1,0:T(8,128)} %bitcast.71), calls=%async_computation | async-start | bytes 786432 | tf_op jit(solution)/shard_map/coupling/all_to_all | solution.py:205
  106.2 37.3 %collective-permute-start.16 = (bf16[3,1024,256]{2,1,0:T(8,128)(2,1)S(1)}, bf16[3,1024,256]{2,1,0:T(8,128)(2,1)}, u32[]{:S(2)}, u32[]{:S(2)}) collective-permute-start(bf16[3,1024,256]{2,1,0:T(8,128)(2,1)S(1)} %bitcast.66), channel_id=1, source_target_pairs={{0,1},{1,0},{2,3},{3,2},{4,5},{5,4},{6,7},{7,6},{8,9},{9,8},{10,11... | collective-permute-start | bytes 4718600 | tf_op jit(solution)/shard_map/panels/ppermute | solution.py:21
  117.3 17.5 %all-to-all-start.1 = ((f32[16,24,256]{2,1,0:T(8,128)}), f32[16,24,256]{2,1,0:T(8,128)S(1)}, u32[]{:S(2)}, u32[]{:S(2)}) async-start(f32[16,24,256]{2,1,0:T(8,128)} %bitcast.70), calls=%async_computation.1 | async-start | bytes 786432 | tf_op jit(solution)/shard_map/coupling/all_to_all | solution.py:207
  137.0 16.8 %all-to-all-start.2 = ((bf16[32,24,256]{2,1,0:T(8,128)(2,1)}), bf16[32,24,256]{2,1,0:T(8,128)(2,1)S(1)}, u32[]{:S(2)}, u32[]{:S(2)}) async-start(bf16[32,24,256]{2,1,0:T(8,128)(2,1)} %broadcast_in_dim.137), calls=%async_computation.2 | async-start | bytes 786432 | tf_op jit(solution)/shard_map/coupling/all_to_all | solution.py:212

commit v3 on v0

v3 whole, which is shorter than its diff:
```python
import jax
import jax.numpy as jnp
from jax import lax
from jax.experimental import pallas as pl
from jax.experimental.pallas import tpu as pltpu
from jax.sharding import Mesh
from jax.sharding import PartitionSpec as P

ROW = ("yl", "x")
COL = ("yh", "z", "core")
F32 = jnp.float32
BF16 = jnp.bfloat16
RING = 8
REACH = RING // 2
MIB = 1024 * 1024

VMEM = pl.BlockSpec(memory_space=pltpu.VMEM)
SMEM = pl.BlockSpec(memory_space=pltpu.SMEM)
HBM = pl.BlockSpec(memory_space=pltpu.HBM)
ANY = pl.BlockSpec(memory_space=pl.ANY)


def swap(x, axis):
    return lax.ppermute(x, axis, [(0, 1), (1, 0)])


def shift(x, by):
    return lax.ppermute(x, "z", [(i, (i + by) % RING) for i in range(RING)])


def call(kernel, args, in_specs, out_specs, out_shape, flops=0, scratch=(), limit=16):
    moved = sum(a.size * a.dtype.itemsize for a in args)
    return pl.pallas_call(
        kernel,
        in_specs=in_specs,
        out_specs=out_specs,
        out_shape=out_shape,
        scratch_shapes=scratch,
        compiler_params=pltpu.CompilerParams(vmem_limit_bytes=limit * MIB),
        cost_estimate=pl.CostEstimate(flops=flops, bytes_accessed=moved, transcendentals=0),
    )(*args)


def owner_of(at_ref, k):
    number = at_ref[3 + k]
    return number & 1, (number >> 1) & (RING - 1), number >> 4


def picked(at_ref, k, own_ref, other_ref, index, put):
    core, _, _ = owner_of(at_ref, k)
    rows = own_ref.shape[0] // RING
    span = pl.ds(pl.multiple_of((index & (RING - 1)) * rows, rows), rows)
    pl.when(core == at_ref[0])(lambda: put(own_ref[span]))
    pl.when(core != at_ref[0])(lambda: put(other_ref[span]))


def start_kernel(at_ref, own_ref, other_ref, up_ref, down_ref):
    here = at_ref[2]
    for k in range(up_ref.shape[0]):
        picked(at_ref, k, own_ref, other_ref, here + REACH - 1, lambda x, k=k: up_ref.__setitem__(k, x))
        picked(at_ref, k, own_ref, other_ref, here - REACH + RING, lambda x, k=k: down_ref.__setitem__(k, x))


def merge_kernel(step, at_ref, own_ref, other_ref, came_up_ref, came_down_ref, *refs):
    up_ref, down_ref = refs[-2:]
    here = at_ref[2]
    for k in range(up_ref.shape[0]):
        _, place, _ = owner_of(at_ref, k)

        @pl.when(place == here)
        def _():
            picked(at_ref, k, own_ref, other_ref, here + REACH - 1 - step, lambda x: up_ref.__setitem__(k, x))
            picked(at_ref, k, own_ref, other_ref, here - REACH + RING + step, lambda x: down_ref.__setitem__(k, x))

        @pl.when(place != here)
        def _():
            up_ref[k] = came_up_ref[k]
            down_ref[k] = came_down_ref[k]


def last_kernel(at_ref, own_ref, other_ref, up_ref, came_down_ref, out_ref):
    here = at_ref[2]
    for k in range(out_ref.shape[0]):
        _, place, _ = owner_of(at_ref, k)
        below = ((here - place) & (RING - 1)) < REACH

        @pl.when(below)
        def _():
            out_ref[k] = up_ref[k]

        @pl.when(jnp.logical_not(below))
        def _():
            out_ref[k] = came_down_ref[k]


def level_kernel(at_ref, mine_ref, other_ref, *refs):
    out_ref = refs[-1]
    for k in range(out_ref.shape[0]):
        _, _, high = owner_of(at_ref, k)

        @pl.when(high == at_ref[1])
        def _():
            out_ref[k] = mine_ref[k]

        @pl.when(high != at_ref[1])
        def _():
            out_ref[k] = other_ref[k]


def project_kernel(at_ref, gradient_ref, panels_ref, *refs):
    out_ref, rows_ref, sems = refs[-3:]
    blocks, size, _ = rows_ref.shape
    first = at_ref[0] * (blocks * size)
    copies = []
    for i in range(blocks):
        start = pl.multiple_of(first + i * size, size)
        copies.append(pltpu.make_async_copy(gradient_ref.at[pl.ds(start, size)], rows_ref.at[i], sems.at[i]))
        copies[-1].start()
    for i in range(blocks):
        copies[i].wait()
        for k in range(panels_ref.shape[0]):
            out_ref[k, i * size : (i + 1) * size] = jnp.dot(rows_ref[i], panels_ref[k], preferred_element_type=F32)


def project(gradient, panels, half, after):
    count, width, vec = panels.shape
    rows = gradient.shape[0] // 2
    blocks = 4
    return call(
        project_kernel,
        (half[None], gradient, panels, after),
        [SMEM, HBM, VMEM, ANY],
        VMEM,
        jax.ShapeDtypeStruct((count, rows, vec), F32),
        2 * rows * width * vec * count,
        [pltpu.VMEM((blocks, rows // blocks, width), BF16), pltpu.SemaphoreType.DMA((blocks,))],
    )


def split_kernel(own_ref, other_ref, values_ref, out_ref, below_ref):
    vec = own_ref.shape[2]
    total = (own_ref[0] + other_ref[0]).T
    high = total.astype(BF16)
    out_ref[0, :vec] = high
    out_ref[0, vec:] = (total - high.astype(F32)).astype(BF16)
    values = values_ref[0]
    below_ref[...] = (values + 0.1 * jnp.mean(values)).T


def split(own, other, values):
    count, rows, vec = own.shape
    return pl.pallas_call(
        split_kernel,
        grid=(count,),
        in_specs=[pl.BlockSpec((1, rows, vec), lambda k: (k, 0, 0))] * 2 + [pl.BlockSpec((1, vec, vec), lambda k: (k, 0, 0))],
        out_specs=[pl.BlockSpec((1, 2 * vec, rows), lambda k: (k, 0, 0)), pl.BlockSpec((vec, vec), lambda k: (k, 0))],
        out_shape=[jax.ShapeDtypeStruct((count, 2 * vec, rows), BF16), jax.ShapeDtypeStruct((count * vec, vec), F32)],
        compiler_params=pltpu.CompilerParams(vmem_limit_bytes=20 * MIB),
        cost_estimate=pl.CostEstimate(flops=3 * own.size, bytes_accessed=12 * own.size, transcendentals=0),
    )(own, other, values)


def offsets():
    order = [0]
    for step in range(1, REACH + 1):
        order.append(-step)
        if step < REACH:
            order.append(step)
    return order


def couple_kernel(at_ref, terms_ref, *refs):
    pieces, (keep_ref, send_ref, total_ref) = refs[:RING], refs[RING:]
    count, rows, vec = pieces[0].shape
    for k in range(count):
        both = None
        for piece, offset in zip(pieces, offsets()):
            at = pl.multiple_of(((at_ref[2] + offset + RING) & (RING - 1)) * rows, rows)
            term = jnp.dot(terms_ref[k, :, pl.ds(at, rows)], piece[k], preferred_element_type=F32)
            both = term if both is None else both + term
        total_ref[k * vec : (k + 1) * vec] = both[:vec] + both[vec:]
    size = keep_ref.shape[0]
    keep_ref[...] = total_ref[pl.ds(pl.multiple_of(at_ref[0] * size, size), size)]
    send_ref[...] = total_ref[pl.ds(pl.multiple_of((1 - at_ref[0]) * size, size), size)]


def couple(at, terms, pieces):
    count, rows, vec = pieces[0].shape
    half = jax.ShapeDtypeStruct((count * vec // 2, vec), F32)
    return call(
        couple_kernel,
        (at, terms, *pieces),
        [SMEM] + [VMEM] * (1 + RING),
        [VMEM, VMEM],
        [half, half],
        4 * count * RING * rows * vec * vec,
        [pltpu.VMEM((count * vec, vec), F32)],
    )


def pack_kernel(at_ref, *refs):
    pieces, out_ref = refs[:RING], refs[-1]
    count, rows, _ = pieces[0].shape
    for piece, offset in zip(pieces, offsets()):
        at = pl.multiple_of(((at_ref[2] + offset + RING) & (RING - 1)) * rows, rows)
        for k in range(count):
            out_ref[k, pl.ds(at, rows)] = piece[k]


def pack(at, pieces, after):
    count, rows, vec = pieces[0].shape
    shape = jax.ShapeDtypeStruct((count, RING * rows, vec), BF16)
    return call(pack_kernel, (at, *pieces, after), [SMEM] + [VMEM] * RING + [ANY], VMEM, shape)


def spread_kernel(part_ref, out_ref):
    total = jnp.sum(part_ref[...], axis=0)
    half = total.shape[0] // 2
    for j in range(2 * RING):
        out_ref[j] = total[:half] if j < RING else total[half:]


def spread(parts):
    _, rows, vec = parts.shape
    return call(spread_kernel, (parts,), [VMEM], VMEM, jax.ShapeDtypeStruct((2 * RING, rows // 2, vec), F32))


def scale_kernel(place_ref, parts_ref, below_ref, out_ref):
    total = jnp.sum(parts_ref[...], axis=0)
    size = total.shape[0]
    below = below_ref[pl.ds(pl.multiple_of(place_ref[0] * size, size), size)]
    out_ref[...] = (total / below).astype(BF16)


def apply_kernel(at_ref, own_ref, other_ref, scaled_ref, panels_ref, out_ref, block_ref, sems):
    count, rows, vec = own_ref.shape
    size = block_ref.shape[1]
    steps = rows // size
    core = at_ref[0]
    copies = []
    for number in range(2 * steps):
        fetched_ref, half = (own_ref, core) if number < steps else (other_ref, 1 - core)
        start = (number % steps) * size
        total = None
        for k in range(count):
            rotated = lax.dot_general(fetched_ref[k, start : start + size], scaled_ref[k], (((1,), (1,)), ((), ())), preferred_element_type=F32)
            term = lax.dot_general(rotated.astype(BF16), panels_ref[k], (((1,), (1,)), ((), ())), preferred_element_type=F32)
            total = term if total is None else total + term
        block_ref[number] = total.astype(BF16)
        target = pl.multiple_of(half * rows + start, size)
        copies.append(pltpu.make_async_copy(block_ref.at[number], out_ref.at[pl.ds(target, size)], sems.at[number]))
        copies[-1].start()
    for copy in copies:
        copy.wait()


def apply(at, own, other, scaled, panels):
    count, rows, vec = own.shape
    width = panels.shape[1]
    blocks = 4
    size = 2 * rows // blocks
    return call(
        apply_kernel,
        (at, own, other, scaled, panels),
        [SMEM, VMEM, VMEM, VMEM, VMEM],
        HBM,
        jax.ShapeDtypeStruct((2 * rows, width), BF16),
        4 * count * rows * vec * (vec + width),
        [pltpu.VMEM((blocks, size, width), BF16), pltpu.SemaphoreType.DMA((blocks,))],
        limit=40,
    )


def body(gradient, in_panels, out_pool, eigenvalues, owners):
    core, high, here = (lax.axis_index(a) for a in ("core", "yh", "z"))
    at = jnp.concatenate([jnp.stack([core, high, here]).astype(jnp.int32), owners])
    count, _, vec = in_panels.shape
    panel = out_pool[0]
    half = panel.shape[0] // 2
    piece = jax.ShapeDtypeStruct((count, half // RING, vec), BF16)

    with jax.named_scope("select"):
        own = lax.dynamic_slice_in_dim(panel, core * half, half, 0)
        other = swap(lax.dynamic_slice_in_dim(panel, (1 - core) * half, half, 0), "core")
        up, down = call(start_kernel, (at, own, other), [SMEM, VMEM, VMEM], [VMEM] * 2, [piece] * 2)
        sent = project(gradient, in_panels, 1 - core, up)
        kept = project(gradient, in_panels, core, sent)
        came = swap(sent, "core")
        for step in range(1, REACH):
            after = [(), (sent,), (kept,)][step - 1]
            args = (at, own, other, shift(up, 1), shift(down, -1), *after)

            def kernel(*refs, step=step):
                merge_kernel(step, *refs)

            up, down = call(kernel, args, [SMEM] + [VMEM] * 4 + [ANY] * len(after), [VMEM] * 2, [piece] * 2)
        mine = call(last_kernel, (at, own, other, up, shift(down, -1)), [SMEM] + [VMEM] * 4, VMEM, piece)
        terms, below = split(kept, came, eigenvalues)
        mine = call(level_kernel, (at, mine, swap(mine, "yh"), terms), [SMEM, VMEM, VMEM, ANY], VMEM, piece)

    with jax.named_scope("gather"):
        pieces = [mine]
        up = down = mine
        for step in range(1, REACH + 1):
            up = shift(up, 1)
            pieces.append(up)
            if step < REACH:
                down = shift(down, -1)
                pieces.append(down)

    with jax.named_scope("coupling"):
        keep, send = couple(at, terms, pieces)
        part = keep + swap(send, "core")
        own = pack(at, pieces, part)
        other = swap(own, "core")
        part = spread(lax.all_to_all(part.reshape(8, -1, vec), ROW, 0, 0))
        part = lax.all_to_all(part, ("yh", "z"), 0, 0)
        place = (core * 8 + lax.axis_index(ROW)) * 2 + high
        shape = jax.ShapeDtypeStruct(part.shape[1:], BF16)
        scaled = call(scale_kernel, (place[None], part, below), [SMEM, VMEM, VMEM], VMEM, shape)
        copies = jnp.broadcast_to(scaled[None], (32,) + scaled.shape)
        scaled = lax.all_to_all(copies, ("core",) + ROW + ("yh",), 0, 0).reshape(count, vec, vec)

    with jax.named_scope("output"):
        return apply(at, own, other, scaled, in_panels)


def solution(mesh):
    fine = Mesh(mesh.devices.reshape(2, 4, 2, 8, 2), ROW + COL)
    return jax.shard_map(
        body,
        mesh=fine,
        in_specs=(P(ROW, COL), P(None, COL, None), P(COL, ROW, None), P(), P()),
        out_specs=P(ROW, COL),
        check_vma=False,
    )
```

time: 581 us -> 149 us (0.26)
  waiting for transfers between devices: 520 us -> 48.1 us
  starting transfers between devices: 0.04 us -> 43.3 us
  matrix products: 37.7 us -> 0 us
  blocking collectives: 0 us -> 29.2 us
  Pallas kernels: 0 us -> 23.5 us
  between operations: 17.2 us -> 0.36 us
    psum x2 -> x0, waiting for transfers between devices: 520 us -> none  [the longest x1 270 us: from_root(): return lax.psum(jnp.where(mine, x, jnp.zeros_like(x)), axis)]
    dot_general x9 -> x0, matrix products: 37.7 us -> none  [the longest x3 20.8 us: body(): jnp.dot(rotated, basis.T, preferred_element_type=jnp.float32)]
    ppermute x0 -> x19, starting transfers between devices: none -> 37.6 us  [the longest x14 21 us: shift(): return lax.ppermute(x, 'z', [(i, (i + by) % RING) for i in range(RING)])]
    ppermute x0 -> x19, waiting for transfers between devices: none -> 35.8 us  [the longest x14 31.9 us: shift(): return lax.ppermute(x, 'z', [(i, (i + by) % RING) for i in range(RING)])]
    all_to_all x0 -> x2, blocking collectives: none -> 29.2 us  [the longest x1 15.8 us: body(): lax.all_to_all(copies, ('core',) + ROW + ('yh',), 0, 0)]
    pallas_call x0 -> x14, Pallas kernels: none -> 23.5 us  [the longest x13 22.1 us: call(): pl.pallas_call(kernel, in_specs=in_specs, out_specs=out_specs, out_shape=...]
    all_to_all x0 -> x1, waiting for transfers between devices: none -> 12.3 us  [body(): part = lax.all_to_all(part, ('yh', 'z'), 0, 0)]
  transfers between devices with their start and end apart: 2 -> 20, of which waited for: 2 -> 12; matrix products, arithmetic and copies ran while one was open for 2% -> 1% of each run, Pallas kernels for 0% -> 5%
where the time goes in v3:
time: 149 us
  waiting for transfers between devices  48.1 us (32%)
  starting transfers between devices  43.3 us (29%)
  blocking collectives  29.2 us (20%)
  Pallas kernels  23.5 us (16%)
  local copies, waits for them, and re-layouts  3.62 us (2%)
    ppermute x14, waiting for transfers between devices, shift(): return lax.ppermute(x, 'z', [(i, (i + by) % RING) for i in range(RING)])  31.9 us
    pallas_call x13, Pallas kernels, call(): pl.pallas_call(kernel, in_specs=in_specs, out_specs=out_specs, out_shape=...  22.1 us
    ppermute x14, starting transfers between devices, shift(): return lax.ppermute(x, 'z', [(i, (i + by) % RING) for i in range(RING)])  21 us
    ppermute x5, starting transfers between devices, swap(): return lax.ppermute(x, axis, [(0, 1), (1, 0)])  16.6 us
    all_to_all x1, blocking collectives, body(): lax.all_to_all(copies, ('core',) + ROW + ('yh',), 0, 0)  15.8 us
    all_to_all x1, blocking collectives, body(): part = spread(lax.all_to_all(part.reshape(8, -1, vec), ROW, 0, 0))  13.3 us
    all_to_all x1, waiting for transfers between devices, body(): part = lax.all_to_all(part, ('yh', 'z'), 0, 0)  12.3 us
    all_to_all x1, starting transfers between devices, body(): part = lax.all_to_all(part, ('yh', 'z'), 0, 0)  5.71 us
  transfers between devices with their start and end apart: 20, of which 12 were waited for; matrix products, arithmetic and copies ran while one was open for 1% of the time, Pallas kernels for 5%

profile of v3, /device:TPU:1, one launch (start us, length us, event | category | flops | bytes accessed | tf_op | source)
XLA Modules:
  0.0 148.8 jit_solution(3493442085012197590)
XLA Ops:
  0.0 1.4 dynamic-slice_bitcast_fusion
  1.4 3.3 %collective-permute-start = (bf16[1024,256]{1,0:T(8,128)(2,1)S(1)}, bf16[1024,256]{1,0:T(8,128)(2,1)S(1)}, u32[]{:S(2)}, u32[]{:S(2)}) collective-permute-start(bf16[1024,256]{1,0:T(8,128)(2,1)S(1)} %get-tuple-element.29), channel_id=1, source_target_pairs={{0,1},{1,0},{2,3},{3,2},{4,5},{5,4},{6,7},{7,6},{8,9},{9,8},{10,11... | collective-permute-start | bytes 1572872 | tf_op jit(solution)/shard_map/select/ppermute | solution.py:24
  4.7 0.7 pad_add_fusion.at_ref.refs_0_
  5.5 0.8 collective-permute-done.other_ref.refs_2_
  6.3 0.6 select.9
  6.9 2.2 %copy-done = bf16[2048,1024]{1,0:T(8,128)(2,1)S(1)} copy-done((bf16[2048,1024]{1,0:T(8,128)(2,1)S(1)}, bf16[2048,1024]{1,0:T(8,128)(2,1)}, u32[]{:S(2)}) %copy-start) | copy-done | bytes 4194328
  9.1 3.0 %select.11.refs_5_.refs_0_ = f32[3,1024,256]{2,1,0:T(8,128)S(1)} custom-call(s32[1]{0:T(128)} %bitcast.5.at_ref, bf16[2048,1024]{1,0:T(8,128)(2,1)S(1)} %copy-done, bf16[3,1024,256]{2,1,0:T(8,128)(2,1)S(1)} %copy-done.2, bf16[3,128,256]{2,1,0:T(8,128)(2,1)S(1)} %get-tuple-element.17.refs_0_), custom_call_target="tpu_custom_call" | custom-call | flops 1610612736 | bytes 5963780 | tf_op jit(solution)/shard_map/select/pallas_call | solution.py:33
  12.2 0.5 collective-permute-start.9
  12.6 3.8 %collective-permute-start.2 = (bf16[3,128,256]{2,1,0:T(8,128)(2,1)S(1)}, bf16[3,128,256]{2,1,0:T(8,128)(2,1)S(1)}, u32[]{:S(2)}, u32[]{:S(2)}) collective-permute-start(bf16[3,128,256]{2,1,0:T(8,128)(2,1)S(1)} %get-tuple-element.18), channel_id=1, source_target_pairs={{0,14},{2,0},{4,2},{6,4},{8,6},{10,8},{12,10},{14,12},{1,15},{3,1}... | collective-permute-start | bytes 589832 | tf_op jit(solution)/shard_map/select/ppermute | solution.py:28
  16.5 4.2 %collective-permute-done.2.refs_4_ = bf16[3,128,256]{2,1,0:T(8,128)(2,1)S(1)} collective-permute-done((bf16[3,128,256]{2,1,0:T(8,128)(2,1)S(1)}, bf16[3,128,256]{2,1,0:T(8,128)(2,1)S(1)}, u32[]{:S(2)}, u32[]{:S(2)}) %collective-permute-start.2) | collective-permute-done | bytes 196640 | tf_op jit(solution)/shard_map/select/ppermute | solution.py:28
  20.6 3.1 %collective-permute-done.1.refs_3_ = bf16[3,128,256]{2,1,0:T(8,128)(2,1)S(1)} collective-permute-done((bf16[3,128,256]{2,1,0:T(8,128)(2,1)S(1)}, bf16[3,128,256]{2,1,0:T(8,128)(2,1)S(1)}, u32[]{:S(2)}, u32[]{:S(2)}) %collective-permute-start.1) | collective-permute-done | bytes 196640 | tf_op jit(solution)/shard_map/select/ppermute | solution.py:28
  23.7 0.6 select.10
  24.3 0.1 collective-permute-start.3
  24.4 2.7 %collective-permute-start.4 = (bf16[3,128,256]{2,1,0:T(8,128)(2,1)S(1)}, bf16[3,128,256]{2,1,0:T(8,128)(2,1)S(1)}, u32[]{:S(2)}, u32[]{:S(2)}) collective-permute-start(bf16[3,128,256]{2,1,0:T(8,128)(2,1)S(1)} %get-tuple-element.20), channel_id=1, source_target_pairs={{0,14},{2,0},{4,2},{6,4},{8,6},{10,8},{12,10},{14,12},{1,15},{3,1}... | collective-permute-start | bytes 589832 | tf_op jit(solution)/shard_map/select/ppermute | solution.py:28
  27.1 3.7 %collective-permute-done.3.refs_3_ = bf16[3,128,256]{2,1,0:T(8,128)(2,1)S(1)} collective-permute-done((bf16[3,128,256]{2,1,0:T(8,128)(2,1)S(1)}, bf16[3,128,256]{2,1,0:T(8,128)(2,1)S(1)}, u32[]{:S(2)}, u32[]{:S(2)}) %collective-permute-start.3) | collective-permute-done | bytes 196640 | tf_op jit(solution)/shard_map/select/ppermute | solution.py:28
  30.7 0.6 select.12
  31.3 0.1 collective-permute-start.5
  31.4 2.7 %collective-permute-start.6 = (bf16[3,128,256]{2,1,0:T(8,128)(2,1)S(1)}, bf16[3,128,256]{2,1,0:T(8,128)(2,1)S(1)}, u32[]{:S(2)}, u32[]{:S(2)}) collective-permute-start(bf16[3,128,256]{2,1,0:T(8,128)(2,1)S(1)} %get-tuple-element.22), channel_id=1, source_target_pairs={{0,14},{2,0},{4,2},{6,4},{8,6},{10,8},{12,10},{14,12},{1,15},{3,1}... | collective-permute-start | bytes 589832 | tf_op jit(solution)/shard_map/select/ppermute | solution.py:28
  34.1 3.0 %select.13.refs_5_.own_ref = f32[3,1024,256]{2,1,0:T(8,128)S(1)} custom-call(s32[1]{0:T(128)} %bitcast.at_ref, bf16[2048,1024]{1,0:T(8,128)(2,1)S(1)} %copy-done.1, bf16[3,1024,256]{2,1,0:T(8,128)(2,1)S(1)} %copy-done.2, f32[3,1024,256]{2,1,0:T(8,128)S(1)} %select.11.refs_5_.refs_0_), custom_call_target="tpu_custom_call" | custom-call | flops 1610612736 | bytes 8912900 | tf_op jit(solution)/shard_map/select/pallas_call | solution.py:33
  37.1 0.0 collective-permute-done.5.refs_3_
  37.2 0.6 select.14
  37.8 2.8 %collective-permute-start.7 = (bf16[3,128,256]{2,1,0:T(8,128)(2,1)S(1)}, bf16[3,128,256]{2,1,0:T(8,128)(2,1)S(1)}, u32[]{:S(2)}, u32[]{:S(2)}) collective-permute-start(bf16[3,128,256]{2,1,0:T(8,128)(2,1)S(1)} %get-tuple-element.24), channel_id=1, source_target_pairs={{0,14},{2,0},{4,2},{6,4},{8,6},{10,8},{12,10},{14,12},{1,15},{3,1}... | collective-permute-start | bytes 589832 | tf_op jit(solution)/shard_map/select/ppermute | solution.py:28
  40.5 2.6 %collective-permute-done.7.came_down_ref = bf16[3,128,256]{2,1,0:T(8,128)(2,1)S(1)} collective-permute-done((bf16[3,128,256]{2,1,0:T(8,128)(2,1)S(1)}, bf16[3,128,256]{2,1,0:T(8,128)(2,1)S(1)}, u32[]{:S(2)}, u32[]{:S(2)}) %collective-permute-start.7) | collective-permute-done | bytes 196640 | tf_op jit(solution)/shard_map/select/ppermute | solution.py:28
  43.1 0.6 select.15.mine_ref
  43.7 3.0 %collective-permute-start.8 = (bf16[3,128,256]{2,1,0:T(8,128)(2,1)S(1)}, bf16[3,128,256]{2,1,0:T(8,128)(2,1)S(1)}, u32[]{:S(2)}, u32[]{:S(2)}) collective-permute-start(bf16[3,128,256]{2,1,0:T(8,128)(2,1)S(1)} %select.15.mine_ref), channel_id=1, source_target_pairs={{0,16},{16,0},{1,17},{17,1},{2,18},{18,2},{3,19},{19,3},{4,20},{20... | collective-permute-start | bytes 589832 | tf_op jit(solution)/shard_map/select/ppermute | solution.py:24
  46.7 1.4 select.16
  48.1 1.7 %collective-permute-done.8.other_ref = bf16[3,128,256]{2,1,0:T(8,128)(2,1)S(1)} collective-permute-done((bf16[3,128,256]{2,1,0:T(8,128)(2,1)S(1)}, bf16[3,128,256]{2,1,0:T(8,128)(2,1)S(1)}, u32[]{:S(2)}, u32[]{:S(2)}) %collective-permute-start.8) | collective-permute-done | bytes 196640 | tf_op jit(solution)/shard_map/select/ppermute | solution.py:24
  49.9 0.6 select.17.refs_0_
  50.5 0.3 collective-permute-start.10
  50.7 3.2 %collective-permute-start.11 = (bf16[3,128,256]{2,1,0:T(8,128)(2,1)S(1)}, bf16[3,128,256]{2,1,0:T(8,128)(2,1)S(1)}, u32[]{:S(2)}, u32[]{:S(2)}) collective-permute-start(bf16[3,128,256]{2,1,0:T(8,128)(2,1)S(1)} %select.17.refs_0_), channel_id=1, source_target_pairs={{0,14},{2,0},{4,2},{6,4},{8,6},{10,8},{12,10},{14,12},{1,15},{3,1}... | collective-permute-start | bytes 589832 | tf_op jit(solution)/shard_map/gather/ppermute | solution.py:28
  53.9 3.0 %collective-permute-done.10.refs_1_ = bf16[3,128,256]{2,1,0:T(8,128)(2,1)S(1)} collective-permute-done((bf16[3,128,256]{2,1,0:T(8,128)(2,1)S(1)}, bf16[3,128,256]{2,1,0:T(8,128)(2,1)S(1)}, u32[]{:S(2)}, u32[]{:S(2)}) %collective-permute-start.10) | collective-permute-done | bytes 196640 | tf_op jit(solution)/shard_map/gather/ppermute | solution.py:28
  56.9 2.8 %collective-permute-start.13 = (bf16[3,128,256]{2,1,0:T(8,128)(2,1)S(1)}, bf16[3,128,256]{2,1,0:T(8,128)(2,1)S(1)}, u32[]{:S(2)}, u32[]{:S(2)}) collective-permute-start(bf16[3,128,256]{2,1,0:T(8,128)(2,1)S(1)} %collective-permute-done.11.refs_2_), channel_id=1, source_target_pairs={{0,14},{2,0},{4,2},{6,4},{8,6},{10,8},{12,10},{14,12},{1,15},{3,1}... | collective-permute-start | bytes 589832 | tf_op jit(solution)/shard_map/gather/ppermute | solution.py:28
  59.6 5.1 %collective-permute-done.12.refs_3_ = bf16[3,128,256]{2,1,0:T(8,128)(2,1)S(1)} collective-permute-done((bf16[3,128,256]{2,1,0:T(8,128)(2,1)S(1)}, bf16[3,128,256]{2,1,0:T(8,128)(2,1)S(1)}, u32[]{:S(2)}, u32[]{:S(2)}) %collective-permute-start.12) | collective-permute-done | bytes 196640 | tf_op jit(solution)/shard_map/gather/ppermute | solution.py:28
  64.7 2.7 %collective-permute-start.15 = (bf16[3,128,256]{2,1,0:T(8,128)(2,1)S(1)}, bf16[3,128,256]{2,1,0:T(8,128)(2,1)S(1)}, u32[]{:S(2)}, u32[]{:S(2)}) collective-permute-start(bf16[3,128,256]{2,1,0:T(8,128)(2,1)S(1)} %collective-permute-done.13.refs_4_), channel_id=1, source_target_pairs={{0,14},{2,0},{4,2},{6,4},{8,6},{10,8},{12,10},{14,12},{1,15},{3,1}... | collective-permute-start | bytes 589832 | tf_op jit(solution)/shard_map/gather/ppermute | solution.py:28
  67.4 4.3 %collective-permute-done.14.refs_5_ = bf16[3,128,256]{2,1,0:T(8,128)(2,1)S(1)} collective-permute-done((bf16[3,128,256]{2,1,0:T(8,128)(2,1)S(1)}, bf16[3,128,256]{2,1,0:T(8,128)(2,1)S(1)}, u32[]{:S(2)}, u32[]{:S(2)}) %collective-permute-start.14) | collective-permute-done | bytes 196640 | tf_op jit(solution)/shard_map/gather/ppermute | solution.py:28
  71.7 6.0 %collective-permute-done.16.refs_7_ = bf16[3,128,256]{2,1,0:T(8,128)(2,1)S(1)} collective-permute-done((bf16[3,128,256]{2,1,0:T(8,128)(2,1)S(1)}, bf16[3,128,256]{2,1,0:T(8,128)(2,1)S(1)}, u32[]{:S(2)}, u32[]{:S(2)}) %collective-permute-start.16) | collective-permute-done | bytes 196640 | tf_op jit(solution)/shard_map/gather/ppermute | solution.py:28
  77.8 2.4 %coupling.4 = (f32[384,256]{1,0:T(8,128)S(1)}, f32[384,256]{1,0:T(8,128)S(1)}) custom-call(s32[6]{0:T(128)S(1)} %pad_add_fusion.at_ref.refs_0_, bf16[3,512,1024]{2,1,0:T(8,128)(2,1)S(1)} %get-tuple-element.25.refs_0_.terms_ref, bf16[3,128,256]{2,1,0:T(8,128)(2,1)S(1)} %select.17.refs_0_, bf16[3,128,256]{2,1,0:T(8,128)(2,1)S(1)} %collective-permute-done.10.refs_1_, ...), custom_call_target="tpu_custom_call" | custom-call | flops 805306368 | bytes 4718616 | tf_op jit(solution)/shard_map/coupling/pallas_call | solution.py:33
  80.1 9.4 %collective-permute-start.17 = (f32[384,256]{1,0:T(8,128)S(1)}, f32[384,256]{1,0:T(8,128)S(1)}, u32[]{:S(2)}, u32[]{:S(2)}) collective-permute-start(f32[384,256]{1,0:T(8,128)S(1)} %get-tuple-element.27), channel_id=1, source_target_pairs={{0,1},{1,0},{2,3},{3,2},{4,5},{5,4},{6,7},{7,6},{8,9},{9,8},{10,11... | collective-permute-start | bytes 1179656 | tf_op jit(solution)/shard_map/coupling/ppermute | solution.py:24
  89.6 1.3 collective-permute-done.17
  90.9 0.1 add.20.refs_8_
  91.0 1.8 %coupling.5.own_ref = bf16[3,1024,256]{2,1,0:T(8,128)(2,1)} custom-call(s32[6]{0:T(128)S(1)} %pad_add_fusion.at_ref.refs_0_, bf16[3,128,256]{2,1,0:T(8,128)(2,1)S(1)} %select.17.refs_0_, bf16[3,128,256]{2,1,0:T(8,128)(2,1)S(1)} %collective-permute-done.10.refs_1_, bf16[3,128,256]{2,1,0:T(8,128)(2,1)S(1)} %collective-permute-done.11.refs_2_, ...), custom_call_target="tpu_custom_call" | custom-call | bytes 1966104 | tf_op jit(solution)/shard_map/coupling/pallas_call | solution.py:33
  92.8 0.4 collective-permute-start.18
  93.2 13.3 %all_to_all.15.part_ref = f32[8,48,256]{2,1,0:T(8,128)S(1)} all-to-all(f32[8,48,256]{2,1,0:T(8,128)S(1)} %bitcast.11), channel_id=1, replica_groups=mesh['yl'=2,'x'=4,'yh'=2,'z'=8,'core'=2] {'yl','x'}, dimensions={0} | all-to-all | bytes 786432 | tf_op jit(solution)/shard_map/coupling/all_to_all | solution.py:316
  106.5 0.8 coupling.6
  107.3 5.7 %all-to-all-start.1 = ((f32[16,24,256]{2,1,0:T(8,128)}), f32[16,24,256]{2,1,0:T(8,128)S(1)}, u32[]{:S(2)}, u32[]{:S(2)}) async-start(f32[16,24,256]{2,1,0:T(8,128)} %coupling.6), calls=%async_computation.1 | async-start | bytes 786432 | tf_op jit(solution)/shard_map/coupling/all_to_all | solution.py:317
  113.1 12.3 %all-to-all-done.1.parts_ref = f32[16,24,256]{2,1,0:T(8,128)S(1)} async-done(((f32[16,24,256]{2,1,0:T(8,128)}), f32[16,24,256]{2,1,0:T(8,128)S(1)}, u32[]{:S(2)}, u32[]{:S(2)}) %all-to-all-start.1) | async-done | bytes 393248 | tf_op jit(solution)/shard_map/coupling/all_to_all | solution.py:317
  125.4 15.8 %all_to_all.16 = bf16[32,24,256]{2,1,0:T(8,128)(2,1)S(1)} all-to-all(bf16[32,24,256]{2,1,0:T(8,128)(2,1)S(1)} %broadcast_in_dim.15), channel_id=1, replica_groups=mesh['yl'=2,'x'=4,'yh'=2,'z'=8,'core'=2] {'core','yl','x','yh'}, dimensions={0} | all-to-all | bytes 786432 | tf_op jit(solution)/shard_map/coupling/all_to_all | solution.py:322
  141.2 7.4 %output.1 = bf16[2048,1024]{1,0:T(8,128)(2,1)} custom-call(s32[6]{0:T(128)S(1)} %pad_add_fusion.at_ref.refs_0_, bf16[3,1024,256]{2,1,0:T(8,128)(2,1)} %coupling.5.own_ref, bf16[3,1024,256]{2,1,0:T(8,128)(2,1)} %collective-permute-done.18.other_ref, bf16[3,256,256]{2,1,0:T(8,128)(2,1)S(1)} %bitcast.12, bf16[3,1024,256]{2,1,0:T(8,128)(2,1)S(1)} %copy-done.2), custom_call_target="tpu_custom_call" | custom-call | flops 4026531840 | bytes 5111832 | tf_op jit(solution)/shard_map/output/pallas_call | solution.py:33
  (20 shorter events, 0.1 us)
Async XLA Ops:
  0.0 6.9 %copy-start.2 = (bf16[3,1024,256]{2,1,0:T(8,128)(2,1)S(1)}, bf16[3,1024,256]{2,1,0:T(8,128)(2,1)}, u32[]{:S(2)}) copy-start(bf16[3,1024,256]{2,1,0:T(8,128)(2,1)} %panels_ref.5) | copy-start | bytes 4718596
  1.4 4.9 %collective-permute-start = (bf16[1024,256]{1,0:T(8,128)(2,1)S(1)}, bf16[1024,256]{1,0:T(8,128)(2,1)S(1)}, u32[]{:S(2)}, u32[]{:S(2)}) collective-permute-start(bf16[1024,256]{1,0:T(8,128)(2,1)S(1)} %get-tuple-element.29), channel_id=1, source_target_pairs={{0,1},{1,0},{2,3},{3,2},{4,5},{5,4},{6,7},{7,6},{8,9},{9,8},{10,11... | collective-permute-start | bytes 1572872 | tf_op jit(solution)/shard_map/select/ppermute | solution.py:24
  6.9 2.2 %copy-start = (bf16[2048,1024]{1,0:T(8,128)(2,1)S(1)}, bf16[2048,1024]{1,0:T(8,128)(2,1)}, u32[]{:S(2)}) copy-start(bf16[2048,1024]{1,0:T(8,128)(2,1)} %gradient_ref.3) | copy-start | bytes 12582916
  12.1 22.0 %copy-start.1 = (bf16[2048,1024]{1,0:T(8,128)(2,1)S(1)}, bf16[2048,1024]{1,0:T(8,128)(2,1)}, u32[]{:S(2)}) copy-start(bf16[2048,1024]{1,0:T(8,128)(2,1)} %gradient_ref.3) | copy-start | bytes 12582916
  12.2 34.6 %collective-permute-start.9 = (f32[3,1024,256]{2,1,0:T(8,128)S(1)}, f32[3,1024,256]{2,1,0:T(8,128)S(1)}, u32[]{:S(2)}, u32[]{:S(2)}) collective-permute-start(f32[3,1024,256]{2,1,0:T(8,128)S(1)} %select.11.refs_5_.refs_0_), channel_id=1, source_target_pairs={{0,1},{1,0},{2,3},{3,2},{4,5},{5,4},{6,7},{7,6},{8,9},{9,8},{10,11... | collective-permute-start | bytes 9437192 | tf_op jit(solution)/shard_map/select/ppermute | solution.py:24
  12.6 8.0 %collective-permute-start.2 = (bf16[3,128,256]{2,1,0:T(8,128)(2,1)S(1)}, bf16[3,128,256]{2,1,0:T(8,128)(2,1)S(1)}, u32[]{:S(2)}, u32[]{:S(2)}) collective-permute-start(bf16[3,128,256]{2,1,0:T(8,128)(2,1)S(1)} %get-tuple-element.18), channel_id=1, source_target_pairs={{0,14},{2,0},{4,2},{6,4},{8,6},{10,8},{12,10},{14,12},{1,15},{3,1}... | collective-permute-start | bytes 589832 | tf_op jit(solution)/shard_map/select/ppermute | solution.py:28
  16.5 7.3 %collective-permute-start.1 = (bf16[3,128,256]{2,1,0:T(8,128)(2,1)S(1)}, bf16[3,128,256]{2,1,0:T(8,128)(2,1)S(1)}, u32[]{:S(2)}, u32[]{:S(2)}) collective-permute-start(bf16[3,128,256]{2,1,0:T(8,128)(2,1)S(1)} %get-tuple-element.17.refs_0_), channel_id=1, source_target_pairs={{0,2},{2,4},{4,6},{6,8},{8,10},{10,12},{12,14},{14,0},{1,3},{3,5},... | collective-permute-start | bytes 589832 | tf_op jit(solution)/shard_map/select/ppermute | solution.py:28
  24.3 6.4 %collective-permute-start.3 = (bf16[3,128,256]{2,1,0:T(8,128)(2,1)S(1)}, bf16[3,128,256]{2,1,0:T(8,128)(2,1)S(1)}, u32[]{:S(2)}, u32[]{:S(2)}) collective-permute-start(bf16[3,128,256]{2,1,0:T(8,128)(2,1)S(1)} %get-tuple-element.19), channel_id=1, source_target_pairs={{0,2},{2,4},{4,6},{6,8},{8,10},{10,12},{12,14},{14,0},{1,3},{3,5},... | collective-permute-start | bytes 589832 | tf_op jit(solution)/shard_map/select/ppermute | solution.py:28
  24.4 6.3 %collective-permute-start.4 = (bf16[3,128,256]{2,1,0:T(8,128)(2,1)S(1)}, bf16[3,128,256]{2,1,0:T(8,128)(2,1)S(1)}, u32[]{:S(2)}, u32[]{:S(2)}) collective-permute-start(bf16[3,128,256]{2,1,0:T(8,128)(2,1)S(1)} %get-tuple-element.20), channel_id=1, source_target_pairs={{0,14},{2,0},{4,2},{6,4},{8,6},{10,8},{12,10},{14,12},{1,15},{3,1}... | collective-permute-start | bytes 589832 | tf_op jit(solution)/shard_map/select/ppermute | solution.py:28
  31.3 5.8 %collective-permute-start.5 = (bf16[3,128,256]{2,1,0:T(8,128)(2,1)S(1)}, bf16[3,128,256]{2,1,0:T(8,128)(2,1)S(1)}, u32[]{:S(2)}, u32[]{:S(2)}) collective-permute-start(bf16[3,128,256]{2,1,0:T(8,128)(2,1)S(1)} %get-tuple-element.21), channel_id=1, source_target_pairs={{0,2},{2,4},{4,6},{6,8},{8,10},{10,12},{12,14},{14,0},{1,3},{3,5},... | collective-permute-start | bytes 589832 | tf_op jit(solution)/shard_map/select/ppermute | solution.py:28
  31.4 5.7 %collective-permute-start.6 = (bf16[3,128,256]{2,1,0:T(8,128)(2,1)S(1)}, bf16[3,128,256]{2,1,0:T(8,128)(2,1)S(1)}, u32[]{:S(2)}, u32[]{:S(2)}) collective-permute-start(bf16[3,128,256]{2,1,0:T(8,128)(2,1)S(1)} %get-tuple-element.22), channel_id=1, source_target_pairs={{0,14},{2,0},{4,2},{6,4},{8,6},{10,8},{12,10},{14,12},{1,15},{3,1}... | collective-permute-start | bytes 589832 | tf_op jit(solution)/shard_map/select/ppermute | solution.py:28
  37.1 9.6 %copy-start.3 = (f32[3,256,256]{2,1,0:T(8,128)S(1)}, f32[3,256,256]{2,1,0:T(8,128)}, u32[]{:S(2)}) copy-start(f32[3,256,256]{2,1,0:T(8,128)} %values_ref.1) | copy-start | bytes 2359300
  37.8 5.4 %collective-permute-start.7 = (bf16[3,128,256]{2,1,0:T(8,128)(2,1)S(1)}, bf16[3,128,256]{2,1,0:T(8,128)(2,1)S(1)}, u32[]{:S(2)}, u32[]{:S(2)}) collective-permute-start(bf16[3,128,256]{2,1,0:T(8,128)(2,1)S(1)} %get-tuple-element.24), channel_id=1, source_target_pairs={{0,14},{2,0},{4,2},{6,4},{8,6},{10,8},{12,10},{14,12},{1,15},{3,1}... | collective-permute-start | bytes 589832 | tf_op jit(solution)/shard_map/select/ppermute | solution.py:28
  43.7 6.1 %collective-permute-start.8 = (bf16[3,128,256]{2,1,0:T(8,128)(2,1)S(1)}, bf16[3,128,256]{2,1,0:T(8,128)(2,1)S(1)}, u32[]{:S(2)}, u32[]{:S(2)}) collective-permute-start(bf16[3,128,256]{2,1,0:T(8,128)(2,1)S(1)} %select.15.mine_ref), channel_id=1, source_target_pairs={{0,16},{16,0},{1,17},{17,1},{2,18},{18,2},{3,19},{19,3},{4,20},{20... | collective-permute-start | bytes 589832 | tf_op jit(solution)/shard_map/select/ppermute | solution.py:24
  50.5 6.4 %collective-permute-start.10 = (bf16[3,128,256]{2,1,0:T(8,128)(2,1)S(1)}, bf16[3,128,256]{2,1,0:T(8,128)(2,1)S(1)}, u32[]{:S(2)}, u32[]{:S(2)}) collective-permute-start(bf16[3,128,256]{2,1,0:T(8,128)(2,1)S(1)} %select.17.refs_0_), channel_id=1, source_target_pairs={{0,2},{2,4},{4,6},{6,8},{8,10},{10,12},{12,14},{14,0},{1,3},{3,5},... | collective-permute-start | bytes 589832 | tf_op jit(solution)/shard_map/gather/ppermute | solution.py:28
  50.7 6.2 %collective-permute-start.11 = (bf16[3,128,256]{2,1,0:T(8,128)(2,1)S(1)}, bf16[3,128,256]{2,1,0:T(8,128)(2,1)S(1)}, u32[]{:S(2)}, u32[]{:S(2)}) collective-permute-start(bf16[3,128,256]{2,1,0:T(8,128)(2,1)S(1)} %select.17.refs_0_), channel_id=1, source_target_pairs={{0,14},{2,0},{4,2},{6,4},{8,6},{10,8},{12,10},{14,12},{1,15},{3,1}... | collective-permute-start | bytes 589832 | tf_op jit(solution)/shard_map/gather/ppermute | solution.py:28
  56.9 7.8 %collective-permute-start.12 = (bf16[3,128,256]{2,1,0:T(8,128)(2,1)S(1)}, bf16[3,128,256]{2,1,0:T(8,128)(2,1)S(1)}, u32[]{:S(2)}, u32[]{:S(2)}) collective-permute-start(bf16[3,128,256]{2,1,0:T(8,128)(2,1)S(1)} %collective-permute-done.10.refs_1_), channel_id=1, source_target_pairs={{0,2},{2,4},{4,6},{6,8},{8,10},{10,12},{12,14},{14,0},{1,3},{3,5},... | collective-permute-start | bytes 589832 | tf_op jit(solution)/shard_map/gather/ppermute | solution.py:28
  56.9 7.8 %collective-permute-start.13 = (bf16[3,128,256]{2,1,0:T(8,128)(2,1)S(1)}, bf16[3,128,256]{2,1,0:T(8,128)(2,1)S(1)}, u32[]{:S(2)}, u32[]{:S(2)}) collective-permute-start(bf16[3,128,256]{2,1,0:T(8,128)(2,1)S(1)} %collective-permute-done.11.refs_2_), channel_id=1, source_target_pairs={{0,14},{2,0},{4,2},{6,4},{8,6},{10,8},{12,10},{14,12},{1,15},{3,1}... | collective-permute-start | bytes 589832 | tf_op jit(solution)/shard_map/gather/ppermute | solution.py:28
  64.7 7.0 %collective-permute-start.14 = (bf16[3,128,256]{2,1,0:T(8,128)(2,1)S(1)}, bf16[3,128,256]{2,1,0:T(8,128)(2,1)S(1)}, u32[]{:S(2)}, u32[]{:S(2)}) collective-permute-start(bf16[3,128,256]{2,1,0:T(8,128)(2,1)S(1)} %collective-permute-done.12.refs_3_), channel_id=1, source_target_pairs={{0,2},{2,4},{4,6},{6,8},{8,10},{10,12},{12,14},{14,0},{1,3},{3,5},... | collective-permute-start | bytes 589832 | tf_op jit(solution)/shard_map/gather/ppermute | solution.py:28
  64.7 7.0 %collective-permute-start.15 = (bf16[3,128,256]{2,1,0:T(8,128)(2,1)S(1)}, bf16[3,128,256]{2,1,0:T(8,128)(2,1)S(1)}, u32[]{:S(2)}, u32[]{:S(2)}) collective-permute-start(bf16[3,128,256]{2,1,0:T(8,128)(2,1)S(1)} %collective-permute-done.13.refs_4_), channel_id=1, source_target_pairs={{0,14},{2,0},{4,2},{6,4},{8,6},{10,8},{12,10},{14,12},{1,15},{3,1}... | collective-permute-start | bytes 589832 | tf_op jit(solution)/shard_map/gather/ppermute | solution.py:28
  71.7 6.1 %collective-permute-start.16 = (bf16[3,128,256]{2,1,0:T(8,128)(2,1)S(1)}, bf16[3,128,256]{2,1,0:T(8,128)(2,1)S(1)}, u32[]{:S(2)}, u32[]{:S(2)}) collective-permute-start(bf16[3,128,256]{2,1,0:T(8,128)(2,1)S(1)} %collective-permute-done.14.refs_5_), channel_id=1, source_target_pairs={{0,2},{2,4},{4,6},{6,8},{8,10},{10,12},{12,14},{14,0},{1,3},{3,5},... | collective-permute-start | bytes 589832 | tf_op jit(solution)/shard_map/gather/ppermute | solution.py:28
  80.1 10.8 %collective-permute-start.17 = (f32[384,256]{1,0:T(8,128)S(1)}, f32[384,256]{1,0:T(8,128)S(1)}, u32[]{:S(2)}, u32[]{:S(2)}) collective-permute-start(f32[384,256]{1,0:T(8,128)S(1)} %get-tuple-element.27), channel_id=1, source_target_pairs={{0,1},{1,0},{2,3},{3,2},{4,5},{5,4},{6,7},{7,6},{8,9},{9,8},{10,11... | collective-permute-start | bytes 1179656 | tf_op jit(solution)/shard_map/coupling/ppermute | solution.py:24
  92.8 48.4 %collective-permute-start.18 = (bf16[3,1024,256]{2,1,0:T(8,128)(2,1)}, bf16[3,1024,256]{2,1,0:T(8,128)(2,1)}, u32[]{:S(2)}, u32[]{:S(2)}) collective-permute-start(bf16[3,1024,256]{2,1,0:T(8,128)(2,1)} %coupling.5.own_ref), channel_id=1, source_target_pairs={{0,1},{1,0},{2,3},{3,2},{4,5},{5,4},{6,7},{7,6},{8,9},{9,8},{10,11... | collective-permute-start | bytes 4718600 | tf_op jit(solution)/shard_map/coupling/ppermute | solution.py:24
  107.3 18.0 %all-to-all-start.1 = ((f32[16,24,256]{2,1,0:T(8,128)}), f32[16,24,256]{2,1,0:T(8,128)S(1)}, u32[]{:S(2)}, u32[]{:S(2)}) async-start(f32[16,24,256]{2,1,0:T(8,128)} %coupling.6), calls=%async_computation.1 | async-start | bytes 786432 | tf_op jit(solution)/shard_map/coupling/all_to_all | solution.py:317

commit v4 on v3

v4 whole, which is shorter than its diff:
```python
import functools

import jax
import jax.numpy as jnp
from jax import lax
from jax.experimental import pallas as pl
from jax.experimental.pallas import tpu as pltpu
from jax.sharding import Mesh
from jax.sharding import PartitionSpec as P

ROW = ("yl", "x")
COL = ("yh", "z", "core")
PLANE = ("core", "yl", "x", "yh")
F32 = jnp.float32
BF16 = jnp.bfloat16
RING = 8
REACH = RING // 2
BLOCKS = 4
MIB = 1024 * 1024

VMEM = pl.BlockSpec(memory_space=pltpu.VMEM)
SMEM = pl.BlockSpec(memory_space=pltpu.SMEM)
ANY = pl.BlockSpec(memory_space=pl.ANY)
TOKEN = jax.ShapeDtypeStruct((8, 128), F32)


def swap(x, axis):
    return lax.ppermute(x, axis, [(0, 1), (1, 0)])


def shift(x, by):
    return lax.ppermute(x, "z", [(i, (i + by) % RING) for i in range(RING)])


def call(kernel, args, in_specs, out_specs, out_shape, flops=0, scratch=(), limit=16):
    moved = sum(a.size * a.dtype.itemsize for a in args)
    return pl.pallas_call(
        kernel,
        in_specs=in_specs,
        out_specs=out_specs,
        out_shape=out_shape,
        scratch_shapes=scratch,
        compiler_params=pltpu.CompilerParams(vmem_limit_bytes=limit * MIB),
        cost_estimate=pl.CostEstimate(flops=flops, bytes_accessed=moved, transcendentals=0),
    )(*args)


def owner_of(at_ref, k):
    number = at_ref[4 + k]
    return number & 1, (number >> 1) & (RING - 1), number >> 4


def picked(at_ref, k, own_ref, other_ref, index, put):
    core, _, _ = owner_of(at_ref, k)
    rows = own_ref.shape[0] // RING
    span = pl.ds(pl.multiple_of((index & (RING - 1)) * rows, rows), rows)
    pl.when(core == at_ref[0])(lambda: put(own_ref[span]))
    pl.when(core != at_ref[0])(lambda: put(other_ref[span]))


def start_kernel(at_ref, own_ref, other_ref, up_ref, down_ref, token_ref):
    here = at_ref[2]
    for k in range(up_ref.shape[0]):
        picked(at_ref, k, own_ref, other_ref, here + REACH - 1, lambda x, k=k: up_ref.__setitem__(k, x))
        picked(at_ref, k, own_ref, other_ref, here - REACH + RING, lambda x, k=k: down_ref.__setitem__(k, x))
    token_ref[...] = jnp.zeros_like(token_ref)


def merge_kernel(step, at_ref, own_ref, other_ref, came_up_ref, came_down_ref, _, up_ref, down_ref, token_ref):
    here = at_ref[2]
    for k in range(up_ref.shape[0]):
        _, place, _ = owner_of(at_ref, k)

        @pl.when(place == here)
        def _():
            picked(at_ref, k, own_ref, other_ref, here + REACH - 1 - step, lambda x: up_ref.__setitem__(k, x))
            picked(at_ref, k, own_ref, other_ref, here - REACH + RING + step, lambda x: down_ref.__setitem__(k, x))

        @pl.when(place != here)
        def _():
            up_ref[k] = came_up_ref[k]
            down_ref[k] = came_down_ref[k]

    token_ref[...] = jnp.zeros_like(token_ref)


def last_kernel(at_ref, up_ref, came_down_ref, _, out_ref, token_ref):
    here = at_ref[2]
    for k in range(out_ref.shape[0]):
        _, place, _ = owner_of(at_ref, k)
        below = ((here - place) & (RING - 1)) < REACH

        @pl.when(below)
        def _():
            out_ref[k] = up_ref[k]

        @pl.when(jnp.logical_not(below))
        def _():
            out_ref[k] = came_down_ref[k]

    token_ref[...] = jnp.zeros_like(token_ref)


def level_kernel(at_ref, mine_ref, other_ref, _, out_ref):
    for k in range(out_ref.shape[0]):
        _, _, high = owner_of(at_ref, k)

        @pl.when(high == at_ref[1])
        def _():
            out_ref[k] = mine_ref[k]

        @pl.when(high != at_ref[1])
        def _():
            out_ref[k] = other_ref[k]


def project_kernel(number, _, gradient_ref, panels_ref, out_ref, token_ref, rows_ref, sem):
    size = rows_ref.shape[0]
    vec = panels_ref.shape[2]
    copy = pltpu.make_async_copy(gradient_ref.at[pl.ds(number * size, size)], rows_ref, sem)
    copy.start()
    copy.wait()
    for k in range(panels_ref.shape[0]):
        total = jnp.dot(rows_ref[...], panels_ref[k], preferred_element_type=F32).T
        high = total.astype(BF16)
        out_ref[k, :vec] = high
        out_ref[k, vec:] = (total - high.astype(F32)).astype(BF16)
    token_ref[...] = jnp.zeros_like(token_ref)


def project(number, token, gradient, panels):
    count, width, vec = panels.shape
    size = gradient.shape[0] // BLOCKS
    return call(
        functools.partial(project_kernel, number),
        (token, gradient, panels),
        [ANY, ANY, VMEM],
        [VMEM, VMEM],
        [jax.ShapeDtypeStruct((count, 2 * vec, size), BF16), TOKEN],
        2 * size * width * vec * count,
        [pltpu.VMEM((size, width), BF16), pltpu.SemaphoreType.DMA],
    )


def damp_kernel(at_ref, values_ref, _, out_ref, token_ref, all_ref):
    count, vec, _ = values_ref.shape
    for k in range(count):
        values = values_ref[k]
        all_ref[k * vec : (k + 1) * vec] = (values + 0.1 * jnp.mean(values)).T
    size = out_ref.shape[0]
    out_ref[...] = all_ref[pl.ds(pl.multiple_of(at_ref[3] * size, size), size)]
    token_ref[...] = jnp.zeros_like(token_ref)


def damp(at, values, places, token):
    count, vec, _ = values.shape
    size = count * vec // places
    shapes = [jax.ShapeDtypeStruct((size, vec), F32), TOKEN]
    return call(damp_kernel, (at, values, token), [SMEM, VMEM, ANY], [VMEM, VMEM], shapes, scratch=[pltpu.VMEM((count * vec, vec), F32)])


def offsets():
    order = [0]
    for step in range(1, REACH + 1):
        order.append(-step)
        if step < REACH:
            order.append(step)
    return order


def first_row(at_ref, own, offset, rows):
    half = at_ref[0] if own else 1 - at_ref[0]
    return pl.multiple_of((half * RING + ((at_ref[2] + offset + RING) & (RING - 1))) * rows, rows)


def early_kernel(at_ref, *refs):
    terms, refs = refs[:BLOCKS], refs[BLOCKS:]
    pieces, (total_ref, all_ref) = refs[: 2 * (RING - 1)], refs[2 * (RING - 1) :]
    count, rows, vec = pieces[0].shape
    order = [(own, offset) for offset in offsets()[:-1] for own in (True, False)]
    for piece, (own, offset) in zip(pieces, order):
        span = pl.ds(first_row(at_ref, own, offset, rows), rows)
        for k in range(count):
            all_ref[k, span] = piece[k]
    for own in (True, False):
        span = pl.ds(first_row(at_ref, own, REACH, rows), rows)
        for k in range(count):
            all_ref[k, span] = jnp.zeros((rows, vec), BF16)
    size = all_ref.shape[1] // BLOCKS
    for k in range(count):
        both = None
        for b in range(BLOCKS):
            term = jnp.dot(terms[b][k], all_ref[k, b * size : (b + 1) * size], preferred_element_type=F32)
            both = term if both is None else both + term
        total_ref[k * vec : (k + 1) * vec] = both[:vec] + both[vec:]


def early(at, terms, pieces):
    count, rows, vec = pieces[0].shape
    shapes = [jax.ShapeDtypeStruct((count * vec, vec), F32), jax.ShapeDtypeStruct((count, 2 * RING * rows, vec), BF16)]
    specs = [SMEM] + [VMEM] * (BLOCKS + len(pieces))
    return call(early_kernel, (at, *terms, *pieces), specs, [VMEM, VMEM], shapes, 4 * count * RING * rows * vec * vec)


def late_kernel(at_ref, *refs):
    terms, (total_ref, own_ref, other_ref, out_ref) = refs[:BLOCKS], refs[BLOCKS:]
    count, rows, vec = own_ref.shape
    size = terms[0].shape[2]
    out_ref[...] = total_ref[...]
    for own, piece in ((True, own_ref), (False, other_ref)):
        first = first_row(at_ref, own, REACH, rows)
        for b in range(BLOCKS):

            @pl.when(first // size == b)
            def _():
                span = pl.ds(pl.multiple_of(first - b * size, rows), rows)
                for k in range(count):
                    both = jnp.dot(terms[b][k, :, span], piece[k], preferred_element_type=F32)
                    out_ref[k * vec : (k + 1) * vec] += both[:vec] + both[vec:]


def late(at, terms, total, own, other):
    specs = [SMEM] + [VMEM] * (BLOCKS + 3)
    return call(late_kernel, (at, *terms, total, own, other), specs, VMEM, jax.ShapeDtypeStruct(total.shape, F32))


def spread_kernel(part_ref, out_ref):
    total = jnp.sum(part_ref[...], axis=0)
    for j in range(RING):
        out_ref[j] = total


def spread(parts):
    return call(spread_kernel, (parts,), [VMEM], VMEM, jax.ShapeDtypeStruct((RING,) + parts.shape[1:], F32))


def scale_kernel(parts_ref, below_ref, out_ref):
    out_ref[...] = (jnp.sum(parts_ref[...], axis=0) / below_ref[...]).astype(BF16)


def apply_kernel(at_ref, own_ref, other_ref, all_ref, scaled_ref, panels_ref, out_ref, fetched_ref, block_ref, in_sem, sems):
    steps, size, _ = block_ref.shape
    count, rows, _ = own_ref.shape
    fetch = pltpu.make_async_copy(all_ref, fetched_ref, in_sem)
    fetch.start()
    fetch.wait()
    for own, piece in ((True, own_ref), (False, other_ref)):
        span = pl.ds(first_row(at_ref, own, REACH, rows), rows)
        for k in range(count):
            fetched_ref[k, span] = piece[k]
    copies = []
    for number in range(steps):
        total = None
        span = slice(number * size, (number + 1) * size)
        for k in range(count):
            rotated = lax.dot_general(fetched_ref[k, span], scaled_ref[k], (((1,), (1,)), ((), ())), preferred_element_type=F32)
            term = lax.dot_general(rotated.astype(BF16), panels_ref[k], (((1,), (1,)), ((), ())), preferred_element_type=F32)
            total = term if total is None else total + term
        block_ref[number] = total.astype(BF16)
        copies.append(pltpu.make_async_copy(block_ref.at[number], out_ref.at[pl.ds(number * size, size)], sems.at[number]))
        copies[-1].start()
    for copy in copies:
        copy.wait()


def apply(at, own, other, fetched, scaled, panels):
    count, rows, vec = fetched.shape
    width = panels.shape[1]
    steps = 4
    return call(
        apply_kernel,
        (at, own, other, fetched, scaled, panels),
        [SMEM, VMEM, VMEM, ANY, VMEM, VMEM],
        ANY,
        jax.ShapeDtypeStruct((rows, width), BF16),
        2 * count * rows * vec * (vec + width),
        [
            pltpu.VMEM(fetched.shape, BF16),
            pltpu.VMEM((steps, rows // steps, width), BF16),
            pltpu.SemaphoreType.DMA,
            pltpu.SemaphoreType.DMA((steps,)),
        ],
        limit=24,
    )


def body(gradient, in_panels, out_pool, eigenvalues, owners):
    core, high, here = (lax.axis_index(a) for a in ("core", "yh", "z"))
    at = jnp.concatenate([jnp.stack([core, high, here, lax.axis_index(PLANE)]).astype(jnp.int32), owners])
    count, _, vec = in_panels.shape
    panel = out_pool[0]
    half = panel.shape[0] // 2
    piece = jax.ShapeDtypeStruct((count, half // RING, vec), BF16)
    terms = []

    with jax.named_scope("select"):
        own = lax.dynamic_slice_in_dim(panel, core * half, half, 0)
        other = swap(lax.dynamic_slice_in_dim(panel, (1 - core) * half, half, 0), "core")
        up, down, token = call(start_kernel, (at, own, other), [SMEM, VMEM, VMEM], [VMEM] * 3, [piece] * 2 + [TOKEN])
        for step in range(1, REACH):
            term, token = project(step - 1, token, gradient, in_panels)
            terms.append(term)
            args = (at, own, other, shift(up, 1), shift(down, -1), token)
            kernel = functools.partial(merge_kernel, step)
            up, down, token = call(kernel, args, [SMEM] + [VMEM] * 4 + [ANY], [VMEM] * 3, [piece] * 2 + [TOKEN])
        term, token = project(REACH - 1, token, gradient, in_panels)
        terms.append(term)
        mine, token = call(last_kernel, (at, up, shift(down, -1), token), [SMEM] + [VMEM] * 2 + [ANY], [VMEM] * 2, [piece, TOKEN])
        below, token = damp(at, eigenvalues, 32, token)
        mine = call(level_kernel, (at, mine, swap(mine, "yh"), token), [SMEM] + [VMEM] * 2 + [ANY], VMEM, piece)

    with jax.named_scope("gather"):
        pieces = [mine, swap(mine, "core")]
        up = down = mine
        for _ in range(1, REACH):
            up, down = shift(up, 1), shift(down, -1)
            pieces += [up, swap(up, "core"), down, swap(down, "core")]
        pieces += [shift(up, 1), shift(pieces[-1], -1)]

    with jax.named_scope("coupling"):
        part, fetched = early(at, terms, pieces[:-2])
        part = late(at, terms, part, *pieces[-2:])
        part = spread(lax.all_to_all(part.reshape(32, -1, vec), PLANE, 0, 0))
        part = lax.all_to_all(part, "z", 0, 0)
        scaled = call(scale_kernel, (part, below), [VMEM, VMEM], VMEM, jax.ShapeDtypeStruct(part.shape[1:], BF16))
        copies = jnp.broadcast_to(scaled[None], (32,) + scaled.shape)
        scaled = lax.all_to_all(copies, PLANE, 0, 0).reshape(count, vec, vec)

    with jax.named_scope("output"):
        return apply(at, *pieces[-2:], fetched, scaled, in_panels)


def solution(mesh):
    fine = Mesh(mesh.devices.reshape(2, 4, 2, 8, 2), ROW + COL)
    return jax.shard_map(
        body,
        mesh=fine,
        in_specs=(P(ROW, COL), P(None, COL, None), P(COL, ROW, None), P(), P()),
        out_specs=P(ROW, COL),
        check_vma=False,
    )
```

time: 149 us -> 145 us (0.973)
  waiting for transfers between devices: 48.1 us -> 24 us
  blocking collectives: 29.2 us -> 51.5 us
  Pallas kernels: 23.5 us -> 19.9 us
  starting transfers between devices: 43.3 us -> 45.1 us
    all_to_all x2 -> x3, blocking collectives: 29.2 us -> 51.5 us  [the longest x1 22.2 us: body(): part = spread(lax.all_to_all(part.reshape(32, -1, vec), PLANE, 0, 0))]
    all_to_all x1 -> x0, waiting for transfers between devices: 12.3 us -> none  [body(): part = lax.all_to_all(part, ('yh', 'z'), 0, 0)]
    ppermute x14 -> x15, waiting for transfers between devices: 31.9 us -> 20.4 us  [shift(): return lax.ppermute(x, 'z', [(i, (i + by) % RING) for i in range(RING)])]
    all_to_all x1 -> x0, starting transfers between devices: 5.71 us -> none  [body(): part = lax.all_to_all(part, ('yh', 'z'), 0, 0)]
    ppermute x14 -> x15, starting transfers between devices: 21 us -> 24.9 us  [shift(): return lax.ppermute(x, 'z', [(i, (i + by) % RING) for i in range(RING)])]
    ppermute x5 -> x9, starting transfers between devices: 16.6 us -> 20.2 us  [swap(): return lax.ppermute(x, axis, [(0, 1), (1, 0)])]
    pallas_call x13 -> x16, Pallas kernels: 22.1 us -> 19.9 us  [call(): pl.pallas_call(kernel, in_specs=in_specs, out_specs=out_specs, out_shape=...]
    ppermute x5 -> x9, waiting for transfers between devices: 3.89 us -> 3.58 us  [swap(): return lax.ppermute(x, axis, [(0, 1), (1, 0)])]
  transfers between devices with their start and end apart: 20 -> 24, of which waited for: 12 -> 10; matrix products, arithmetic and copies ran while one was open for 1% -> 0% of each run, Pallas kernels for 5% -> 6%
where the time goes in v4:
time: 145 us
  blocking collectives  51.5 us (36%)
  starting transfers between devices  45.1 us (31%)
  waiting for transfers between devices  24 us (17%)
  Pallas kernels  19.9 us (14%)
  local copies, waits for them, and re-layouts  3.7 us (3%)
    ppermute x15, starting transfers between devices, shift(): return lax.ppermute(x, 'z', [(i, (i + by) % RING) for i in range(RING)])  24.9 us
    all_to_all x1, blocking collectives, body(): part = spread(lax.all_to_all(part.reshape(32, -1, vec), PLANE, 0, 0))  22.2 us
    ppermute x15, waiting for transfers between devices, shift(): return lax.ppermute(x, 'z', [(i, (i + by) % RING) for i in range(RING)])  20.4 us
    ppermute x9, starting transfers between devices, swap(): return lax.ppermute(x, axis, [(0, 1), (1, 0)])  20.2 us
    pallas_call x16, Pallas kernels, call(): pl.pallas_call(kernel, in_specs=in_specs, out_specs=out_specs, out_shape=...  19.9 us
    all_to_all x1, blocking collectives, body(): scaled = lax.all_to_all(copies, PLANE, 0, 0).reshape(count, vec, vec)  15.4 us
    all_to_all x1, blocking collectives, body(): part = lax.all_to_all(part, 'z', 0, 0)  13.9 us
    ppermute x9, waiting for transfers between devices, swap(): return lax.ppermute(x, axis, [(0, 1), (1, 0)])  3.58 us
  transfers between devices with their start and end apart: 24, of which 10 were waited for; matrix products, arithmetic and copies ran while one was open for 0% of the time, Pallas kernels for 6%

profile of v4, /device:TPU:1, one launch (start us, length us, event | category | flops | bytes accessed | tf_op | source)
XLA Modules:
  0.0 144.5 jit_solution(9060786639651950462)
XLA Ops:
  0.0 1.4 dynamic-slice_bitcast_fusion
  1.4 3.3 %collective-permute-start = (bf16[1024,256]{1,0:T(8,128)(2,1)S(1)}, bf16[1024,256]{1,0:T(8,128)(2,1)S(1)}, u32[]{:S(2)}, u32[]{:S(2)}) collective-permute-start(bf16[1024,256]{1,0:T(8,128)(2,1)S(1)} %get-tuple-element.57), channel_id=1, source_target_pairs={{0,1},{1,0},{2,3},{3,2},{4,5},{5,4},{6,7},{7,6},{8,9},{9,8},{10,11... | collective-permute-start | bytes 1572872 | tf_op jit(solution)/shard_map/select/ppermute | solution.py:28
  4.7 0.1 concatenate.3.at_ref
  4.8 1.5 %collective-permute-done.other_ref = bf16[1024,256]{1,0:T(8,128)(2,1)S(1)} collective-permute-done((bf16[1024,256]{1,0:T(8,128)(2,1)S(1)}, bf16[1024,256]{1,0:T(8,128)(2,1)S(1)}, u32[]{:S(2)}, u32[]{:S(2)}) %collective-permute-start) | collective-permute-done | bytes 524320 | tf_op jit(solution)/shard_map/select/ppermute | solution.py:28
  6.3 0.7 select.11
  6.9 0.1 collective-permute-start.1
  7.0 3.9 %collective-permute-start.2 = (bf16[3,128,256]{2,1,0:T(8,128)(2,1)S(1)}, bf16[3,128,256]{2,1,0:T(8,128)(2,1)S(1)}, u32[]{:S(2)}, u32[]{:S(2)}) collective-permute-start(bf16[3,128,256]{2,1,0:T(8,128)(2,1)S(1)} %get-tuple-element.32), channel_id=1, source_target_pairs={{0,14},{2,0},{4,2},{6,4},{8,6},{10,8},{12,10},{14,12},{1,15},{3,1}... | collective-permute-start | bytes 589832 | tf_op jit(solution)/shard_map/select/ppermute | solution.py:32
  10.9 2.2 %copy-done = bf16[2048,1024]{1,0:T(8,128)(2,1)S(1)} copy-done((bf16[2048,1024]{1,0:T(8,128)(2,1)S(1)}, bf16[2048,1024]{1,0:T(8,128)(2,1)}, u32[]{:S(2)}) %copy-start) | copy-done | bytes 4194328
  13.1 1.3 select.12
  14.4 1.4 collective-permute-done.1.came_up_ref
  15.8 0.6 select.13
  16.4 0.1 collective-permute-start.3
  16.5 2.7 %collective-permute-start.4 = (bf16[3,128,256]{2,1,0:T(8,128)(2,1)S(1)}, bf16[3,128,256]{2,1,0:T(8,128)(2,1)S(1)}, u32[]{:S(2)}, u32[]{:S(2)}) collective-permute-start(bf16[3,128,256]{2,1,0:T(8,128)(2,1)S(1)} %get-tuple-element.36), channel_id=1, source_target_pairs={{0,14},{2,0},{4,2},{6,4},{8,6},{10,8},{12,10},{14,12},{1,15},{3,1}... | collective-permute-start | bytes 589832 | tf_op jit(solution)/shard_map/select/ppermute | solution.py:32
  19.2 1.3 select.14
  20.5 2.8 %collective-permute-done.3.came_up_ref = bf16[3,128,256]{2,1,0:T(8,128)(2,1)S(1)} collective-permute-done((bf16[3,128,256]{2,1,0:T(8,128)(2,1)S(1)}, bf16[3,128,256]{2,1,0:T(8,128)(2,1)S(1)}, u32[]{:S(2)}, u32[]{:S(2)}) %collective-permute-start.3) | collective-permute-done | bytes 196640 | tf_op jit(solution)/shard_map/select/ppermute | solution.py:32
  23.2 0.6 select.15
  23.9 1.0 collective-permute-start.5
  24.8 1.8 %collective-permute-start.6 = (bf16[3,128,256]{2,1,0:T(8,128)(2,1)S(1)}, bf16[3,128,256]{2,1,0:T(8,128)(2,1)S(1)}, u32[]{:S(2)}, u32[]{:S(2)}) collective-permute-start(bf16[3,128,256]{2,1,0:T(8,128)(2,1)S(1)} %get-tuple-element.40), channel_id=1, source_target_pairs={{0,14},{2,0},{4,2},{6,4},{8,6},{10,8},{12,10},{14,12},{1,15},{3,1}... | collective-permute-start | bytes 589832 | tf_op jit(solution)/shard_map/select/ppermute | solution.py:32
  26.6 1.3 select.16
  27.9 1.8 %collective-permute-done.5.came_up_ref = bf16[3,128,256]{2,1,0:T(8,128)(2,1)S(1)} collective-permute-done((bf16[3,128,256]{2,1,0:T(8,128)(2,1)S(1)}, bf16[3,128,256]{2,1,0:T(8,128)(2,1)S(1)}, u32[]{:S(2)}, u32[]{:S(2)}) %collective-permute-start.5) | collective-permute-done | bytes 196640 | tf_op jit(solution)/shard_map/select/ppermute | solution.py:32
  29.7 0.6 select.17
  30.3 2.8 %collective-permute-start.7 = (bf16[3,128,256]{2,1,0:T(8,128)(2,1)S(1)}, bf16[3,128,256]{2,1,0:T(8,128)(2,1)S(1)}, u32[]{:S(2)}, u32[]{:S(2)}) collective-permute-start(bf16[3,128,256]{2,1,0:T(8,128)(2,1)S(1)} %get-tuple-element.44), channel_id=1, source_target_pairs={{0,14},{2,0},{4,2},{6,4},{8,6},{10,8},{12,10},{14,12},{1,15},{3,1}... | collective-permute-start | bytes 589832 | tf_op jit(solution)/shard_map/select/ppermute | solution.py:32
  33.1 1.3 select.18
  34.4 1.3 collective-permute-done.7.came_down_ref
  35.7 0.6 select.19
  36.3 3.0 %collective-permute-start.8 = (bf16[3,128,256]{2,1,0:T(8,128)(2,1)S(1)}, bf16[3,128,256]{2,1,0:T(8,128)(2,1)S(1)}, u32[]{:S(2)}, u32[]{:S(2)}) collective-permute-start(bf16[3,128,256]{2,1,0:T(8,128)(2,1)S(1)} %get-tuple-element.47.mine_ref), channel_id=1, source_target_pairs={{0,16},{16,0},{1,17},{17,1},{2,18},{18,2},{3,19},{19,3},{4,20},{20... | collective-permute-start | bytes 589832 | tf_op jit(solution)/shard_map/select/ppermute | solution.py:28
  39.3 1.0 select.20
  40.3 2.1 %collective-permute-done.8.other_ref = bf16[3,128,256]{2,1,0:T(8,128)(2,1)S(1)} collective-permute-done((bf16[3,128,256]{2,1,0:T(8,128)(2,1)S(1)}, bf16[3,128,256]{2,1,0:T(8,128)(2,1)S(1)}, u32[]{:S(2)}, u32[]{:S(2)}) %collective-permute-start.8) | collective-permute-done | bytes 196640 | tf_op jit(solution)/shard_map/select/ppermute | solution.py:28
  42.4 0.6 select.21.refs_4_
  43.0 3.4 %collective-permute-start.13 = (bf16[3,128,256]{2,1,0:T(8,128)(2,1)S(1)}, bf16[3,128,256]{2,1,0:T(8,128)(2,1)S(1)}, u32[]{:S(2)}, u32[]{:S(2)}) collective-permute-start(bf16[3,128,256]{2,1,0:T(8,128)(2,1)S(1)} %select.21.refs_4_), channel_id=1, source_target_pairs={{0,14},{2,0},{4,2},{6,4},{8,6},{10,8},{12,10},{14,12},{1,15},{3,1}... | collective-permute-start | bytes 589832 | tf_op jit(solution)/shard_map/gather/ppermute | solution.py:32
  46.4 2.6 %collective-permute-done.13.refs_8_ = bf16[3,128,256]{2,1,0:T(8,128)(2,1)S(1)} collective-permute-done((bf16[3,128,256]{2,1,0:T(8,128)(2,1)S(1)}, bf16[3,128,256]{2,1,0:T(8,128)(2,1)S(1)}, u32[]{:S(2)}, u32[]{:S(2)}) %collective-permute-start.13) | collective-permute-done | bytes 196640 | tf_op jit(solution)/shard_map/gather/ppermute | solution.py:32
  49.0 3.1 %collective-permute-start.14 = (bf16[3,128,256]{2,1,0:T(8,128)(2,1)S(1)}, bf16[3,128,256]{2,1,0:T(8,128)(2,1)S(1)}, u32[]{:S(2)}, u32[]{:S(2)}) collective-permute-start(bf16[3,128,256]{2,1,0:T(8,128)(2,1)S(1)} %collective-permute-done.13.refs_8_), channel_id=1, source_target_pairs={{0,14},{2,0},{4,2},{6,4},{8,6},{10,8},{12,10},{14,12},{1,15},{3,1}... | collective-permute-start | bytes 589832 | tf_op jit(solution)/shard_map/gather/ppermute | solution.py:32
  52.1 4.5 %collective-permute-done.14.refs_12_ = bf16[3,128,256]{2,1,0:T(8,128)(2,1)S(1)} collective-permute-done((bf16[3,128,256]{2,1,0:T(8,128)(2,1)S(1)}, bf16[3,128,256]{2,1,0:T(8,128)(2,1)S(1)}, u32[]{:S(2)}, u32[]{:S(2)}) %collective-permute-start.14) | collective-permute-done | bytes 196640 | tf_op jit(solution)/shard_map/gather/ppermute | solution.py:32
  56.6 3.4 %collective-permute-start.15 = (bf16[3,128,256]{2,1,0:T(8,128)(2,1)S(1)}, bf16[3,128,256]{2,1,0:T(8,128)(2,1)S(1)}, u32[]{:S(2)}, u32[]{:S(2)}) collective-permute-start(bf16[3,128,256]{2,1,0:T(8,128)(2,1)S(1)} %collective-permute-done.14.refs_12_), channel_id=1, source_target_pairs={{0,14},{2,0},{4,2},{6,4},{8,6},{10,8},{12,10},{14,12},{1,15},{3,1}... | collective-permute-start | bytes 589832 | tf_op jit(solution)/shard_map/gather/ppermute | solution.py:32
  60.0 8.8 %collective-permute-start.18 = (bf16[3,128,256]{2,1,0:T(8,128)(2,1)S(1)}, bf16[3,128,256]{2,1,0:T(8,128)(2,1)S(1)}, u32[]{:S(2)}, u32[]{:S(2)}) collective-permute-start(bf16[3,128,256]{2,1,0:T(8,128)(2,1)S(1)} %select.21.refs_4_), channel_id=1, source_target_pairs={{0,1},{1,0},{2,3},{3,2},{4,5},{5,4},{6,7},{7,6},{8,9},{9,8},{10,11... | collective-permute-start | bytes 589832 | tf_op jit(solution)/shard_map/gather/ppermute | solution.py:28
  68.8 0.5 collective-permute-start.20
  69.4 2.7 %collective-permute-start.16 = (bf16[3,128,256]{2,1,0:T(8,128)(2,1)S(1)}, bf16[3,128,256]{2,1,0:T(8,128)(2,1)S(1)}, u32[]{:S(2)}, u32[]{:S(2)}) collective-permute-start(bf16[3,128,256]{2,1,0:T(8,128)(2,1)S(1)} %collective-permute-done.15.refs_16_), channel_id=1, source_target_pairs={{0,1},{1,0},{2,3},{3,2},{4,5},{5,4},{6,7},{7,6},{8,9},{9,8},{10,11... | collective-permute-start | bytes 589832 | tf_op jit(solution)/shard_map/gather/ppermute | solution.py:28
  72.0 0.5 collective-permute-start.22
  72.5 3.5 %collective-permute-done.11.refs_14_ = bf16[3,128,256]{2,1,0:T(8,128)(2,1)S(1)} collective-permute-done((bf16[3,128,256]{2,1,0:T(8,128)(2,1)S(1)}, bf16[3,128,256]{2,1,0:T(8,128)(2,1)S(1)}, u32[]{:S(2)}, u32[]{:S(2)}) %collective-permute-start.11) | collective-permute-done | bytes 196640 | tf_op jit(solution)/shard_map/gather/ppermute | solution.py:32
  76.0 1.4 collective-permute-start.23
  77.4 2.7 %collective-permute-start.17 = (bf16[3,128,256]{2,1,0:T(8,128)(2,1)S(1)}, bf16[3,128,256]{2,1,0:T(8,128)(2,1)S(1)}, u32[]{:S(2)}, u32[]{:S(2)}) collective-permute-start(bf16[3,128,256]{2,1,0:T(8,128)(2,1)S(1)} %collective-permute-done.16.refs_17_), channel_id=1, source_target_pairs={{0,14},{2,0},{4,2},{6,4},{8,6},{10,8},{12,10},{14,12},{1,15},{3,1}... | collective-permute-start | bytes 589832 | tf_op jit(solution)/shard_map/gather/ppermute | solution.py:32
  80.1 2.5 %coupling.4 = (f32[768,256]{1,0:T(8,128)S(1)}, bf16[3,2048,256]{2,1,0:T(8,128)(2,1)S(1)}) custom-call(s32[7]{0:T(128)S(1)} %concatenate.3.at_ref, bf16[3,512,512]{2,1,0:T(8,128)(2,1)S(1)} %get-tuple-element.50.refs_0_, bf16[3,512,512]{2,1,0:T(8,128)(2,1)S(1)} %get-tuple-element.51.refs_1_, bf16[3,512,512]{2,1,0:T(8,128)(2,1)S(1)} %get-tuple-element.52.refs_2_, ...), custom_call_target="tpu_custom_call" | custom-call | flops 805306368 | bytes 9043996 | tf_op jit(solution)/shard_map/coupling/pallas_call | solution.py:37
  82.6 2.5 %collective-permute-done.12.refs_5_.own_ref = bf16[3,128,256]{2,1,0:T(8,128)(2,1)S(1)} collective-permute-done((bf16[3,128,256]{2,1,0:T(8,128)(2,1)S(1)}, bf16[3,128,256]{2,1,0:T(8,128)(2,1)S(1)}, u32[]{:S(2)}, u32[]{:S(2)}) %collective-permute-start.12) | collective-permute-done | bytes 196640 | tf_op jit(solution)/shard_map/gather/ppermute | solution.py:32
  85.1 1.3 coupling.5
  86.4 22.2 %all_to_all.15.part_ref = f32[32,24,256]{2,1,0:T(8,128)S(1)} all-to-all(f32[32,24,256]{2,1,0:T(8,128)S(1)} %bitcast.10), channel_id=1, replica_groups=mesh['yl'=2,'x'=4,'yh'=2,'z'=8,'core'=2] {'core','yl','x','yh'}, dimensions={0} | all-to-all | bytes 1572864 | tf_op jit(solution)/shard_map/coupling/all_to_all | solution.py:323
  108.7 13.9 %all_to_all.16.parts_ref = f32[8,24,256]{2,1,0:T(8,128)S(1)} all-to-all(f32[8,24,256]{2,1,0:T(8,128)S(1)} %coupling.6), channel_id=1, replica_groups=mesh['yl'=2,'x'=4,'yh'=2,'z'=8,'core'=2] {'z'}, dimensions={0} | all-to-all | bytes 393216 | tf_op jit(solution)/shard_map/coupling/all_to_all | solution.py:324
  122.7 15.4 %all_to_all.17 = bf16[32,24,256]{2,1,0:T(8,128)(2,1)S(1)} all-to-all(bf16[32,24,256]{2,1,0:T(8,128)(2,1)S(1)} %broadcast_in_dim.2), channel_id=1, replica_groups=mesh['yl'=2,'x'=4,'yh'=2,'z'=8,'core'=2] {'core','yl','x','yh'}, dimensions={0} | all-to-all | bytes 786432 | tf_op jit(solution)/shard_map/coupling/all_to_all | solution.py:327
  138.1 6.3 %output.1 = bf16[2048,1024]{1,0:T(8,128)(2,1)} custom-call(s32[7]{0:T(128)S(1)} %concatenate.3.at_ref, bf16[3,128,256]{2,1,0:T(8,128)(2,1)S(1)} %collective-permute-done.12.refs_5_.own_ref, bf16[3,128,256]{2,1,0:T(8,128)(2,1)S(1)} %collective-permute-done.17.refs_6_.other_ref, bf16[3,2048,256]{2,1,0:T(8,128)(2,1)S(1)} %get-tuple-element.54.all_ref, ...), custom_call_target="tpu_custom_call" | custom-call | flops 4026531840 | bytes 5505052 | tf_op jit(solution)/shard_map/output/pallas_call | solution.py:37
  (32 shorter events, 0.2 us)
Async XLA Ops:
  0.0 4.7 %copy-start.4 = (s32[3]{0:T(128)S(1)}, s32[3]{0:T(128)}, u32[]{:S(2)}) copy-start(s32[3]{0:T(128)} %param.9) | copy-start | bytes 40
  0.0 10.9 %copy-start.2 = (bf16[3,1024,256]{2,1,0:T(8,128)(2,1)S(1)}, bf16[3,1024,256]{2,1,0:T(8,128)(2,1)}, u32[]{:S(2)}) copy-start(bf16[3,1024,256]{2,1,0:T(8,128)(2,1)} %panels_ref.9) | copy-start | bytes 4718596
  1.4 4.9 %collective-permute-start = (bf16[1024,256]{1,0:T(8,128)(2,1)S(1)}, bf16[1024,256]{1,0:T(8,128)(2,1)S(1)}, u32[]{:S(2)}, u32[]{:S(2)}) collective-permute-start(bf16[1024,256]{1,0:T(8,128)(2,1)S(1)} %get-tuple-element.57), channel_id=1, source_target_pairs={{0,1},{1,0},{2,3},{3,2},{4,5},{5,4},{6,7},{7,6},{8,9},{9,8},{10,11... | collective-permute-start | bytes 1572872 | tf_op jit(solution)/shard_map/select/ppermute | solution.py:28
  6.9 8.9 %collective-permute-start.1 = (bf16[3,128,256]{2,1,0:T(8,128)(2,1)S(1)}, bf16[3,128,256]{2,1,0:T(8,128)(2,1)S(1)}, u32[]{:S(2)}, u32[]{:S(2)}) collective-permute-start(bf16[3,128,256]{2,1,0:T(8,128)(2,1)S(1)} %get-tuple-element.31), channel_id=1, source_target_pairs={{0,2},{2,4},{4,6},{6,8},{8,10},{10,12},{12,14},{14,0},{1,3},{3,5},... | collective-permute-start | bytes 589832 | tf_op jit(solution)/shard_map/select/ppermute | solution.py:32
  7.0 8.8 %collective-permute-start.2 = (bf16[3,128,256]{2,1,0:T(8,128)(2,1)S(1)}, bf16[3,128,256]{2,1,0:T(8,128)(2,1)S(1)}, u32[]{:S(2)}, u32[]{:S(2)}) collective-permute-start(bf16[3,128,256]{2,1,0:T(8,128)(2,1)S(1)} %get-tuple-element.32), channel_id=1, source_target_pairs={{0,14},{2,0},{4,2},{6,4},{8,6},{10,8},{12,10},{14,12},{1,15},{3,1}... | collective-permute-start | bytes 589832 | tf_op jit(solution)/shard_map/select/ppermute | solution.py:32
  10.9 2.2 %copy-start = (bf16[2048,1024]{1,0:T(8,128)(2,1)S(1)}, bf16[2048,1024]{1,0:T(8,128)(2,1)}, u32[]{:S(2)}) copy-start(bf16[2048,1024]{1,0:T(8,128)(2,1)} %gradient_ref.7) | copy-start | bytes 12582916
  13.1 6.1 %copy-start.1 = (bf16[2048,1024]{1,0:T(8,128)(2,1)S(1)}, bf16[2048,1024]{1,0:T(8,128)(2,1)}, u32[]{:S(2)}) copy-start(bf16[2048,1024]{1,0:T(8,128)(2,1)} %gradient_ref.7) | copy-start | bytes 12582916
  16.4 6.8 %collective-permute-start.3 = (bf16[3,128,256]{2,1,0:T(8,128)(2,1)S(1)}, bf16[3,128,256]{2,1,0:T(8,128)(2,1)S(1)}, u32[]{:S(2)}, u32[]{:S(2)}) collective-permute-start(bf16[3,128,256]{2,1,0:T(8,128)(2,1)S(1)} %get-tuple-element.35), channel_id=1, source_target_pairs={{0,2},{2,4},{4,6},{6,8},{8,10},{10,12},{12,14},{14,0},{1,3},{3,5},... | collective-permute-start | bytes 589832 | tf_op jit(solution)/shard_map/select/ppermute | solution.py:32
  16.5 6.7 %collective-permute-start.4 = (bf16[3,128,256]{2,1,0:T(8,128)(2,1)S(1)}, bf16[3,128,256]{2,1,0:T(8,128)(2,1)S(1)}, u32[]{:S(2)}, u32[]{:S(2)}) collective-permute-start(bf16[3,128,256]{2,1,0:T(8,128)(2,1)S(1)} %get-tuple-element.36), channel_id=1, source_target_pairs={{0,14},{2,0},{4,2},{6,4},{8,6},{10,8},{12,10},{14,12},{1,15},{3,1}... | collective-permute-start | bytes 589832 | tf_op jit(solution)/shard_map/select/ppermute | solution.py:32
  23.9 5.8 %collective-permute-start.5 = (bf16[3,128,256]{2,1,0:T(8,128)(2,1)S(1)}, bf16[3,128,256]{2,1,0:T(8,128)(2,1)S(1)}, u32[]{:S(2)}, u32[]{:S(2)}) collective-permute-start(bf16[3,128,256]{2,1,0:T(8,128)(2,1)S(1)} %get-tuple-element.39), channel_id=1, source_target_pairs={{0,2},{2,4},{4,6},{6,8},{8,10},{10,12},{12,14},{14,0},{1,3},{3,5},... | collective-permute-start | bytes 589832 | tf_op jit(solution)/shard_map/select/ppermute | solution.py:32
  24.8 4.9 %collective-permute-start.6 = (bf16[3,128,256]{2,1,0:T(8,128)(2,1)S(1)}, bf16[3,128,256]{2,1,0:T(8,128)(2,1)S(1)}, u32[]{:S(2)}, u32[]{:S(2)}) collective-permute-start(bf16[3,128,256]{2,1,0:T(8,128)(2,1)S(1)} %get-tuple-element.40), channel_id=1, source_target_pairs={{0,14},{2,0},{4,2},{6,4},{8,6},{10,8},{12,10},{14,12},{1,15},{3,1}... | collective-permute-start | bytes 589832 | tf_op jit(solution)/shard_map/select/ppermute | solution.py:32
  30.3 5.4 %collective-permute-start.7 = (bf16[3,128,256]{2,1,0:T(8,128)(2,1)S(1)}, bf16[3,128,256]{2,1,0:T(8,128)(2,1)S(1)}, u32[]{:S(2)}, u32[]{:S(2)}) collective-permute-start(bf16[3,128,256]{2,1,0:T(8,128)(2,1)S(1)} %get-tuple-element.44), channel_id=1, source_target_pairs={{0,14},{2,0},{4,2},{6,4},{8,6},{10,8},{12,10},{14,12},{1,15},{3,1}... | collective-permute-start | bytes 589832 | tf_op jit(solution)/shard_map/select/ppermute | solution.py:32
  33.1 6.2 %copy-start.3 = (f32[3,256,256]{2,1,0:T(8,128)S(1)}, f32[3,256,256]{2,1,0:T(8,128)}, u32[]{:S(2)}) copy-start(f32[3,256,256]{2,1,0:T(8,128)} %values_ref.1) | copy-start | bytes 2359300
  36.3 6.1 %collective-permute-start.8 = (bf16[3,128,256]{2,1,0:T(8,128)(2,1)S(1)}, bf16[3,128,256]{2,1,0:T(8,128)(2,1)S(1)}, u32[]{:S(2)}, u32[]{:S(2)}) collective-permute-start(bf16[3,128,256]{2,1,0:T(8,128)(2,1)S(1)} %get-tuple-element.47.mine_ref), channel_id=1, source_target_pairs={{0,16},{16,0},{1,17},{17,1},{2,18},{18,2},{3,19},{19,3},{4,20},{20... | collective-permute-start | bytes 589832 | tf_op jit(solution)/shard_map/select/ppermute | solution.py:28
  43.0 6.0 %collective-permute-start.13 = (bf16[3,128,256]{2,1,0:T(8,128)(2,1)S(1)}, bf16[3,128,256]{2,1,0:T(8,128)(2,1)S(1)}, u32[]{:S(2)}, u32[]{:S(2)}) collective-permute-start(bf16[3,128,256]{2,1,0:T(8,128)(2,1)S(1)} %select.21.refs_4_), channel_id=1, source_target_pairs={{0,14},{2,0},{4,2},{6,4},{8,6},{10,8},{12,10},{14,12},{1,15},{3,1}... | collective-permute-start | bytes 589832 | tf_op jit(solution)/shard_map/gather/ppermute | solution.py:32
  46.4 5.7 %collective-permute-start.9 = (bf16[3,128,256]{2,1,0:T(8,128)(2,1)S(1)}, bf16[3,128,256]{2,1,0:T(8,128)(2,1)S(1)}, u32[]{:S(2)}, u32[]{:S(2)}) collective-permute-start(bf16[3,128,256]{2,1,0:T(8,128)(2,1)S(1)} %select.21.refs_4_), channel_id=1, source_target_pairs={{0,2},{2,4},{4,6},{6,8},{8,10},{10,12},{12,14},{14,0},{1,3},{3,5},... | collective-permute-start | bytes 589832 | tf_op jit(solution)/shard_map/gather/ppermute | solution.py:32
  49.0 7.6 %collective-permute-start.14 = (bf16[3,128,256]{2,1,0:T(8,128)(2,1)S(1)}, bf16[3,128,256]{2,1,0:T(8,128)(2,1)S(1)}, u32[]{:S(2)}, u32[]{:S(2)}) collective-permute-start(bf16[3,128,256]{2,1,0:T(8,128)(2,1)S(1)} %collective-permute-done.13.refs_8_), channel_id=1, source_target_pairs={{0,14},{2,0},{4,2},{6,4},{8,6},{10,8},{12,10},{14,12},{1,15},{3,1}... | collective-permute-start | bytes 589832 | tf_op jit(solution)/shard_map/gather/ppermute | solution.py:32
  52.1 16.7 %collective-permute-start.10 = (bf16[3,128,256]{2,1,0:T(8,128)(2,1)S(1)}, bf16[3,128,256]{2,1,0:T(8,128)(2,1)S(1)}, u32[]{:S(2)}, u32[]{:S(2)}) collective-permute-start(bf16[3,128,256]{2,1,0:T(8,128)(2,1)S(1)} %collective-permute-done.9.refs_6_), channel_id=1, source_target_pairs={{0,2},{2,4},{4,6},{6,8},{8,10},{10,12},{12,14},{14,0},{1,3},{3,5},... | collective-permute-start | bytes 589832 | tf_op jit(solution)/shard_map/gather/ppermute | solution.py:32
  56.6 12.7 %collective-permute-start.15 = (bf16[3,128,256]{2,1,0:T(8,128)(2,1)S(1)}, bf16[3,128,256]{2,1,0:T(8,128)(2,1)S(1)}, u32[]{:S(2)}, u32[]{:S(2)}) collective-permute-start(bf16[3,128,256]{2,1,0:T(8,128)(2,1)S(1)} %collective-permute-done.14.refs_12_), channel_id=1, source_target_pairs={{0,14},{2,0},{4,2},{6,4},{8,6},{10,8},{12,10},{14,12},{1,15},{3,1}... | collective-permute-start | bytes 589832 | tf_op jit(solution)/shard_map/gather/ppermute | solution.py:32
  60.0 12.0 %collective-permute-start.18 = (bf16[3,128,256]{2,1,0:T(8,128)(2,1)S(1)}, bf16[3,128,256]{2,1,0:T(8,128)(2,1)S(1)}, u32[]{:S(2)}, u32[]{:S(2)}) collective-permute-start(bf16[3,128,256]{2,1,0:T(8,128)(2,1)S(1)} %select.21.refs_4_), channel_id=1, source_target_pairs={{0,1},{1,0},{2,3},{3,2},{4,5},{5,4},{6,7},{7,6},{8,9},{9,8},{10,11... | collective-permute-start | bytes 589832 | tf_op jit(solution)/shard_map/gather/ppermute | solution.py:28
  68.8 3.2 %collective-permute-start.19 = (bf16[3,128,256]{2,1,0:T(8,128)(2,1)S(1)}, bf16[3,128,256]{2,1,0:T(8,128)(2,1)S(1)}, u32[]{:S(2)}, u32[]{:S(2)}) collective-permute-start(bf16[3,128,256]{2,1,0:T(8,128)(2,1)S(1)} %collective-permute-done.9.refs_6_), channel_id=1, source_target_pairs={{0,1},{1,0},{2,3},{3,2},{4,5},{5,4},{6,7},{7,6},{8,9},{9,8},{10,11... | collective-permute-start | bytes 589832 | tf_op jit(solution)/shard_map/gather/ppermute | solution.py:28
  68.8 7.2 %collective-permute-start.11 = (bf16[3,128,256]{2,1,0:T(8,128)(2,1)S(1)}, bf16[3,128,256]{2,1,0:T(8,128)(2,1)S(1)}, u32[]{:S(2)}, u32[]{:S(2)}) collective-permute-start(bf16[3,128,256]{2,1,0:T(8,128)(2,1)S(1)} %collective-permute-done.10.refs_10_), channel_id=1, source_target_pairs={{0,2},{2,4},{4,6},{6,8},{8,10},{10,12},{12,14},{14,0},{1,3},{3,5},... | collective-permute-start | bytes 589832 | tf_op jit(solution)/shard_map/gather/ppermute | solution.py:32
  68.8 8.5 %collective-permute-start.20 = (bf16[3,128,256]{2,1,0:T(8,128)(2,1)S(1)}, bf16[3,128,256]{2,1,0:T(8,128)(2,1)S(1)}, u32[]{:S(2)}, u32[]{:S(2)}) collective-permute-start(bf16[3,128,256]{2,1,0:T(8,128)(2,1)S(1)} %collective-permute-done.13.refs_8_), channel_id=1, source_target_pairs={{0,1},{1,0},{2,3},{3,2},{4,5},{5,4},{6,7},{7,6},{8,9},{9,8},{10,11... | collective-permute-start | bytes 589832 | tf_op jit(solution)/shard_map/gather/ppermute | solution.py:28
  69.4 8.0 %collective-permute-start.16 = (bf16[3,128,256]{2,1,0:T(8,128)(2,1)S(1)}, bf16[3,128,256]{2,1,0:T(8,128)(2,1)S(1)}, u32[]{:S(2)}, u32[]{:S(2)}) collective-permute-start(bf16[3,128,256]{2,1,0:T(8,128)(2,1)S(1)} %collective-permute-done.15.refs_16_), channel_id=1, source_target_pairs={{0,1},{1,0},{2,3},{3,2},{4,5},{5,4},{6,7},{7,6},{8,9},{9,8},{10,11... | collective-permute-start | bytes 589832 | tf_op jit(solution)/shard_map/gather/ppermute | solution.py:28
  72.0 8.0 %collective-permute-start.21 = (bf16[3,128,256]{2,1,0:T(8,128)(2,1)S(1)}, bf16[3,128,256]{2,1,0:T(8,128)(2,1)S(1)}, u32[]{:S(2)}, u32[]{:S(2)}) collective-permute-start(bf16[3,128,256]{2,1,0:T(8,128)(2,1)S(1)} %collective-permute-done.10.refs_10_), channel_id=1, source_target_pairs={{0,1},{1,0},{2,3},{3,2},{4,5},{5,4},{6,7},{7,6},{8,9},{9,8},{10,11... | collective-permute-start | bytes 589832 | tf_op jit(solution)/shard_map/gather/ppermute | solution.py:28
  72.0 8.0 %collective-permute-start.22 = (bf16[3,128,256]{2,1,0:T(8,128)(2,1)S(1)}, bf16[3,128,256]{2,1,0:T(8,128)(2,1)S(1)}, u32[]{:S(2)}, u32[]{:S(2)}) collective-permute-start(bf16[3,128,256]{2,1,0:T(8,128)(2,1)S(1)} %collective-permute-done.14.refs_12_), channel_id=1, source_target_pairs={{0,1},{1,0},{2,3},{3,2},{4,5},{5,4},{6,7},{7,6},{8,9},{9,8},{10,11... | collective-permute-start | bytes 589832 | tf_op jit(solution)/shard_map/gather/ppermute | solution.py:28
  76.0 4.1 %collective-permute-start.23 = (bf16[3,128,256]{2,1,0:T(8,128)(2,1)S(1)}, bf16[3,128,256]{2,1,0:T(8,128)(2,1)S(1)}, u32[]{:S(2)}, u32[]{:S(2)}) collective-permute-start(bf16[3,128,256]{2,1,0:T(8,128)(2,1)S(1)} %collective-permute-done.11.refs_14_), channel_id=1, source_target_pairs={{0,1},{1,0},{2,3},{3,2},{4,5},{5,4},{6,7},{7,6},{8,9},{9,8},{10,11... | collective-permute-start | bytes 589832 | tf_op jit(solution)/shard_map/gather/ppermute | solution.py:28
  77.4 7.7 %collective-permute-start.12 = (bf16[3,128,256]{2,1,0:T(8,128)(2,1)S(1)}, bf16[3,128,256]{2,1,0:T(8,128)(2,1)S(1)}, u32[]{:S(2)}, u32[]{:S(2)}) collective-permute-start(bf16[3,128,256]{2,1,0:T(8,128)(2,1)S(1)} %collective-permute-done.11.refs_14_), channel_id=1, source_target_pairs={{0,2},{2,4},{4,6},{6,8},{8,10},{10,12},{12,14},{14,0},{1,3},{3,5},... | collective-permute-start | bytes 589832 | tf_op jit(solution)/shard_map/gather/ppermute | solution.py:32
  77.4 7.7 %collective-permute-start.17 = (bf16[3,128,256]{2,1,0:T(8,128)(2,1)S(1)}, bf16[3,128,256]{2,1,0:T(8,128)(2,1)S(1)}, u32[]{:S(2)}, u32[]{:S(2)}) collective-permute-start(bf16[3,128,256]{2,1,0:T(8,128)(2,1)S(1)} %collective-permute-done.16.refs_17_), channel_id=1, source_target_pairs={{0,14},{2,0},{4,2},{6,4},{8,6},{10,8},{12,10},{14,12},{1,15},{3,1}... | collective-permute-start | bytes 589832 | tf_op jit(solution)/shard_map/gather/ppermute | solution.py:32

commit v5 on v0

v5 whole, which is shorter than its diff:
```python
import functools

import jax
import jax.numpy as jnp
from jax import lax
from jax.experimental import pallas as pl
from jax.experimental.pallas import tpu as pltpu
from jax.sharding import Mesh
from jax.sharding import PartitionSpec as P

ROW = ("yl", "x")
COL = ("yh", "z", "core")
SPREAD = ("core", "z", "yh")
PLANE = ("core", "yl", "x", "yh")
F32 = jnp.float32
BF16 = jnp.bfloat16
RING = 8
REACH = RING // 2
BLOCKS = 4
MIB = 1024 * 1024

VMEM = pl.BlockSpec(memory_space=pltpu.VMEM)
SMEM = pl.BlockSpec(memory_space=pltpu.SMEM)
ANY = pl.BlockSpec(memory_space=pl.ANY)
TOKEN = jax.ShapeDtypeStruct((8, 128), F32)


def swap(x, axis):
    return lax.ppermute(x, axis, [(0, 1), (1, 0)])


def shift(x, by):
    return lax.ppermute(x, "z", [(i, (i + by) % RING) for i in range(RING)])


def call(kernel, args, in_specs, out_specs, out_shape, flops=0, scratch=(), limit=16):
    moved = sum(a.size * a.dtype.itemsize for a in args)
    return pl.pallas_call(
        kernel,
        in_specs=in_specs,
        out_specs=out_specs,
        out_shape=out_shape,
        scratch_shapes=scratch,
        compiler_params=pltpu.CompilerParams(vmem_limit_bytes=limit * MIB),
        cost_estimate=pl.CostEstimate(flops=flops, bytes_accessed=moved, transcendentals=0),
    )(*args)


def owner_of(at_ref, k):
    number = at_ref[4 + k]
    return number & 1, (number >> 1) & (RING - 1), number >> 4


def pick_kernel(at_ref, all_ref, _, out_ref, sems):
    copies = []
    for k in range(out_ref.shape[0]):
        core, place, high = owner_of(at_ref, k)
        number = core * (2 * RING) + place * 2 + high
        copies.append(pltpu.make_async_copy(all_ref.at[number], out_ref.at[k], sems.at[k]))
        copies[-1].start()
    for copy in copies:
        copy.wait()


def pair_kernel(at_ref, mine_ref, other_ref, out_ref):
    rows = mine_ref.shape[1]
    mine = pl.ds(pl.multiple_of(at_ref[1] * rows, rows), rows)
    other = pl.ds(pl.multiple_of((1 - at_ref[1]) * rows, rows), rows)
    for k in range(mine_ref.shape[0]):
        out_ref[k, mine] = mine_ref[k]
        out_ref[k, other] = other_ref[k]


def project_kernel(own, at_ref, gradient_ref, panels_ref, out_ref, rows_ref, sems):
    blocks, size, _ = rows_ref.shape
    half = at_ref[0] if own else 1 - at_ref[0]
    copies = []
    for i in range(blocks):
        start = pl.multiple_of((half * blocks + i) * size, size)
        copies.append(pltpu.make_async_copy(gradient_ref.at[pl.ds(start, size)], rows_ref.at[i], sems.at[i]))
        copies[-1].start()
    for i in range(blocks):
        copies[i].wait()
        for k in range(panels_ref.shape[0]):
            out_ref[k, i * size : (i + 1) * size] = jnp.dot(rows_ref[i], panels_ref[k], preferred_element_type=F32)


def project(at, own, gradient, panels):
    count, width, vec = panels.shape
    rows = gradient.shape[0] // 2
    return call(
        functools.partial(project_kernel, own),
        (at, gradient, panels),
        [SMEM, ANY, VMEM],
        VMEM,
        jax.ShapeDtypeStruct((count, rows, vec), F32),
        2 * rows * width * vec * count,
        [pltpu.VMEM((BLOCKS, rows // BLOCKS, width), BF16), pltpu.SemaphoreType.DMA((BLOCKS,))],
        limit=60,
    )


def split_kernel(at_ref, own_ref, other_ref, values_ref, out_ref, below_ref, token_ref, all_ref):
    count, _, vec = own_ref.shape
    for k in range(count):
        total = (own_ref[k] + other_ref[k]).T
        high = total.astype(BF16)
        out_ref[k, :vec] = high
        out_ref[k, vec:] = (total - high.astype(F32)).astype(BF16)
        values = values_ref[k]
        all_ref[k * vec : (k + 1) * vec] = (values + 0.1 * jnp.mean(values)).T
    size = below_ref.shape[0]
    below_ref[...] = all_ref[pl.ds(pl.multiple_of(at_ref[3] * size, size), size)]
    token_ref[...] = jnp.zeros_like(token_ref)


def split(at, own, other, values, places):
    count, rows, vec = own.shape
    shapes = [jax.ShapeDtypeStruct((count, 2 * vec, rows), BF16), jax.ShapeDtypeStruct((count * vec // places, vec), F32), TOKEN]
    return call(split_kernel, (at, own, other, values), [SMEM] + [VMEM] * 3, [VMEM] * 3, shapes, scratch=[pltpu.VMEM((count * vec, vec), F32)])


def offsets():
    order = [0]
    for step in range(1, REACH + 1):
        order.append(-step)
        if step < REACH:
            order.append(step)
    return order


def first_row(at_ref, offset, rows):
    return pl.multiple_of(((at_ref[2] + offset + RING) & (RING - 1)) * rows, rows)


def early_kernel(at_ref, terms_ref, *refs):
    pieces, (total_ref, half_ref) = refs[: RING - 1], refs[RING - 1 :]
    count, rows, vec = pieces[0].shape
    for piece, offset in zip(pieces, offsets()):
        span = pl.ds(first_row(at_ref, offset, rows), rows)
        for k in range(count):
            half_ref[k, span] = piece[k]
    span = pl.ds(first_row(at_ref, REACH, rows), rows)
    for k in range(count):
        half_ref[k, span] = jnp.zeros((rows, vec), BF16)
        both = jnp.dot(terms_ref[k], half_ref[k], preferred_element_type=F32)
        total_ref[k * vec : (k + 1) * vec] = both[:vec] + both[vec:]


def early(at, terms, pieces):
    count, rows, vec = pieces[0].shape
    shapes = [jax.ShapeDtypeStruct((count * vec, vec), F32), jax.ShapeDtypeStruct((count, RING * rows, vec), BF16)]
    specs = [SMEM] + [VMEM] * (1 + len(pieces))
    return call(early_kernel, (at, terms, *pieces), specs, [VMEM, VMEM], shapes, 4 * count * RING * rows * vec * vec)


def late_kernel(at_ref, terms_ref, total_ref, half_ref, piece_ref, out_ref, whole_ref):
    count, rows, vec = piece_ref.shape
    span = pl.ds(first_row(at_ref, REACH, rows), rows)
    for k in range(count):
        both = jnp.dot(terms_ref[k, :, span], piece_ref[k], preferred_element_type=F32)
        panel = slice(k * vec, (k + 1) * vec)
        out_ref[panel] = total_ref[panel] + both[:vec] + both[vec:]
        whole_ref[k] = half_ref[k]
        whole_ref[k, span] = piece_ref[k]


def late(at, terms, total, half, piece):
    shapes = [jax.ShapeDtypeStruct(total.shape, F32), jax.ShapeDtypeStruct(half.shape, BF16)]
    return call(late_kernel, (at, terms, total, half, piece), [SMEM] + [VMEM] * 4, [VMEM, VMEM], shapes)


def spread_kernel(part_ref, out_ref):
    total = jnp.sum(part_ref[...], axis=0)
    for j in range(RING):
        out_ref[j] = total


def spread(parts):
    return call(spread_kernel, (parts,), [VMEM], VMEM, jax.ShapeDtypeStruct((RING,) + parts.shape[1:], F32))


def scale_kernel(parts_ref, below_ref, out_ref):
    out_ref[...] = (jnp.sum(parts_ref[...], axis=0) / below_ref[...]).astype(BF16)


def apply_kernel(at_ref, own_ref, other_ref, scaled_ref, panels_ref, out_ref, fetched_ref, block_ref, in_sems, out_sems):
    steps, size, _ = block_ref.shape
    count, half, _ = own_ref.shape
    near = steps // 2
    fetches, copies = [], []
    for number in range(steps):
        ref = own_ref if number < near else other_ref
        rows = pl.ds((number % near) * size, size)
        fetches.append(pltpu.make_async_copy(ref.at[:, rows], fetched_ref.at[number], in_sems.at[number]))
        fetches[-1].start()
    for number in range(steps):
        fetches[number].wait()
        total = None
        for k in range(count):
            rotated = lax.dot_general(fetched_ref[number, k], scaled_ref[k], (((1,), (1,)), ((), ())), preferred_element_type=F32)
            term = lax.dot_general(rotated.astype(BF16), panels_ref[k], (((1,), (1,)), ((), ())), preferred_element_type=F32)
            total = term if total is None else total + term
        block_ref[number] = total.astype(BF16)
        first = at_ref[0] if number < near else 1 - at_ref[0]
        target = pl.multiple_of(first * half + (number % near) * size, size)
        copies.append(pltpu.make_async_copy(block_ref.at[number], out_ref.at[pl.ds(target, size)], out_sems.at[number]))
        copies[-1].start()
    for copy in copies:
        copy.wait()


def apply(at, own, other, scaled, panels):
    count, rows, vec = other.shape
    width = panels.shape[1]
    steps = 4
    size = 2 * rows // steps
    return call(
        apply_kernel,
        (at, own, other, scaled, panels),
        [SMEM, ANY, ANY, VMEM, VMEM],
        ANY,
        jax.ShapeDtypeStruct((2 * rows, width), BF16),
        4 * count * rows * vec * (vec + width),
        [
            pltpu.VMEM((steps, count, size, vec), BF16),
            pltpu.VMEM((steps, size, width), BF16),
            pltpu.SemaphoreType.DMA((steps,)),
            pltpu.SemaphoreType.DMA((steps,)),
        ],
        limit=24,
    )


def body(gradient, in_panels, out_pool, eigenvalues, owners):
    core, high, here = (lax.axis_index(a) for a in ("core", "yh", "z"))
    at = jnp.concatenate([jnp.stack([core, high, here, lax.axis_index(PLANE)]).astype(jnp.int32), owners])
    count, _, vec = in_panels.shape
    size = out_pool.shape[1] // 32
    piece = jax.ShapeDtypeStruct((count, size, vec), BF16)
    pair = jax.ShapeDtypeStruct((count, 2 * size, vec), BF16)

    with jax.named_scope("scatter"):
        every = lax.all_to_all(out_pool.reshape(32, size, vec), SPREAD, 0, 0)

    with jax.named_scope("projection"):
        came = swap(project(at, False, gradient, in_panels), "core")
        terms, below, token = split(at, project(at, True, gradient, in_panels), came, eigenvalues, 32)

    with jax.named_scope("gather"):
        mine = call(pick_kernel, (at, every, token), [SMEM, ANY, ANY], VMEM, piece, scratch=[pltpu.SemaphoreType.DMA((count,))])
        mine = call(pair_kernel, (at, mine, swap(mine, "yh")), [SMEM, VMEM, VMEM], VMEM, pair)
        pieces = [mine]
        up = down = mine
        for _ in range(1, REACH):
            up, down = shift(up, 1), shift(down, -1)
            pieces += [up, down]
        pieces.append(shift(up, 1))

    with jax.named_scope("coupling"):
        part, own = early(at, terms, pieces[:-1])
        part, own = late(at, terms, part, own, pieces[-1])
        other = swap(own, "core")
        part = spread(lax.all_to_all(part.reshape(32, -1, vec), PLANE, 0, 0))
        part = lax.all_to_all(part, "z", 0, 0)
        scaled = call(scale_kernel, (part, below), [VMEM, VMEM], VMEM, jax.ShapeDtypeStruct(part.shape[1:], BF16))
        copies = jnp.broadcast_to(scaled[None], (32,) + scaled.shape)
        scaled = lax.all_to_all(copies, PLANE, 0, 0).reshape(count, vec, vec)

    with jax.named_scope("output"):
        return apply(at, own, other, scaled, in_panels)


def solution(mesh):
    fine = Mesh(mesh.devices.reshape(2, 4, 2, 8, 2), ROW + COL)
    return jax.shard_map(
        body,
        mesh=fine,
        in_specs=(P(ROW, COL), P(None, COL, None), P(COL, ROW, None), P(), P()),
        out_specs=P(ROW, COL),
        check_vma=False,
    )
```

time: 581 us -> 144 us (0.25)
  waiting for transfers between devices: 520 us -> 30.9 us
  blocking collectives: 0 us -> 47.7 us
  matrix products: 37.7 us -> 0 us
  starting transfers between devices: 0.04 us -> 29.3 us
  Pallas kernels: 0 us -> 27.6 us
  between operations: 17.2 us -> 0.28 us
  local copies, waits for them, and re-layouts: 1.44 us -> 7.91 us
    psum x2 -> x0, waiting for transfers between devices: 520 us -> none  [the longest x1 270 us: from_root(): return lax.psum(jnp.where(mine, x, jnp.zeros_like(x)), axis)]
    all_to_all x0 -> x3, blocking collectives: none -> 47.7 us  [the longest x1 19.6 us: body(): part = spread(lax.all_to_all(part.reshape(32, -1, vec), PLANE, 0, 0))]
    dot_general x9 -> x0, matrix products: 37.7 us -> none  [the longest x3 20.8 us: body(): jnp.dot(rotated, basis.T, preferred_element_type=jnp.float32)]
    pallas_call x0 -> x10, Pallas kernels: none -> 27.6 us  [call(): pl.pallas_call(kernel, in_specs=in_specs, out_specs=out_specs, out_shape=...]
    ppermute x0 -> x10, starting transfers between devices: none -> 19.6 us  [the longest x3 11 us: swap(): return lax.ppermute(x, axis, [(0, 1), (1, 0)])]
    ppermute x0 -> x10, waiting for transfers between devices: none -> 17.7 us  [the longest x7 14 us: shift(): return lax.ppermute(x, 'z', [(i, (i + by) % RING) for i in range(RING)])]
    all_to_all x0 -> x1, waiting for transfers between devices: none -> 13.2 us  [body(): every = lax.all_to_all(out_pool.reshape(32, size, vec), SPREAD, 0, 0)]
    all_to_all x0 -> x1, starting transfers between devices: none -> 9.69 us  [body(): every = lax.all_to_all(out_pool.reshape(32, size, vec), SPREAD, 0, 0)]
  transfers between devices with their start and end apart: 2 -> 11, of which waited for: 2 -> 6; matrix products, arithmetic and copies ran while one was open for 2% -> 0% of each run, Pallas kernels for 0% -> 7%
where the time goes in v5:
time: 144 us
  blocking collectives  47.7 us (33%)
  waiting for transfers between devices  30.9 us (21%)
  starting transfers between devices  29.3 us (20%)
  Pallas kernels  27.6 us (19%)
  local copies, waits for them, and re-layouts  7.91 us (5%)
    pallas_call x10, Pallas kernels, call(): pl.pallas_call(kernel, in_specs=in_specs, out_specs=out_specs, out_shape=...  27.6 us
    all_to_all x1, blocking collectives, body(): part = spread(lax.all_to_all(part.reshape(32, -1, vec), PLANE, 0, 0))  19.6 us
    all_to_all x1, blocking collectives, body(): scaled = lax.all_to_all(copies, PLANE, 0, 0).reshape(count, vec, vec)  15.4 us
    ppermute x7, waiting for transfers between devices, shift(): return lax.ppermute(x, 'z', [(i, (i + by) % RING) for i in range(RING)])  14 us
    all_to_all x1, waiting for transfers between devices, body(): every = lax.all_to_all(out_pool.reshape(32, size, vec), SPREAD, 0, 0)  13.2 us
    all_to_all x1, blocking collectives, body(): part = lax.all_to_all(part, 'z', 0, 0)  12.8 us
    ppermute x3, starting transfers between devices, swap(): return lax.ppermute(x, axis, [(0, 1), (1, 0)])  11 us
    all_to_all x1, starting transfers between devices, body(): every = lax.all_to_all(out_pool.reshape(32, size, vec), SPREAD, 0, 0)  9.69 us
  transfers between devices with their start and end apart: 11, of which 6 were waited for; matrix products, arithmetic and copies ran while one was open for 0% of the time, Pallas kernels for 7%

profile of v5, /device:TPU:1, one launch (start us, length us, event | category | flops | bytes accessed | tf_op | source)
XLA Modules:
  0.0 143.7 jit_solution(10468339494598902619)
XLA Ops:
  0.0 1.3 concatenate.3.at_ref
  1.3 7.0 %projection.4 = f32[3,1024,256]{2,1,0:T(8,128)} custom-call(s32[7]{0:T(128)} %concatenate.3.at_ref, bf16[2048,1024]{1,0:T(8,128)(2,1)} %gradient_ref.3, bf16[3,1024,256]{2,1,0:T(8,128)(2,1)} %panels_ref.5), custom_call_target="tpu_custom_call" | custom-call | flops 1610612736 | bytes 5767196 | tf_op jit(solution)/shard_map/projection/pallas_call | solution.py:38
  8.3 3.3 %collective-permute-start = (f32[3,1024,256]{2,1,0:T(8,128)}, f32[3,1024,256]{2,1,0:T(8,128)S(1)}, u32[]{:S(2)}, u32[]{:S(2)}) collective-permute-start(f32[3,1024,256]{2,1,0:T(8,128)} %projection.4), channel_id=1, source_target_pairs={{0,1},{1,0},{2,3},{3,2},{4,5},{5,4},{6,7},{7,6},{8,9},{9,8},{10,11... | collective-permute-start | bytes 9437192 | tf_op jit(solution)/shard_map/projection/ppermute | solution.py:29
  11.6 9.7 %all-to-all-start = ((bf16[32,64,256]{2,1,0:T(8,128)(2,1)}), bf16[32,64,256]{2,1,0:T(8,128)(2,1)}, u32[]{:S(2)}, u32[]{:S(2)}) async-start(bf16[32,64,256]{2,1,0:T(8,128)(2,1)} %bitcast.9), calls=%async_computation | async-start | bytes 2097152 | tf_op jit(solution)/shard_map/scatter/all_to_all | solution.py:244
  21.3 0.0 copy-start.5
  21.4 7.0 %projection.3.own_ref = f32[3,1024,256]{2,1,0:T(8,128)} custom-call(s32[7]{0:T(128)} %concatenate.3.at_ref, bf16[2048,1024]{1,0:T(8,128)(2,1)} %gradient_ref.3, bf16[3,1024,256]{2,1,0:T(8,128)(2,1)} %panels_ref.5), custom_call_target="tpu_custom_call" | custom-call | flops 1610612736 | bytes 5767196 | tf_op jit(solution)/shard_map/projection/pallas_call | solution.py:38
  28.4 0.0 collective-permute-done.other_ref
  28.4 0.0 copy-start.2
  28.4 1.6 %copy-done.2 = f32[3,1024,256]{2,1,0:T(8,128)} copy-done((f32[3,1024,256]{2,1,0:T(8,128)}, f32[3,1024,256]{2,1,0:T(8,128)S(1)}, u32[]{:S(2)}) %copy-start.2) | copy-done | bytes 3145752
  30.0 0.0 copy-done.5
  30.0 0.0 copy-start
  30.0 1.9 %copy-done = f32[3,1024,256]{2,1,0:T(8,128)S(1)} copy-done((f32[3,1024,256]{2,1,0:T(8,128)S(1)}, f32[3,1024,256]{2,1,0:T(8,128)}, u32[]{:S(2)}) %copy-start) | copy-done | bytes 3145752
  31.9 0.0 copy-start.3
  31.9 1.9 %copy-done.3 = f32[3,1024,256]{2,1,0:T(8,128)S(1)} copy-done((f32[3,1024,256]{2,1,0:T(8,128)S(1)}, f32[3,1024,256]{2,1,0:T(8,128)}, u32[]{:S(2)}) %copy-start.3) | copy-done | bytes 3145752
  33.8 0.0 copy-start.4
  33.8 1.1 copy-done.4
  34.9 1.8 %projection.5 = (bf16[3,512,1024]{2,1,0:T(8,128)(2,1)S(1)}, f32[24,256]{1,0:T(8,128)S(1)}, f32[8,128]{1,0:T(8,128)S(1)}) custom-call(s32[7]{0:T(128)S(1)} %copy-done.5, f32[3,1024,256]{2,1,0:T(8,128)S(1)} %copy-done, f32[3,1024,256]{2,1,0:T(8,128)S(1)} %copy-done.3, f32[3,256,256]{2,1,0:T(8,128)S(1)} %copy-done.4), custom_call_target="tpu_custom_call" | custom-call | bytes 7077916 | tf_op jit(solution)/shard_map/projection/pallas_call | solution.py:38
  36.7 13.2 %all-to-all-done.all_ref = bf16[32,64,256]{2,1,0:T(8,128)(2,1)} async-done(((bf16[32,64,256]{2,1,0:T(8,128)(2,1)}), bf16[32,64,256]{2,1,0:T(8,128)(2,1)}, u32[]{:S(2)}, u32[]{:S(2)}) %all-to-all-start) | async-done | bytes 1048608 | tf_op jit(solution)/shard_map/scatter/all_to_all | solution.py:244
  49.9 1.4 gather.2.mine_ref
  51.3 1.3 collective-permute-start.1
  52.6 3.8 %collective-permute-done.1.other_ref = bf16[3,64,256]{2,1,0:T(8,128)(2,1)S(1)} collective-permute-done((bf16[3,64,256]{2,1,0:T(8,128)(2,1)S(1)}, bf16[3,64,256]{2,1,0:T(8,128)(2,1)S(1)}, u32[]{:S(2)}, u32[]{:S(2)}) %collective-permute-start.1) | collective-permute-done | bytes 98336 | tf_op jit(solution)/shard_map/gather/ppermute | solution.py:29
  56.3 0.6 gather.3.refs_0_
  56.9 1.7 %collective-permute-start.2 = (bf16[3,128,256]{2,1,0:T(8,128)(2,1)S(1)}, bf16[3,128,256]{2,1,0:T(8,128)(2,1)S(1)}, u32[]{:S(2)}, u32[]{:S(2)}) collective-permute-start(bf16[3,128,256]{2,1,0:T(8,128)(2,1)S(1)} %gather.3.refs_0_), channel_id=1, source_target_pairs={{0,2},{2,4},{4,6},{6,8},{8,10},{10,12},{12,14},{14,0},{1,3},{3,5},... | collective-permute-start | bytes 589832 | tf_op jit(solution)/shard_map/gather/ppermute | solution.py:33
  58.6 1.4 collective-permute-start.3
  59.9 3.0 %collective-permute-done.2.refs_1_ = bf16[3,128,256]{2,1,0:T(8,128)(2,1)S(1)} collective-permute-done((bf16[3,128,256]{2,1,0:T(8,128)(2,1)S(1)}, bf16[3,128,256]{2,1,0:T(8,128)(2,1)S(1)}, u32[]{:S(2)}, u32[]{:S(2)}) %collective-permute-start.2) | collective-permute-done | bytes 196640 | tf_op jit(solution)/shard_map/gather/ppermute | solution.py:33
  62.9 1.0 collective-permute-start.4
  63.9 0.0 collective-permute-done.3.refs_2_
  63.9 1.8 %collective-permute-start.5 = (bf16[3,128,256]{2,1,0:T(8,128)(2,1)S(1)}, bf16[3,128,256]{2,1,0:T(8,128)(2,1)S(1)}, u32[]{:S(2)}, u32[]{:S(2)}) collective-permute-start(bf16[3,128,256]{2,1,0:T(8,128)(2,1)S(1)} %collective-permute-done.3.refs_2_), channel_id=1, source_target_pairs={{0,14},{2,0},{4,2},{6,4},{8,6},{10,8},{12,10},{14,12},{1,15},{3,1}... | collective-permute-start | bytes 589832 | tf_op jit(solution)/shard_map/gather/ppermute | solution.py:33
  65.6 3.0 %collective-permute-done.4.refs_3_ = bf16[3,128,256]{2,1,0:T(8,128)(2,1)S(1)} collective-permute-done((bf16[3,128,256]{2,1,0:T(8,128)(2,1)S(1)}, bf16[3,128,256]{2,1,0:T(8,128)(2,1)S(1)}, u32[]{:S(2)}, u32[]{:S(2)}) %collective-permute-start.4) | collective-permute-done | bytes 196640 | tf_op jit(solution)/shard_map/gather/ppermute | solution.py:33
  68.6 0.0 collective-permute-start.6
  68.6 0.0 collective-permute-done.5.refs_4_
  68.6 2.8 %collective-permute-start.7 = (bf16[3,128,256]{2,1,0:T(8,128)(2,1)S(1)}, bf16[3,128,256]{2,1,0:T(8,128)(2,1)S(1)}, u32[]{:S(2)}, u32[]{:S(2)}) collective-permute-start(bf16[3,128,256]{2,1,0:T(8,128)(2,1)S(1)} %collective-permute-done.5.refs_4_), channel_id=1, source_target_pairs={{0,14},{2,0},{4,2},{6,4},{8,6},{10,8},{12,10},{14,12},{1,15},{3,1}... | collective-permute-start | bytes 589832 | tf_op jit(solution)/shard_map/gather/ppermute | solution.py:33
  71.4 3.0 %collective-permute-done.6.refs_5_ = bf16[3,128,256]{2,1,0:T(8,128)(2,1)S(1)} collective-permute-done((bf16[3,128,256]{2,1,0:T(8,128)(2,1)S(1)}, bf16[3,128,256]{2,1,0:T(8,128)(2,1)S(1)}, u32[]{:S(2)}, u32[]{:S(2)}) %collective-permute-start.6) | collective-permute-done | bytes 196640 | tf_op jit(solution)/shard_map/gather/ppermute | solution.py:33
  74.3 0.0 collective-permute-start.8
  74.3 0.0 collective-permute-done.7.refs_6_
  74.3 1.6 %coupling.4 = (f32[768,256]{1,0:T(8,128)S(1)}, bf16[3,1024,256]{2,1,0:T(8,128)(2,1)S(1)}) custom-call(s32[7]{0:T(128)S(1)} %copy-done.5, bf16[3,512,1024]{2,1,0:T(8,128)(2,1)S(1)} %get-tuple-element.12.terms_ref, bf16[3,128,256]{2,1,0:T(8,128)(2,1)S(1)} %gather.3.refs_0_, bf16[3,128,256]{2,1,0:T(8,128)(2,1)S(1)} %collective-permute-done.2.refs_1_, ...), custom_call_target="tpu_custom_call" | custom-call | flops 805306368 | bytes 4522012 | tf_op jit(solution)/shard_map/coupling/pallas_call | solution.py:38
  75.9 5.0 %collective-permute-done.8.piece_ref = bf16[3,128,256]{2,1,0:T(8,128)(2,1)S(1)} collective-permute-done((bf16[3,128,256]{2,1,0:T(8,128)(2,1)S(1)}, bf16[3,128,256]{2,1,0:T(8,128)(2,1)S(1)}, u32[]{:S(2)}, u32[]{:S(2)}) %collective-permute-start.8) | collective-permute-done | bytes 196640 | tf_op jit(solution)/shard_map/gather/ppermute | solution.py:33
  81.0 1.0 coupling.5
  82.0 0.0 copy-start.1
  82.0 6.4 %collective-permute-start.9 = (bf16[3,1024,256]{2,1,0:T(8,128)(2,1)S(1)}, bf16[3,1024,256]{2,1,0:T(8,128)(2,1)S(1)}, u32[]{:S(2)}, u32[]{:S(2)}) collective-permute-start(bf16[3,1024,256]{2,1,0:T(8,128)(2,1)S(1)} %get-tuple-element.16.own_ref), channel_id=1, source_target_pairs={{0,1},{1,0},{2,3},{3,2},{4,5},{5,4},{6,7},{7,6},{8,9},{9,8},{10,11... | collective-permute-start | bytes 4718600 | tf_op jit(solution)/shard_map/coupling/ppermute | solution.py:29
  88.4 19.6 %all_to_all.20.part_ref = f32[32,24,256]{2,1,0:T(8,128)S(1)} all-to-all(f32[32,24,256]{2,1,0:T(8,128)S(1)} %bitcast.7), channel_id=1, replica_groups=mesh['yl'=2,'x'=4,'yh'=2,'z'=8,'core'=2] {'core','yl','x','yh'}, dimensions={0} | all-to-all | bytes 1572864 | tf_op jit(solution)/shard_map/coupling/all_to_all | solution.py:264
  108.0 0.1 coupling.6
  108.0 12.8 %all_to_all.21.parts_ref = f32[8,24,256]{2,1,0:T(8,128)S(1)} all-to-all(f32[8,24,256]{2,1,0:T(8,128)S(1)} %coupling.6), channel_id=1, replica_groups=mesh['yl'=2,'x'=4,'yh'=2,'z'=8,'core'=2] {'z'}, dimensions={0} | all-to-all | bytes 393216 | tf_op jit(solution)/shard_map/coupling/all_to_all | solution.py:265
  120.9 15.4 %all_to_all.22 = bf16[32,24,256]{2,1,0:T(8,128)(2,1)S(1)} all-to-all(bf16[32,24,256]{2,1,0:T(8,128)(2,1)S(1)} %broadcast_in_dim.2), channel_id=1, replica_groups=mesh['yl'=2,'x'=4,'yh'=2,'z'=8,'core'=2] {'core','yl','x','yh'}, dimensions={0} | all-to-all | bytes 786432 | tf_op jit(solution)/shard_map/coupling/all_to_all | solution.py:268
  136.3 0.0 collective-permute-done.9.other_ref
  136.3 0.0 copy-done.1
  136.3 7.3 %output.1 = bf16[2048,1024]{1,0:T(8,128)(2,1)} custom-call(s32[7]{0:T(128)S(1)} %copy-done.5, bf16[3,1024,256]{2,1,0:T(8,128)(2,1)S(1)} %get-tuple-element.16.own_ref, bf16[3,1024,256]{2,1,0:T(8,128)(2,1)S(1)} %collective-permute-done.9.other_ref, bf16[3,256,256]{2,1,0:T(8,128)(2,1)S(1)} %bitcast.8, bf16[3,1024,256]{2,1,0:T(8,128)(2,1)S(1)} %copy-done.1), custom_call_target="tpu_custom_call" | custom-call | flops 4026531840 | bytes 5111836 | tf_op jit(solution)/shard_map/output/pallas_call | solution.py:38
  (2 shorter events, 0.0 us)
Async XLA Ops:
  8.3 20.1 %collective-permute-start = (f32[3,1024,256]{2,1,0:T(8,128)}, f32[3,1024,256]{2,1,0:T(8,128)S(1)}, u32[]{:S(2)}, u32[]{:S(2)}) collective-permute-start(f32[3,1024,256]{2,1,0:T(8,128)} %projection.4), channel_id=1, source_target_pairs={{0,1},{1,0},{2,3},{3,2},{4,5},{5,4},{6,7},{7,6},{8,9},{9,8},{10,11... | collective-permute-start | bytes 9437192 | tf_op jit(solution)/shard_map/projection/ppermute | solution.py:29
  11.6 38.3 %all-to-all-start = ((bf16[32,64,256]{2,1,0:T(8,128)(2,1)}), bf16[32,64,256]{2,1,0:T(8,128)(2,1)}, u32[]{:S(2)}, u32[]{:S(2)}) async-start(bf16[32,64,256]{2,1,0:T(8,128)(2,1)} %bitcast.9), calls=%async_computation | async-start | bytes 2097152 | tf_op jit(solution)/shard_map/scatter/all_to_all | solution.py:244
  21.3 8.7 %copy-start.5 = (s32[7]{0:T(128)S(1)}, s32[7]{0:T(128)}, u32[]{:S(2)}) copy-start(s32[7]{0:T(128)} %concatenate.3.at_ref) | copy-start | bytes 88
  28.4 1.7 %copy-start.2 = (f32[3,1024,256]{2,1,0:T(8,128)}, f32[3,1024,256]{2,1,0:T(8,128)S(1)}, u32[]{:S(2)}) copy-start(f32[3,1024,256]{2,1,0:T(8,128)S(1)} %collective-permute-done.other_ref) | copy-start | bytes 9437188
  30.0 1.9 %copy-start = (f32[3,1024,256]{2,1,0:T(8,128)S(1)}, f32[3,1024,256]{2,1,0:T(8,128)}, u32[]{:S(2)}) copy-start(f32[3,1024,256]{2,1,0:T(8,128)} %projection.3.own_ref) | copy-start | bytes 9437188
  31.9 1.9 %copy-start.3 = (f32[3,1024,256]{2,1,0:T(8,128)S(1)}, f32[3,1024,256]{2,1,0:T(8,128)}, u32[]{:S(2)}) copy-start(f32[3,1024,256]{2,1,0:T(8,128)} %copy-done.2) | copy-start | bytes 9437188
  33.8 1.1 copy-start.4
  51.3 5.1 %collective-permute-start.1 = (bf16[3,64,256]{2,1,0:T(8,128)(2,1)S(1)}, bf16[3,64,256]{2,1,0:T(8,128)(2,1)S(1)}, u32[]{:S(2)}, u32[]{:S(2)}) collective-permute-start(bf16[3,64,256]{2,1,0:T(8,128)(2,1)S(1)} %gather.2.mine_ref), channel_id=1, source_target_pairs={{0,16},{16,0},{1,17},{17,1},{2,18},{18,2},{3,19},{19,3},{4,20},{20... | collective-permute-start | bytes 294920 | tf_op jit(solution)/shard_map/gather/ppermute | solution.py:29
  56.9 6.0 %collective-permute-start.2 = (bf16[3,128,256]{2,1,0:T(8,128)(2,1)S(1)}, bf16[3,128,256]{2,1,0:T(8,128)(2,1)S(1)}, u32[]{:S(2)}, u32[]{:S(2)}) collective-permute-start(bf16[3,128,256]{2,1,0:T(8,128)(2,1)S(1)} %gather.3.refs_0_), channel_id=1, source_target_pairs={{0,2},{2,4},{4,6},{6,8},{8,10},{10,12},{12,14},{14,0},{1,3},{3,5},... | collective-permute-start | bytes 589832 | tf_op jit(solution)/shard_map/gather/ppermute | solution.py:33
  58.6 5.3 %collective-permute-start.3 = (bf16[3,128,256]{2,1,0:T(8,128)(2,1)S(1)}, bf16[3,128,256]{2,1,0:T(8,128)(2,1)S(1)}, u32[]{:S(2)}, u32[]{:S(2)}) collective-permute-start(bf16[3,128,256]{2,1,0:T(8,128)(2,1)S(1)} %gather.3.refs_0_), channel_id=1, source_target_pairs={{0,14},{2,0},{4,2},{6,4},{8,6},{10,8},{12,10},{14,12},{1,15},{3,1}... | collective-permute-start | bytes 589832 | tf_op jit(solution)/shard_map/gather/ppermute | solution.py:33
  62.9 5.7 %collective-permute-start.4 = (bf16[3,128,256]{2,1,0:T(8,128)(2,1)S(1)}, bf16[3,128,256]{2,1,0:T(8,128)(2,1)S(1)}, u32[]{:S(2)}, u32[]{:S(2)}) collective-permute-start(bf16[3,128,256]{2,1,0:T(8,128)(2,1)S(1)} %collective-permute-done.2.refs_1_), channel_id=1, source_target_pairs={{0,2},{2,4},{4,6},{6,8},{8,10},{10,12},{12,14},{14,0},{1,3},{3,5},... | collective-permute-start | bytes 589832 | tf_op jit(solution)/shard_map/gather/ppermute | solution.py:33
  63.9 4.8 %collective-permute-start.5 = (bf16[3,128,256]{2,1,0:T(8,128)(2,1)S(1)}, bf16[3,128,256]{2,1,0:T(8,128)(2,1)S(1)}, u32[]{:S(2)}, u32[]{:S(2)}) collective-permute-start(bf16[3,128,256]{2,1,0:T(8,128)(2,1)S(1)} %collective-permute-done.3.refs_2_), channel_id=1, source_target_pairs={{0,14},{2,0},{4,2},{6,4},{8,6},{10,8},{12,10},{14,12},{1,15},{3,1}... | collective-permute-start | bytes 589832 | tf_op jit(solution)/shard_map/gather/ppermute | solution.py:33
  68.6 5.7 %collective-permute-start.6 = (bf16[3,128,256]{2,1,0:T(8,128)(2,1)S(1)}, bf16[3,128,256]{2,1,0:T(8,128)(2,1)S(1)}, u32[]{:S(2)}, u32[]{:S(2)}) collective-permute-start(bf16[3,128,256]{2,1,0:T(8,128)(2,1)S(1)} %collective-permute-done.4.refs_3_), channel_id=1, source_target_pairs={{0,2},{2,4},{4,6},{6,8},{8,10},{10,12},{12,14},{14,0},{1,3},{3,5},... | collective-permute-start | bytes 589832 | tf_op jit(solution)/shard_map/gather/ppermute | solution.py:33
  68.6 5.7 %collective-permute-start.7 = (bf16[3,128,256]{2,1,0:T(8,128)(2,1)S(1)}, bf16[3,128,256]{2,1,0:T(8,128)(2,1)S(1)}, u32[]{:S(2)}, u32[]{:S(2)}) collective-permute-start(bf16[3,128,256]{2,1,0:T(8,128)(2,1)S(1)} %collective-permute-done.5.refs_4_), channel_id=1, source_target_pairs={{0,14},{2,0},{4,2},{6,4},{8,6},{10,8},{12,10},{14,12},{1,15},{3,1}... | collective-permute-start | bytes 589832 | tf_op jit(solution)/shard_map/gather/ppermute | solution.py:33
  74.3 6.6 %collective-permute-start.8 = (bf16[3,128,256]{2,1,0:T(8,128)(2,1)S(1)}, bf16[3,128,256]{2,1,0:T(8,128)(2,1)S(1)}, u32[]{:S(2)}, u32[]{:S(2)}) collective-permute-start(bf16[3,128,256]{2,1,0:T(8,128)(2,1)S(1)} %collective-permute-done.6.refs_5_), channel_id=1, source_target_pairs={{0,2},{2,4},{4,6},{6,8},{8,10},{10,12},{12,14},{14,0},{1,3},{3,5},... | collective-permute-start | bytes 589832 | tf_op jit(solution)/shard_map/gather/ppermute | solution.py:33
  82.0 54.3 %copy-start.1 = (bf16[3,1024,256]{2,1,0:T(8,128)(2,1)S(1)}, bf16[3,1024,256]{2,1,0:T(8,128)(2,1)}, u32[]{:S(2)}) copy-start(bf16[3,1024,256]{2,1,0:T(8,128)(2,1)} %panels_ref.5) | copy-start | bytes 4718596
  82.0 54.3 %collective-permute-start.9 = (bf16[3,1024,256]{2,1,0:T(8,128)(2,1)S(1)}, bf16[3,1024,256]{2,1,0:T(8,128)(2,1)S(1)}, u32[]{:S(2)}, u32[]{:S(2)}) collective-permute-start(bf16[3,1024,256]{2,1,0:T(8,128)(2,1)S(1)} %get-tuple-element.16.own_ref), channel_id=1, source_target_pairs={{0,1},{1,0},{2,3},{3,2},{4,5},{5,4},{6,7},{7,6},{8,9},{9,8},{10,11... | collective-permute-start | bytes 4718600 | tf_op jit(solution)/shard_map/coupling/ppermute | solution.py:29

commit v6 on v5

--- a/solution.py
+++ b/solution.py
@@ -10,7 +10,6 @@
 
 ROW = ("yl", "x")
 COL = ("yh", "z", "core")
-SPREAD = ("core", "z", "yh")
 PLANE = ("core", "yl", "x", "yh")
 F32 = jnp.float32
 BF16 = jnp.bfloat16
@@ -51,38 +50,54 @@
     return number & 1, (number >> 1) & (RING - 1), number >> 4
 
 
-def pick_kernel(at_ref, all_ref, _, out_ref, sems):
+def pick_kernel(at_ref, all_ref, _one, _two, keep_ref, send_ref, sems):
+    rows = keep_ref.shape[1]
     copies = []
-    for k in range(out_ref.shape[0]):
-        core, place, high = owner_of(at_ref, k)
-        number = core * (2 * RING) + place * 2 + high
-        copies.append(pltpu.make_async_copy(all_ref.at[number], out_ref.at[k], sems.at[k]))
-        copies[-1].start()
+    for k in range(keep_ref.shape[0]):
+        _, place, _ = owner_of(at_ref, k)
+        for half, ref in ((at_ref[0], keep_ref), (1 - at_ref[0], send_ref)):
+            span = pl.ds(pl.multiple_of(half * rows, rows), rows)
+            copies.append(pltpu.make_async_copy(all_ref.at[place, span], ref.at[k], sems.at[len(copies)]))
+            copies[-1].start()
     for copy in copies:
         copy.wait()
 
 
-def pair_kernel(at_ref, mine_ref, other_ref, out_ref):
-    rows = mine_ref.shape[1]
-    mine = pl.ds(pl.multiple_of(at_ref[1] * rows, rows), rows)
-    other = pl.ds(pl.multiple_of((1 - at_ref[1]) * rows, rows), rows)
-    for k in range(mine_ref.shape[0]):
-        out_ref[k, mine] = mine_ref[k]
-        out_ref[k, other] = other_ref[k]
-
-
-def project_kernel(own, at_ref, gradient_ref, panels_ref, out_ref, rows_ref, sems):
-    blocks, size, _ = rows_ref.shape
+def level_kernel(axis, at_ref, mine_ref, other_ref, out_ref, token_ref):
+    for k in range(out_ref.shape[0]):
+        core, _, high = owner_of(at_ref, k)
+        mine = (core, high)[axis] == at_ref[axis]
+
+        @pl.when(mine)
+        def _():
+            out_ref[k] = mine_ref[k]
+
+        @pl.when(jnp.logical_not(mine))
+        def _():
+            out_ref[k] = other_ref[k]
+
+    token_ref[...] = jnp.zeros_like(token_ref)
+
+
+def level(axis, at, mine, other):
+    return call(functools.partial(level_kernel, axis), (at, mine, other), [SMEM, VMEM, VMEM], [VMEM] * 2, [jax.ShapeDtypeStruct(mine.shape, mine.dtype), TOKEN])
+
+
+def project_kernel(own, at_ref, gradient_ref, panels_ref, out_ref, token_ref, rows_ref, sems):
+    rows = rows_ref.shape[0] // RING
     half = at_ref[0] if own else 1 - at_ref[0]
     copies = []
-    for i in range(blocks):
-        start = pl.multiple_of((half * blocks + i) * size, size)
-        copies.append(pltpu.make_async_copy(gradient_ref.at[pl.ds(start, size)], rows_ref.at[i], sems.at[i]))
+    for i in range(RING):
+        start = pl.multiple_of((2 * i + half) * rows, rows)
+        copies.append(pltpu.make_async_copy(gradient_ref.at[pl.ds(start, rows)], rows_ref.at[pl.ds(i * rows, rows)], sems.at[i]))
         copies[-1].start()
-    for i in range(blocks):
+    for i in range(0, RING, 2):
         copies[i].wait()
+        copies[i + 1].wait()
+        span = slice(i * rows, (i + 2) * rows)
         for k in range(panels_ref.shape[0]):
-            out_ref[k, i * size : (i + 1) * size] = jnp.dot(rows_ref[i], panels_ref[k], preferred_element_type=F32)
+            out_ref[k, span] = jnp.dot(rows_ref[span], panels_ref[k], preferred_element_type=F32)
+    token_ref[...] = jnp.zeros_like(token_ref)
 
 
 def project(at, own, gradient, panels):
@@ -92,15 +107,14 @@
         functools.partial(project_kernel, own),
         (at, gradient, panels),
         [SMEM, ANY, VMEM],
-        VMEM,
-        jax.ShapeDtypeStruct((count, rows, vec), F32),
+        [VMEM, VMEM],
+        [jax.ShapeDtypeStruct((count, rows, vec), F32), TOKEN],
         2 * rows * width * vec * count,
-        [pltpu.VMEM((BLOCKS, rows // BLOCKS, width), BF16), pltpu.SemaphoreType.DMA((BLOCKS,))],
-        limit=60,
+        [pltpu.VMEM((rows, width), BF16), pltpu.SemaphoreType.DMA((RING,))],
     )
 
 
-def split_kernel(at_ref, own_ref, other_ref, values_ref, out_ref, below_ref, token_ref, all_ref):
+def split_kernel(at_ref, own_ref, other_ref, values_ref, _, out_ref, below_ref, all_ref):
     count, _, vec = own_ref.shape
     for k in range(count):
         total = (own_ref[k] + other_ref[k]).T
@@ -111,13 +125,12 @@
         all_ref[k * vec : (k + 1) * vec] = (values + 0.1 * jnp.mean(values)).T
     size = below_ref.shape[0]
     below_ref[...] = all_ref[pl.ds(pl.multiple_of(at_ref[3] * size, size), size)]
-    token_ref[...] = jnp.zeros_like(token_ref)
-
-
-def split(at, own, other, values, places):
+
+
+def split(at, own, other, values, places, token):
     count, rows, vec = own.shape
-    shapes = [jax.ShapeDtypeStruct((count, 2 * vec, rows), BF16), jax.ShapeDtypeStruct((count * vec // places, vec), F32), TOKEN]
-    return call(split_kernel, (at, own, other, values), [SMEM] + [VMEM] * 3, [VMEM] * 3, shapes, scratch=[pltpu.VMEM((count * vec, vec), F32)])
+    shapes = [jax.ShapeDtypeStruct((count, 2 * vec, rows), BF16), jax.ShapeDtypeStruct((count * vec // places, vec), F32)]
+    return call(split_kernel, (at, own, other, values, token), [SMEM] + [VMEM] * 3 + [ANY], [VMEM] * 2, shapes, scratch=[pltpu.VMEM((count * vec, vec), F32)])
 
 
 def offsets():
@@ -170,17 +183,18 @@
     return call(late_kernel, (at, terms, total, half, piece), [SMEM] + [VMEM] * 4, [VMEM, VMEM], shapes)
 
 
-def spread_kernel(part_ref, out_ref):
+def spread_kernel(part_ref, out_ref, token_ref):
     total = jnp.sum(part_ref[...], axis=0)
     for j in range(RING):
         out_ref[j] = total
+    token_ref[...] = jnp.zeros_like(token_ref)
 
 
 def spread(parts):
-    return call(spread_kernel, (parts,), [VMEM], VMEM, jax.ShapeDtypeStruct((RING,) + parts.shape[1:], F32))
-
-
-def scale_kernel(parts_ref, below_ref, out_ref):
+    return call(spread_kernel, (parts,), [VMEM], [VMEM] * 2, [jax.ShapeDtypeStruct((RING,) + parts.shape[1:], F32), TOKEN])
+
+
+def scale_kernel(parts_ref, below_ref, _, out_ref):
     out_ref[...] = (jnp.sum(parts_ref[...], axis=0) / below_ref[...]).astype(BF16)
 
 
@@ -203,9 +217,12 @@
             total = term if total is None else total + term
         block_ref[number] = total.astype(BF16)
         first = at_ref[0] if number < near else 1 - at_ref[0]
-        target = pl.multiple_of(first * half + (number % near) * size, size)
-        copies.append(pltpu.make_async_copy(block_ref.at[number], out_ref.at[pl.ds(target, size)], out_sems.at[number]))
-        copies[-1].start()
+        rows = half // RING
+        for i in range(size // rows):
+            target = pl.multiple_of((((number % near) * size // rows + i) * 2 + first) * rows, rows)
+            source = block_ref.at[number, pl.ds(i * rows, rows)]
+            copies.append(pltpu.make_async_copy(source, out_ref.at[pl.ds(target, rows)], out_sems.at[len(copies)]))
+            copies[-1].start()
     for copy in copies:
         copy.wait()
 
@@ -226,7 +243,7 @@
             pltpu.VMEM((steps, count, size, vec), BF16),
             pltpu.VMEM((steps, size, width), BF16),
             pltpu.SemaphoreType.DMA((steps,)),
-            pltpu.SemaphoreType.DMA((steps,)),
+            pltpu.SemaphoreType.DMA((2 * RING,)),
         ],
         limit=24,
     )
@@ -236,20 +253,24 @@
     core, high, here = (lax.axis_index(a) for a in ("core", "yh", "z"))
     at = jnp.concatenate([jnp.stack([core, high, here, lax.axis_index(PLANE)]).astype(jnp.int32), owners])
     count, _, vec = in_panels.shape
-    size = out_pool.shape[1] // 32
-    piece = jax.ShapeDtypeStruct((count, size, vec), BF16)
-    pair = jax.ShapeDtypeStruct((count, 2 * size, vec), BF16)
+    size = out_pool.shape[1] // RING
+    piece = jax.ShapeDtypeStruct((count, size // 2, vec), BF16)
 
     with jax.named_scope("scatter"):
-        every = lax.all_to_all(out_pool.reshape(32, size, vec), SPREAD, 0, 0)
+        every = lax.all_to_all(out_pool.reshape(RING, size, vec), "z", 0, 0)
 
     with jax.named_scope("projection"):
-        came = swap(project(at, False, gradient, in_panels), "core")
-        terms, below, token = split(at, project(at, True, gradient, in_panels), came, eigenvalues, 32)
+        sent, one = project(at, False, gradient, in_panels)
+        kept, two = project(at, True, gradient, in_panels)
 
     with jax.named_scope("gather"):
-        mine = call(pick_kernel, (at, every, token), [SMEM, ANY, ANY], VMEM, piece, scratch=[pltpu.SemaphoreType.DMA((count,))])
-        mine = call(pair_kernel, (at, mine, swap(mine, "yh")), [SMEM, VMEM, VMEM], VMEM, pair)
+        scratch = [pltpu.SemaphoreType.DMA((2 * count,))]
+        specs = [SMEM, ANY, ANY, ANY]
+        mine, send = call(pick_kernel, (at, every, one, two), specs, [VMEM] * 2, [piece] * 2, scratch=scratch)
+        mine, token = level(0, at, mine, swap(send, "core"))
+        sent, token = lax.optimization_barrier((sent, token))
+        terms, below = split(at, kept, swap(sent, "core"), eigenvalues, 32, token)
+        mine, _ = level(1, at, mine, swap(mine, "yh"))
         pieces = [mine]
         up = down = mine
         for _ in range(1, REACH):
@@ -260,10 +281,11 @@
     with jax.named_scope("coupling"):
         part, own = early(at, terms, pieces[:-1])
         part, own = late(at, terms, part, own, pieces[-1])
+        part, token = spread(lax.all_to_all(part.reshape(32, -1, vec), PLANE, 0, 0))
+        own, token = lax.optimization_barrier((own, token))
         other = swap(own, "core")
-        part = spread(lax.all_to_all(part.reshape(32, -1, vec), PLANE, 0, 0))
         part = lax.all_to_all(part, "z", 0, 0)
-        scaled = call(scale_kernel, (part, below), [VMEM, VMEM], VMEM, jax.ShapeDtypeStruct(part.shape[1:], BF16))
+        scaled = call(scale_kernel, (part, below, token), [VMEM, VMEM, ANY], VMEM, jax.ShapeDtypeStruct(part.shape[1:], BF16))
         copies = jnp.broadcast_to(scaled[None], (32,) + scaled.shape)
         scaled = lax.all_to_all(copies, PLANE, 0, 0).reshape(count, vec, vec)
 

time: 144 us -> 139 us (0.965)
  starting transfers between devices: 29.3 us -> 21.3 us
  blocking collectives: 47.7 us -> 54.5 us
  Pallas kernels: 27.6 us -> 22 us
  local copies, waits for them, and re-layouts: 7.91 us -> 9.54 us
    all_to_all x1, blocking collectives: 19.6 us -> 26.8 us  [body(): part, token = spread(lax.all_to_all(part.reshape(32, -1, vec), PLANE, 0, 0))]
    ppermute x3 -> x4, starting transfers between devices: 11 us -> 4.3 us  [swap(): return lax.ppermute(x, axis, [(0, 1), (1, 0)])]
    pallas_call x10 -> x11, Pallas kernels: 27.6 us -> 22 us  [call(): pl.pallas_call(kernel, in_specs=in_specs, out_specs=out_specs, out_shape=...]
    ppermute x7, waiting for transfers between devices: 14 us -> 10.5 us  [shift(): return lax.ppermute(x, 'z', [(i, (i + by) % RING) for i in range(RING)])]
    ppermute x3 -> x4, waiting for transfers between devices: 3.78 us -> 6.03 us  [swap(): return lax.ppermute(x, axis, [(0, 1), (1, 0)])]
    unnamed x12 -> x14, local copies, waits for them, and re-layouts: 6.57 us -> 8.78 us
  transfers between devices with their start and end apart: 11 -> 12, of which waited for: 6 -> 7; matrix products, arithmetic and copies ran while one was open for 0% -> 1% of each run, Pallas kernels for 7% -> 9%
where the time goes in v6:
time: 139 us; the launch traced here: 138 us
  blocking collectives  54.5 us (39%)
  waiting for transfers between devices  30.8 us (22%)
  Pallas kernels  22 us (16%)
  starting transfers between devices  21.3 us (15%)
  local copies, waits for them, and re-layouts  9.54 us (7%)
    all_to_all x1, blocking collectives, body(): part, token = spread(lax.all_to_all(part.reshape(32, -1, vec), PLANE, 0, 0))  26.8 us
    pallas_call x11, Pallas kernels, call(): pl.pallas_call(kernel, in_specs=in_specs, out_specs=out_specs, out_shape=...  22 us
    all_to_all x1, blocking collectives, body(): scaled = lax.all_to_all(copies, PLANE, 0, 0).reshape(count, vec, vec)  15.6 us
    all_to_all x1, waiting for transfers between devices, body(): every = lax.all_to_all(out_pool.reshape(RING, size, vec), 'z', 0, 0)  14.3 us
    all_to_all x1, blocking collectives, body(): part = lax.all_to_all(part, 'z', 0, 0)  12.1 us
    ppermute x7, waiting for transfers between devices, shift(): return lax.ppermute(x, 'z', [(i, (i + by) % RING) for i in range(RING)])  10.5 us
    all_to_all x1, starting transfers between devices, body(): every = lax.all_to_all(out_pool.reshape(RING, size, vec), 'z', 0, 0)  9.01 us
    unnamed x14, local copies, waits for them, and re-layouts  8.78 us
  transfers between devices with their start and end apart: 12, of which 7 were waited for; matrix products, arithmetic and copies ran while one was open for 1% of the time, Pallas kernels for 9%

profile of v6, /device:TPU:1, one launch (start us, length us, event | category | flops | bytes accessed | tf_op | source)
XLA Modules:
  0.0 138.5 jit_solution(885985225323822720)
XLA Ops:
  0.0 9.0 %all-to-all-start = ((bf16[8,256,256]{2,1,0:T(8,128)(2,1)}), bf16[8,256,256]{2,1,0:T(8,128)(2,1)S(1)}, u32[]{:S(2)}, u32[]{:S(2)}) async-start(bf16[8,256,256]{2,1,0:T(8,128)(2,1)} %bitcast.9), calls=%async_computation | async-start | bytes 2097152 | tf_op jit(solution)/shard_map/scatter/all_to_all | solution.py:260
  9.0 0.7 concatenate.3.at_ref
  9.8 2.2 %copy-done.3 = bf16[2048,1024]{1,0:T(8,128)(2,1)S(1)} copy-done((bf16[2048,1024]{1,0:T(8,128)(2,1)S(1)}, bf16[2048,1024]{1,0:T(8,128)(2,1)}, u32[]{:S(2)}) %copy-start.3) | copy-done | bytes 4194328
  11.9 1.4 %copy-done.5 = bf16[3,1024,256]{2,1,0:T(8,128)(2,1)S(1)} copy-done((bf16[3,1024,256]{2,1,0:T(8,128)(2,1)S(1)}, bf16[3,1024,256]{2,1,0:T(8,128)(2,1)}, u32[]{:S(2)}) %copy-start.5) | copy-done | bytes 1572888
  13.3 3.6 %projection.2 = (f32[3,1024,256]{2,1,0:T(8,128)S(1)}, f32[8,128]{1,0:T(8,128)S(1)}) custom-call(s32[7]{0:T(128)S(1)} %concatenate.3.at_ref, bf16[2048,1024]{1,0:T(8,128)(2,1)S(1)} %copy-done.3, bf16[3,1024,256]{2,1,0:T(8,128)(2,1)S(1)} %copy-done.5), custom_call_target="tpu_custom_call" | custom-call | flops 1610612736 | bytes 5767196 | tf_op jit(solution)/shard_map/projection/pallas_call | solution.py:37
  17.0 0.0 copy-start
  17.0 1.7 %copy-done = f32[3,1024,256]{2,1,0:T(8,128)} copy-done((f32[3,1024,256]{2,1,0:T(8,128)}, f32[3,1024,256]{2,1,0:T(8,128)S(1)}, u32[]{:S(2)}) %copy-start) | copy-done | bytes 3145752
  18.7 3.6 %projection.3 = (f32[3,1024,256]{2,1,0:T(8,128)S(1)}, f32[8,128]{1,0:T(8,128)S(1)}) custom-call(s32[7]{0:T(128)S(1)} %concatenate.3.at_ref, bf16[2048,1024]{1,0:T(8,128)(2,1)S(1)} %copy-done.3, bf16[3,1024,256]{2,1,0:T(8,128)(2,1)S(1)} %copy-done.5), custom_call_target="tpu_custom_call" | custom-call | flops 1610612736 | bytes 5767196 | tf_op jit(solution)/shard_map/projection/pallas_call | solution.py:37
  22.3 0.0 copy-start.4
  22.3 1.6 %copy-done.4 = f32[3,1024,256]{2,1,0:T(8,128)} copy-done((f32[3,1024,256]{2,1,0:T(8,128)}, f32[3,1024,256]{2,1,0:T(8,128)S(1)}, u32[]{:S(2)}) %copy-start.4) | copy-done | bytes 3145752
  24.0 14.3 %all-to-all-done.all_ref = bf16[8,256,256]{2,1,0:T(8,128)(2,1)S(1)} async-done(((bf16[8,256,256]{2,1,0:T(8,128)(2,1)}), bf16[8,256,256]{2,1,0:T(8,128)(2,1)S(1)}, u32[]{:S(2)}, u32[]{:S(2)}) %all-to-all-start) | async-done | bytes 1048608 | tf_op jit(solution)/shard_map/scatter/all_to_all | solution.py:260
  38.2 1.1 gather.4
  39.4 0.6 collective-permute-start
  39.9 1.1 collective-permute-done.other_ref
  41.0 0.6 gather.5
  41.6 0.5 collective-permute-start.1
  42.1 2.9 %collective-permute-start.2 = (bf16[3,128,256]{2,1,0:T(8,128)(2,1)S(1)}, bf16[3,128,256]{2,1,0:T(8,128)(2,1)S(1)}, u32[]{:S(2)}, u32[]{:S(2)}) collective-permute-start(bf16[3,128,256]{2,1,0:T(8,128)(2,1)S(1)} %get-tuple-element.36.mine_ref), channel_id=1, source_target_pairs={{0,16},{16,0},{1,17},{17,1},{2,18},{18,2},{3,19},{19,3},{4,20},{20... | collective-permute-start | bytes 589832 | tf_op jit(solution)/shard_map/gather/ppermute | solution.py:28
  45.0 5.0 %collective-permute-done.2.other_ref = bf16[3,128,256]{2,1,0:T(8,128)(2,1)S(1)} collective-permute-done((bf16[3,128,256]{2,1,0:T(8,128)(2,1)S(1)}, bf16[3,128,256]{2,1,0:T(8,128)(2,1)S(1)}, u32[]{:S(2)}, u32[]{:S(2)}) %collective-permute-start.2) | collective-permute-done | bytes 196640 | tf_op jit(solution)/shard_map/gather/ppermute | solution.py:28
  49.9 1.2 gather.7
  51.1 0.3 collective-permute-start.3
  51.4 2.4 %collective-permute-start.4 = (bf16[3,128,256]{2,1,0:T(8,128)(2,1)S(1)}, bf16[3,128,256]{2,1,0:T(8,128)(2,1)S(1)}, u32[]{:S(2)}, u32[]{:S(2)}) collective-permute-start(bf16[3,128,256]{2,1,0:T(8,128)(2,1)S(1)} %get-tuple-element.37.refs_0_), channel_id=1, source_target_pairs={{0,14},{2,0},{4,2},{6,4},{8,6},{10,8},{12,10},{14,12},{1,15},{3,1}... | collective-permute-start | bytes 589832 | tf_op jit(solution)/shard_map/gather/ppermute | solution.py:32
  53.8 4.0 %collective-permute-done.3.refs_1_ = bf16[3,128,256]{2,1,0:T(8,128)(2,1)S(1)} collective-permute-done((bf16[3,128,256]{2,1,0:T(8,128)(2,1)S(1)}, bf16[3,128,256]{2,1,0:T(8,128)(2,1)S(1)}, u32[]{:S(2)}, u32[]{:S(2)}) %collective-permute-start.3) | collective-permute-done | bytes 196640 | tf_op jit(solution)/shard_map/gather/ppermute | solution.py:32
  57.8 0.0 collective-permute-start.5
  57.8 0.0 collective-permute-done.4.refs_2_
  57.8 2.7 %collective-permute-start.6 = (bf16[3,128,256]{2,1,0:T(8,128)(2,1)S(1)}, bf16[3,128,256]{2,1,0:T(8,128)(2,1)S(1)}, u32[]{:S(2)}, u32[]{:S(2)}) collective-permute-start(bf16[3,128,256]{2,1,0:T(8,128)(2,1)S(1)} %collective-permute-done.4.refs_2_), channel_id=1, source_target_pairs={{0,14},{2,0},{4,2},{6,4},{8,6},{10,8},{12,10},{14,12},{1,15},{3,1}... | collective-permute-start | bytes 589832 | tf_op jit(solution)/shard_map/gather/ppermute | solution.py:32
  60.4 3.0 %collective-permute-done.5.refs_3_ = bf16[3,128,256]{2,1,0:T(8,128)(2,1)S(1)} collective-permute-done((bf16[3,128,256]{2,1,0:T(8,128)(2,1)S(1)}, bf16[3,128,256]{2,1,0:T(8,128)(2,1)S(1)}, u32[]{:S(2)}, u32[]{:S(2)}) %collective-permute-start.5) | collective-permute-done | bytes 196640 | tf_op jit(solution)/shard_map/gather/ppermute | solution.py:32
  63.5 0.0 collective-permute-start.7
  63.5 0.0 collective-permute-done.6.refs_4_
  63.5 2.7 %collective-permute-start.8 = (bf16[3,128,256]{2,1,0:T(8,128)(2,1)S(1)}, bf16[3,128,256]{2,1,0:T(8,128)(2,1)S(1)}, u32[]{:S(2)}, u32[]{:S(2)}) collective-permute-start(bf16[3,128,256]{2,1,0:T(8,128)(2,1)S(1)} %collective-permute-done.6.refs_4_), channel_id=1, source_target_pairs={{0,14},{2,0},{4,2},{6,4},{8,6},{10,8},{12,10},{14,12},{1,15},{3,1}... | collective-permute-start | bytes 589832 | tf_op jit(solution)/shard_map/gather/ppermute | solution.py:32
  66.2 3.0 %collective-permute-done.7.refs_5_ = bf16[3,128,256]{2,1,0:T(8,128)(2,1)S(1)} collective-permute-done((bf16[3,128,256]{2,1,0:T(8,128)(2,1)S(1)}, bf16[3,128,256]{2,1,0:T(8,128)(2,1)S(1)}, u32[]{:S(2)}, u32[]{:S(2)}) %collective-permute-start.7) | collective-permute-done | bytes 196640 | tf_op jit(solution)/shard_map/gather/ppermute | solution.py:32
  69.2 0.0 collective-permute-start.9
  69.2 0.0 collective-permute-done.1.other_ref
  69.2 0.0 copy-done.2
  69.2 0.0 copy-start.1
  69.2 1.9 %copy-done.1 = f32[3,1024,256]{2,1,0:T(8,128)S(1)} copy-done((f32[3,1024,256]{2,1,0:T(8,128)S(1)}, f32[3,1024,256]{2,1,0:T(8,128)}, u32[]{:S(2)}) %copy-start.1) | copy-done | bytes 3145752
  71.1 1.8 %gather.6 = (bf16[3,512,1024]{2,1,0:T(8,128)(2,1)S(1)}, f32[24,256]{1,0:T(8,128)S(1)}) custom-call(s32[7]{0:T(128)S(1)} %concatenate.3.at_ref, f32[3,1024,256]{2,1,0:T(8,128)S(1)} %copy-done.1, f32[3,1024,256]{2,1,0:T(8,128)S(1)} %collective-permute-done.1.other_ref, f32[3,256,256]{2,1,0:T(8,128)S(1)} %copy-done.2, f32[8,128]{1,0:T(8,128)S(1)} %get-tuple-element.34._), custom_call_target="tpu_custom_call" | custom-call | bytes 7082012 | tf_op jit(solution)/shard_map/gather/pallas_call | solution.py:37
  72.9 0.0 collective-permute-done.8.refs_6_
  72.9 1.6 %coupling.4 = (f32[768,256]{1,0:T(8,128)S(1)}, bf16[3,1024,256]{2,1,0:T(8,128)(2,1)S(1)}) custom-call(s32[7]{0:T(128)S(1)} %concatenate.3.at_ref, bf16[3,512,1024]{2,1,0:T(8,128)(2,1)S(1)} %get-tuple-element.35.terms_ref, bf16[3,128,256]{2,1,0:T(8,128)(2,1)S(1)} %get-tuple-element.37.refs_0_, bf16[3,128,256]{2,1,0:T(8,128)(2,1)S(1)} %collective-permute-done.3.refs_1_, ...), custom_call_target="tpu_custom_call" | custom-call | flops 805306368 | bytes 4522012 | tf_op jit(solution)/shard_map/coupling/pallas_call | solution.py:37
  74.5 0.4 collective-permute-done.9.piece_ref
  74.9 1.0 coupling.5
  76.0 0.0 copy-start.6
  76.0 26.8 %all_to_all.20.part_ref = f32[32,24,256]{2,1,0:T(8,128)S(1)} all-to-all(f32[32,24,256]{2,1,0:T(8,128)S(1)} %bitcast.7), channel_id=1, replica_groups=mesh['yl'=2,'x'=4,'yh'=2,'z'=8,'core'=2] {'core','yl','x','yh'}, dimensions={0} | all-to-all | bytes 1572864 | tf_op jit(solution)/shard_map/coupling/all_to_all | solution.py:284
  102.8 0.1 coupling.6
  102.9 0.3 collective-permute-start.10
  103.2 12.1 %all_to_all.21.parts_ref = f32[8,24,256]{2,1,0:T(8,128)S(1)} all-to-all(f32[8,24,256]{2,1,0:T(8,128)S(1)} %get-tuple-element.44), channel_id=1, replica_groups=mesh['yl'=2,'x'=4,'yh'=2,'z'=8,'core'=2] {'z'}, dimensions={0} | all-to-all | bytes 393216 | tf_op jit(solution)/shard_map/coupling/all_to_all | solution.py:287
  115.3 15.6 %all_to_all.22 = bf16[32,24,256]{2,1,0:T(8,128)(2,1)S(1)} all-to-all(bf16[32,24,256]{2,1,0:T(8,128)(2,1)S(1)} %broadcast_in_dim.2), channel_id=1, replica_groups=mesh['yl'=2,'x'=4,'yh'=2,'z'=8,'core'=2] {'core','yl','x','yh'}, dimensions={0} | all-to-all | bytes 786432 | tf_op jit(solution)/shard_map/coupling/all_to_all | solution.py:290
  130.9 0.0 collective-permute-done.10.other_ref
  130.9 7.4 %output.1 = bf16[2048,1024]{1,0:T(8,128)(2,1)} custom-call(s32[7]{0:T(128)S(1)} %concatenate.3.at_ref, bf16[3,1024,256]{2,1,0:T(8,128)(2,1)S(1)} %get-tuple-element.43.own_ref, bf16[3,1024,256]{2,1,0:T(8,128)(2,1)S(1)} %collective-permute-done.10.other_ref, bf16[3,256,256]{2,1,0:T(8,128)(2,1)S(1)} %bitcast.8, bf16[3,1024,256]{2,1,0:T(8,128)(2,1)S(1)} %copy-done.6), custom_call_target="tpu_custom_call" | custom-call | flops 4026531840 | bytes 5111836 | tf_op jit(solution)/shard_map/output/pallas_call | solution.py:37
  (6 shorter events, 0.1 us)
Async XLA Ops:
  0.0 38.2 %all-to-all-start = ((bf16[8,256,256]{2,1,0:T(8,128)(2,1)}), bf16[8,256,256]{2,1,0:T(8,128)(2,1)S(1)}, u32[]{:S(2)}, u32[]{:S(2)}) async-start(bf16[8,256,256]{2,1,0:T(8,128)(2,1)} %bitcast.9), calls=%async_computation | async-start | bytes 2097152 | tf_op jit(solution)/shard_map/scatter/all_to_all | solution.py:260
  9.7 2.2 %copy-start.3 = (bf16[2048,1024]{1,0:T(8,128)(2,1)S(1)}, bf16[2048,1024]{1,0:T(8,128)(2,1)}, u32[]{:S(2)}) copy-start(bf16[2048,1024]{1,0:T(8,128)(2,1)} %gradient_ref.3) | copy-start | bytes 12582916
  11.9 1.4 %copy-start.5 = (bf16[3,1024,256]{2,1,0:T(8,128)(2,1)S(1)}, bf16[3,1024,256]{2,1,0:T(8,128)(2,1)}, u32[]{:S(2)}) copy-start(bf16[3,1024,256]{2,1,0:T(8,128)(2,1)} %panels_ref.5) | copy-start | bytes 4718596
  17.0 1.7 %copy-start = (f32[3,1024,256]{2,1,0:T(8,128)}, f32[3,1024,256]{2,1,0:T(8,128)S(1)}, u32[]{:S(2)}) copy-start(f32[3,1024,256]{2,1,0:T(8,128)S(1)} %get-tuple-element.26.own_ref) | copy-start | bytes 9437188
  18.7 50.6 %copy-start.2 = (f32[3,256,256]{2,1,0:T(8,128)S(1)}, f32[3,256,256]{2,1,0:T(8,128)}, u32[]{:S(2)}) copy-start(f32[3,256,256]{2,1,0:T(8,128)} %values_ref.1) | copy-start | bytes 2359300
  22.3 1.6 %copy-start.4 = (f32[3,1024,256]{2,1,0:T(8,128)}, f32[3,1024,256]{2,1,0:T(8,128)S(1)}, u32[]{:S(2)}) copy-start(f32[3,1024,256]{2,1,0:T(8,128)S(1)} %get-tuple-element.33) | copy-start | bytes 9437188
  39.4 1.7 %collective-permute-start = (bf16[3,128,256]{2,1,0:T(8,128)(2,1)S(1)}, bf16[3,128,256]{2,1,0:T(8,128)(2,1)S(1)}, u32[]{:S(2)}, u32[]{:S(2)}) collective-permute-start(bf16[3,128,256]{2,1,0:T(8,128)(2,1)S(1)} %get-tuple-element.31), channel_id=1, source_target_pairs={{0,1},{1,0},{2,3},{3,2},{4,5},{5,4},{6,7},{7,6},{8,9},{9,8},{10,11... | collective-permute-start | bytes 589832 | tf_op jit(solution)/shard_map/gather/ppermute | solution.py:28
  41.6 27.6 %collective-permute-start.1 = (f32[3,1024,256]{2,1,0:T(8,128)}, f32[3,1024,256]{2,1,0:T(8,128)S(1)}, u32[]{:S(2)}, u32[]{:S(2)}) collective-permute-start(f32[3,1024,256]{2,1,0:T(8,128)} %copy-done.4), channel_id=1, source_target_pairs={{0,1},{1,0},{2,3},{3,2},{4,5},{5,4},{6,7},{7,6},{8,9},{9,8},{10,11... | collective-permute-start | bytes 9437192 | tf_op jit(solution)/shard_map/gather/ppermute | solution.py:28
  42.1 7.9 %collective-permute-start.2 = (bf16[3,128,256]{2,1,0:T(8,128)(2,1)S(1)}, bf16[3,128,256]{2,1,0:T(8,128)(2,1)S(1)}, u32[]{:S(2)}, u32[]{:S(2)}) collective-permute-start(bf16[3,128,256]{2,1,0:T(8,128)(2,1)S(1)} %get-tuple-element.36.mine_ref), channel_id=1, source_target_pairs={{0,16},{16,0},{1,17},{17,1},{2,18},{18,2},{3,19},{19,3},{4,20},{20... | collective-permute-start | bytes 589832 | tf_op jit(solution)/shard_map/gather/ppermute | solution.py:28
  51.1 6.7 %collective-permute-start.3 = (bf16[3,128,256]{2,1,0:T(8,128)(2,1)S(1)}, bf16[3,128,256]{2,1,0:T(8,128)(2,1)S(1)}, u32[]{:S(2)}, u32[]{:S(2)}) collective-permute-start(bf16[3,128,256]{2,1,0:T(8,128)(2,1)S(1)} %get-tuple-element.37.refs_0_), channel_id=1, source_target_pairs={{0,2},{2,4},{4,6},{6,8},{8,10},{10,12},{12,14},{14,0},{1,3},{3,5},... | collective-permute-start | bytes 589832 | tf_op jit(solution)/shard_map/gather/ppermute | solution.py:32
  51.4 6.4 %collective-permute-start.4 = (bf16[3,128,256]{2,1,0:T(8,128)(2,1)S(1)}, bf16[3,128,256]{2,1,0:T(8,128)(2,1)S(1)}, u32[]{:S(2)}, u32[]{:S(2)}) collective-permute-start(bf16[3,128,256]{2,1,0:T(8,128)(2,1)S(1)} %get-tuple-element.37.refs_0_), channel_id=1, source_target_pairs={{0,14},{2,0},{4,2},{6,4},{8,6},{10,8},{12,10},{14,12},{1,15},{3,1}... | collective-permute-start | bytes 589832 | tf_op jit(solution)/shard_map/gather/ppermute | solution.py:32
  57.8 5.7 %collective-permute-start.5 = (bf16[3,128,256]{2,1,0:T(8,128)(2,1)S(1)}, bf16[3,128,256]{2,1,0:T(8,128)(2,1)S(1)}, u32[]{:S(2)}, u32[]{:S(2)}) collective-permute-start(bf16[3,128,256]{2,1,0:T(8,128)(2,1)S(1)} %collective-permute-done.3.refs_1_), channel_id=1, source_target_pairs={{0,2},{2,4},{4,6},{6,8},{8,10},{10,12},{12,14},{14,0},{1,3},{3,5},... | collective-permute-start | bytes 589832 | tf_op jit(solution)/shard_map/gather/ppermute | solution.py:32
  57.8 5.7 %collective-permute-start.6 = (bf16[3,128,256]{2,1,0:T(8,128)(2,1)S(1)}, bf16[3,128,256]{2,1,0:T(8,128)(2,1)S(1)}, u32[]{:S(2)}, u32[]{:S(2)}) collective-permute-start(bf16[3,128,256]{2,1,0:T(8,128)(2,1)S(1)} %collective-permute-done.4.refs_2_), channel_id=1, source_target_pairs={{0,14},{2,0},{4,2},{6,4},{8,6},{10,8},{12,10},{14,12},{1,15},{3,1}... | collective-permute-start | bytes 589832 | tf_op jit(solution)/shard_map/gather/ppermute | solution.py:32
  63.5 5.7 %collective-permute-start.7 = (bf16[3,128,256]{2,1,0:T(8,128)(2,1)S(1)}, bf16[3,128,256]{2,1,0:T(8,128)(2,1)S(1)}, u32[]{:S(2)}, u32[]{:S(2)}) collective-permute-start(bf16[3,128,256]{2,1,0:T(8,128)(2,1)S(1)} %collective-permute-done.5.refs_3_), channel_id=1, source_target_pairs={{0,2},{2,4},{4,6},{6,8},{8,10},{10,12},{12,14},{14,0},{1,3},{3,5},... | collective-permute-start | bytes 589832 | tf_op jit(solution)/shard_map/gather/ppermute | solution.py:32
  63.5 9.4 %collective-permute-start.8 = (bf16[3,128,256]{2,1,0:T(8,128)(2,1)S(1)}, bf16[3,128,256]{2,1,0:T(8,128)(2,1)S(1)}, u32[]{:S(2)}, u32[]{:S(2)}) collective-permute-start(bf16[3,128,256]{2,1,0:T(8,128)(2,1)S(1)} %collective-permute-done.6.refs_4_), channel_id=1, source_target_pairs={{0,14},{2,0},{4,2},{6,4},{8,6},{10,8},{12,10},{14,12},{1,15},{3,1}... | collective-permute-start | bytes 589832 | tf_op jit(solution)/shard_map/gather/ppermute | solution.py:32
  69.2 5.7 %collective-permute-start.9 = (bf16[3,128,256]{2,1,0:T(8,128)(2,1)S(1)}, bf16[3,128,256]{2,1,0:T(8,128)(2,1)S(1)}, u32[]{:S(2)}, u32[]{:S(2)}) collective-permute-start(bf16[3,128,256]{2,1,0:T(8,128)(2,1)S(1)} %collective-permute-done.7.refs_5_), channel_id=1, source_target_pairs={{0,2},{2,4},{4,6},{6,8},{8,10},{10,12},{12,14},{14,0},{1,3},{3,5},... | collective-permute-start | bytes 589832 | tf_op jit(solution)/shard_map/gather/ppermute | solution.py:32
  69.2 1.9 %copy-start.1 = (f32[3,1024,256]{2,1,0:T(8,128)S(1)}, f32[3,1024,256]{2,1,0:T(8,128)}, u32[]{:S(2)}) copy-start(f32[3,1024,256]{2,1,0:T(8,128)} %copy-done) | copy-start | bytes 9437188
  76.0 55.0 %copy-start.6 = (bf16[3,1024,256]{2,1,0:T(8,128)(2,1)S(1)}, bf16[3,1024,256]{2,1,0:T(8,128)(2,1)}, u32[]{:S(2)}) copy-start(bf16[3,1024,256]{2,1,0:T(8,128)(2,1)} %panels_ref.5) | copy-start | bytes 4718596
  102.9 28.1 %collective-permute-start.10 = (bf16[3,1024,256]{2,1,0:T(8,128)(2,1)S(1)}, bf16[3,1024,256]{2,1,0:T(8,128)(2,1)S(1)}, u32[]{:S(2)}, u32[]{:S(2)}) collective-permute-start(bf16[3,1024,256]{2,1,0:T(8,128)(2,1)S(1)} %get-tuple-element.43.own_ref), channel_id=1, source_target_pairs={{0,1},{1,0},{2,3},{3,2},{4,5},{5,4},{6,7},{7,6},{8,9},{9,8},{10,11... | collective-permute-start | bytes 4718600 | tf_op jit(solution)/shard_map/coupling/ppermute | solution.py:28

commit v7 on v6

v7 whole, which is shorter than its diff:
```python
import functools

import jax
import jax.numpy as jnp
from jax import lax
from jax.experimental import pallas as pl
from jax.experimental.pallas import tpu as pltpu
from jax.sharding import Mesh
from jax.sharding import PartitionSpec as P

ROW = ("yl", "x")
COL = ("yh", "z", "core")
PLANE = ("core", "yl", "x", "yh")
F32 = jnp.float32
BF16 = jnp.bfloat16
RING = 8
REACH = RING // 2
MIB = 1024 * 1024

VMEM = pl.BlockSpec(memory_space=pltpu.VMEM)
SMEM = pl.BlockSpec(memory_space=pltpu.SMEM)
ANY = pl.BlockSpec(memory_space=pl.ANY)
TOKEN = jax.ShapeDtypeStruct((8, 128), F32)


def swap(x, axis):
    return lax.ppermute(x, axis, [(0, 1), (1, 0)])


def shift(x, by):
    return lax.ppermute(x, "z", [(i, (i + by) % RING) for i in range(RING)])


def call(kernel, args, in_specs, out_specs, out_shape, flops=0, scratch=(), limit=16):
    moved = sum(a.size * a.dtype.itemsize for a in args)
    return pl.pallas_call(
        kernel,
        in_specs=in_specs,
        out_specs=out_specs,
        out_shape=out_shape,
        scratch_shapes=scratch,
        compiler_params=pltpu.CompilerParams(vmem_limit_bytes=limit * MIB),
        cost_estimate=pl.CostEstimate(flops=flops, bytes_accessed=moved, transcendentals=0),
    )(*args)


def owner_of(at_ref, k):
    number = at_ref[4 + k]
    return number & 1, (number >> 1) & (RING - 1), number >> 4


def pick_kernel(at_ref, all_ref, _one, _two, keep_ref, send_ref, sems):
    rows = keep_ref.shape[1]
    copies = []
    for k in range(keep_ref.shape[0]):
        _, place, high = owner_of(at_ref, k)
        for half, ref in ((at_ref[0], keep_ref), (1 - at_ref[0], send_ref)):
            span = pl.ds(pl.multiple_of(half * rows, rows), rows)
            copies.append(pltpu.make_async_copy(all_ref.at[place * 2 + high, span], ref.at[k], sems.at[len(copies)]))
            copies[-1].start()
    for copy in copies:
        copy.wait()


def level_kernel(at_ref, mine_ref, other_ref, out_ref):
    for k in range(out_ref.shape[0]):
        core, _, _ = owner_of(at_ref, k)

        @pl.when(core == at_ref[0])
        def _():
            out_ref[k] = mine_ref[k]

        @pl.when(core != at_ref[0])
        def _():
            out_ref[k] = other_ref[k]


def level(at, mine, other):
    return call(level_kernel, (at, mine, other), [SMEM, VMEM, VMEM], VMEM, jax.ShapeDtypeStruct(mine.shape, mine.dtype))


def project_kernel(own, at_ref, gradient_ref, panels_ref, *refs):
    outs, (token_ref, rows_ref, sems) = refs[:-3], refs[-3:]
    size = rows_ref.shape[0] // (2 * RING)
    half = at_ref[0] if own else 1 - at_ref[0]
    copies = []
    for high in range(2):
        for place in range(RING):
            start = pl.multiple_of((place * 4 + high * 2 + half) * size, size)
            target = rows_ref.at[pl.ds(len(copies) * size, size)]
            copies.append(pltpu.make_async_copy(gradient_ref.at[pl.ds(start, size)], target, sems.at[len(copies)]))
            copies[-1].start()
    for i in range(0, len(copies), 4):
        for copy in copies[i : i + 4]:
            copy.wait()
        span = slice(i * size, (i + 4) * size)
        for k, out_ref in enumerate(outs):
            out_ref[span] = jnp.dot(rows_ref[span], panels_ref[k], preferred_element_type=F32)
    token_ref[...] = jnp.zeros_like(token_ref)


def project(at, own, gradient, panels):
    count, width, vec = panels.shape
    rows = gradient.shape[0] // 2
    *outs, token = call(
        functools.partial(project_kernel, own),
        (at, gradient, panels),
        [SMEM, ANY, VMEM],
        [VMEM] * (count + 1),
        [jax.ShapeDtypeStruct((rows, vec), F32)] * count + [TOKEN],
        2 * rows * width * vec * count,
        [pltpu.VMEM((rows, width), BF16), pltpu.SemaphoreType.DMA((2 * RING,))],
    )
    return outs, token


def pool_kernel(count, at_ref, *refs):
    kept, came, keeps = (refs[i * count : (i + 1) * count] for i in range(3))
    send_ref, token_ref = refs[3 * count :]
    rows = keeps[0].shape[0]
    mine = pl.ds(pl.multiple_of(at_ref[1] * rows, rows), rows)
    other = pl.ds(pl.multiple_of((1 - at_ref[1]) * rows, rows), rows)
    for k in range(count):
        keeps[k][...] = kept[k][mine] + came[k][mine]
        send_ref[k] = (kept[k][other] + came[k][other]).astype(BF16)
    token_ref[...] = jnp.zeros_like(token_ref)


def pool(at, kept, came):
    count = len(kept)
    rows, vec = kept[0].shape
    shapes = [jax.ShapeDtypeStruct((rows // 2, vec), F32)] * count + [jax.ShapeDtypeStruct((count, rows // 2, vec), BF16), TOKEN]
    out = call(functools.partial(pool_kernel, count), (at, *kept, *came), [SMEM] + [VMEM] * (2 * count), [VMEM] * (count + 2), shapes)
    return out[:count], out[count], out[count + 1]


def split_kernel(count, at_ref, values_ref, *refs):
    kept, (came_ref, out_ref, below_ref, all_ref) = refs[:count], refs[count:]
    vec = kept[0].shape[1]
    for k in range(count):
        total = (kept[k][...] + came_ref[k].astype(F32)).T
        high = total.astype(BF16)
        out_ref[k, :vec] = high
        out_ref[k, vec:] = (total - high.astype(F32)).astype(BF16)
        values = values_ref[k]
        all_ref[k * vec : (k + 1) * vec] = (values + 0.1 * jnp.mean(values)).T
    size = below_ref.shape[0]
    below_ref[...] = all_ref[pl.ds(pl.multiple_of(at_ref[3] * size, size), size)]


def split(at, values, kept, came, places):
    count = len(kept)
    rows, vec = kept[0].shape
    shapes = [jax.ShapeDtypeStruct((count, 2 * vec, rows), BF16), jax.ShapeDtypeStruct((count * vec // places, vec), F32)]
    specs = [SMEM] + [VMEM] * (2 + count)
    return call(functools.partial(split_kernel, count), (at, values, *kept, came), specs, [VMEM] * 2, shapes, scratch=[pltpu.VMEM((count * vec, vec), F32)])


def offsets():
    order = [0]
    for step in range(1, REACH + 1):
        order.append(-step)
        if step < REACH:
            order.append(step)
    return order


def couple_kernel(at_ref, terms_ref, *refs):
    pieces, (total_ref, own_ref) = refs[:RING], refs[RING:]
    count, rows, vec = pieces[0].shape
    for piece, offset in zip(pieces, offsets()):
        place = (at_ref[2] + offset + RING) & (RING - 1)
        span = pl.ds(pl.multiple_of(place * rows, rows), rows)
        for k in range(count):
            own_ref[k, span] = piece[k]
    for k in range(count):
        both = jnp.dot(terms_ref[k], own_ref[k], preferred_element_type=F32)
        total_ref[k * vec : (k + 1) * vec] = both[:vec] + both[vec:]


def couple(at, terms, pieces):
    count, rows, vec = pieces[0].shape
    shapes = [jax.ShapeDtypeStruct((count * vec, vec), F32), jax.ShapeDtypeStruct((count, RING * rows, vec), BF16)]
    return call(couple_kernel, (at, terms, *pieces), [SMEM] + [VMEM] * (1 + RING), [VMEM, VMEM], shapes, 4 * count * RING * rows * vec * vec)


def spread_kernel(part_ref, out_ref, token_ref):
    total = jnp.sum(part_ref[...], axis=0)
    for j in range(RING):
        out_ref[j] = total
    token_ref[...] = jnp.zeros_like(token_ref)


def spread(parts):
    return call(spread_kernel, (parts,), [VMEM], [VMEM] * 2, [jax.ShapeDtypeStruct((RING,) + parts.shape[1:], F32), TOKEN])


def scale_kernel(parts_ref, below_ref, _, out_ref):
    out_ref[...] = (jnp.sum(parts_ref[...], axis=0) / below_ref[...]).astype(BF16)


def apply_kernel(near, at_ref, own_ref, other_ref, scaled_ref, panels_ref, _, out_ref, block_ref, sems):
    count, rows, _ = own_ref.shape
    size = rows // RING
    high = at_ref[1] if near else 1 - at_ref[1]
    copies = []
    for number, (ref, core) in enumerate(((own_ref, at_ref[0]), (other_ref, 1 - at_ref[0]))):
        total = None
        for k in range(count):
            rotated = lax.dot_general(ref[k], scaled_ref[k], (((1,), (1,)), ((), ())), preferred_element_type=F32)
            term = lax.dot_general(rotated.astype(BF16), panels_ref[k], (((1,), (1,)), ((), ())), preferred_element_type=F32)
            total = term if total is None else total + term
        block_ref[number] = total.astype(BF16)
        for place in range(RING):
            target = pl.multiple_of((place * 4 + high * 2 + core) * size, size)
            source = block_ref.at[number, pl.ds(place * size, size)]
            copies.append(pltpu.make_async_copy(source, out_ref.at[pl.ds(target, size)], sems.at[len(copies)]))
            copies[-1].start()
    for copy in copies:
        copy.wait()


def apply(near, at, own, other, scaled, panels, into):
    count, rows, vec = own.shape
    width = panels.shape[1]
    return pl.pallas_call(
        functools.partial(apply_kernel, near),
        in_specs=[SMEM, VMEM, VMEM, VMEM, VMEM, ANY],
        out_specs=ANY,
        out_shape=jax.ShapeDtypeStruct((4 * rows, width), BF16),
        input_output_aliases={} if near else {5: 0},
        scratch_shapes=[pltpu.VMEM((2, rows, width), BF16), pltpu.SemaphoreType.DMA((2 * RING,))],
        compiler_params=pltpu.CompilerParams(vmem_limit_bytes=24 * MIB),
        cost_estimate=pl.CostEstimate(flops=4 * count * rows * vec * (vec + width), bytes_accessed=4 * rows * width, transcendentals=0),
    )(at, own, other, scaled, panels, into)


def body(gradient, in_panels, out_pool, eigenvalues, owners):
    core, high, here = (lax.axis_index(a) for a in ("core", "yh", "z"))
    at = jnp.concatenate([jnp.stack([core, high, here, lax.axis_index(PLANE)]).astype(jnp.int32), owners])
    count, _, vec = in_panels.shape
    size = out_pool.shape[1] // (4 * RING)
    piece = jax.ShapeDtypeStruct((count, size, vec), BF16)

    with jax.named_scope("scatter"):
        every = lax.all_to_all(out_pool.reshape(2 * RING, 2 * size, vec), ("z", "yh"), 0, 0)

    with jax.named_scope("projection"):
        sent, _ = project(at, False, gradient, in_panels)
        kept, one = project(at, True, gradient, in_panels)
        kept, sent, two = pool(at, kept, [swap(x, "core") for x in sent])
        terms, below = split(at, eigenvalues, kept, swap(sent, "yh"), 32)

    with jax.named_scope("gather"):
        scratch = [pltpu.SemaphoreType.DMA((2 * count,))]
        specs = [SMEM, ANY, ANY, ANY]
        mine, send = call(pick_kernel, (at, every, one, two), specs, [VMEM] * 2, [piece] * 2, scratch=scratch)
        mine = level(at, mine, swap(send, "core"))
        pieces = [mine]
        up = down = mine
        for _ in range(1, REACH):
            up, down = shift(up, 1), shift(down, -1)
            pieces += [up, down]
        pieces.append(shift(up, 1))

    with jax.named_scope("coupling"):
        part, own = couple(at, terms, pieces)
        part, token = spread(lax.all_to_all(part.reshape(32, -1, vec), PLANE, 0, 0))
        own, token = lax.optimization_barrier((own, token))
        far, other = swap(own, "yh"), swap(own, "core")
        part = lax.all_to_all(part, "z", 0, 0)
        scaled = call(scale_kernel, (part, below, token), [VMEM, VMEM, ANY], VMEM, jax.ShapeDtypeStruct(part.shape[1:], BF16))
        copies = jnp.broadcast_to(scaled[None], (32,) + scaled.shape)
        scaled = lax.all_to_all(copies, PLANE, 0, 0).reshape(count, vec, vec)

    with jax.named_scope("output"):
        far, token = lax.optimization_barrier((far, scaled[0, :16, :128]))
        out = apply(True, at, own, other, scaled, in_panels, token)
        return apply(False, at, far, swap(far, "core"), scaled, in_panels, out)


def solution(mesh):
    fine = Mesh(mesh.devices.reshape(2, 4, 2, 8, 2), ROW + COL)
    return jax.shard_map(
        body,
        mesh=fine,
        in_specs=(P(ROW, COL), P(None, COL, None), P(COL, ROW, None), P(), P()),
        out_specs=P(ROW, COL),
        check_vma=False,
    )
```

time: 139 us -> 130 us (0.935)
  blocking collectives: 54.5 us -> 23.2 us
  starting transfers between devices: 21.3 us -> 37.6 us
  Pallas kernels: 22 us -> 28.1 us
    all_to_all x2 -> x0, blocking collectives: 27.7 us -> none  [the longest x1 15.6 us: body(): scaled = lax.all_to_all(copies, PLANE, 0, 0).reshape(count, vec, vec)]
    all_to_all x1 -> x3, starting transfers between devices: 9.01 us -> 19.3 us  [the longest x1 11.7 us: body(): lax.all_to_all(out_pool.reshape(2 * RING, 2 * size, vec), ('z', 'yh'), 0, 0)]
    pallas_call x0 -> x2, Pallas kernels: none -> 8.62 us  [apply(): pl.pallas_call(functools.partial(apply_kernel, near), in_specs=[SMEM, VME...]
    all_to_all x1 -> x3, waiting for transfers between devices: 14.3 us -> 21.7 us  [the longest x1 10.3 us: body(): part = lax.all_to_all(part, 'z', 0, 0)]
    ppermute x4 -> x8, starting transfers between devices: 4.3 us -> 10.2 us  [swap(): return lax.ppermute(x, axis, [(0, 1), (1, 0)])]
    ppermute x4 -> x8, waiting for transfers between devices: 6.03 us -> 0.96 us  [swap(): return lax.ppermute(x, axis, [(0, 1), (1, 0)])]
    all_to_all x1, blocking collectives: 26.8 us -> 23.2 us  [body(): part, token = spread(lax.all_to_all(part.reshape(32, -1, vec), PLANE, 0, 0))]
    ppermute x7, waiting for transfers between devices: 10.5 us -> 7 us  [shift(): return lax.ppermute(x, 'z', [(i, (i + by) % RING) for i in range(RING)])]
  transfers between devices with their start and end apart: 12 -> 18, of which waited for: 7 -> 8; matrix products, arithmetic and copies ran while one was open for 1% -> 1% of each run, Pallas kernels for 9% -> 17%
where the time goes in v7:
time: 130 us
  starting transfers between devices  37.6 us (29%)
  waiting for transfers between devices  29.6 us (23%)
  Pallas kernels  28.1 us (22%)
  blocking collectives  23.2 us (18%)
  local copies, waits for them, and re-layouts  10.6 us (8%)
    all_to_all x1, blocking collectives, body(): part, token = spread(lax.all_to_all(part.reshape(32, -1, vec), PLANE, 0, 0))  23.2 us
    pallas_call x9, Pallas kernels, call(): pl.pallas_call(kernel, in_specs=in_specs, out_specs=out_specs, out_shape=...  19.4 us
    all_to_all x1, starting transfers between devices, body(): lax.all_to_all(out_pool.reshape(2 * RING, 2 * size, vec), ('z', 'yh'), 0, 0)  11.7 us
    all_to_all x1, waiting for transfers between devices, body(): part = lax.all_to_all(part, 'z', 0, 0)  10.3 us
    ppermute x8, starting transfers between devices, swap(): return lax.ppermute(x, axis, [(0, 1), (1, 0)])  10.2 us
    all_to_all x1, waiting for transfers between devices, body(): scaled = lax.all_to_all(copies, PLANE, 0, 0).reshape(count, vec, vec)  9.98 us
    unnamed x24, local copies, waits for them, and re-layouts  9.07 us
    pallas_call x2, Pallas kernels, apply(): pl.pallas_call(functools.partial(apply_kernel, near), in_specs=[SMEM, VME...  8.62 us
  transfers between devices with their start and end apart: 18, of which 8 were waited for; matrix products, arithmetic and copies ran while one was open for 1% of the time, Pallas kernels for 17%

profile of v7, /device:TPU:1, one launch (start us, length us, event | category | flops | bytes accessed | tf_op | source)
XLA Modules:
  0.0 129.5 jit_solution(6917251833390978994)
XLA Ops:
  0.0 11.7 %all-to-all-start = ((bf16[16,128,256]{2,1,0:T(8,128)(2,1)}), bf16[16,128,256]{2,1,0:T(8,128)(2,1)S(1)}, u32[]{:S(2)}, u32[]{:S(2)}) async-start(bf16[16,128,256]{2,1,0:T(8,128)(2,1)} %bitcast.13), calls=%async_computation | async-start | bytes 2097152 | tf_op jit(solution)/shard_map/scatter/all_to_all | solution.py:246
  11.8 0.7 concatenate.3.at_ref
  12.5 1.4 %copy-done = bf16[3,1024,256]{2,1,0:T(8,128)(2,1)S(1)} copy-done((bf16[3,1024,256]{2,1,0:T(8,128)(2,1)S(1)}, bf16[3,1024,256]{2,1,0:T(8,128)(2,1)}, u32[]{:S(2)}) %copy-start) | copy-done | bytes 1572888
  13.9 2.2 %copy-done.11 = bf16[2048,1024]{1,0:T(8,128)(2,1)S(1)} copy-done((bf16[2048,1024]{1,0:T(8,128)(2,1)S(1)}, bf16[2048,1024]{1,0:T(8,128)(2,1)}, u32[]{:S(2)}) %copy-start.11) | copy-done | bytes 4194328
  16.1 6.7 %projection.5 = (f32[1024,256]{1,0:T(8,128)S(1)}, f32[1024,256]{1,0:T(8,128)S(1)}, f32[1024,256]{1,0:T(8,128)S(1)}, f32[8,128]{1,0:T(8,128)}) custom-call(s32[7]{0:T(128)S(1)} %concatenate.3.at_ref, bf16[2048,1024]{1,0:T(8,128)(2,1)S(1)} %copy-done.11, bf16[3,1024,256]{2,1,0:T(8,128)(2,1)S(1)} %copy-done), custom_call_target="tpu_custom_call" | custom-call | flops 1610612736 | bytes 5767196 | tf_op jit(solution)/shard_map/projection/pallas_call | solution.py:36
  22.8 1.0 collective-permute-start
  23.8 0.1 collective-permute-start.1
  23.9 0.4 collective-permute-start.2
  24.3 6.3 %projection.4 = (f32[1024,256]{1,0:T(8,128)S(1)}, f32[1024,256]{1,0:T(8,128)S(1)}, f32[1024,256]{1,0:T(8,128)S(1)}, f32[8,128]{1,0:T(8,128)S(1)}) custom-call(s32[7]{0:T(128)S(1)} %concatenate.3.at_ref, bf16[2048,1024]{1,0:T(8,128)(2,1)S(1)} %copy-done.11, bf16[3,1024,256]{2,1,0:T(8,128)(2,1)S(1)} %copy-done), custom_call_target="tpu_custom_call" | custom-call | flops 1610612736 | bytes 5767196 | tf_op jit(solution)/shard_map/projection/pallas_call | solution.py:36
  30.7 0.0 copy-start.2
  30.7 0.0 collective-permute-done.refs_3_
  30.7 1.7 %projection.6 = (f32[512,256]{1,0:T(8,128)S(1)}, f32[512,256]{1,0:T(8,128)S(1)}, f32[512,256]{1,0:T(8,128)S(1)}, bf16[3,512,256]{2,1,0:T(8,128)(2,1)}, f32[8,128]{1,0:T(8,128)S(1)}) custom-call(s32[7]{0:T(128)S(1)} %concatenate.3.at_ref, f32[1024,256]{1,0:T(8,128)S(1)} %get-tuple-element.29.refs_0_, f32[1024,256]{1,0:T(8,128)S(1)} %get-tuple-element.30.refs_1_, ...), custom_call_target="tpu_custom_call" | custom-call | bytes 6291484 | tf_op jit(solution)/shard_map/projection/pallas_call | solution.py:36
  32.4 0.8 copy-done.5
  33.2 0.8 copy-done.7
  34.0 3.2 %collective-permute-start.3 = (bf16[3,512,256]{2,1,0:T(8,128)(2,1)}, bf16[3,512,256]{2,1,0:T(8,128)(2,1)S(1)}, u32[]{:S(2)}, u32[]{:S(2)}) collective-permute-start(bf16[3,512,256]{2,1,0:T(8,128)(2,1)} %get-tuple-element.38), channel_id=1, source_target_pairs={{0,16},{16,0},{1,17},{17,1},{2,18},{18,2},{3,19},{19,3},{4,20},{20... | collective-permute-start | bytes 2359304 | tf_op jit(solution)/shard_map/projection/ppermute | solution.py:27
  37.2 1.4 %all-to-all-done.all_ref = bf16[16,128,256]{2,1,0:T(8,128)(2,1)S(1)} async-done(((bf16[16,128,256]{2,1,0:T(8,128)(2,1)}), bf16[16,128,256]{2,1,0:T(8,128)(2,1)S(1)}, u32[]{:S(2)}, u32[]{:S(2)}) %all-to-all-start) | async-done | bytes 1048608 | tf_op jit(solution)/shard_map/scatter/all_to_all | solution.py:246
  38.6 0.9 gather.2
  39.5 4.4 %collective-permute-start.4 = (bf16[3,64,256]{2,1,0:T(8,128)(2,1)S(1)}, bf16[3,64,256]{2,1,0:T(8,128)(2,1)S(1)}, u32[]{:S(2)}, u32[]{:S(2)}) collective-permute-start(bf16[3,64,256]{2,1,0:T(8,128)(2,1)S(1)} %get-tuple-element.43), channel_id=1, source_target_pairs={{0,1},{1,0},{2,3},{3,2},{4,5},{5,4},{6,7},{7,6},{8,9},{9,8},{10,11... | collective-permute-start | bytes 294920 | tf_op jit(solution)/shard_map/gather/ppermute | solution.py:27
  43.9 0.9 collective-permute-done.4.other_ref
  44.8 0.6 gather.3.refs_0_
  45.4 0.1 collective-permute-start.5
  45.5 2.7 %collective-permute-start.6 = (bf16[3,64,256]{2,1,0:T(8,128)(2,1)S(1)}, bf16[3,64,256]{2,1,0:T(8,128)(2,1)S(1)}, u32[]{:S(2)}, u32[]{:S(2)}) collective-permute-start(bf16[3,64,256]{2,1,0:T(8,128)(2,1)S(1)} %gather.3.refs_0_), channel_id=1, source_target_pairs={{0,14},{2,0},{4,2},{6,4},{8,6},{10,8},{12,10},{14,12},{1,15},{3,1}... | collective-permute-start | bytes 294920 | tf_op jit(solution)/shard_map/gather/ppermute | solution.py:31
  48.2 2.6 %collective-permute-done.5.refs_1_ = bf16[3,64,256]{2,1,0:T(8,128)(2,1)S(1)} collective-permute-done((bf16[3,64,256]{2,1,0:T(8,128)(2,1)S(1)}, bf16[3,64,256]{2,1,0:T(8,128)(2,1)S(1)}, u32[]{:S(2)}, u32[]{:S(2)}) %collective-permute-start.5) | collective-permute-done | bytes 98336 | tf_op jit(solution)/shard_map/gather/ppermute | solution.py:31
  50.7 0.0 collective-permute-start.7
  50.7 2.7 %collective-permute-start.8 = (bf16[3,64,256]{2,1,0:T(8,128)(2,1)S(1)}, bf16[3,64,256]{2,1,0:T(8,128)(2,1)S(1)}, u32[]{:S(2)}, u32[]{:S(2)}) collective-permute-start(bf16[3,64,256]{2,1,0:T(8,128)(2,1)S(1)} %collective-permute-done.6.refs_2_), channel_id=1, source_target_pairs={{0,14},{2,0},{4,2},{6,4},{8,6},{10,8},{12,10},{14,12},{1,15},{3,1}... | collective-permute-start | bytes 294920 | tf_op jit(solution)/shard_map/gather/ppermute | solution.py:31
  53.4 2.3 %collective-permute-done.7.refs_3_ = bf16[3,64,256]{2,1,0:T(8,128)(2,1)S(1)} collective-permute-done((bf16[3,64,256]{2,1,0:T(8,128)(2,1)S(1)}, bf16[3,64,256]{2,1,0:T(8,128)(2,1)S(1)}, u32[]{:S(2)}, u32[]{:S(2)}) %collective-permute-start.7) | collective-permute-done | bytes 98336 | tf_op jit(solution)/shard_map/gather/ppermute | solution.py:31
  55.7 2.7 %collective-permute-start.10 = (bf16[3,64,256]{2,1,0:T(8,128)(2,1)S(1)}, bf16[3,64,256]{2,1,0:T(8,128)(2,1)S(1)}, u32[]{:S(2)}, u32[]{:S(2)}) collective-permute-start(bf16[3,64,256]{2,1,0:T(8,128)(2,1)S(1)} %collective-permute-done.8.refs_4_), channel_id=1, source_target_pairs={{0,14},{2,0},{4,2},{6,4},{8,6},{10,8},{12,10},{14,12},{1,15},{3,1}... | collective-permute-start | bytes 294920 | tf_op jit(solution)/shard_map/gather/ppermute | solution.py:31
  58.4 2.0 %collective-permute-done.9.refs_5_ = bf16[3,64,256]{2,1,0:T(8,128)(2,1)S(1)} collective-permute-done((bf16[3,64,256]{2,1,0:T(8,128)(2,1)S(1)}, bf16[3,64,256]{2,1,0:T(8,128)(2,1)S(1)}, u32[]{:S(2)}, u32[]{:S(2)}) %collective-permute-start.9) | collective-permute-done | bytes 98336 | tf_op jit(solution)/shard_map/gather/ppermute | solution.py:31
  60.4 0.0 collective-permute-start.11
  60.4 1.0 copy-done.4
  61.4 1.0 copy-done.6
  62.5 1.0 copy-done.8
  63.5 1.4 %projection.7 = (bf16[3,512,512]{2,1,0:T(8,128)(2,1)S(1)}, f32[24,256]{1,0:T(8,128)S(1)}) custom-call(s32[7]{0:T(128)S(1)} %concatenate.3.at_ref, f32[3,256,256]{2,1,0:T(8,128)S(1)} %copy-done.2, f32[512,256]{1,0:T(8,128)S(1)} %copy-done.4, f32[512,256]{1,0:T(8,128)S(1)} %copy-done.6, f32[512,256]{1,0:T(8,128)S(1)} %copy-done.8, ...), custom_call_target="tpu_custom_call" | custom-call | bytes 3145756 | tf_op jit(solution)/shard_map/projection/pallas_call | solution.py:36
  64.9 0.1 collective-permute-done.11.refs_7_
  65.1 1.1 coupling.3
  66.2 23.2 %all_to_all.20.part_ref = f32[32,24,256]{2,1,0:T(8,128)S(1)} all-to-all(f32[32,24,256]{2,1,0:T(8,128)S(1)} %bitcast.12), channel_id=1, replica_groups=mesh['yl'=2,'x'=4,'yh'=2,'z'=8,'core'=2] {'core','yl','x','yh'}, dimensions={0} | all-to-all | bytes 1572864 | tf_op jit(solution)/shard_map/coupling/all_to_all | solution.py:268
  89.4 0.7 coupling.4
  90.2 3.4 %all-to-all-start.2 = ((f32[8,24,256]{2,1,0:T(8,128)}), f32[8,24,256]{2,1,0:T(8,128)S(1)}, u32[]{:S(2)}, u32[]{:S(2)}) async-start(f32[8,24,256]{2,1,0:T(8,128)} %get-tuple-element.48), calls=%async_computation.2 | async-start | bytes 393216 | tf_op jit(solution)/shard_map/coupling/all_to_all | solution.py:271
  93.6 0.5 collective-permute-start.12
  94.1 10.3 %all-to-all-done.2.parts_ref = f32[8,24,256]{2,1,0:T(8,128)S(1)} async-done(((f32[8,24,256]{2,1,0:T(8,128)}), f32[8,24,256]{2,1,0:T(8,128)S(1)}, u32[]{:S(2)}, u32[]{:S(2)}) %all-to-all-start.2) | async-done | bytes 196640 | tf_op jit(solution)/shard_map/coupling/all_to_all | solution.py:271
  104.4 0.7 copy-done.10
  105.1 0.8 broadcast_in_dim.2
  105.9 4.2 %all-to-all-start.3 = ((bf16[32,24,256]{2,1,0:T(8,128)(2,1)}), bf16[32,24,256]{2,1,0:T(8,128)(2,1)S(1)}, u32[]{:S(2)}, u32[]{:S(2)}) async-start(bf16[32,24,256]{2,1,0:T(8,128)(2,1)} %broadcast_in_dim.2), calls=%async_computation.3 | async-start | bytes 786432 | tf_op jit(solution)/shard_map/coupling/all_to_all | solution.py:274
  110.1 0.3 collective-permute-start.14
  110.4 10.0 %all-to-all-done.3 = bf16[32,24,256]{2,1,0:T(8,128)(2,1)S(1)} async-done(((bf16[32,24,256]{2,1,0:T(8,128)(2,1)}), bf16[32,24,256]{2,1,0:T(8,128)(2,1)S(1)}, u32[]{:S(2)}, u32[]{:S(2)}) %all-to-all-start.3) | async-done | bytes 393248 | tf_op jit(solution)/shard_map/coupling/all_to_all | solution.py:274
  120.4 0.3 collective-permute-start.13
  120.7 4.6 %output.2._ = bf16[2048,1024]{1,0:T(8,128)(2,1)} custom-call(s32[7]{0:T(128)S(1)} %concatenate.3.at_ref, bf16[3,512,256]{2,1,0:T(8,128)(2,1)S(1)} %get-tuple-element.47.own_ref, bf16[3,512,256]{2,1,0:T(8,128)(2,1)} %collective-permute-done.14.other_ref, bf16[3,256,256]{2,1,0:T(8,128)(2,1)S(1)} %bitcast.10, bf16[3,1024,256]{2,1,0:T(8,128)(2,1)S(1)} %copy-done.1, ...), custom_call_target="tpu_custom_call" | custom-call | flops 2013265920 | bytes 2097152 | tf_op jit(solution)/shard_map/output/pallas_call | solution.py:226
  125.3 4.0 %output.3 = bf16[2048,1024]{1,0:T(8,128)(2,1)} custom-call(s32[7]{0:T(128)S(1)} %concatenate.3.at_ref, bf16[3,512,256]{2,1,0:T(8,128)(2,1)S(1)} %collective-permute-done.12.own_ref, bf16[3,512,256]{2,1,0:T(8,128)(2,1)S(1)} %collective-permute-done.13.other_ref, bf16[3,256,256]{2,1,0:T(8,128)(2,1)S(1)} %bitcast.11, ...), custom_call_target="tpu_custom_call", output_to_operand_aliasing={{}: (5, {})} | custom-call | flops 2013265920 | bytes 2097152 | tf_op jit(solution)/shard_map/output/pallas_call | solution.py:226
  (27 shorter events, 0.1 us)
Async XLA Ops:
  0.0 38.6 %all-to-all-start = ((bf16[16,128,256]{2,1,0:T(8,128)(2,1)}), bf16[16,128,256]{2,1,0:T(8,128)(2,1)S(1)}, u32[]{:S(2)}, u32[]{:S(2)}) async-start(bf16[16,128,256]{2,1,0:T(8,128)(2,1)} %bitcast.13), calls=%async_computation | async-start | bytes 2097152 | tf_op jit(solution)/shard_map/scatter/all_to_all | solution.py:246
  12.5 1.4 %copy-start = (bf16[3,1024,256]{2,1,0:T(8,128)(2,1)S(1)}, bf16[3,1024,256]{2,1,0:T(8,128)(2,1)}, u32[]{:S(2)}) copy-start(bf16[3,1024,256]{2,1,0:T(8,128)(2,1)} %panels_ref.7) | copy-start | bytes 4718596
  13.9 2.2 %copy-start.11 = (bf16[2048,1024]{1,0:T(8,128)(2,1)S(1)}, bf16[2048,1024]{1,0:T(8,128)(2,1)}, u32[]{:S(2)}) copy-start(bf16[2048,1024]{1,0:T(8,128)(2,1)} %gradient_ref.3) | copy-start | bytes 12582916
  22.8 7.9 %collective-permute-start = (f32[1024,256]{1,0:T(8,128)S(1)}, f32[1024,256]{1,0:T(8,128)S(1)}, u32[]{:S(2)}, u32[]{:S(2)}) collective-permute-start(f32[1024,256]{1,0:T(8,128)S(1)} %get-tuple-element.32), channel_id=1, source_target_pairs={{0,1},{1,0},{2,3},{3,2},{4,5},{5,4},{6,7},{7,6},{8,9},{9,8},{10,11... | collective-permute-start | bytes 3145736 | tf_op jit(solution)/shard_map/projection/ppermute | solution.py:27
  23.8 6.9 %collective-permute-start.1 = (f32[1024,256]{1,0:T(8,128)S(1)}, f32[1024,256]{1,0:T(8,128)S(1)}, u32[]{:S(2)}, u32[]{:S(2)}) collective-permute-start(f32[1024,256]{1,0:T(8,128)S(1)} %get-tuple-element.33), channel_id=1, source_target_pairs={{0,1},{1,0},{2,3},{3,2},{4,5},{5,4},{6,7},{7,6},{8,9},{9,8},{10,11... | collective-permute-start | bytes 3145736 | tf_op jit(solution)/shard_map/projection/ppermute | solution.py:27
  23.9 6.8 %collective-permute-start.2 = (f32[1024,256]{1,0:T(8,128)S(1)}, f32[1024,256]{1,0:T(8,128)S(1)}, u32[]{:S(2)}, u32[]{:S(2)}) collective-permute-start(f32[1024,256]{1,0:T(8,128)S(1)} %get-tuple-element.34), channel_id=1, source_target_pairs={{0,1},{1,0},{2,3},{3,2},{4,5},{5,4},{6,7},{7,6},{8,9},{9,8},{10,11... | collective-permute-start | bytes 3145736 | tf_op jit(solution)/shard_map/projection/ppermute | solution.py:27
  30.7 29.7 %copy-start.2 = (f32[3,256,256]{2,1,0:T(8,128)S(1)}, f32[3,256,256]{2,1,0:T(8,128)}, u32[]{:S(2)}) copy-start(f32[3,256,256]{2,1,0:T(8,128)} %values_ref.1) | copy-start | bytes 2359300
  32.4 0.8 copy-start.5
  33.2 0.8 copy-start.7
  34.0 26.4 %copy-start.3 = (f32[512,256]{1,0:T(8,128)}, f32[512,256]{1,0:T(8,128)S(1)}, u32[]{:S(2)}) copy-start(f32[512,256]{1,0:T(8,128)S(1)} %get-tuple-element.35.refs_0_) | copy-start | bytes 1572868
  34.0 26.4 %collective-permute-start.3 = (bf16[3,512,256]{2,1,0:T(8,128)(2,1)}, bf16[3,512,256]{2,1,0:T(8,128)(2,1)S(1)}, u32[]{:S(2)}, u32[]{:S(2)}) collective-permute-start(bf16[3,512,256]{2,1,0:T(8,128)(2,1)} %get-tuple-element.38), channel_id=1, source_target_pairs={{0,16},{16,0},{1,17},{17,1},{2,18},{18,2},{3,19},{19,3},{4,20},{20... | collective-permute-start | bytes 2359304 | tf_op jit(solution)/shard_map/projection/ppermute | solution.py:27
  39.5 5.3 %collective-permute-start.4 = (bf16[3,64,256]{2,1,0:T(8,128)(2,1)S(1)}, bf16[3,64,256]{2,1,0:T(8,128)(2,1)S(1)}, u32[]{:S(2)}, u32[]{:S(2)}) collective-permute-start(bf16[3,64,256]{2,1,0:T(8,128)(2,1)S(1)} %get-tuple-element.43), channel_id=1, source_target_pairs={{0,1},{1,0},{2,3},{3,2},{4,5},{5,4},{6,7},{7,6},{8,9},{9,8},{10,11... | collective-permute-start | bytes 294920 | tf_op jit(solution)/shard_map/gather/ppermute | solution.py:27
  45.4 5.3 %collective-permute-start.5 = (bf16[3,64,256]{2,1,0:T(8,128)(2,1)S(1)}, bf16[3,64,256]{2,1,0:T(8,128)(2,1)S(1)}, u32[]{:S(2)}, u32[]{:S(2)}) collective-permute-start(bf16[3,64,256]{2,1,0:T(8,128)(2,1)S(1)} %gather.3.refs_0_), channel_id=1, source_target_pairs={{0,2},{2,4},{4,6},{6,8},{8,10},{10,12},{12,14},{14,0},{1,3},{3,5},... | collective-permute-start | bytes 294920 | tf_op jit(solution)/shard_map/gather/ppermute | solution.py:31
  45.5 5.2 %collective-permute-start.6 = (bf16[3,64,256]{2,1,0:T(8,128)(2,1)S(1)}, bf16[3,64,256]{2,1,0:T(8,128)(2,1)S(1)}, u32[]{:S(2)}, u32[]{:S(2)}) collective-permute-start(bf16[3,64,256]{2,1,0:T(8,128)(2,1)S(1)} %gather.3.refs_0_), channel_id=1, source_target_pairs={{0,14},{2,0},{4,2},{6,4},{8,6},{10,8},{12,10},{14,12},{1,15},{3,1}... | collective-permute-start | bytes 294920 | tf_op jit(solution)/shard_map/gather/ppermute | solution.py:31
  50.7 5.0 %collective-permute-start.7 = (bf16[3,64,256]{2,1,0:T(8,128)(2,1)S(1)}, bf16[3,64,256]{2,1,0:T(8,128)(2,1)S(1)}, u32[]{:S(2)}, u32[]{:S(2)}) collective-permute-start(bf16[3,64,256]{2,1,0:T(8,128)(2,1)S(1)} %collective-permute-done.5.refs_1_), channel_id=1, source_target_pairs={{0,2},{2,4},{4,6},{6,8},{8,10},{10,12},{12,14},{14,0},{1,3},{3,5},... | collective-permute-start | bytes 294920 | tf_op jit(solution)/shard_map/gather/ppermute | solution.py:31
  50.7 5.0 %collective-permute-start.8 = (bf16[3,64,256]{2,1,0:T(8,128)(2,1)S(1)}, bf16[3,64,256]{2,1,0:T(8,128)(2,1)S(1)}, u32[]{:S(2)}, u32[]{:S(2)}) collective-permute-start(bf16[3,64,256]{2,1,0:T(8,128)(2,1)S(1)} %collective-permute-done.6.refs_2_), channel_id=1, source_target_pairs={{0,14},{2,0},{4,2},{6,4},{8,6},{10,8},{12,10},{14,12},{1,15},{3,1}... | collective-permute-start | bytes 294920 | tf_op jit(solution)/shard_map/gather/ppermute | solution.py:31
  55.7 4.7 %collective-permute-start.9 = (bf16[3,64,256]{2,1,0:T(8,128)(2,1)S(1)}, bf16[3,64,256]{2,1,0:T(8,128)(2,1)S(1)}, u32[]{:S(2)}, u32[]{:S(2)}) collective-permute-start(bf16[3,64,256]{2,1,0:T(8,128)(2,1)S(1)} %collective-permute-done.7.refs_3_), channel_id=1, source_target_pairs={{0,2},{2,4},{4,6},{6,8},{8,10},{10,12},{12,14},{14,0},{1,3},{3,5},... | collective-permute-start | bytes 294920 | tf_op jit(solution)/shard_map/gather/ppermute | solution.py:31
  55.7 9.2 %collective-permute-start.10 = (bf16[3,64,256]{2,1,0:T(8,128)(2,1)S(1)}, bf16[3,64,256]{2,1,0:T(8,128)(2,1)S(1)}, u32[]{:S(2)}, u32[]{:S(2)}) collective-permute-start(bf16[3,64,256]{2,1,0:T(8,128)(2,1)S(1)} %collective-permute-done.8.refs_4_), channel_id=1, source_target_pairs={{0,14},{2,0},{4,2},{6,4},{8,6},{10,8},{12,10},{14,12},{1,15},{3,1}... | collective-permute-start | bytes 294920 | tf_op jit(solution)/shard_map/gather/ppermute | solution.py:31
  60.4 4.7 %collective-permute-start.11 = (bf16[3,64,256]{2,1,0:T(8,128)(2,1)S(1)}, bf16[3,64,256]{2,1,0:T(8,128)(2,1)S(1)}, u32[]{:S(2)}, u32[]{:S(2)}) collective-permute-start(bf16[3,64,256]{2,1,0:T(8,128)(2,1)S(1)} %collective-permute-done.9.refs_5_), channel_id=1, source_target_pairs={{0,2},{2,4},{4,6},{6,8},{8,10},{10,12},{12,14},{14,0},{1,3},{3,5},... | collective-permute-start | bytes 294920 | tf_op jit(solution)/shard_map/gather/ppermute | solution.py:31
  60.4 1.0 copy-start.4
  61.4 1.0 copy-start.6
  62.5 1.0 copy-start.8
  63.5 57.2 %copy-start.1 = (bf16[3,1024,256]{2,1,0:T(8,128)(2,1)S(1)}, bf16[3,1024,256]{2,1,0:T(8,128)(2,1)}, u32[]{:S(2)}) copy-start(bf16[3,1024,256]{2,1,0:T(8,128)(2,1)} %panels_ref.7) | copy-start | bytes 4718596
  64.9 25.3 %copy-start.9 = (f32[24,256]{1,0:T(8,128)}, f32[24,256]{1,0:T(8,128)S(1)}, u32[]{:S(2)}) copy-start(f32[24,256]{1,0:T(8,128)S(1)} %get-tuple-element.49.below_ref) | copy-start | bytes 73732
  90.2 14.2 %all-to-all-start.2 = ((f32[8,24,256]{2,1,0:T(8,128)}), f32[8,24,256]{2,1,0:T(8,128)S(1)}, u32[]{:S(2)}, u32[]{:S(2)}) async-start(f32[8,24,256]{2,1,0:T(8,128)} %get-tuple-element.48), calls=%async_computation.2 | async-start | bytes 393216 | tf_op jit(solution)/shard_map/coupling/all_to_all | solution.py:271
  93.6 26.8 %collective-permute-start.12 = (bf16[3,512,256]{2,1,0:T(8,128)(2,1)S(1)}, bf16[3,512,256]{2,1,0:T(8,128)(2,1)S(1)}, u32[]{:S(2)}, u32[]{:S(2)}) collective-permute-start(bf16[3,512,256]{2,1,0:T(8,128)(2,1)S(1)} %get-tuple-element.47.own_ref), channel_id=1, source_target_pairs={{0,16},{16,0},{1,17},{17,1},{2,18},{18,2},{3,19},{19,3},{4,20},{20... | collective-permute-start | bytes 2359304 | tf_op jit(solution)/shard_map/coupling/ppermute | solution.py:27
  104.4 0.7 copy-start.10
  105.9 14.5 %all-to-all-start.3 = ((bf16[32,24,256]{2,1,0:T(8,128)(2,1)}), bf16[32,24,256]{2,1,0:T(8,128)(2,1)S(1)}, u32[]{:S(2)}, u32[]{:S(2)}) async-start(bf16[32,24,256]{2,1,0:T(8,128)(2,1)} %broadcast_in_dim.2), calls=%async_computation.3 | async-start | bytes 786432 | tf_op jit(solution)/shard_map/coupling/all_to_all | solution.py:274
  110.1 10.6 %collective-permute-start.14 = (bf16[3,512,256]{2,1,0:T(8,128)(2,1)S(1)}, bf16[3,512,256]{2,1,0:T(8,128)(2,1)}, u32[]{:S(2)}, u32[]{:S(2)}) collective-permute-start(bf16[3,512,256]{2,1,0:T(8,128)(2,1)S(1)} %get-tuple-element.47.own_ref), channel_id=1, source_target_pairs={{0,1},{1,0},{2,3},{3,2},{4,5},{5,4},{6,7},{7,6},{8,9},{9,8},{10,11... | collective-permute-start | bytes 2359304 | tf_op jit(solution)/shard_map/coupling/ppermute | solution.py:27
  120.4 4.9 %collective-permute-start.13 = (bf16[3,512,256]{2,1,0:T(8,128)(2,1)S(1)}, bf16[3,512,256]{2,1,0:T(8,128)(2,1)S(1)}, u32[]{:S(2)}, u32[]{:S(2)}) collective-permute-start(bf16[3,512,256]{2,1,0:T(8,128)(2,1)S(1)} %collective-permute-done.12.own_ref), channel_id=1, source_target_pairs={{0,1},{1,0},{2,3},{3,2},{4,5},{5,4},{6,7},{7,6},{8,9},{9,8},{10,11... | collective-permute-start | bytes 2359304 | tf_op jit(solution)/shard_map/output/ppermute | solution.py:27

commit v8 on v7

--- a/solution.py
+++ b/solution.py
@@ -115,13 +115,13 @@
 
 
 def pool_kernel(count, at_ref, *refs):
-    kept, came, keeps = (refs[i * count : (i + 1) * count] for i in range(3))
-    send_ref, token_ref = refs[3 * count :]
-    rows = keeps[0].shape[0]
+    kept, came = refs[:count], refs[count : 2 * count]
+    keep_ref, send_ref, token_ref = refs[2 * count :]
+    rows = keep_ref.shape[1]
     mine = pl.ds(pl.multiple_of(at_ref[1] * rows, rows), rows)
     other = pl.ds(pl.multiple_of((1 - at_ref[1]) * rows, rows), rows)
     for k in range(count):
-        keeps[k][...] = kept[k][mine] + came[k][mine]
+        keep_ref[k] = kept[k][mine] + came[k][mine]
         send_ref[k] = (kept[k][other] + came[k][other]).astype(BF16)
     token_ref[...] = jnp.zeros_like(token_ref)
 
@@ -129,16 +129,15 @@
 def pool(at, kept, came):
     count = len(kept)
     rows, vec = kept[0].shape
-    shapes = [jax.ShapeDtypeStruct((rows // 2, vec), F32)] * count + [jax.ShapeDtypeStruct((count, rows // 2, vec), BF16), TOKEN]
-    out = call(functools.partial(pool_kernel, count), (at, *kept, *came), [SMEM] + [VMEM] * (2 * count), [VMEM] * (count + 2), shapes)
-    return out[:count], out[count], out[count + 1]
-
-
-def split_kernel(count, at_ref, values_ref, *refs):
-    kept, (came_ref, out_ref, below_ref, all_ref) = refs[:count], refs[count:]
-    vec = kept[0].shape[1]
+    half = (count, rows // 2, vec)
+    shapes = [jax.ShapeDtypeStruct(half, F32), jax.ShapeDtypeStruct(half, BF16), TOKEN]
+    return call(functools.partial(pool_kernel, count), (at, *kept, *came), [SMEM] + [VMEM] * (2 * count), [VMEM] * 3, shapes)
+
+
+def split_kernel(at_ref, values_ref, kept_ref, came_ref, out_ref, below_ref, all_ref):
+    count, _, vec = kept_ref.shape
     for k in range(count):
-        total = (kept[k][...] + came_ref[k].astype(F32)).T
+        total = (kept_ref[k] + came_ref[k].astype(F32)).T
         high = total.astype(BF16)
         out_ref[k, :vec] = high
         out_ref[k, vec:] = (total - high.astype(F32)).astype(BF16)
@@ -149,11 +148,9 @@
 
 
 def split(at, values, kept, came, places):
-    count = len(kept)
-    rows, vec = kept[0].shape
+    count, rows, vec = kept.shape
     shapes = [jax.ShapeDtypeStruct((count, 2 * vec, rows), BF16), jax.ShapeDtypeStruct((count * vec // places, vec), F32)]
-    specs = [SMEM] + [VMEM] * (2 + count)
-    return call(functools.partial(split_kernel, count), (at, values, *kept, came), specs, [VMEM] * 2, shapes, scratch=[pltpu.VMEM((count * vec, vec), F32)])
+    return call(split_kernel, (at, values, kept, came), [SMEM] + [VMEM] * 3, [VMEM] * 2, shapes, scratch=[pltpu.VMEM((count * vec, vec), F32)])
 
 
 def offsets():
@@ -184,19 +181,19 @@
     return call(couple_kernel, (at, terms, *pieces), [SMEM] + [VMEM] * (1 + RING), [VMEM, VMEM], shapes, 4 * count * RING * rows * vec * vec)
 
 
-def spread_kernel(part_ref, out_ref, token_ref):
-    total = jnp.sum(part_ref[...], axis=0)
+def spread_kernel(part_ref, below_ref, out_ref, token_ref):
+    total = jnp.sum(part_ref[...], axis=0) / below_ref[...]
     for j in range(RING):
         out_ref[j] = total
     token_ref[...] = jnp.zeros_like(token_ref)
 
 
-def spread(parts):
-    return call(spread_kernel, (parts,), [VMEM], [VMEM] * 2, [jax.ShapeDtypeStruct((RING,) + parts.shape[1:], F32), TOKEN])
-
-
-def scale_kernel(parts_ref, below_ref, _, out_ref):
-    out_ref[...] = (jnp.sum(parts_ref[...], axis=0) / below_ref[...]).astype(BF16)
+def spread(parts, below):
+    return call(spread_kernel, (parts, below), [VMEM, VMEM], [VMEM] * 2, [jax.ShapeDtypeStruct((RING,) + parts.shape[1:], F32), TOKEN])
+
+
+def scale_kernel(parts_ref, _, out_ref):
+    out_ref[...] = jnp.sum(parts_ref[...], axis=0).astype(BF16)
 
 
 def apply_kernel(near, at_ref, own_ref, other_ref, scaled_ref, panels_ref, _, out_ref, block_ref, sems):
@@ -265,11 +262,11 @@
 
     with jax.named_scope("coupling"):
         part, own = couple(at, terms, pieces)
-        part, token = spread(lax.all_to_all(part.reshape(32, -1, vec), PLANE, 0, 0))
+        part, token = spread(lax.all_to_all(part.reshape(32, -1, vec), PLANE, 0, 0), below)
         own, token = lax.optimization_barrier((own, token))
         far, other = swap(own, "yh"), swap(own, "core")
         part = lax.all_to_all(part, "z", 0, 0)
-        scaled = call(scale_kernel, (part, below, token), [VMEM, VMEM, ANY], VMEM, jax.ShapeDtypeStruct(part.shape[1:], BF16))
+        scaled = call(scale_kernel, (part, token), [VMEM, ANY], VMEM, jax.ShapeDtypeStruct(part.shape[1:], BF16))
         copies = jnp.broadcast_to(scaled[None], (32,) + scaled.shape)
         scaled = lax.all_to_all(copies, PLANE, 0, 0).reshape(count, vec, vec)
 

time: 130 us -> 129 us (level)
  local copies, waits for them, and re-layouts: 10.6 us -> 6.24 us
  waiting for transfers between devices: 29.6 us -> 32.8 us
    unnamed x24 -> x8, local copies, waits for them, and re-layouts: 9.07 us -> 4.73 us
    all_to_all x1, waiting for transfers between devices: 1.4 us -> 3.08 us  [body(): lax.all_to_all(out_pool.reshape(2 * RING, 2 * size, vec), ('z', 'yh'), 0, 0)]
    ppermute x7, waiting for transfers between devices: 7 us -> 8.49 us  [shift(): return lax.ppermute(x, 'z', [(i, (i + by) % RING) for i in range(RING)])]
  transfers between devices with their start and end apart: 18 -> 18, of which waited for: 8 -> 8; matrix products, arithmetic and copies ran while one was open for 1% -> 1% of each run, Pallas kernels for 17% -> 18%
where the time goes in v8:
time: 129 us
  starting transfers between devices  37.7 us (29%)
  waiting for transfers between devices  32.8 us (25%)
  Pallas kernels  28.7 us (22%)
  blocking collectives  23 us (18%)
  local copies, waits for them, and re-layouts  6.24 us (5%)
    all_to_all x1, blocking collectives, body(): lax.all_to_all(part.reshape(32, -1, vec), PLANE, 0, 0)  23 us
    pallas_call x9, Pallas kernels, call(): pl.pallas_call(kernel, in_specs=in_specs, out_specs=out_specs, out_shape=...  20.1 us
    all_to_all x1, starting transfers between devices, body(): lax.all_to_all(out_pool.reshape(2 * RING, 2 * size, vec), ('z', 'yh'), 0, 0)  11.7 us
    all_to_all x1, waiting for transfers between devices, body(): part = lax.all_to_all(part, 'z', 0, 0)  10.3 us
    ppermute x8, starting transfers between devices, swap(): return lax.ppermute(x, axis, [(0, 1), (1, 0)])  10.2 us
    all_to_all x1, waiting for transfers between devices, body(): scaled = lax.all_to_all(copies, PLANE, 0, 0).reshape(count, vec, vec)  9.98 us
    pallas_call x2, Pallas kernels, apply(): pl.pallas_call(functools.partial(apply_kernel, near), in_specs=[SMEM, VME...  8.62 us
    ppermute x7, waiting for transfers between devices, shift(): return lax.ppermute(x, 'z', [(i, (i + by) % RING) for i in range(RING)])  8.49 us
  transfers between devices with their start and end apart: 18, of which 8 were waited for; matrix products, arithmetic and copies ran while one was open for 1% of the time, Pallas kernels for 18%

profile of v8, /device:TPU:1, one launch (start us, length us, event | category | flops | bytes accessed | tf_op | source)
XLA Modules:
  0.0 128.8 jit_solution(15744951593603633582)
XLA Ops:
  0.0 11.7 %all-to-all-start = ((bf16[16,128,256]{2,1,0:T(8,128)(2,1)}), bf16[16,128,256]{2,1,0:T(8,128)(2,1)S(1)}, u32[]{:S(2)}, u32[]{:S(2)}) async-start(bf16[16,128,256]{2,1,0:T(8,128)(2,1)} %bitcast.13), calls=%async_computation | async-start | bytes 2097152 | tf_op jit(solution)/shard_map/scatter/all_to_all | solution.py:243
  11.8 0.7 concatenate.3.at_ref
  12.5 1.4 %copy-done = bf16[3,1024,256]{2,1,0:T(8,128)(2,1)S(1)} copy-done((bf16[3,1024,256]{2,1,0:T(8,128)(2,1)S(1)}, bf16[3,1024,256]{2,1,0:T(8,128)(2,1)}, u32[]{:S(2)}) %copy-start) | copy-done | bytes 1572888
  13.9 2.2 %copy-done.3 = bf16[2048,1024]{1,0:T(8,128)(2,1)S(1)} copy-done((bf16[2048,1024]{1,0:T(8,128)(2,1)S(1)}, bf16[2048,1024]{1,0:T(8,128)(2,1)}, u32[]{:S(2)}) %copy-start.3) | copy-done | bytes 4194328
  16.1 6.6 %projection.5 = (f32[1024,256]{1,0:T(8,128)S(1)}, f32[1024,256]{1,0:T(8,128)S(1)}, f32[1024,256]{1,0:T(8,128)S(1)}, f32[8,128]{1,0:T(8,128)}) custom-call(s32[7]{0:T(128)S(1)} %concatenate.3.at_ref, bf16[2048,1024]{1,0:T(8,128)(2,1)S(1)} %copy-done.3, bf16[3,1024,256]{2,1,0:T(8,128)(2,1)S(1)} %copy-done), custom_call_target="tpu_custom_call" | custom-call | flops 1610612736 | bytes 5767196 | tf_op jit(solution)/shard_map/projection/pallas_call | solution.py:36
  22.8 1.0 collective-permute-start
  23.8 0.1 collective-permute-start.1
  23.9 0.4 collective-permute-start.2
  24.3 6.3 %projection.4 = (f32[1024,256]{1,0:T(8,128)S(1)}, f32[1024,256]{1,0:T(8,128)S(1)}, f32[1024,256]{1,0:T(8,128)S(1)}, f32[8,128]{1,0:T(8,128)S(1)}) custom-call(s32[7]{0:T(128)S(1)} %concatenate.3.at_ref, bf16[2048,1024]{1,0:T(8,128)(2,1)S(1)} %copy-done.3, bf16[3,1024,256]{2,1,0:T(8,128)(2,1)S(1)} %copy-done), custom_call_target="tpu_custom_call" | custom-call | flops 1610612736 | bytes 5767196 | tf_op jit(solution)/shard_map/projection/pallas_call | solution.py:36
  30.6 0.0 collective-permute-done.1.refs_4_
  30.6 0.0 collective-permute-done.2.refs_5_
  30.6 1.7 %projection.6 = (f32[3,512,256]{2,1,0:T(8,128)S(1)}, bf16[3,512,256]{2,1,0:T(8,128)(2,1)}, f32[8,128]{1,0:T(8,128)S(1)}) custom-call(s32[7]{0:T(128)S(1)} %concatenate.3.at_ref, f32[1024,256]{1,0:T(8,128)S(1)} %get-tuple-element.27.refs_0_, f32[1024,256]{1,0:T(8,128)S(1)} %get-tuple-element.28.refs_1_, f32[1024,256]{1,0:T(8,128)S(1)} %get-tuple-element.29.refs_2_, ...), custom_call_target="tpu_custom_call" | custom-call | bytes 6291484 | tf_op jit(solution)/shard_map/projection/pallas_call | solution.py:36
  32.3 3.2 %collective-permute-start.3 = (bf16[3,512,256]{2,1,0:T(8,128)(2,1)}, bf16[3,512,256]{2,1,0:T(8,128)(2,1)}, u32[]{:S(2)}, u32[]{:S(2)}) collective-permute-start(bf16[3,512,256]{2,1,0:T(8,128)(2,1)} %get-tuple-element.34), channel_id=1, source_target_pairs={{0,16},{16,0},{1,17},{17,1},{2,18},{18,2},{3,19},{19,3},{4,20},{20... | collective-permute-start | bytes 2359304 | tf_op jit(solution)/shard_map/projection/ppermute | solution.py:27
  35.5 3.1 %all-to-all-done.all_ref = bf16[16,128,256]{2,1,0:T(8,128)(2,1)S(1)} async-done(((bf16[16,128,256]{2,1,0:T(8,128)(2,1)}), bf16[16,128,256]{2,1,0:T(8,128)(2,1)S(1)}, u32[]{:S(2)}, u32[]{:S(2)}) %all-to-all-start) | async-done | bytes 1048608 | tf_op jit(solution)/shard_map/scatter/all_to_all | solution.py:243
  38.6 0.9 gather.2
  39.5 4.4 %collective-permute-start.4 = (bf16[3,64,256]{2,1,0:T(8,128)(2,1)S(1)}, bf16[3,64,256]{2,1,0:T(8,128)(2,1)S(1)}, u32[]{:S(2)}, u32[]{:S(2)}) collective-permute-start(bf16[3,64,256]{2,1,0:T(8,128)(2,1)S(1)} %get-tuple-element.39), channel_id=1, source_target_pairs={{0,1},{1,0},{2,3},{3,2},{4,5},{5,4},{6,7},{7,6},{8,9},{9,8},{10,11... | collective-permute-start | bytes 294920 | tf_op jit(solution)/shard_map/gather/ppermute | solution.py:27
  43.9 0.9 collective-permute-done.4.other_ref
  44.8 0.6 gather.3.refs_0_
  45.4 0.1 collective-permute-start.5
  45.5 2.7 %collective-permute-start.6 = (bf16[3,64,256]{2,1,0:T(8,128)(2,1)S(1)}, bf16[3,64,256]{2,1,0:T(8,128)(2,1)S(1)}, u32[]{:S(2)}, u32[]{:S(2)}) collective-permute-start(bf16[3,64,256]{2,1,0:T(8,128)(2,1)S(1)} %gather.3.refs_0_), channel_id=1, source_target_pairs={{0,14},{2,0},{4,2},{6,4},{8,6},{10,8},{12,10},{14,12},{1,15},{3,1}... | collective-permute-start | bytes 294920 | tf_op jit(solution)/shard_map/gather/ppermute | solution.py:31
  48.2 2.7 %collective-permute-done.5.refs_1_ = bf16[3,64,256]{2,1,0:T(8,128)(2,1)S(1)} collective-permute-done((bf16[3,64,256]{2,1,0:T(8,128)(2,1)S(1)}, bf16[3,64,256]{2,1,0:T(8,128)(2,1)S(1)}, u32[]{:S(2)}, u32[]{:S(2)}) %collective-permute-start.5) | collective-permute-done | bytes 98336 | tf_op jit(solution)/shard_map/gather/ppermute | solution.py:31
  50.8 0.0 collective-permute-start.7
  50.8 0.0 collective-permute-done.6.refs_2_
  50.8 2.7 %collective-permute-start.8 = (bf16[3,64,256]{2,1,0:T(8,128)(2,1)S(1)}, bf16[3,64,256]{2,1,0:T(8,128)(2,1)S(1)}, u32[]{:S(2)}, u32[]{:S(2)}) collective-permute-start(bf16[3,64,256]{2,1,0:T(8,128)(2,1)S(1)} %collective-permute-done.6.refs_2_), channel_id=1, source_target_pairs={{0,14},{2,0},{4,2},{6,4},{8,6},{10,8},{12,10},{14,12},{1,15},{3,1}... | collective-permute-start | bytes 294920 | tf_op jit(solution)/shard_map/gather/ppermute | solution.py:31
  53.5 2.4 %collective-permute-done.7.refs_3_ = bf16[3,64,256]{2,1,0:T(8,128)(2,1)S(1)} collective-permute-done((bf16[3,64,256]{2,1,0:T(8,128)(2,1)S(1)}, bf16[3,64,256]{2,1,0:T(8,128)(2,1)S(1)}, u32[]{:S(2)}, u32[]{:S(2)}) %collective-permute-start.7) | collective-permute-done | bytes 98336 | tf_op jit(solution)/shard_map/gather/ppermute | solution.py:31
  55.9 0.0 collective-permute-start.9
  55.9 0.0 collective-permute-done.8.refs_4_
  55.9 2.7 %collective-permute-start.10 = (bf16[3,64,256]{2,1,0:T(8,128)(2,1)S(1)}, bf16[3,64,256]{2,1,0:T(8,128)(2,1)S(1)}, u32[]{:S(2)}, u32[]{:S(2)}) collective-permute-start(bf16[3,64,256]{2,1,0:T(8,128)(2,1)S(1)} %collective-permute-done.8.refs_4_), channel_id=1, source_target_pairs={{0,14},{2,0},{4,2},{6,4},{8,6},{10,8},{12,10},{14,12},{1,15},{3,1}... | collective-permute-start | bytes 294920 | tf_op jit(solution)/shard_map/gather/ppermute | solution.py:31
  58.6 2.0 %collective-permute-done.9.refs_5_ = bf16[3,64,256]{2,1,0:T(8,128)(2,1)S(1)} collective-permute-done((bf16[3,64,256]{2,1,0:T(8,128)(2,1)S(1)}, bf16[3,64,256]{2,1,0:T(8,128)(2,1)S(1)}, u32[]{:S(2)}, u32[]{:S(2)}) %collective-permute-start.9) | collective-permute-done | bytes 98336 | tf_op jit(solution)/shard_map/gather/ppermute | solution.py:31
  60.6 0.0 collective-permute-start.11
  60.6 0.0 collective-permute-done.3.came_ref
  60.6 1.1 copy-done.2
  61.7 2.1 %projection.7 = (bf16[3,512,512]{2,1,0:T(8,128)(2,1)S(1)}, f32[24,256]{1,0:T(8,128)S(1)}) custom-call(s32[7]{0:T(128)S(1)} %concatenate.3.at_ref, f32[3,256,256]{2,1,0:T(8,128)S(1)} %copy-done.2, f32[3,512,256]{2,1,0:T(8,128)S(1)} %get-tuple-element.33.kept_ref, bf16[3,512,256]{2,1,0:T(8,128)(2,1)} %collective-permute-done.3.came_ref), custom_call_target="tpu_custom_call" | custom-call | bytes 3145756 | tf_op jit(solution)/shard_map/projection/pallas_call | solution.py:36
  63.8 0.0 collective-permute-done.10.refs_6_
  63.8 1.4 %collective-permute-done.11.refs_7_ = bf16[3,64,256]{2,1,0:T(8,128)(2,1)S(1)} collective-permute-done((bf16[3,64,256]{2,1,0:T(8,128)(2,1)S(1)}, bf16[3,64,256]{2,1,0:T(8,128)(2,1)S(1)}, u32[]{:S(2)}, u32[]{:S(2)}) %collective-permute-start.11) | collective-permute-done | bytes 98336 | tf_op jit(solution)/shard_map/gather/ppermute | solution.py:31
  65.3 1.1 coupling.3
  66.4 23.0 %all_to_all.20.part_ref = f32[32,24,256]{2,1,0:T(8,128)S(1)} all-to-all(f32[32,24,256]{2,1,0:T(8,128)S(1)} %bitcast.12), channel_id=1, replica_groups=mesh['yl'=2,'x'=4,'yh'=2,'z'=8,'core'=2] {'core','yl','x','yh'}, dimensions={0} | all-to-all | bytes 1572864 | tf_op jit(solution)/shard_map/coupling/all_to_all | solution.py:265
  89.4 0.7 coupling.4
  90.2 3.4 %all-to-all-start.2 = ((f32[8,24,256]{2,1,0:T(8,128)}), f32[8,24,256]{2,1,0:T(8,128)S(1)}, u32[]{:S(2)}, u32[]{:S(2)}) async-start(f32[8,24,256]{2,1,0:T(8,128)} %get-tuple-element.45), calls=%async_computation.2 | async-start | bytes 393216 | tf_op jit(solution)/shard_map/coupling/all_to_all | solution.py:268
  93.6 0.5 collective-permute-start.12
  94.0 10.3 %all-to-all-done.2.parts_ref = f32[8,24,256]{2,1,0:T(8,128)S(1)} async-done(((f32[8,24,256]{2,1,0:T(8,128)}), f32[8,24,256]{2,1,0:T(8,128)S(1)}, u32[]{:S(2)}, u32[]{:S(2)}) %all-to-all-start.2) | async-done | bytes 196640 | tf_op jit(solution)/shard_map/coupling/all_to_all | solution.py:268
  104.4 0.8 broadcast_in_dim.2
  105.1 4.2 %all-to-all-start.3 = ((bf16[32,24,256]{2,1,0:T(8,128)(2,1)}), bf16[32,24,256]{2,1,0:T(8,128)(2,1)S(1)}, u32[]{:S(2)}, u32[]{:S(2)}) async-start(bf16[32,24,256]{2,1,0:T(8,128)(2,1)} %broadcast_in_dim.2), calls=%async_computation.3 | async-start | bytes 786432 | tf_op jit(solution)/shard_map/coupling/all_to_all | solution.py:271
  109.3 0.3 collective-permute-start.14
  109.7 10.0 %all-to-all-done.3 = bf16[32,24,256]{2,1,0:T(8,128)(2,1)S(1)} async-done(((bf16[32,24,256]{2,1,0:T(8,128)(2,1)}), bf16[32,24,256]{2,1,0:T(8,128)(2,1)S(1)}, u32[]{:S(2)}, u32[]{:S(2)}) %all-to-all-start.3) | async-done | bytes 393248 | tf_op jit(solution)/shard_map/coupling/all_to_all | solution.py:271
  119.7 0.3 collective-permute-start.13
  120.0 4.6 %output.2._ = bf16[2048,1024]{1,0:T(8,128)(2,1)} custom-call(s32[7]{0:T(128)S(1)} %concatenate.3.at_ref, bf16[3,512,256]{2,1,0:T(8,128)(2,1)S(1)} %get-tuple-element.44.own_ref, bf16[3,512,256]{2,1,0:T(8,128)(2,1)} %collective-permute-done.14.other_ref, bf16[3,256,256]{2,1,0:T(8,128)(2,1)S(1)} %bitcast.10, bf16[3,1024,256]{2,1,0:T(8,128)(2,1)S(1)} %copy-done.1, ...), custom_call_target="tpu_custom_call" | custom-call | flops 2013265920 | bytes 2097152 | tf_op jit(solution)/shard_map/output/pallas_call | solution.py:223
  124.6 4.0 %output.3 = bf16[2048,1024]{1,0:T(8,128)(2,1)} custom-call(s32[7]{0:T(128)S(1)} %concatenate.3.at_ref, bf16[3,512,256]{2,1,0:T(8,128)(2,1)S(1)} %collective-permute-done.12.own_ref, bf16[3,512,256]{2,1,0:T(8,128)(2,1)S(1)} %collective-permute-done.13.other_ref, bf16[3,256,256]{2,1,0:T(8,128)(2,1)S(1)} %bitcast.11, ...), custom_call_target="tpu_custom_call", output_to_operand_aliasing={{}: (5, {})} | custom-call | flops 2013265920 | bytes 2097152 | tf_op jit(solution)/shard_map/output/pallas_call | solution.py:223
  (11 shorter events, 0.0 us)
Async XLA Ops:
  0.0 38.6 %all-to-all-start = ((bf16[16,128,256]{2,1,0:T(8,128)(2,1)}), bf16[16,128,256]{2,1,0:T(8,128)(2,1)S(1)}, u32[]{:S(2)}, u32[]{:S(2)}) async-start(bf16[16,128,256]{2,1,0:T(8,128)(2,1)} %bitcast.13), calls=%async_computation | async-start | bytes 2097152 | tf_op jit(solution)/shard_map/scatter/all_to_all | solution.py:243
  12.5 1.4 %copy-start = (bf16[3,1024,256]{2,1,0:T(8,128)(2,1)S(1)}, bf16[3,1024,256]{2,1,0:T(8,128)(2,1)}, u32[]{:S(2)}) copy-start(bf16[3,1024,256]{2,1,0:T(8,128)(2,1)} %panels_ref.7) | copy-start | bytes 4718596
  13.9 2.2 %copy-start.3 = (bf16[2048,1024]{1,0:T(8,128)(2,1)S(1)}, bf16[2048,1024]{1,0:T(8,128)(2,1)}, u32[]{:S(2)}) copy-start(bf16[2048,1024]{1,0:T(8,128)(2,1)} %gradient_ref.3) | copy-start | bytes 12582916
  22.8 7.8 %collective-permute-start = (f32[1024,256]{1,0:T(8,128)S(1)}, f32[1024,256]{1,0:T(8,128)S(1)}, u32[]{:S(2)}, u32[]{:S(2)}) collective-permute-start(f32[1024,256]{1,0:T(8,128)S(1)} %get-tuple-element.30), channel_id=1, source_target_pairs={{0,1},{1,0},{2,3},{3,2},{4,5},{5,4},{6,7},{7,6},{8,9},{9,8},{10,11... | collective-permute-start | bytes 3145736 | tf_op jit(solution)/shard_map/projection/ppermute | solution.py:27
  23.8 6.8 %collective-permute-start.1 = (f32[1024,256]{1,0:T(8,128)S(1)}, f32[1024,256]{1,0:T(8,128)S(1)}, u32[]{:S(2)}, u32[]{:S(2)}) collective-permute-start(f32[1024,256]{1,0:T(8,128)S(1)} %get-tuple-element.31), channel_id=1, source_target_pairs={{0,1},{1,0},{2,3},{3,2},{4,5},{5,4},{6,7},{7,6},{8,9},{9,8},{10,11... | collective-permute-start | bytes 3145736 | tf_op jit(solution)/shard_map/projection/ppermute | solution.py:27
  23.9 6.7 %collective-permute-start.2 = (f32[1024,256]{1,0:T(8,128)S(1)}, f32[1024,256]{1,0:T(8,128)S(1)}, u32[]{:S(2)}, u32[]{:S(2)}) collective-permute-start(f32[1024,256]{1,0:T(8,128)S(1)} %get-tuple-element.32), channel_id=1, source_target_pairs={{0,1},{1,0},{2,3},{3,2},{4,5},{5,4},{6,7},{7,6},{8,9},{9,8},{10,11... | collective-permute-start | bytes 3145736 | tf_op jit(solution)/shard_map/projection/ppermute | solution.py:27
  32.3 28.3 %collective-permute-start.3 = (bf16[3,512,256]{2,1,0:T(8,128)(2,1)}, bf16[3,512,256]{2,1,0:T(8,128)(2,1)}, u32[]{:S(2)}, u32[]{:S(2)}) collective-permute-start(bf16[3,512,256]{2,1,0:T(8,128)(2,1)} %get-tuple-element.34), channel_id=1, source_target_pairs={{0,16},{16,0},{1,17},{17,1},{2,18},{18,2},{3,19},{19,3},{4,20},{20... | collective-permute-start | bytes 2359304 | tf_op jit(solution)/shard_map/projection/ppermute | solution.py:27
  39.5 5.4 %collective-permute-start.4 = (bf16[3,64,256]{2,1,0:T(8,128)(2,1)S(1)}, bf16[3,64,256]{2,1,0:T(8,128)(2,1)S(1)}, u32[]{:S(2)}, u32[]{:S(2)}) collective-permute-start(bf16[3,64,256]{2,1,0:T(8,128)(2,1)S(1)} %get-tuple-element.39), channel_id=1, source_target_pairs={{0,1},{1,0},{2,3},{3,2},{4,5},{5,4},{6,7},{7,6},{8,9},{9,8},{10,11... | collective-permute-start | bytes 294920 | tf_op jit(solution)/shard_map/gather/ppermute | solution.py:27
  45.4 5.4 %collective-permute-start.5 = (bf16[3,64,256]{2,1,0:T(8,128)(2,1)S(1)}, bf16[3,64,256]{2,1,0:T(8,128)(2,1)S(1)}, u32[]{:S(2)}, u32[]{:S(2)}) collective-permute-start(bf16[3,64,256]{2,1,0:T(8,128)(2,1)S(1)} %gather.3.refs_0_), channel_id=1, source_target_pairs={{0,2},{2,4},{4,6},{6,8},{8,10},{10,12},{12,14},{14,0},{1,3},{3,5},... | collective-permute-start | bytes 294920 | tf_op jit(solution)/shard_map/gather/ppermute | solution.py:31
  45.5 5.3 %collective-permute-start.6 = (bf16[3,64,256]{2,1,0:T(8,128)(2,1)S(1)}, bf16[3,64,256]{2,1,0:T(8,128)(2,1)S(1)}, u32[]{:S(2)}, u32[]{:S(2)}) collective-permute-start(bf16[3,64,256]{2,1,0:T(8,128)(2,1)S(1)} %gather.3.refs_0_), channel_id=1, source_target_pairs={{0,14},{2,0},{4,2},{6,4},{8,6},{10,8},{12,10},{14,12},{1,15},{3,1}... | collective-permute-start | bytes 294920 | tf_op jit(solution)/shard_map/gather/ppermute | solution.py:31
  50.8 5.1 %collective-permute-start.7 = (bf16[3,64,256]{2,1,0:T(8,128)(2,1)S(1)}, bf16[3,64,256]{2,1,0:T(8,128)(2,1)S(1)}, u32[]{:S(2)}, u32[]{:S(2)}) collective-permute-start(bf16[3,64,256]{2,1,0:T(8,128)(2,1)S(1)} %collective-permute-done.5.refs_1_), channel_id=1, source_target_pairs={{0,2},{2,4},{4,6},{6,8},{8,10},{10,12},{12,14},{14,0},{1,3},{3,5},... | collective-permute-start | bytes 294920 | tf_op jit(solution)/shard_map/gather/ppermute | solution.py:31
  50.8 5.1 %collective-permute-start.8 = (bf16[3,64,256]{2,1,0:T(8,128)(2,1)S(1)}, bf16[3,64,256]{2,1,0:T(8,128)(2,1)S(1)}, u32[]{:S(2)}, u32[]{:S(2)}) collective-permute-start(bf16[3,64,256]{2,1,0:T(8,128)(2,1)S(1)} %collective-permute-done.6.refs_2_), channel_id=1, source_target_pairs={{0,14},{2,0},{4,2},{6,4},{8,6},{10,8},{12,10},{14,12},{1,15},{3,1}... | collective-permute-start | bytes 294920 | tf_op jit(solution)/shard_map/gather/ppermute | solution.py:31
  55.9 4.7 %collective-permute-start.9 = (bf16[3,64,256]{2,1,0:T(8,128)(2,1)S(1)}, bf16[3,64,256]{2,1,0:T(8,128)(2,1)S(1)}, u32[]{:S(2)}, u32[]{:S(2)}) collective-permute-start(bf16[3,64,256]{2,1,0:T(8,128)(2,1)S(1)} %collective-permute-done.7.refs_3_), channel_id=1, source_target_pairs={{0,2},{2,4},{4,6},{6,8},{8,10},{10,12},{12,14},{14,0},{1,3},{3,5},... | collective-permute-start | bytes 294920 | tf_op jit(solution)/shard_map/gather/ppermute | solution.py:31
  55.9 7.9 %collective-permute-start.10 = (bf16[3,64,256]{2,1,0:T(8,128)(2,1)S(1)}, bf16[3,64,256]{2,1,0:T(8,128)(2,1)S(1)}, u32[]{:S(2)}, u32[]{:S(2)}) collective-permute-start(bf16[3,64,256]{2,1,0:T(8,128)(2,1)S(1)} %collective-permute-done.8.refs_4_), channel_id=1, source_target_pairs={{0,14},{2,0},{4,2},{6,4},{8,6},{10,8},{12,10},{14,12},{1,15},{3,1}... | collective-permute-start | bytes 294920 | tf_op jit(solution)/shard_map/gather/ppermute | solution.py:31
  60.6 4.7 %collective-permute-start.11 = (bf16[3,64,256]{2,1,0:T(8,128)(2,1)S(1)}, bf16[3,64,256]{2,1,0:T(8,128)(2,1)S(1)}, u32[]{:S(2)}, u32[]{:S(2)}) collective-permute-start(bf16[3,64,256]{2,1,0:T(8,128)(2,1)S(1)} %collective-permute-done.9.refs_5_), channel_id=1, source_target_pairs={{0,2},{2,4},{4,6},{6,8},{8,10},{10,12},{12,14},{14,0},{1,3},{3,5},... | collective-permute-start | bytes 294920 | tf_op jit(solution)/shard_map/gather/ppermute | solution.py:31
  60.6 1.1 copy-start.2
  61.7 58.2 %copy-start.1 = (bf16[3,1024,256]{2,1,0:T(8,128)(2,1)S(1)}, bf16[3,1024,256]{2,1,0:T(8,128)(2,1)}, u32[]{:S(2)}) copy-start(bf16[3,1024,256]{2,1,0:T(8,128)(2,1)} %panels_ref.7) | copy-start | bytes 4718596
  90.2 14.2 %all-to-all-start.2 = ((f32[8,24,256]{2,1,0:T(8,128)}), f32[8,24,256]{2,1,0:T(8,128)S(1)}, u32[]{:S(2)}, u32[]{:S(2)}) async-start(f32[8,24,256]{2,1,0:T(8,128)} %get-tuple-element.45), calls=%async_computation.2 | async-start | bytes 393216 | tf_op jit(solution)/shard_map/coupling/all_to_all | solution.py:268
  93.6 26.1 %collective-permute-start.12 = (bf16[3,512,256]{2,1,0:T(8,128)(2,1)S(1)}, bf16[3,512,256]{2,1,0:T(8,128)(2,1)S(1)}, u32[]{:S(2)}, u32[]{:S(2)}) collective-permute-start(bf16[3,512,256]{2,1,0:T(8,128)(2,1)S(1)} %get-tuple-element.44.own_ref), channel_id=1, source_target_pairs={{0,16},{16,0},{1,17},{17,1},{2,18},{18,2},{3,19},{19,3},{4,20},{20... | collective-permute-start | bytes 2359304 | tf_op jit(solution)/shard_map/coupling/ppermute | solution.py:27
  105.1 14.5 %all-to-all-start.3 = ((bf16[32,24,256]{2,1,0:T(8,128)(2,1)}), bf16[32,24,256]{2,1,0:T(8,128)(2,1)S(1)}, u32[]{:S(2)}, u32[]{:S(2)}) async-start(bf16[32,24,256]{2,1,0:T(8,128)(2,1)} %broadcast_in_dim.2), calls=%async_computation.3 | async-start | bytes 786432 | tf_op jit(solution)/shard_map/coupling/all_to_all | solution.py:271
  109.3 10.6 %collective-permute-start.14 = (bf16[3,512,256]{2,1,0:T(8,128)(2,1)S(1)}, bf16[3,512,256]{2,1,0:T(8,128)(2,1)}, u32[]{:S(2)}, u32[]{:S(2)}) collective-permute-start(bf16[3,512,256]{2,1,0:T(8,128)(2,1)S(1)} %get-tuple-element.44.own_ref), channel_id=1, source_target_pairs={{0,1},{1,0},{2,3},{3,2},{4,5},{5,4},{6,7},{7,6},{8,9},{9,8},{10,11... | collective-permute-start | bytes 2359304 | tf_op jit(solution)/shard_map/coupling/ppermute | solution.py:27
  119.7 4.9 %collective-permute-start.13 = (bf16[3,512,256]{2,1,0:T(8,128)(2,1)S(1)}, bf16[3,512,256]{2,1,0:T(8,128)(2,1)S(1)}, u32[]{:S(2)}, u32[]{:S(2)}) collective-permute-start(bf16[3,512,256]{2,1,0:T(8,128)(2,1)S(1)} %collective-permute-done.12.own_ref), channel_id=1, source_target_pairs={{0,1},{1,0},{2,3},{3,2},{4,5},{5,4},{6,7},{7,6},{8,9},{9,8},{10,11... | collective-permute-start | bytes 2359304 | tf_op jit(solution)/shard_map/output/ppermute | solution.py:27

commit v9 on v8

--- a/solution.py
+++ b/solution.py
@@ -192,16 +192,19 @@
     return call(spread_kernel, (parts, below), [VMEM, VMEM], [VMEM] * 2, [jax.ShapeDtypeStruct((RING,) + parts.shape[1:], F32), TOKEN])
 
 
-def scale_kernel(parts_ref, _, out_ref):
+def scale_kernel(parts_ref, _, out_ref, token_ref):
     out_ref[...] = jnp.sum(parts_ref[...], axis=0).astype(BF16)
-
-
-def apply_kernel(near, at_ref, own_ref, other_ref, scaled_ref, panels_ref, _, out_ref, block_ref, sems):
-    count, rows, _ = own_ref.shape
+    token_ref[...] = jnp.zeros_like(token_ref)
+
+
+def apply_kernel(at_ref, *refs):
+    quarters, (scaled_ref, panels_ref, _, out_ref, block_ref, sems) = refs[:4], refs[4:]
+    count, rows, _ = quarters[0].shape
     size = rows // RING
-    high = at_ref[1] if near else 1 - at_ref[1]
     copies = []
-    for number, (ref, core) in enumerate(((own_ref, at_ref[0]), (other_ref, 1 - at_ref[0]))):
+    for number, ref in enumerate(quarters):
+        high = at_ref[1] if number < 2 else 1 - at_ref[1]
+        core = at_ref[0] if number % 2 == 0 else 1 - at_ref[0]
         total = None
         for k in range(count):
             rotated = lax.dot_general(ref[k], scaled_ref[k], (((1,), (1,)), ((), ())), preferred_element_type=F32)
@@ -217,19 +220,19 @@
         copy.wait()
 
 
-def apply(near, at, own, other, scaled, panels, into):
-    count, rows, vec = own.shape
+def apply(at, quarters, scaled, panels, token):
+    count, rows, vec = quarters[0].shape
     width = panels.shape[1]
-    return pl.pallas_call(
-        functools.partial(apply_kernel, near),
-        in_specs=[SMEM, VMEM, VMEM, VMEM, VMEM, ANY],
-        out_specs=ANY,
-        out_shape=jax.ShapeDtypeStruct((4 * rows, width), BF16),
-        input_output_aliases={} if near else {5: 0},
-        scratch_shapes=[pltpu.VMEM((2, rows, width), BF16), pltpu.SemaphoreType.DMA((2 * RING,))],
-        compiler_params=pltpu.CompilerParams(vmem_limit_bytes=24 * MIB),
-        cost_estimate=pl.CostEstimate(flops=4 * count * rows * vec * (vec + width), bytes_accessed=4 * rows * width, transcendentals=0),
-    )(at, own, other, scaled, panels, into)
+    return call(
+        apply_kernel,
+        (at, *quarters, scaled, panels, token),
+        [SMEM] + [VMEM] * 6 + [ANY],
+        ANY,
+        jax.ShapeDtypeStruct((4 * rows, width), BF16),
+        8 * count * rows * vec * (vec + width),
+        [pltpu.VMEM((4, rows, width), BF16), pltpu.SemaphoreType.DMA((4 * RING,))],
+        limit=24,
+    )
 
 
 def body(gradient, in_panels, out_pool, eigenvalues, owners):
@@ -262,18 +265,20 @@
 
     with jax.named_scope("coupling"):
         part, own = couple(at, terms, pieces)
+        far = swap(own, "yh")
         part, token = spread(lax.all_to_all(part.reshape(32, -1, vec), PLANE, 0, 0), below)
-        own, token = lax.optimization_barrier((own, token))
-        far, other = swap(own, "yh"), swap(own, "core")
+        near, token = lax.optimization_barrier((own, token))
+        near = swap(near, "core")
         part = lax.all_to_all(part, "z", 0, 0)
-        scaled = call(scale_kernel, (part, token), [VMEM, ANY], VMEM, jax.ShapeDtypeStruct(part.shape[1:], BF16))
+        shapes = [jax.ShapeDtypeStruct(part.shape[1:], BF16), TOKEN]
+        scaled, token = call(scale_kernel, (part, token), [VMEM, ANY], [VMEM, VMEM], shapes)
+        far, token = lax.optimization_barrier((far, token))
+        quarters = [own, near, far, swap(far, "core")]
         copies = jnp.broadcast_to(scaled[None], (32,) + scaled.shape)
         scaled = lax.all_to_all(copies, PLANE, 0, 0).reshape(count, vec, vec)
 
     with jax.named_scope("output"):
-        far, token = lax.optimization_barrier((far, scaled[0, :16, :128]))
-        out = apply(True, at, own, other, scaled, in_panels, token)
-        return apply(False, at, far, swap(far, "core"), scaled, in_panels, out)
+        return apply(at, quarters, scaled, in_panels, token)
 
 
 def solution(mesh):

time: 129 us -> 129 us (level)
  blocking collectives: 23 us -> 14.7 us
  starting transfers between devices: 37.7 us -> 44.7 us
  waiting for transfers between devices: 32.8 us -> 38.6 us
  local copies, waits for them, and re-layouts: 6.24 us -> 2.32 us
    pallas_call x2 -> x0, Pallas kernels: 8.62 us -> none  [apply(): pl.pallas_call(functools.partial(apply_kernel, near), in_specs=[SMEM, VME...]
    all_to_all x1, blocking collectives: 23 us -> 14.7 us  [body(): scaled = lax.all_to_all(copies, PLANE, 0, 0).reshape(count, vec, vec)]
    pallas_call x9 -> x10, Pallas kernels: 20.1 us -> 28.1 us  [call(): pl.pallas_call(kernel, in_specs=in_specs, out_specs=out_specs, out_shape=...]
    all_to_all x1, starting transfers between devices: 4.19 us -> 8.71 us  [body(): lax.all_to_all(part.reshape(32, -1, vec), PLANE, 0, 0)]
    unnamed x8 -> x10, local copies, waits for them, and re-layouts: 4.73 us -> 2.21 us
    ppermute x8, starting transfers between devices: 10.2 us -> 12.7 us  [swap(): return lax.ppermute(x, axis, [(0, 1), (1, 0)])]
    all_to_all x1, waiting for transfers between devices: 9.98 us -> 12 us  [body(): lax.all_to_all(part.reshape(32, -1, vec), PLANE, 0, 0)]
    all_to_all x1, waiting for transfers between devices: 3.08 us -> 5.07 us  [body(): lax.all_to_all(out_pool.reshape(2 * RING, 2 * size, vec), ('z', 'yh'), 0, 0)]
  transfers between devices with their start and end apart: 18 -> 18, of which waited for: 8 -> 8; matrix products, arithmetic and copies ran while one was open for 1% -> 0% of each run, Pallas kernels for 18% -> 15%
where the time goes in v9:
time: 129 us
  starting transfers between devices  44.7 us (35%)
  waiting for transfers between devices  38.6 us (30%)
  Pallas kernels  28.1 us (22%)
  blocking collectives  14.7 us (11%)
  local copies, waits for them, and re-layouts  2.32 us (2%)
    pallas_call x10, Pallas kernels, call(): pl.pallas_call(kernel, in_specs=in_specs, out_specs=out_specs, out_shape=...  28.1 us
    all_to_all x1, blocking collectives, body(): scaled = lax.all_to_all(copies, PLANE, 0, 0).reshape(count, vec, vec)  14.7 us
    ppermute x8, starting transfers between devices, swap(): return lax.ppermute(x, axis, [(0, 1), (1, 0)])  12.7 us
    all_to_all x1, waiting for transfers between devices, body(): lax.all_to_all(part.reshape(32, -1, vec), PLANE, 0, 0)  12 us
    all_to_all x1, starting transfers between devices, body(): lax.all_to_all(out_pool.reshape(2 * RING, 2 * size, vec), ('z', 'yh'), 0, 0)  11.9 us
    all_to_all x1, waiting for transfers between devices, body(): part = lax.all_to_all(part, 'z', 0, 0)  10.8 us
    ppermute x7, waiting for transfers between devices, shift(): return lax.ppermute(x, 'z', [(i, (i + by) % RING) for i in range(RING)])  9.75 us
    all_to_all x1, starting transfers between devices, body(): lax.all_to_all(part.reshape(32, -1, vec), PLANE, 0, 0)  8.71 us
  transfers between devices with their start and end apart: 18, of which 8 were waited for; matrix products, arithmetic and copies ran while one was open for 0% of the time, Pallas kernels for 15%

profile of v9, /device:TPU:1, one launch (start us, length us, event | category | flops | bytes accessed | tf_op | source)
XLA Modules:
  0.0 128.8 jit_solution(4005491353362111382)
XLA Ops:
  0.0 11.9 %all-to-all-start = ((bf16[16,128,256]{2,1,0:T(8,128)(2,1)}), bf16[16,128,256]{2,1,0:T(8,128)(2,1)S(1)}, u32[]{:S(2)}, u32[]{:S(2)}) async-start(bf16[16,128,256]{2,1,0:T(8,128)(2,1)} %bitcast.8), calls=%async_computation | async-start | bytes 2097152 | tf_op jit(solution)/shard_map/scatter/all_to_all | solution.py:246
  11.9 0.1 concatenate.3.at_ref
  12.0 2.2 %copy-done.1 = bf16[2048,1024]{1,0:T(8,128)(2,1)S(1)} copy-done((bf16[2048,1024]{1,0:T(8,128)(2,1)S(1)}, bf16[2048,1024]{1,0:T(8,128)(2,1)}, u32[]{:S(2)}) %copy-start.1) | copy-done | bytes 4194328
  14.2 6.7 %projection.5 = (f32[1024,256]{1,0:T(8,128)S(1)}, f32[1024,256]{1,0:T(8,128)S(1)}, f32[1024,256]{1,0:T(8,128)S(1)}, f32[8,128]{1,0:T(8,128)}) custom-call(s32[7]{0:T(128)S(1)} %concatenate.3.at_ref, bf16[2048,1024]{1,0:T(8,128)(2,1)S(1)} %copy-done.1, bf16[3,1024,256]{2,1,0:T(8,128)(2,1)S(1)} %copy-done.2), custom_call_target="tpu_custom_call" | custom-call | flops 1610612736 | bytes 5767196 | tf_op jit(solution)/shard_map/projection/pallas_call | solution.py:36
  20.9 1.0 collective-permute-start
  21.9 0.1 collective-permute-start.1
  22.0 0.4 collective-permute-start.2
  22.4 6.3 %projection.4 = (f32[1024,256]{1,0:T(8,128)S(1)}, f32[1024,256]{1,0:T(8,128)S(1)}, f32[1024,256]{1,0:T(8,128)S(1)}, f32[8,128]{1,0:T(8,128)S(1)}) custom-call(s32[7]{0:T(128)S(1)} %concatenate.3.at_ref, bf16[2048,1024]{1,0:T(8,128)(2,1)S(1)} %copy-done.1, bf16[3,1024,256]{2,1,0:T(8,128)(2,1)S(1)} %copy-done.2), custom_call_target="tpu_custom_call" | custom-call | flops 1610612736 | bytes 5767196 | tf_op jit(solution)/shard_map/projection/pallas_call | solution.py:36
  28.7 0.0 collective-permute-done.refs_3_
  28.8 0.0 collective-permute-done.1.refs_4_
  28.8 0.0 collective-permute-done.2.refs_5_
  28.8 1.7 %projection.6 = (f32[3,512,256]{2,1,0:T(8,128)S(1)}, bf16[3,512,256]{2,1,0:T(8,128)(2,1)}, f32[8,128]{1,0:T(8,128)S(1)}) custom-call(s32[7]{0:T(128)S(1)} %concatenate.3.at_ref, f32[1024,256]{1,0:T(8,128)S(1)} %get-tuple-element.29.refs_0_, f32[1024,256]{1,0:T(8,128)S(1)} %get-tuple-element.30.refs_1_, f32[1024,256]{1,0:T(8,128)S(1)} %get-tuple-element.31.refs_2_, ...), custom_call_target="tpu_custom_call" | custom-call | bytes 6291484 | tf_op jit(solution)/shard_map/projection/pallas_call | solution.py:36
  30.5 3.2 %collective-permute-start.3 = (bf16[3,512,256]{2,1,0:T(8,128)(2,1)}, bf16[3,512,256]{2,1,0:T(8,128)(2,1)}, u32[]{:S(2)}, u32[]{:S(2)}) collective-permute-start(bf16[3,512,256]{2,1,0:T(8,128)(2,1)} %get-tuple-element.36), channel_id=1, source_target_pairs={{0,16},{16,0},{1,17},{17,1},{2,18},{18,2},{3,19},{19,3},{4,20},{20... | collective-permute-start | bytes 2359304 | tf_op jit(solution)/shard_map/projection/ppermute | solution.py:27
  33.7 5.1 %all-to-all-done.all_ref = bf16[16,128,256]{2,1,0:T(8,128)(2,1)S(1)} async-done(((bf16[16,128,256]{2,1,0:T(8,128)(2,1)}), bf16[16,128,256]{2,1,0:T(8,128)(2,1)S(1)}, u32[]{:S(2)}, u32[]{:S(2)}) %all-to-all-start) | async-done | bytes 1048608 | tf_op jit(solution)/shard_map/scatter/all_to_all | solution.py:246
  38.7 0.9 gather.2
  39.6 4.4 %collective-permute-start.4 = (bf16[3,64,256]{2,1,0:T(8,128)(2,1)S(1)}, bf16[3,64,256]{2,1,0:T(8,128)(2,1)S(1)}, u32[]{:S(2)}, u32[]{:S(2)}) collective-permute-start(bf16[3,64,256]{2,1,0:T(8,128)(2,1)S(1)} %get-tuple-element.41), channel_id=1, source_target_pairs={{0,1},{1,0},{2,3},{3,2},{4,5},{5,4},{6,7},{7,6},{8,9},{9,8},{10,11... | collective-permute-start | bytes 294920 | tf_op jit(solution)/shard_map/gather/ppermute | solution.py:27
  44.0 0.9 collective-permute-done.4.other_ref
  45.0 0.6 gather.3.refs_0_
  45.5 0.1 collective-permute-start.5
  45.6 2.7 %collective-permute-start.6 = (bf16[3,64,256]{2,1,0:T(8,128)(2,1)S(1)}, bf16[3,64,256]{2,1,0:T(8,128)(2,1)S(1)}, u32[]{:S(2)}, u32[]{:S(2)}) collective-permute-start(bf16[3,64,256]{2,1,0:T(8,128)(2,1)S(1)} %gather.3.refs_0_), channel_id=1, source_target_pairs={{0,14},{2,0},{4,2},{6,4},{8,6},{10,8},{12,10},{14,12},{1,15},{3,1}... | collective-permute-start | bytes 294920 | tf_op jit(solution)/shard_map/gather/ppermute | solution.py:31
  48.3 2.7 %collective-permute-done.5.refs_1_ = bf16[3,64,256]{2,1,0:T(8,128)(2,1)S(1)} collective-permute-done((bf16[3,64,256]{2,1,0:T(8,128)(2,1)S(1)}, bf16[3,64,256]{2,1,0:T(8,128)(2,1)S(1)}, u32[]{:S(2)}, u32[]{:S(2)}) %collective-permute-start.5) | collective-permute-done | bytes 98336 | tf_op jit(solution)/shard_map/gather/ppermute | solution.py:31
  51.0 0.0 collective-permute-start.7
  51.0 0.0 collective-permute-done.6.refs_2_
  51.0 2.7 %collective-permute-start.8 = (bf16[3,64,256]{2,1,0:T(8,128)(2,1)S(1)}, bf16[3,64,256]{2,1,0:T(8,128)(2,1)S(1)}, u32[]{:S(2)}, u32[]{:S(2)}) collective-permute-start(bf16[3,64,256]{2,1,0:T(8,128)(2,1)S(1)} %collective-permute-done.6.refs_2_), channel_id=1, source_target_pairs={{0,14},{2,0},{4,2},{6,4},{8,6},{10,8},{12,10},{14,12},{1,15},{3,1}... | collective-permute-start | bytes 294920 | tf_op jit(solution)/shard_map/gather/ppermute | solution.py:31
  53.6 2.4 %collective-permute-done.7.refs_3_ = bf16[3,64,256]{2,1,0:T(8,128)(2,1)S(1)} collective-permute-done((bf16[3,64,256]{2,1,0:T(8,128)(2,1)S(1)}, bf16[3,64,256]{2,1,0:T(8,128)(2,1)S(1)}, u32[]{:S(2)}, u32[]{:S(2)}) %collective-permute-start.7) | collective-permute-done | bytes 98336 | tf_op jit(solution)/shard_map/gather/ppermute | solution.py:31
  56.0 0.0 collective-permute-start.9
  56.1 0.0 collective-permute-done.8.refs_4_
  56.1 2.7 %collective-permute-start.10 = (bf16[3,64,256]{2,1,0:T(8,128)(2,1)S(1)}, bf16[3,64,256]{2,1,0:T(8,128)(2,1)S(1)}, u32[]{:S(2)}, u32[]{:S(2)}) collective-permute-start(bf16[3,64,256]{2,1,0:T(8,128)(2,1)S(1)} %collective-permute-done.8.refs_4_), channel_id=1, source_target_pairs={{0,14},{2,0},{4,2},{6,4},{8,6},{10,8},{12,10},{14,12},{1,15},{3,1}... | collective-permute-start | bytes 294920 | tf_op jit(solution)/shard_map/gather/ppermute | solution.py:31
  58.7 2.0 %collective-permute-done.9.refs_5_ = bf16[3,64,256]{2,1,0:T(8,128)(2,1)S(1)} collective-permute-done((bf16[3,64,256]{2,1,0:T(8,128)(2,1)S(1)}, bf16[3,64,256]{2,1,0:T(8,128)(2,1)S(1)}, u32[]{:S(2)}, u32[]{:S(2)}) %collective-permute-start.9) | collective-permute-done | bytes 98336 | tf_op jit(solution)/shard_map/gather/ppermute | solution.py:31
  60.7 0.0 collective-permute-start.11
  60.7 0.0 collective-permute-done.3.came_ref
  60.7 2.0 %projection.7 = (bf16[3,512,512]{2,1,0:T(8,128)(2,1)S(1)}, f32[24,256]{1,0:T(8,128)S(1)}) custom-call(s32[7]{0:T(128)S(1)} %concatenate.3.at_ref, f32[3,256,256]{2,1,0:T(8,128)S(1)} %copy-done, f32[3,512,256]{2,1,0:T(8,128)S(1)} %get-tuple-element.35.kept_ref, bf16[3,512,256]{2,1,0:T(8,128)(2,1)} %collective-permute-done.3.came_ref), custom_call_target="tpu_custom_call" | custom-call | bytes 3145756 | tf_op jit(solution)/shard_map/projection/pallas_call | solution.py:36
  62.7 0.0 collective-permute-done.10.refs_6_
  62.7 2.7 %collective-permute-done.11.refs_7_ = bf16[3,64,256]{2,1,0:T(8,128)(2,1)S(1)} collective-permute-done((bf16[3,64,256]{2,1,0:T(8,128)(2,1)S(1)}, bf16[3,64,256]{2,1,0:T(8,128)(2,1)S(1)}, u32[]{:S(2)}, u32[]{:S(2)}) %collective-permute-start.11) | collective-permute-done | bytes 98336 | tf_op jit(solution)/shard_map/gather/ppermute | solution.py:31
  65.4 2.0 %coupling.3 = (f32[768,256]{1,0:T(8,128)}, bf16[3,512,256]{2,1,0:T(8,128)(2,1)S(1)}) custom-call(s32[7]{0:T(128)S(1)} %concatenate.3.at_ref, bf16[3,512,512]{2,1,0:T(8,128)(2,1)S(1)} %get-tuple-element.37.terms_ref, bf16[3,64,256]{2,1,0:T(8,128)(2,1)S(1)} %gather.3.refs_0_, bf16[3,64,256]{2,1,0:T(8,128)(2,1)S(1)} %collective-permute-done.5.refs_1_, ...), custom_call_target="tpu_custom_call" | custom-call | flops 402653184 | bytes 2359324 | tf_op jit(solution)/shard_map/coupling/pallas_call | solution.py:36
  67.4 8.7 %all-to-all-start.1 = ((f32[32,24,256]{2,1,0:T(8,128)}), f32[32,24,256]{2,1,0:T(8,128)S(1)}, u32[]{:S(2)}, u32[]{:S(2)}) async-start(f32[32,24,256]{2,1,0:T(8,128)} %bitcast.5), calls=%async_computation.1 | async-start | bytes 1572864 | tf_op jit(solution)/shard_map/coupling/all_to_all | solution.py:269
  76.2 0.0 copy-start.3
  76.2 3.0 %collective-permute-start.13 = (bf16[3,512,256]{2,1,0:T(8,128)(2,1)S(1)}, bf16[3,512,256]{2,1,0:T(8,128)(2,1)}, u32[]{:S(2)}, u32[]{:S(2)}) collective-permute-start(bf16[3,512,256]{2,1,0:T(8,128)(2,1)S(1)} %get-tuple-element.46.refs_0_), channel_id=1, source_target_pairs={{0,16},{16,0},{1,17},{17,1},{2,18},{18,2},{3,19},{19,3},{4,20},{20... | collective-permute-start | bytes 2359304 | tf_op jit(solution)/shard_map/coupling/ppermute | solution.py:27
  79.1 12.0 %all-to-all-done.1.part_ref = f32[32,24,256]{2,1,0:T(8,128)S(1)} async-done(((f32[32,24,256]{2,1,0:T(8,128)}), f32[32,24,256]{2,1,0:T(8,128)S(1)}, u32[]{:S(2)}, u32[]{:S(2)}) %all-to-all-start.1) | async-done | bytes 786464 | tf_op jit(solution)/shard_map/coupling/all_to_all | solution.py:269
  91.1 0.7 coupling.4
  91.9 3.4 %all-to-all-start.2 = ((f32[8,24,256]{2,1,0:T(8,128)}), f32[8,24,256]{2,1,0:T(8,128)S(1)}, u32[]{:S(2)}, u32[]{:S(2)}) async-start(f32[8,24,256]{2,1,0:T(8,128)} %get-tuple-element.47), calls=%async_computation.2 | async-start | bytes 393216 | tf_op jit(solution)/shard_map/coupling/all_to_all | solution.py:272
  95.3 0.1 collective-permute-start.12
  95.4 10.8 %all-to-all-done.2.parts_ref = f32[8,24,256]{2,1,0:T(8,128)S(1)} async-done(((f32[8,24,256]{2,1,0:T(8,128)}), f32[8,24,256]{2,1,0:T(8,128)S(1)}, u32[]{:S(2)}, u32[]{:S(2)}) %all-to-all-start.2) | async-done | bytes 196640 | tf_op jit(solution)/shard_map/coupling/all_to_all | solution.py:272
  106.2 0.0 collective-permute-done.13.refs_2_
  106.2 0.5 collective-permute-start.14
  106.7 14.7 %all_to_all.20 = bf16[32,24,256]{2,1,0:T(8,128)(2,1)S(1)} all-to-all(bf16[32,24,256]{2,1,0:T(8,128)(2,1)S(1)} %broadcast_in_dim.2), channel_id=1, replica_groups=mesh['yl'=2,'x'=4,'yh'=2,'z'=8,'core'=2] {'core','yl','x','yh'}, dimensions={0} | all-to-all | bytes 786432 | tf_op jit(solution)/shard_map/coupling/all_to_all | solution.py:278
  121.4 0.0 collective-permute-done.12.refs_1_
  121.5 7.1 %output.1 = bf16[2048,1024]{1,0:T(8,128)(2,1)} custom-call(s32[7]{0:T(128)S(1)} %concatenate.3.at_ref, bf16[3,512,256]{2,1,0:T(8,128)(2,1)S(1)} %get-tuple-element.46.refs_0_, bf16[3,512,256]{2,1,0:T(8,128)(2,1)} %collective-permute-done.12.refs_1_, bf16[3,512,256]{2,1,0:T(8,128)(2,1)} %collective-permute-done.13.refs_2_, ...), custom_call_target="tpu_custom_call" | custom-call | flops 4026531840 | bytes 5115932 | tf_op jit(solution)/shard_map/output/pallas_call | solution.py:36
  (11 shorter events, 0.1 us)
Async XLA Ops:
  0.0 11.9 %copy-start.4 = (s32[3]{0:T(128)S(1)}, s32[3]{0:T(128)}, u32[]{:S(2)}) copy-start(s32[3]{0:T(128)} %param.9) | copy-start | bytes 40
  0.0 12.0 %copy-start.2 = (bf16[3,1024,256]{2,1,0:T(8,128)(2,1)S(1)}, bf16[3,1024,256]{2,1,0:T(8,128)(2,1)}, u32[]{:S(2)}) copy-start(bf16[3,1024,256]{2,1,0:T(8,128)(2,1)} %refs_5_.1) | copy-start | bytes 4718596
  0.0 38.7 %all-to-all-start = ((bf16[16,128,256]{2,1,0:T(8,128)(2,1)}), bf16[16,128,256]{2,1,0:T(8,128)(2,1)S(1)}, u32[]{:S(2)}, u32[]{:S(2)}) async-start(bf16[16,128,256]{2,1,0:T(8,128)(2,1)} %bitcast.8), calls=%async_computation | async-start | bytes 2097152 | tf_op jit(solution)/shard_map/scatter/all_to_all | solution.py:246
  12.0 2.2 %copy-start.1 = (bf16[2048,1024]{1,0:T(8,128)(2,1)S(1)}, bf16[2048,1024]{1,0:T(8,128)(2,1)}, u32[]{:S(2)}) copy-start(bf16[2048,1024]{1,0:T(8,128)(2,1)} %gradient_ref.3) | copy-start | bytes 12582916
  20.9 7.8 %collective-permute-start = (f32[1024,256]{1,0:T(8,128)S(1)}, f32[1024,256]{1,0:T(8,128)S(1)}, u32[]{:S(2)}, u32[]{:S(2)}) collective-permute-start(f32[1024,256]{1,0:T(8,128)S(1)} %get-tuple-element.32), channel_id=1, source_target_pairs={{0,1},{1,0},{2,3},{3,2},{4,5},{5,4},{6,7},{7,6},{8,9},{9,8},{10,11... | collective-permute-start | bytes 3145736 | tf_op jit(solution)/shard_map/projection/ppermute | solution.py:27
  21.9 6.8 %collective-permute-start.1 = (f32[1024,256]{1,0:T(8,128)S(1)}, f32[1024,256]{1,0:T(8,128)S(1)}, u32[]{:S(2)}, u32[]{:S(2)}) collective-permute-start(f32[1024,256]{1,0:T(8,128)S(1)} %get-tuple-element.33), channel_id=1, source_target_pairs={{0,1},{1,0},{2,3},{3,2},{4,5},{5,4},{6,7},{7,6},{8,9},{9,8},{10,11... | collective-permute-start | bytes 3145736 | tf_op jit(solution)/shard_map/projection/ppermute | solution.py:27
  22.0 6.7 %collective-permute-start.2 = (f32[1024,256]{1,0:T(8,128)S(1)}, f32[1024,256]{1,0:T(8,128)S(1)}, u32[]{:S(2)}, u32[]{:S(2)}) collective-permute-start(f32[1024,256]{1,0:T(8,128)S(1)} %get-tuple-element.34), channel_id=1, source_target_pairs={{0,1},{1,0},{2,3},{3,2},{4,5},{5,4},{6,7},{7,6},{8,9},{9,8},{10,11... | collective-permute-start | bytes 3145736 | tf_op jit(solution)/shard_map/projection/ppermute | solution.py:27
  30.5 30.2 %copy-start = (f32[3,256,256]{2,1,0:T(8,128)S(1)}, f32[3,256,256]{2,1,0:T(8,128)}, u32[]{:S(2)}) copy-start(f32[3,256,256]{2,1,0:T(8,128)} %values_ref.1) | copy-start | bytes 2359300
  30.5 30.2 %collective-permute-start.3 = (bf16[3,512,256]{2,1,0:T(8,128)(2,1)}, bf16[3,512,256]{2,1,0:T(8,128)(2,1)}, u32[]{:S(2)}, u32[]{:S(2)}) collective-permute-start(bf16[3,512,256]{2,1,0:T(8,128)(2,1)} %get-tuple-element.36), channel_id=1, source_target_pairs={{0,16},{16,0},{1,17},{17,1},{2,18},{18,2},{3,19},{19,3},{4,20},{20... | collective-permute-start | bytes 2359304 | tf_op jit(solution)/shard_map/projection/ppermute | solution.py:27
  39.6 5.3 %collective-permute-start.4 = (bf16[3,64,256]{2,1,0:T(8,128)(2,1)S(1)}, bf16[3,64,256]{2,1,0:T(8,128)(2,1)S(1)}, u32[]{:S(2)}, u32[]{:S(2)}) collective-permute-start(bf16[3,64,256]{2,1,0:T(8,128)(2,1)S(1)} %get-tuple-element.41), channel_id=1, source_target_pairs={{0,1},{1,0},{2,3},{3,2},{4,5},{5,4},{6,7},{7,6},{8,9},{9,8},{10,11... | collective-permute-start | bytes 294920 | tf_op jit(solution)/shard_map/gather/ppermute | solution.py:27
  45.5 5.4 %collective-permute-start.5 = (bf16[3,64,256]{2,1,0:T(8,128)(2,1)S(1)}, bf16[3,64,256]{2,1,0:T(8,128)(2,1)S(1)}, u32[]{:S(2)}, u32[]{:S(2)}) collective-permute-start(bf16[3,64,256]{2,1,0:T(8,128)(2,1)S(1)} %gather.3.refs_0_), channel_id=1, source_target_pairs={{0,2},{2,4},{4,6},{6,8},{8,10},{10,12},{12,14},{14,0},{1,3},{3,5},... | collective-permute-start | bytes 294920 | tf_op jit(solution)/shard_map/gather/ppermute | solution.py:31
  45.6 5.3 %collective-permute-start.6 = (bf16[3,64,256]{2,1,0:T(8,128)(2,1)S(1)}, bf16[3,64,256]{2,1,0:T(8,128)(2,1)S(1)}, u32[]{:S(2)}, u32[]{:S(2)}) collective-permute-start(bf16[3,64,256]{2,1,0:T(8,128)(2,1)S(1)} %gather.3.refs_0_), channel_id=1, source_target_pairs={{0,14},{2,0},{4,2},{6,4},{8,6},{10,8},{12,10},{14,12},{1,15},{3,1}... | collective-permute-start | bytes 294920 | tf_op jit(solution)/shard_map/gather/ppermute | solution.py:31
  51.0 5.1 %collective-permute-start.7 = (bf16[3,64,256]{2,1,0:T(8,128)(2,1)S(1)}, bf16[3,64,256]{2,1,0:T(8,128)(2,1)S(1)}, u32[]{:S(2)}, u32[]{:S(2)}) collective-permute-start(bf16[3,64,256]{2,1,0:T(8,128)(2,1)S(1)} %collective-permute-done.5.refs_1_), channel_id=1, source_target_pairs={{0,2},{2,4},{4,6},{6,8},{8,10},{10,12},{12,14},{14,0},{1,3},{3,5},... | collective-permute-start | bytes 294920 | tf_op jit(solution)/shard_map/gather/ppermute | solution.py:31
  51.0 5.1 %collective-permute-start.8 = (bf16[3,64,256]{2,1,0:T(8,128)(2,1)S(1)}, bf16[3,64,256]{2,1,0:T(8,128)(2,1)S(1)}, u32[]{:S(2)}, u32[]{:S(2)}) collective-permute-start(bf16[3,64,256]{2,1,0:T(8,128)(2,1)S(1)} %collective-permute-done.6.refs_2_), channel_id=1, source_target_pairs={{0,14},{2,0},{4,2},{6,4},{8,6},{10,8},{12,10},{14,12},{1,15},{3,1}... | collective-permute-start | bytes 294920 | tf_op jit(solution)/shard_map/gather/ppermute | solution.py:31
  56.0 4.7 %collective-permute-start.9 = (bf16[3,64,256]{2,1,0:T(8,128)(2,1)S(1)}, bf16[3,64,256]{2,1,0:T(8,128)(2,1)S(1)}, u32[]{:S(2)}, u32[]{:S(2)}) collective-permute-start(bf16[3,64,256]{2,1,0:T(8,128)(2,1)S(1)} %collective-permute-done.7.refs_3_), channel_id=1, source_target_pairs={{0,2},{2,4},{4,6},{6,8},{8,10},{10,12},{12,14},{14,0},{1,3},{3,5},... | collective-permute-start | bytes 294920 | tf_op jit(solution)/shard_map/gather/ppermute | solution.py:31
  56.1 6.7 %collective-permute-start.10 = (bf16[3,64,256]{2,1,0:T(8,128)(2,1)S(1)}, bf16[3,64,256]{2,1,0:T(8,128)(2,1)S(1)}, u32[]{:S(2)}, u32[]{:S(2)}) collective-permute-start(bf16[3,64,256]{2,1,0:T(8,128)(2,1)S(1)} %collective-permute-done.8.refs_4_), channel_id=1, source_target_pairs={{0,14},{2,0},{4,2},{6,4},{8,6},{10,8},{12,10},{14,12},{1,15},{3,1}... | collective-permute-start | bytes 294920 | tf_op jit(solution)/shard_map/gather/ppermute | solution.py:31
  60.7 4.7 %collective-permute-start.11 = (bf16[3,64,256]{2,1,0:T(8,128)(2,1)S(1)}, bf16[3,64,256]{2,1,0:T(8,128)(2,1)S(1)}, u32[]{:S(2)}, u32[]{:S(2)}) collective-permute-start(bf16[3,64,256]{2,1,0:T(8,128)(2,1)S(1)} %collective-permute-done.9.refs_5_), channel_id=1, source_target_pairs={{0,2},{2,4},{4,6},{6,8},{8,10},{10,12},{12,14},{14,0},{1,3},{3,5},... | collective-permute-start | bytes 294920 | tf_op jit(solution)/shard_map/gather/ppermute | solution.py:31
  67.4 23.7 %all-to-all-start.1 = ((f32[32,24,256]{2,1,0:T(8,128)}), f32[32,24,256]{2,1,0:T(8,128)S(1)}, u32[]{:S(2)}, u32[]{:S(2)}) async-start(f32[32,24,256]{2,1,0:T(8,128)} %bitcast.5), calls=%async_computation.1 | async-start | bytes 1572864 | tf_op jit(solution)/shard_map/coupling/all_to_all | solution.py:269
  76.2 45.3 %copy-start.3 = (bf16[3,1024,256]{2,1,0:T(8,128)(2,1)S(1)}, bf16[3,1024,256]{2,1,0:T(8,128)(2,1)}, u32[]{:S(2)}) copy-start(bf16[3,1024,256]{2,1,0:T(8,128)(2,1)} %refs_5_.1) | copy-start | bytes 4718596
  76.2 30.0 %collective-permute-start.13 = (bf16[3,512,256]{2,1,0:T(8,128)(2,1)S(1)}, bf16[3,512,256]{2,1,0:T(8,128)(2,1)}, u32[]{:S(2)}, u32[]{:S(2)}) collective-permute-start(bf16[3,512,256]{2,1,0:T(8,128)(2,1)S(1)} %get-tuple-element.46.refs_0_), channel_id=1, source_target_pairs={{0,16},{16,0},{1,17},{17,1},{2,18},{18,2},{3,19},{19,3},{4,20},{20... | collective-permute-start | bytes 2359304 | tf_op jit(solution)/shard_map/coupling/ppermute | solution.py:27
  91.9 14.3 %all-to-all-start.2 = ((f32[8,24,256]{2,1,0:T(8,128)}), f32[8,24,256]{2,1,0:T(8,128)S(1)}, u32[]{:S(2)}, u32[]{:S(2)}) async-start(f32[8,24,256]{2,1,0:T(8,128)} %get-tuple-element.47), calls=%async_computation.2 | async-start | bytes 393216 | tf_op jit(solution)/shard_map/coupling/all_to_all | solution.py:272
  95.3 26.2 %collective-permute-start.12 = (bf16[3,512,256]{2,1,0:T(8,128)(2,1)S(1)}, bf16[3,512,256]{2,1,0:T(8,128)(2,1)}, u32[]{:S(2)}, u32[]{:S(2)}) collective-permute-start(bf16[3,512,256]{2,1,0:T(8,128)(2,1)S(1)} %get-tuple-element.46.refs_0_), channel_id=1, source_target_pairs={{0,1},{1,0},{2,3},{3,2},{4,5},{5,4},{6,7},{7,6},{8,9},{9,8},{10,11... | collective-permute-start | bytes 2359304 | tf_op jit(solution)/shard_map/coupling/ppermute | solution.py:27
  106.2 15.3 %collective-permute-start.14 = (bf16[3,512,256]{2,1,0:T(8,128)(2,1)}, bf16[3,512,256]{2,1,0:T(8,128)(2,1)S(1)}, u32[]{:S(2)}, u32[]{:S(2)}) collective-permute-start(bf16[3,512,256]{2,1,0:T(8,128)(2,1)} %collective-permute-done.13.refs_2_), channel_id=1, source_target_pairs={{0,1},{1,0},{2,3},{3,2},{4,5},{5,4},{6,7},{7,6},{8,9},{9,8},{10,11... | collective-permute-start | bytes 2359304 | tf_op jit(solution)/shard_map/coupling/ppermute | solution.py:27

commit v10 on v9

--- a/solution.py
+++ b/solution.py
@@ -197,14 +197,19 @@
     token_ref[...] = jnp.zeros_like(token_ref)
 
 
-def apply_kernel(at_ref, *refs):
-    quarters, (scaled_ref, panels_ref, _, out_ref, block_ref, sems) = refs[:4], refs[4:]
-    count, rows, _ = quarters[0].shape
+def apply_kernel(at_ref, own_ref, last_ref, near_ref, far_ref, scaled_ref, panels_ref, _, out_ref, come_ref, block_ref, come_sems, sems):
+    count, rows, _ = own_ref.shape
     size = rows // RING
+    fetches = []
+    for number, ref in enumerate((near_ref, far_ref)):
+        fetches.append(pltpu.make_async_copy(ref, come_ref.at[number], come_sems.at[number]))
+        fetches[-1].start()
+    core, high = at_ref[0], at_ref[1]
+    order = ((own_ref, high, core), (last_ref, 1 - high, 1 - core), (come_ref.at[0], high, 1 - core), (come_ref.at[1], 1 - high, core))
     copies = []
-    for number, ref in enumerate(quarters):
-        high = at_ref[1] if number < 2 else 1 - at_ref[1]
-        core = at_ref[0] if number % 2 == 0 else 1 - at_ref[0]
+    for number, (ref, of_high, of_core) in enumerate(order):
+        if number >= 2:
+            fetches[number - 2].wait()
         total = None
         for k in range(count):
             rotated = lax.dot_general(ref[k], scaled_ref[k], (((1,), (1,)), ((), ())), preferred_element_type=F32)
@@ -212,7 +217,7 @@
             total = term if total is None else total + term
         block_ref[number] = total.astype(BF16)
         for place in range(RING):
-            target = pl.multiple_of((place * 4 + high * 2 + core) * size, size)
+            target = pl.multiple_of((place * 4 + of_high * 2 + of_core) * size, size)
             source = block_ref.at[number, pl.ds(place * size, size)]
             copies.append(pltpu.make_async_copy(source, out_ref.at[pl.ds(target, size)], sems.at[len(copies)]))
             copies[-1].start()
@@ -220,17 +225,22 @@
         copy.wait()
 
 
-def apply(at, quarters, scaled, panels, token):
-    count, rows, vec = quarters[0].shape
+def apply(at, own, last, near, far, scaled, panels, token):
+    count, rows, vec = own.shape
     width = panels.shape[1]
     return call(
         apply_kernel,
-        (at, *quarters, scaled, panels, token),
-        [SMEM] + [VMEM] * 6 + [ANY],
+        (at, own, last, near, far, scaled, panels, token),
+        [SMEM, VMEM, VMEM, ANY, ANY, VMEM, VMEM, ANY],
         ANY,
         jax.ShapeDtypeStruct((4 * rows, width), BF16),
         8 * count * rows * vec * (vec + width),
-        [pltpu.VMEM((4, rows, width), BF16), pltpu.SemaphoreType.DMA((4 * RING,))],
+        [
+            pltpu.VMEM((2, count, rows, vec), BF16),
+            pltpu.VMEM((4, rows, width), BF16),
+            pltpu.SemaphoreType.DMA((2,)),
+            pltpu.SemaphoreType.DMA((4 * RING,)),
+        ],
         limit=24,
     )
 
@@ -273,12 +283,12 @@
         shapes = [jax.ShapeDtypeStruct(part.shape[1:], BF16), TOKEN]
         scaled, token = call(scale_kernel, (part, token), [VMEM, ANY], [VMEM, VMEM], shapes)
         far, token = lax.optimization_barrier((far, token))
-        quarters = [own, near, far, swap(far, "core")]
+        last = swap(far, "core")
         copies = jnp.broadcast_to(scaled[None], (32,) + scaled.shape)
         scaled = lax.all_to_all(copies, PLANE, 0, 0).reshape(count, vec, vec)
 
     with jax.named_scope("output"):
-        return apply(at, quarters, scaled, in_panels, token)
+        return apply(at, own, last, near, far, scaled, in_panels, token)
 
 
 def solution(mesh):

time: 129 us -> 130 us (level)
  no operation moved by 1% of the time
where the time goes in v10:
time: 130 us
  starting transfers between devices  44.7 us (34%)
  waiting for transfers between devices  38.6 us (30%)
  Pallas kernels  29 us (22%)
  blocking collectives  14.7 us (11%)
  local copies, waits for them, and re-layouts  2.32 us (2%)
    pallas_call x10, Pallas kernels, call(): pl.pallas_call(kernel, in_specs=in_specs, out_specs=out_specs, out_shape=...  29 us
    all_to_all x1, blocking collectives, body(): scaled = lax.all_to_all(copies, PLANE, 0, 0).reshape(count, vec, vec)  14.7 us
    ppermute x8, starting transfers between devices, swap(): return lax.ppermute(x, axis, [(0, 1), (1, 0)])  12.7 us
    all_to_all x1, waiting for transfers between devices, body(): lax.all_to_all(part.reshape(32, -1, vec), PLANE, 0, 0)  12 us
    all_to_all x1, starting transfers between devices, body(): lax.all_to_all(out_pool.reshape(2 * RING, 2 * size, vec), ('z', 'yh'), 0, 0)  11.9 us
    all_to_all x1, waiting for transfers between devices, body(): part = lax.all_to_all(part, 'z', 0, 0)  10.8 us
    ppermute x7, waiting for transfers between devices, shift(): return lax.ppermute(x, 'z', [(i, (i + by) % RING) for i in range(RING)])  9.74 us
    all_to_all x1, starting transfers between devices, body(): lax.all_to_all(part.reshape(32, -1, vec), PLANE, 0, 0)  8.71 us
  transfers between devices with their start and end apart: 18, of which 8 were waited for; matrix products, arithmetic and copies ran while one was open for 0% of the time, Pallas kernels for 15%

profile of v10, /device:TPU:1, one launch (start us, length us, event | category | flops | bytes accessed | tf_op | source)
XLA Modules:
  0.0 129.7 jit_solution(9046673344189004477)
XLA Ops:
  0.0 11.9 %all-to-all-start = ((bf16[16,128,256]{2,1,0:T(8,128)(2,1)}), bf16[16,128,256]{2,1,0:T(8,128)(2,1)S(1)}, u32[]{:S(2)}, u32[]{:S(2)}) async-start(bf16[16,128,256]{2,1,0:T(8,128)(2,1)} %bitcast.8), calls=%async_computation | async-start | bytes 2097152 | tf_op jit(solution)/shard_map/scatter/all_to_all | solution.py:256
  11.9 0.1 concatenate.3.at_ref
  12.0 2.2 %copy-done.1 = bf16[2048,1024]{1,0:T(8,128)(2,1)S(1)} copy-done((bf16[2048,1024]{1,0:T(8,128)(2,1)S(1)}, bf16[2048,1024]{1,0:T(8,128)(2,1)}, u32[]{:S(2)}) %copy-start.1) | copy-done | bytes 4194328
  14.2 6.7 %projection.5 = (f32[1024,256]{1,0:T(8,128)S(1)}, f32[1024,256]{1,0:T(8,128)S(1)}, f32[1024,256]{1,0:T(8,128)S(1)}, f32[8,128]{1,0:T(8,128)}) custom-call(s32[7]{0:T(128)S(1)} %concatenate.3.at_ref, bf16[2048,1024]{1,0:T(8,128)(2,1)S(1)} %copy-done.1, bf16[3,1024,256]{2,1,0:T(8,128)(2,1)S(1)} %copy-done.2), custom_call_target="tpu_custom_call" | custom-call | flops 1610612736 | bytes 5767196 | tf_op jit(solution)/shard_map/projection/pallas_call | solution.py:36
  20.9 1.0 collective-permute-start
  21.9 0.1 collective-permute-start.1
  22.0 0.4 collective-permute-start.2
  22.4 6.3 %projection.4 = (f32[1024,256]{1,0:T(8,128)S(1)}, f32[1024,256]{1,0:T(8,128)S(1)}, f32[1024,256]{1,0:T(8,128)S(1)}, f32[8,128]{1,0:T(8,128)S(1)}) custom-call(s32[7]{0:T(128)S(1)} %concatenate.3.at_ref, bf16[2048,1024]{1,0:T(8,128)(2,1)S(1)} %copy-done.1, bf16[3,1024,256]{2,1,0:T(8,128)(2,1)S(1)} %copy-done.2), custom_call_target="tpu_custom_call" | custom-call | flops 1610612736 | bytes 5767196 | tf_op jit(solution)/shard_map/projection/pallas_call | solution.py:36
  28.7 0.0 collective-permute-done.refs_3_
  28.8 0.0 collective-permute-done.1.refs_4_
  28.8 0.0 collective-permute-done.2.refs_5_
  28.8 1.7 %projection.6 = (f32[3,512,256]{2,1,0:T(8,128)S(1)}, bf16[3,512,256]{2,1,0:T(8,128)(2,1)}, f32[8,128]{1,0:T(8,128)S(1)}) custom-call(s32[7]{0:T(128)S(1)} %concatenate.3.at_ref, f32[1024,256]{1,0:T(8,128)S(1)} %get-tuple-element.29.refs_0_, f32[1024,256]{1,0:T(8,128)S(1)} %get-tuple-element.30.refs_1_, f32[1024,256]{1,0:T(8,128)S(1)} %get-tuple-element.31.refs_2_, ...), custom_call_target="tpu_custom_call" | custom-call | bytes 6291484 | tf_op jit(solution)/shard_map/projection/pallas_call | solution.py:36
  30.5 3.2 %collective-permute-start.3 = (bf16[3,512,256]{2,1,0:T(8,128)(2,1)}, bf16[3,512,256]{2,1,0:T(8,128)(2,1)}, u32[]{:S(2)}, u32[]{:S(2)}) collective-permute-start(bf16[3,512,256]{2,1,0:T(8,128)(2,1)} %get-tuple-element.36), channel_id=1, source_target_pairs={{0,16},{16,0},{1,17},{17,1},{2,18},{18,2},{3,19},{19,3},{4,20},{20... | collective-permute-start | bytes 2359304 | tf_op jit(solution)/shard_map/projection/ppermute | solution.py:27
  33.7 5.1 %all-to-all-done.all_ref = bf16[16,128,256]{2,1,0:T(8,128)(2,1)S(1)} async-done(((bf16[16,128,256]{2,1,0:T(8,128)(2,1)}), bf16[16,128,256]{2,1,0:T(8,128)(2,1)S(1)}, u32[]{:S(2)}, u32[]{:S(2)}) %all-to-all-start) | async-done | bytes 1048608 | tf_op jit(solution)/shard_map/scatter/all_to_all | solution.py:256
  38.7 0.9 gather.2
  39.6 4.4 %collective-permute-start.4 = (bf16[3,64,256]{2,1,0:T(8,128)(2,1)S(1)}, bf16[3,64,256]{2,1,0:T(8,128)(2,1)S(1)}, u32[]{:S(2)}, u32[]{:S(2)}) collective-permute-start(bf16[3,64,256]{2,1,0:T(8,128)(2,1)S(1)} %get-tuple-element.41), channel_id=1, source_target_pairs={{0,1},{1,0},{2,3},{3,2},{4,5},{5,4},{6,7},{7,6},{8,9},{9,8},{10,11... | collective-permute-start | bytes 294920 | tf_op jit(solution)/shard_map/gather/ppermute | solution.py:27
  44.0 0.9 collective-permute-done.4.other_ref
  45.0 0.6 gather.3.refs_0_
  45.5 0.1 collective-permute-start.5
  45.6 2.7 %collective-permute-start.6 = (bf16[3,64,256]{2,1,0:T(8,128)(2,1)S(1)}, bf16[3,64,256]{2,1,0:T(8,128)(2,1)S(1)}, u32[]{:S(2)}, u32[]{:S(2)}) collective-permute-start(bf16[3,64,256]{2,1,0:T(8,128)(2,1)S(1)} %gather.3.refs_0_), channel_id=1, source_target_pairs={{0,14},{2,0},{4,2},{6,4},{8,6},{10,8},{12,10},{14,12},{1,15},{3,1}... | collective-permute-start | bytes 294920 | tf_op jit(solution)/shard_map/gather/ppermute | solution.py:31
  48.3 2.7 %collective-permute-done.5.refs_1_ = bf16[3,64,256]{2,1,0:T(8,128)(2,1)S(1)} collective-permute-done((bf16[3,64,256]{2,1,0:T(8,128)(2,1)S(1)}, bf16[3,64,256]{2,1,0:T(8,128)(2,1)S(1)}, u32[]{:S(2)}, u32[]{:S(2)}) %collective-permute-start.5) | collective-permute-done | bytes 98336 | tf_op jit(solution)/shard_map/gather/ppermute | solution.py:31
  51.0 0.0 collective-permute-start.7
  51.0 0.0 collective-permute-done.6.refs_2_
  51.0 2.7 %collective-permute-start.8 = (bf16[3,64,256]{2,1,0:T(8,128)(2,1)S(1)}, bf16[3,64,256]{2,1,0:T(8,128)(2,1)S(1)}, u32[]{:S(2)}, u32[]{:S(2)}) collective-permute-start(bf16[3,64,256]{2,1,0:T(8,128)(2,1)S(1)} %collective-permute-done.6.refs_2_), channel_id=1, source_target_pairs={{0,14},{2,0},{4,2},{6,4},{8,6},{10,8},{12,10},{14,12},{1,15},{3,1}... | collective-permute-start | bytes 294920 | tf_op jit(solution)/shard_map/gather/ppermute | solution.py:31
  53.6 2.4 %collective-permute-done.7.refs_3_ = bf16[3,64,256]{2,1,0:T(8,128)(2,1)S(1)} collective-permute-done((bf16[3,64,256]{2,1,0:T(8,128)(2,1)S(1)}, bf16[3,64,256]{2,1,0:T(8,128)(2,1)S(1)}, u32[]{:S(2)}, u32[]{:S(2)}) %collective-permute-start.7) | collective-permute-done | bytes 98336 | tf_op jit(solution)/shard_map/gather/ppermute | solution.py:31
  56.0 0.0 collective-permute-start.9
  56.0 0.0 collective-permute-done.8.refs_4_
  56.0 2.7 %collective-permute-start.10 = (bf16[3,64,256]{2,1,0:T(8,128)(2,1)S(1)}, bf16[3,64,256]{2,1,0:T(8,128)(2,1)S(1)}, u32[]{:S(2)}, u32[]{:S(2)}) collective-permute-start(bf16[3,64,256]{2,1,0:T(8,128)(2,1)S(1)} %collective-permute-done.8.refs_4_), channel_id=1, source_target_pairs={{0,14},{2,0},{4,2},{6,4},{8,6},{10,8},{12,10},{14,12},{1,15},{3,1}... | collective-permute-start | bytes 294920 | tf_op jit(solution)/shard_map/gather/ppermute | solution.py:31
  58.7 2.0 %collective-permute-done.9.refs_5_ = bf16[3,64,256]{2,1,0:T(8,128)(2,1)S(1)} collective-permute-done((bf16[3,64,256]{2,1,0:T(8,128)(2,1)S(1)}, bf16[3,64,256]{2,1,0:T(8,128)(2,1)S(1)}, u32[]{:S(2)}, u32[]{:S(2)}) %collective-permute-start.9) | collective-permute-done | bytes 98336 | tf_op jit(solution)/shard_map/gather/ppermute | solution.py:31
  60.7 0.0 collective-permute-start.11
  60.7 0.0 collective-permute-done.3.came_ref
  60.7 2.0 %projection.7 = (bf16[3,512,512]{2,1,0:T(8,128)(2,1)S(1)}, f32[24,256]{1,0:T(8,128)S(1)}) custom-call(s32[7]{0:T(128)S(1)} %concatenate.3.at_ref, f32[3,256,256]{2,1,0:T(8,128)S(1)} %copy-done, f32[3,512,256]{2,1,0:T(8,128)S(1)} %get-tuple-element.35.kept_ref, bf16[3,512,256]{2,1,0:T(8,128)(2,1)} %collective-permute-done.3.came_ref), custom_call_target="tpu_custom_call" | custom-call | bytes 3145756 | tf_op jit(solution)/shard_map/projection/pallas_call | solution.py:36
  62.7 2.7 %collective-permute-done.11.refs_7_ = bf16[3,64,256]{2,1,0:T(8,128)(2,1)S(1)} collective-permute-done((bf16[3,64,256]{2,1,0:T(8,128)(2,1)S(1)}, bf16[3,64,256]{2,1,0:T(8,128)(2,1)S(1)}, u32[]{:S(2)}, u32[]{:S(2)}) %collective-permute-start.11) | collective-permute-done | bytes 98336 | tf_op jit(solution)/shard_map/gather/ppermute | solution.py:31
  65.4 2.0 %coupling.3 = (f32[768,256]{1,0:T(8,128)}, bf16[3,512,256]{2,1,0:T(8,128)(2,1)S(1)}) custom-call(s32[7]{0:T(128)S(1)} %concatenate.3.at_ref, bf16[3,512,512]{2,1,0:T(8,128)(2,1)S(1)} %get-tuple-element.37.terms_ref, bf16[3,64,256]{2,1,0:T(8,128)(2,1)S(1)} %gather.3.refs_0_, bf16[3,64,256]{2,1,0:T(8,128)(2,1)S(1)} %collective-permute-done.5.refs_1_, ...), custom_call_target="tpu_custom_call" | custom-call | flops 402653184 | bytes 2359324 | tf_op jit(solution)/shard_map/coupling/pallas_call | solution.py:36
  67.4 8.7 %all-to-all-start.1 = ((f32[32,24,256]{2,1,0:T(8,128)}), f32[32,24,256]{2,1,0:T(8,128)S(1)}, u32[]{:S(2)}, u32[]{:S(2)}) async-start(f32[32,24,256]{2,1,0:T(8,128)} %bitcast.5), calls=%async_computation.1 | async-start | bytes 1572864 | tf_op jit(solution)/shard_map/coupling/all_to_all | solution.py:279
  76.1 0.0 copy-start.3
  76.2 3.0 %collective-permute-start.12 = (bf16[3,512,256]{2,1,0:T(8,128)(2,1)S(1)}, bf16[3,512,256]{2,1,0:T(8,128)(2,1)}, u32[]{:S(2)}, u32[]{:S(2)}) collective-permute-start(bf16[3,512,256]{2,1,0:T(8,128)(2,1)S(1)} %get-tuple-element.50.own_ref), channel_id=1, source_target_pairs={{0,16},{16,0},{1,17},{17,1},{2,18},{18,2},{3,19},{19,3},{4,20},{20... | collective-permute-start | bytes 2359304 | tf_op jit(solution)/shard_map/coupling/ppermute | solution.py:27
  79.1 12.0 %all-to-all-done.1.part_ref = f32[32,24,256]{2,1,0:T(8,128)S(1)} async-done(((f32[32,24,256]{2,1,0:T(8,128)}), f32[32,24,256]{2,1,0:T(8,128)S(1)}, u32[]{:S(2)}, u32[]{:S(2)}) %all-to-all-start.1) | async-done | bytes 786464 | tf_op jit(solution)/shard_map/coupling/all_to_all | solution.py:279
  91.1 0.7 coupling.4
  91.9 3.4 %all-to-all-start.2 = ((f32[8,24,256]{2,1,0:T(8,128)}), f32[8,24,256]{2,1,0:T(8,128)S(1)}, u32[]{:S(2)}, u32[]{:S(2)}) async-start(f32[8,24,256]{2,1,0:T(8,128)} %get-tuple-element.45), calls=%async_computation.2 | async-start | bytes 393216 | tf_op jit(solution)/shard_map/coupling/all_to_all | solution.py:282
  95.3 0.1 collective-permute-start.14
  95.4 10.8 %all-to-all-done.2.parts_ref = f32[8,24,256]{2,1,0:T(8,128)S(1)} async-done(((f32[8,24,256]{2,1,0:T(8,128)}), f32[8,24,256]{2,1,0:T(8,128)S(1)}, u32[]{:S(2)}, u32[]{:S(2)}) %all-to-all-start.2) | async-done | bytes 196640 | tf_op jit(solution)/shard_map/coupling/all_to_all | solution.py:282
  106.2 0.0 collective-permute-done.12.far_ref
  106.2 0.5 collective-permute-start.13
  106.7 14.7 %all_to_all.20 = bf16[32,24,256]{2,1,0:T(8,128)(2,1)S(1)} all-to-all(bf16[32,24,256]{2,1,0:T(8,128)(2,1)S(1)} %broadcast_in_dim.2), channel_id=1, replica_groups=mesh['yl'=2,'x'=4,'yh'=2,'z'=8,'core'=2] {'core','yl','x','yh'}, dimensions={0} | all-to-all | bytes 786432 | tf_op jit(solution)/shard_map/coupling/all_to_all | solution.py:288
  121.4 0.0 collective-permute-done.14.near_ref
  121.4 0.0 collective-permute-done.13.last_ref
  121.5 8.1 %output.1 = bf16[2048,1024]{1,0:T(8,128)(2,1)} custom-call(s32[7]{0:T(128)S(1)} %concatenate.3.at_ref, bf16[3,512,256]{2,1,0:T(8,128)(2,1)S(1)} %get-tuple-element.50.own_ref, bf16[3,512,256]{2,1,0:T(8,128)(2,1)S(1)} %collective-permute-done.13.last_ref, bf16[3,512,256]{2,1,0:T(8,128)(2,1)} %collective-permute-done.14.near_ref, ...), custom_call_target="tpu_custom_call" | custom-call | flops 4026531840 | bytes 5115932 | tf_op jit(solution)/shard_map/output/pallas_call | solution.py:36
  (11 shorter events, 0.1 us)
Async XLA Ops:
  0.0 11.9 %copy-start.4 = (s32[3]{0:T(128)S(1)}, s32[3]{0:T(128)}, u32[]{:S(2)}) copy-start(s32[3]{0:T(128)} %param.9) | copy-start | bytes 40
  0.0 12.0 %copy-start.2 = (bf16[3,1024,256]{2,1,0:T(8,128)(2,1)S(1)}, bf16[3,1024,256]{2,1,0:T(8,128)(2,1)}, u32[]{:S(2)}) copy-start(bf16[3,1024,256]{2,1,0:T(8,128)(2,1)} %panels_ref.5) | copy-start | bytes 4718596
  0.0 38.7 %all-to-all-start = ((bf16[16,128,256]{2,1,0:T(8,128)(2,1)}), bf16[16,128,256]{2,1,0:T(8,128)(2,1)S(1)}, u32[]{:S(2)}, u32[]{:S(2)}) async-start(bf16[16,128,256]{2,1,0:T(8,128)(2,1)} %bitcast.8), calls=%async_computation | async-start | bytes 2097152 | tf_op jit(solution)/shard_map/scatter/all_to_all | solution.py:256
  12.0 2.2 %copy-start.1 = (bf16[2048,1024]{1,0:T(8,128)(2,1)S(1)}, bf16[2048,1024]{1,0:T(8,128)(2,1)}, u32[]{:S(2)}) copy-start(bf16[2048,1024]{1,0:T(8,128)(2,1)} %gradient_ref.3) | copy-start | bytes 12582916
  20.9 7.8 %collective-permute-start = (f32[1024,256]{1,0:T(8,128)S(1)}, f32[1024,256]{1,0:T(8,128)S(1)}, u32[]{:S(2)}, u32[]{:S(2)}) collective-permute-start(f32[1024,256]{1,0:T(8,128)S(1)} %get-tuple-element.32), channel_id=1, source_target_pairs={{0,1},{1,0},{2,3},{3,2},{4,5},{5,4},{6,7},{7,6},{8,9},{9,8},{10,11... | collective-permute-start | bytes 3145736 | tf_op jit(solution)/shard_map/projection/ppermute | solution.py:27
  21.9 6.8 %collective-permute-start.1 = (f32[1024,256]{1,0:T(8,128)S(1)}, f32[1024,256]{1,0:T(8,128)S(1)}, u32[]{:S(2)}, u32[]{:S(2)}) collective-permute-start(f32[1024,256]{1,0:T(8,128)S(1)} %get-tuple-element.33), channel_id=1, source_target_pairs={{0,1},{1,0},{2,3},{3,2},{4,5},{5,4},{6,7},{7,6},{8,9},{9,8},{10,11... | collective-permute-start | bytes 3145736 | tf_op jit(solution)/shard_map/projection/ppermute | solution.py:27
  22.0 6.7 %collective-permute-start.2 = (f32[1024,256]{1,0:T(8,128)S(1)}, f32[1024,256]{1,0:T(8,128)S(1)}, u32[]{:S(2)}, u32[]{:S(2)}) collective-permute-start(f32[1024,256]{1,0:T(8,128)S(1)} %get-tuple-element.34), channel_id=1, source_target_pairs={{0,1},{1,0},{2,3},{3,2},{4,5},{5,4},{6,7},{7,6},{8,9},{9,8},{10,11... | collective-permute-start | bytes 3145736 | tf_op jit(solution)/shard_map/projection/ppermute | solution.py:27
  30.5 30.2 %copy-start = (f32[3,256,256]{2,1,0:T(8,128)S(1)}, f32[3,256,256]{2,1,0:T(8,128)}, u32[]{:S(2)}) copy-start(f32[3,256,256]{2,1,0:T(8,128)} %values_ref.1) | copy-start | bytes 2359300
  30.5 30.2 %collective-permute-start.3 = (bf16[3,512,256]{2,1,0:T(8,128)(2,1)}, bf16[3,512,256]{2,1,0:T(8,128)(2,1)}, u32[]{:S(2)}, u32[]{:S(2)}) collective-permute-start(bf16[3,512,256]{2,1,0:T(8,128)(2,1)} %get-tuple-element.36), channel_id=1, source_target_pairs={{0,16},{16,0},{1,17},{17,1},{2,18},{18,2},{3,19},{19,3},{4,20},{20... | collective-permute-start | bytes 2359304 | tf_op jit(solution)/shard_map/projection/ppermute | solution.py:27
  39.6 5.3 %collective-permute-start.4 = (bf16[3,64,256]{2,1,0:T(8,128)(2,1)S(1)}, bf16[3,64,256]{2,1,0:T(8,128)(2,1)S(1)}, u32[]{:S(2)}, u32[]{:S(2)}) collective-permute-start(bf16[3,64,256]{2,1,0:T(8,128)(2,1)S(1)} %get-tuple-element.41), channel_id=1, source_target_pairs={{0,1},{1,0},{2,3},{3,2},{4,5},{5,4},{6,7},{7,6},{8,9},{9,8},{10,11... | collective-permute-start | bytes 294920 | tf_op jit(solution)/shard_map/gather/ppermute | solution.py:27
  45.5 5.4 %collective-permute-start.5 = (bf16[3,64,256]{2,1,0:T(8,128)(2,1)S(1)}, bf16[3,64,256]{2,1,0:T(8,128)(2,1)S(1)}, u32[]{:S(2)}, u32[]{:S(2)}) collective-permute-start(bf16[3,64,256]{2,1,0:T(8,128)(2,1)S(1)} %gather.3.refs_0_), channel_id=1, source_target_pairs={{0,2},{2,4},{4,6},{6,8},{8,10},{10,12},{12,14},{14,0},{1,3},{3,5},... | collective-permute-start | bytes 294920 | tf_op jit(solution)/shard_map/gather/ppermute | solution.py:31
  45.6 5.3 %collective-permute-start.6 = (bf16[3,64,256]{2,1,0:T(8,128)(2,1)S(1)}, bf16[3,64,256]{2,1,0:T(8,128)(2,1)S(1)}, u32[]{:S(2)}, u32[]{:S(2)}) collective-permute-start(bf16[3,64,256]{2,1,0:T(8,128)(2,1)S(1)} %gather.3.refs_0_), channel_id=1, source_target_pairs={{0,14},{2,0},{4,2},{6,4},{8,6},{10,8},{12,10},{14,12},{1,15},{3,1}... | collective-permute-start | bytes 294920 | tf_op jit(solution)/shard_map/gather/ppermute | solution.py:31
  51.0 5.1 %collective-permute-start.7 = (bf16[3,64,256]{2,1,0:T(8,128)(2,1)S(1)}, bf16[3,64,256]{2,1,0:T(8,128)(2,1)S(1)}, u32[]{:S(2)}, u32[]{:S(2)}) collective-permute-start(bf16[3,64,256]{2,1,0:T(8,128)(2,1)S(1)} %collective-permute-done.5.refs_1_), channel_id=1, source_target_pairs={{0,2},{2,4},{4,6},{6,8},{8,10},{10,12},{12,14},{14,0},{1,3},{3,5},... | collective-permute-start | bytes 294920 | tf_op jit(solution)/shard_map/gather/ppermute | solution.py:31
  51.0 5.1 %collective-permute-start.8 = (bf16[3,64,256]{2,1,0:T(8,128)(2,1)S(1)}, bf16[3,64,256]{2,1,0:T(8,128)(2,1)S(1)}, u32[]{:S(2)}, u32[]{:S(2)}) collective-permute-start(bf16[3,64,256]{2,1,0:T(8,128)(2,1)S(1)} %collective-permute-done.6.refs_2_), channel_id=1, source_target_pairs={{0,14},{2,0},{4,2},{6,4},{8,6},{10,8},{12,10},{14,12},{1,15},{3,1}... | collective-permute-start | bytes 294920 | tf_op jit(solution)/shard_map/gather/ppermute | solution.py:31
  56.0 4.7 %collective-permute-start.9 = (bf16[3,64,256]{2,1,0:T(8,128)(2,1)S(1)}, bf16[3,64,256]{2,1,0:T(8,128)(2,1)S(1)}, u32[]{:S(2)}, u32[]{:S(2)}) collective-permute-start(bf16[3,64,256]{2,1,0:T(8,128)(2,1)S(1)} %collective-permute-done.7.refs_3_), channel_id=1, source_target_pairs={{0,2},{2,4},{4,6},{6,8},{8,10},{10,12},{12,14},{14,0},{1,3},{3,5},... | collective-permute-start | bytes 294920 | tf_op jit(solution)/shard_map/gather/ppermute | solution.py:31
  56.0 6.7 %collective-permute-start.10 = (bf16[3,64,256]{2,1,0:T(8,128)(2,1)S(1)}, bf16[3,64,256]{2,1,0:T(8,128)(2,1)S(1)}, u32[]{:S(2)}, u32[]{:S(2)}) collective-permute-start(bf16[3,64,256]{2,1,0:T(8,128)(2,1)S(1)} %collective-permute-done.8.refs_4_), channel_id=1, source_target_pairs={{0,14},{2,0},{4,2},{6,4},{8,6},{10,8},{12,10},{14,12},{1,15},{3,1}... | collective-permute-start | bytes 294920 | tf_op jit(solution)/shard_map/gather/ppermute | solution.py:31
  60.7 4.7 %collective-permute-start.11 = (bf16[3,64,256]{2,1,0:T(8,128)(2,1)S(1)}, bf16[3,64,256]{2,1,0:T(8,128)(2,1)S(1)}, u32[]{:S(2)}, u32[]{:S(2)}) collective-permute-start(bf16[3,64,256]{2,1,0:T(8,128)(2,1)S(1)} %collective-permute-done.9.refs_5_), channel_id=1, source_target_pairs={{0,2},{2,4},{4,6},{6,8},{8,10},{10,12},{12,14},{14,0},{1,3},{3,5},... | collective-permute-start | bytes 294920 | tf_op jit(solution)/shard_map/gather/ppermute | solution.py:31
  67.4 23.7 %all-to-all-start.1 = ((f32[32,24,256]{2,1,0:T(8,128)}), f32[32,24,256]{2,1,0:T(8,128)S(1)}, u32[]{:S(2)}, u32[]{:S(2)}) async-start(f32[32,24,256]{2,1,0:T(8,128)} %bitcast.5), calls=%async_computation.1 | async-start | bytes 1572864 | tf_op jit(solution)/shard_map/coupling/all_to_all | solution.py:279
  76.1 45.3 %copy-start.3 = (bf16[3,1024,256]{2,1,0:T(8,128)(2,1)S(1)}, bf16[3,1024,256]{2,1,0:T(8,128)(2,1)}, u32[]{:S(2)}) copy-start(bf16[3,1024,256]{2,1,0:T(8,128)(2,1)} %panels_ref.5) | copy-start | bytes 4718596
  76.2 30.0 %collective-permute-start.12 = (bf16[3,512,256]{2,1,0:T(8,128)(2,1)S(1)}, bf16[3,512,256]{2,1,0:T(8,128)(2,1)}, u32[]{:S(2)}, u32[]{:S(2)}) collective-permute-start(bf16[3,512,256]{2,1,0:T(8,128)(2,1)S(1)} %get-tuple-element.50.own_ref), channel_id=1, source_target_pairs={{0,16},{16,0},{1,17},{17,1},{2,18},{18,2},{3,19},{19,3},{4,20},{20... | collective-permute-start | bytes 2359304 | tf_op jit(solution)/shard_map/coupling/ppermute | solution.py:27
  91.9 14.3 %all-to-all-start.2 = ((f32[8,24,256]{2,1,0:T(8,128)}), f32[8,24,256]{2,1,0:T(8,128)S(1)}, u32[]{:S(2)}, u32[]{:S(2)}) async-start(f32[8,24,256]{2,1,0:T(8,128)} %get-tuple-element.45), calls=%async_computation.2 | async-start | bytes 393216 | tf_op jit(solution)/shard_map/coupling/all_to_all | solution.py:282
  95.3 26.2 %collective-permute-start.14 = (bf16[3,512,256]{2,1,0:T(8,128)(2,1)S(1)}, bf16[3,512,256]{2,1,0:T(8,128)(2,1)}, u32[]{:S(2)}, u32[]{:S(2)}) collective-permute-start(bf16[3,512,256]{2,1,0:T(8,128)(2,1)S(1)} %get-tuple-element.50.own_ref), channel_id=1, source_target_pairs={{0,1},{1,0},{2,3},{3,2},{4,5},{5,4},{6,7},{7,6},{8,9},{9,8},{10,11... | collective-permute-start | bytes 2359304 | tf_op jit(solution)/shard_map/coupling/ppermute | solution.py:27
  106.2 15.3 %collective-permute-start.13 = (bf16[3,512,256]{2,1,0:T(8,128)(2,1)}, bf16[3,512,256]{2,1,0:T(8,128)(2,1)S(1)}, u32[]{:S(2)}, u32[]{:S(2)}) collective-permute-start(bf16[3,512,256]{2,1,0:T(8,128)(2,1)} %collective-permute-done.12.far_ref), channel_id=1, source_target_pairs={{0,1},{1,0},{2,3},{3,2},{4,5},{5,4},{6,7},{7,6},{8,9},{9,8},{10,11... | collective-permute-start | bytes 2359304 | tf_op jit(solution)/shard_map/coupling/ppermute | solution.py:27

commit v11 on v8

--- a/solution.py
+++ b/solution.py
@@ -201,13 +201,14 @@
     size = rows // RING
     high = at_ref[1] if near else 1 - at_ref[1]
     copies = []
-    for number, (ref, core) in enumerate(((own_ref, at_ref[0]), (other_ref, 1 - at_ref[0]))):
-        total = None
-        for k in range(count):
-            rotated = lax.dot_general(ref[k], scaled_ref[k], (((1,), (1,)), ((), ())), preferred_element_type=F32)
-            term = lax.dot_general(rotated.astype(BF16), panels_ref[k], (((1,), (1,)), ((), ())), preferred_element_type=F32)
-            total = term if total is None else total + term
-        block_ref[number] = total.astype(BF16)
+    total = None
+    for k in range(count):
+        parts = [lax.dot_general(ref[k], scaled_ref[k], (((1,), (1,)), ((), ())), preferred_element_type=F32) for ref in (own_ref, other_ref)]
+        rotated = jnp.concatenate(parts, axis=0).astype(BF16)
+        term = lax.dot_general(rotated, panels_ref[k], (((1,), (1,)), ((), ())), preferred_element_type=F32)
+        total = term if total is None else total + term
+    for number, core in enumerate((at_ref[0], 1 - at_ref[0])):
+        block_ref[number] = total[number * rows : (number + 1) * rows].astype(BF16)
         for place in range(RING):
             target = pl.multiple_of((place * 4 + high * 2 + core) * size, size)
             source = block_ref.at[number, pl.ds(place * size, size)]

time: 129 us -> 129 us (level)
  no operation moved by 1% of the time
where the time goes in v11:
time: 129 us
  starting transfers between devices  37.7 us (29%)
  waiting for transfers between devices  32.8 us (25%)
  Pallas kernels  28.9 us (22%)
  blocking collectives  23 us (18%)
  local copies, waits for them, and re-layouts  6.24 us (5%)
    all_to_all x1, blocking collectives, body(): lax.all_to_all(part.reshape(32, -1, vec), PLANE, 0, 0)  23 us
    pallas_call x9, Pallas kernels, call(): pl.pallas_call(kernel, in_specs=in_specs, out_specs=out_specs, out_shape=...  20.1 us
    all_to_all x1, starting transfers between devices, body(): lax.all_to_all(out_pool.reshape(2 * RING, 2 * size, vec), ('z', 'yh'), 0, 0)  11.7 us
    all_to_all x1, waiting for transfers between devices, body(): part = lax.all_to_all(part, 'z', 0, 0)  10.3 us
    ppermute x8, starting transfers between devices, swap(): return lax.ppermute(x, axis, [(0, 1), (1, 0)])  10.2 us
    all_to_all x1, waiting for transfers between devices, body(): scaled = lax.all_to_all(copies, PLANE, 0, 0).reshape(count, vec, vec)  9.98 us
    pallas_call x2, Pallas kernels, apply(): pl.pallas_call(functools.partial(apply_kernel, near), in_specs=[SMEM, VME...  8.79 us
    ppermute x7, waiting for transfers between devices, shift(): return lax.ppermute(x, 'z', [(i, (i + by) % RING) for i in range(RING)])  8.49 us
  transfers between devices with their start and end apart: 18, of which 8 were waited for; matrix products, arithmetic and copies ran while one was open for 1% of the time, Pallas kernels for 18%

profile of v11, /device:TPU:1, one launch (start us, length us, event | category | flops | bytes accessed | tf_op | source)
XLA Modules:
  0.0 128.9 jit_solution(5898273807781348742)
XLA Ops:
  0.0 11.7 %all-to-all-start = ((bf16[16,128,256]{2,1,0:T(8,128)(2,1)}), bf16[16,128,256]{2,1,0:T(8,128)(2,1)S(1)}, u32[]{:S(2)}, u32[]{:S(2)}) async-start(bf16[16,128,256]{2,1,0:T(8,128)(2,1)} %bitcast.13), calls=%async_computation | async-start | bytes 2097152 | tf_op jit(solution)/shard_map/scatter/all_to_all | solution.py:244
  11.8 0.7 concatenate.3.at_ref
  12.5 1.4 %copy-done = bf16[3,1024,256]{2,1,0:T(8,128)(2,1)S(1)} copy-done((bf16[3,1024,256]{2,1,0:T(8,128)(2,1)S(1)}, bf16[3,1024,256]{2,1,0:T(8,128)(2,1)}, u32[]{:S(2)}) %copy-start) | copy-done | bytes 1572888
  13.9 2.2 %copy-done.3 = bf16[2048,1024]{1,0:T(8,128)(2,1)S(1)} copy-done((bf16[2048,1024]{1,0:T(8,128)(2,1)S(1)}, bf16[2048,1024]{1,0:T(8,128)(2,1)}, u32[]{:S(2)}) %copy-start.3) | copy-done | bytes 4194328
  16.1 6.6 %projection.5 = (f32[1024,256]{1,0:T(8,128)S(1)}, f32[1024,256]{1,0:T(8,128)S(1)}, f32[1024,256]{1,0:T(8,128)S(1)}, f32[8,128]{1,0:T(8,128)}) custom-call(s32[7]{0:T(128)S(1)} %concatenate.3.at_ref, bf16[2048,1024]{1,0:T(8,128)(2,1)S(1)} %copy-done.3, bf16[3,1024,256]{2,1,0:T(8,128)(2,1)S(1)} %copy-done), custom_call_target="tpu_custom_call" | custom-call | flops 1610612736 | bytes 5767196 | tf_op jit(solution)/shard_map/projection/pallas_call | solution.py:36
  22.8 1.0 collective-permute-start
  23.8 0.1 collective-permute-start.1
  23.9 0.4 collective-permute-start.2
  24.3 6.3 %projection.4 = (f32[1024,256]{1,0:T(8,128)S(1)}, f32[1024,256]{1,0:T(8,128)S(1)}, f32[1024,256]{1,0:T(8,128)S(1)}, f32[8,128]{1,0:T(8,128)S(1)}) custom-call(s32[7]{0:T(128)S(1)} %concatenate.3.at_ref, bf16[2048,1024]{1,0:T(8,128)(2,1)S(1)} %copy-done.3, bf16[3,1024,256]{2,1,0:T(8,128)(2,1)S(1)} %copy-done), custom_call_target="tpu_custom_call" | custom-call | flops 1610612736 | bytes 5767196 | tf_op jit(solution)/shard_map/projection/pallas_call | solution.py:36
  30.6 0.0 collective-permute-done.1.refs_4_
  30.6 0.0 collective-permute-done.2.refs_5_
  30.6 1.7 %projection.6 = (f32[3,512,256]{2,1,0:T(8,128)S(1)}, bf16[3,512,256]{2,1,0:T(8,128)(2,1)}, f32[8,128]{1,0:T(8,128)S(1)}) custom-call(s32[7]{0:T(128)S(1)} %concatenate.3.at_ref, f32[1024,256]{1,0:T(8,128)S(1)} %get-tuple-element.27.refs_0_, f32[1024,256]{1,0:T(8,128)S(1)} %get-tuple-element.28.refs_1_, f32[1024,256]{1,0:T(8,128)S(1)} %get-tuple-element.29.refs_2_, ...), custom_call_target="tpu_custom_call" | custom-call | bytes 6291484 | tf_op jit(solution)/shard_map/projection/pallas_call | solution.py:36
  32.3 3.2 %collective-permute-start.3 = (bf16[3,512,256]{2,1,0:T(8,128)(2,1)}, bf16[3,512,256]{2,1,0:T(8,128)(2,1)}, u32[]{:S(2)}, u32[]{:S(2)}) collective-permute-start(bf16[3,512,256]{2,1,0:T(8,128)(2,1)} %get-tuple-element.34), channel_id=1, source_target_pairs={{0,16},{16,0},{1,17},{17,1},{2,18},{18,2},{3,19},{19,3},{4,20},{20... | collective-permute-start | bytes 2359304 | tf_op jit(solution)/shard_map/projection/ppermute | solution.py:27
  35.5 3.1 %all-to-all-done.all_ref = bf16[16,128,256]{2,1,0:T(8,128)(2,1)S(1)} async-done(((bf16[16,128,256]{2,1,0:T(8,128)(2,1)}), bf16[16,128,256]{2,1,0:T(8,128)(2,1)S(1)}, u32[]{:S(2)}, u32[]{:S(2)}) %all-to-all-start) | async-done | bytes 1048608 | tf_op jit(solution)/shard_map/scatter/all_to_all | solution.py:244
  38.6 0.9 gather.2
  39.5 4.4 %collective-permute-start.4 = (bf16[3,64,256]{2,1,0:T(8,128)(2,1)S(1)}, bf16[3,64,256]{2,1,0:T(8,128)(2,1)S(1)}, u32[]{:S(2)}, u32[]{:S(2)}) collective-permute-start(bf16[3,64,256]{2,1,0:T(8,128)(2,1)S(1)} %get-tuple-element.39), channel_id=1, source_target_pairs={{0,1},{1,0},{2,3},{3,2},{4,5},{5,4},{6,7},{7,6},{8,9},{9,8},{10,11... | collective-permute-start | bytes 294920 | tf_op jit(solution)/shard_map/gather/ppermute | solution.py:27
  43.9 0.9 collective-permute-done.4.other_ref
  44.8 0.6 gather.3.refs_0_
  45.4 0.1 collective-permute-start.5
  45.5 2.7 %collective-permute-start.6 = (bf16[3,64,256]{2,1,0:T(8,128)(2,1)S(1)}, bf16[3,64,256]{2,1,0:T(8,128)(2,1)S(1)}, u32[]{:S(2)}, u32[]{:S(2)}) collective-permute-start(bf16[3,64,256]{2,1,0:T(8,128)(2,1)S(1)} %gather.3.refs_0_), channel_id=1, source_target_pairs={{0,14},{2,0},{4,2},{6,4},{8,6},{10,8},{12,10},{14,12},{1,15},{3,1}... | collective-permute-start | bytes 294920 | tf_op jit(solution)/shard_map/gather/ppermute | solution.py:31
  48.2 2.7 %collective-permute-done.5.refs_1_ = bf16[3,64,256]{2,1,0:T(8,128)(2,1)S(1)} collective-permute-done((bf16[3,64,256]{2,1,0:T(8,128)(2,1)S(1)}, bf16[3,64,256]{2,1,0:T(8,128)(2,1)S(1)}, u32[]{:S(2)}, u32[]{:S(2)}) %collective-permute-start.5) | collective-permute-done | bytes 98336 | tf_op jit(solution)/shard_map/gather/ppermute | solution.py:31
  50.8 0.0 collective-permute-start.7
  50.8 0.0 collective-permute-done.6.refs_2_
  50.8 2.7 %collective-permute-start.8 = (bf16[3,64,256]{2,1,0:T(8,128)(2,1)S(1)}, bf16[3,64,256]{2,1,0:T(8,128)(2,1)S(1)}, u32[]{:S(2)}, u32[]{:S(2)}) collective-permute-start(bf16[3,64,256]{2,1,0:T(8,128)(2,1)S(1)} %collective-permute-done.6.refs_2_), channel_id=1, source_target_pairs={{0,14},{2,0},{4,2},{6,4},{8,6},{10,8},{12,10},{14,12},{1,15},{3,1}... | collective-permute-start | bytes 294920 | tf_op jit(solution)/shard_map/gather/ppermute | solution.py:31
  53.5 2.4 %collective-permute-done.7.refs_3_ = bf16[3,64,256]{2,1,0:T(8,128)(2,1)S(1)} collective-permute-done((bf16[3,64,256]{2,1,0:T(8,128)(2,1)S(1)}, bf16[3,64,256]{2,1,0:T(8,128)(2,1)S(1)}, u32[]{:S(2)}, u32[]{:S(2)}) %collective-permute-start.7) | collective-permute-done | bytes 98336 | tf_op jit(solution)/shard_map/gather/ppermute | solution.py:31
  55.9 0.0 collective-permute-start.9
  55.9 0.0 collective-permute-done.8.refs_4_
  55.9 2.7 %collective-permute-start.10 = (bf16[3,64,256]{2,1,0:T(8,128)(2,1)S(1)}, bf16[3,64,256]{2,1,0:T(8,128)(2,1)S(1)}, u32[]{:S(2)}, u32[]{:S(2)}) collective-permute-start(bf16[3,64,256]{2,1,0:T(8,128)(2,1)S(1)} %collective-permute-done.8.refs_4_), channel_id=1, source_target_pairs={{0,14},{2,0},{4,2},{6,4},{8,6},{10,8},{12,10},{14,12},{1,15},{3,1}... | collective-permute-start | bytes 294920 | tf_op jit(solution)/shard_map/gather/ppermute | solution.py:31
  58.6 2.0 %collective-permute-done.9.refs_5_ = bf16[3,64,256]{2,1,0:T(8,128)(2,1)S(1)} collective-permute-done((bf16[3,64,256]{2,1,0:T(8,128)(2,1)S(1)}, bf16[3,64,256]{2,1,0:T(8,128)(2,1)S(1)}, u32[]{:S(2)}, u32[]{:S(2)}) %collective-permute-start.9) | collective-permute-done | bytes 98336 | tf_op jit(solution)/shard_map/gather/ppermute | solution.py:31
  60.6 0.0 collective-permute-start.11
  60.6 0.0 collective-permute-done.3.came_ref
  60.6 1.1 copy-done.2
  61.7 2.1 %projection.7 = (bf16[3,512,512]{2,1,0:T(8,128)(2,1)S(1)}, f32[24,256]{1,0:T(8,128)S(1)}) custom-call(s32[7]{0:T(128)S(1)} %concatenate.3.at_ref, f32[3,256,256]{2,1,0:T(8,128)S(1)} %copy-done.2, f32[3,512,256]{2,1,0:T(8,128)S(1)} %get-tuple-element.33.kept_ref, bf16[3,512,256]{2,1,0:T(8,128)(2,1)} %collective-permute-done.3.came_ref), custom_call_target="tpu_custom_call" | custom-call | bytes 3145756 | tf_op jit(solution)/shard_map/projection/pallas_call | solution.py:36
  63.8 0.0 collective-permute-done.10.refs_6_
  63.8 1.4 %collective-permute-done.11.refs_7_ = bf16[3,64,256]{2,1,0:T(8,128)(2,1)S(1)} collective-permute-done((bf16[3,64,256]{2,1,0:T(8,128)(2,1)S(1)}, bf16[3,64,256]{2,1,0:T(8,128)(2,1)S(1)}, u32[]{:S(2)}, u32[]{:S(2)}) %collective-permute-start.11) | collective-permute-done | bytes 98336 | tf_op jit(solution)/shard_map/gather/ppermute | solution.py:31
  65.3 1.1 coupling.3
  66.4 23.0 %all_to_all.20.part_ref = f32[32,24,256]{2,1,0:T(8,128)S(1)} all-to-all(f32[32,24,256]{2,1,0:T(8,128)S(1)} %bitcast.12), channel_id=1, replica_groups=mesh['yl'=2,'x'=4,'yh'=2,'z'=8,'core'=2] {'core','yl','x','yh'}, dimensions={0} | all-to-all | bytes 1572864 | tf_op jit(solution)/shard_map/coupling/all_to_all | solution.py:266
  89.4 0.7 coupling.4
  90.2 3.4 %all-to-all-start.2 = ((f32[8,24,256]{2,1,0:T(8,128)}), f32[8,24,256]{2,1,0:T(8,128)S(1)}, u32[]{:S(2)}, u32[]{:S(2)}) async-start(f32[8,24,256]{2,1,0:T(8,128)} %get-tuple-element.45), calls=%async_computation.2 | async-start | bytes 393216 | tf_op jit(solution)/shard_map/coupling/all_to_all | solution.py:269
  93.6 0.5 collective-permute-start.12
  94.0 10.3 %all-to-all-done.2.parts_ref = f32[8,24,256]{2,1,0:T(8,128)S(1)} async-done(((f32[8,24,256]{2,1,0:T(8,128)}), f32[8,24,256]{2,1,0:T(8,128)S(1)}, u32[]{:S(2)}, u32[]{:S(2)}) %all-to-all-start.2) | async-done | bytes 196640 | tf_op jit(solution)/shard_map/coupling/all_to_all | solution.py:269
  104.4 0.8 broadcast_in_dim.2
  105.1 4.2 %all-to-all-start.3 = ((bf16[32,24,256]{2,1,0:T(8,128)(2,1)}), bf16[32,24,256]{2,1,0:T(8,128)(2,1)S(1)}, u32[]{:S(2)}, u32[]{:S(2)}) async-start(bf16[32,24,256]{2,1,0:T(8,128)(2,1)} %broadcast_in_dim.2), calls=%async_computation.3 | async-start | bytes 786432 | tf_op jit(solution)/shard_map/coupling/all_to_all | solution.py:272
  109.3 0.3 collective-permute-start.14
  109.7 10.0 %all-to-all-done.3 = bf16[32,24,256]{2,1,0:T(8,128)(2,1)S(1)} async-done(((bf16[32,24,256]{2,1,0:T(8,128)(2,1)}), bf16[32,24,256]{2,1,0:T(8,128)(2,1)S(1)}, u32[]{:S(2)}, u32[]{:S(2)}) %all-to-all-start.3) | async-done | bytes 393248 | tf_op jit(solution)/shard_map/coupling/all_to_all | solution.py:272
  119.7 0.3 collective-permute-start.13
  120.0 4.7 %output.2._ = bf16[2048,1024]{1,0:T(8,128)(2,1)} custom-call(s32[7]{0:T(128)S(1)} %concatenate.3.at_ref, bf16[3,512,256]{2,1,0:T(8,128)(2,1)S(1)} %get-tuple-element.44.own_ref, bf16[3,512,256]{2,1,0:T(8,128)(2,1)} %collective-permute-done.14.other_ref, bf16[3,256,256]{2,1,0:T(8,128)(2,1)S(1)} %bitcast.10, bf16[3,1024,256]{2,1,0:T(8,128)(2,1)S(1)} %copy-done.1, ...), custom_call_target="tpu_custom_call" | custom-call | flops 2013265920 | bytes 2097152 | tf_op jit(solution)/shard_map/output/pallas_call | solution.py:224
  124.7 4.1 %output.3 = bf16[2048,1024]{1,0:T(8,128)(2,1)} custom-call(s32[7]{0:T(128)S(1)} %concatenate.3.at_ref, bf16[3,512,256]{2,1,0:T(8,128)(2,1)S(1)} %collective-permute-done.12.own_ref, bf16[3,512,256]{2,1,0:T(8,128)(2,1)S(1)} %collective-permute-done.13.other_ref, bf16[3,256,256]{2,1,0:T(8,128)(2,1)S(1)} %bitcast.11, ...), custom_call_target="tpu_custom_call", output_to_operand_aliasing={{}: (5, {})} | custom-call | flops 2013265920 | bytes 2097152 | tf_op jit(solution)/shard_map/output/pallas_call | solution.py:224
  (11 shorter events, 0.0 us)
Async XLA Ops:
  0.0 38.6 %all-to-all-start = ((bf16[16,128,256]{2,1,0:T(8,128)(2,1)}), bf16[16,128,256]{2,1,0:T(8,128)(2,1)S(1)}, u32[]{:S(2)}, u32[]{:S(2)}) async-start(bf16[16,128,256]{2,1,0:T(8,128)(2,1)} %bitcast.13), calls=%async_computation | async-start | bytes 2097152 | tf_op jit(solution)/shard_map/scatter/all_to_all | solution.py:244
  12.5 1.4 %copy-start = (bf16[3,1024,256]{2,1,0:T(8,128)(2,1)S(1)}, bf16[3,1024,256]{2,1,0:T(8,128)(2,1)}, u32[]{:S(2)}) copy-start(bf16[3,1024,256]{2,1,0:T(8,128)(2,1)} %panels_ref.7) | copy-start | bytes 4718596
  13.9 2.2 %copy-start.3 = (bf16[2048,1024]{1,0:T(8,128)(2,1)S(1)}, bf16[2048,1024]{1,0:T(8,128)(2,1)}, u32[]{:S(2)}) copy-start(bf16[2048,1024]{1,0:T(8,128)(2,1)} %gradient_ref.3) | copy-start | bytes 12582916
  22.8 7.8 %collective-permute-start = (f32[1024,256]{1,0:T(8,128)S(1)}, f32[1024,256]{1,0:T(8,128)S(1)}, u32[]{:S(2)}, u32[]{:S(2)}) collective-permute-start(f32[1024,256]{1,0:T(8,128)S(1)} %get-tuple-element.30), channel_id=1, source_target_pairs={{0,1},{1,0},{2,3},{3,2},{4,5},{5,4},{6,7},{7,6},{8,9},{9,8},{10,11... | collective-permute-start | bytes 3145736 | tf_op jit(solution)/shard_map/projection/ppermute | solution.py:27
  23.8 6.8 %collective-permute-start.1 = (f32[1024,256]{1,0:T(8,128)S(1)}, f32[1024,256]{1,0:T(8,128)S(1)}, u32[]{:S(2)}, u32[]{:S(2)}) collective-permute-start(f32[1024,256]{1,0:T(8,128)S(1)} %get-tuple-element.31), channel_id=1, source_target_pairs={{0,1},{1,0},{2,3},{3,2},{4,5},{5,4},{6,7},{7,6},{8,9},{9,8},{10,11... | collective-permute-start | bytes 3145736 | tf_op jit(solution)/shard_map/projection/ppermute | solution.py:27
  23.9 6.7 %collective-permute-start.2 = (f32[1024,256]{1,0:T(8,128)S(1)}, f32[1024,256]{1,0:T(8,128)S(1)}, u32[]{:S(2)}, u32[]{:S(2)}) collective-permute-start(f32[1024,256]{1,0:T(8,128)S(1)} %get-tuple-element.32), channel_id=1, source_target_pairs={{0,1},{1,0},{2,3},{3,2},{4,5},{5,4},{6,7},{7,6},{8,9},{9,8},{10,11... | collective-permute-start | bytes 3145736 | tf_op jit(solution)/shard_map/projection/ppermute | solution.py:27
  32.3 28.3 %collective-permute-start.3 = (bf16[3,512,256]{2,1,0:T(8,128)(2,1)}, bf16[3,512,256]{2,1,0:T(8,128)(2,1)}, u32[]{:S(2)}, u32[]{:S(2)}) collective-permute-start(bf16[3,512,256]{2,1,0:T(8,128)(2,1)} %get-tuple-element.34), channel_id=1, source_target_pairs={{0,16},{16,0},{1,17},{17,1},{2,18},{18,2},{3,19},{19,3},{4,20},{20... | collective-permute-start | bytes 2359304 | tf_op jit(solution)/shard_map/projection/ppermute | solution.py:27
  39.5 5.4 %collective-permute-start.4 = (bf16[3,64,256]{2,1,0:T(8,128)(2,1)S(1)}, bf16[3,64,256]{2,1,0:T(8,128)(2,1)S(1)}, u32[]{:S(2)}, u32[]{:S(2)}) collective-permute-start(bf16[3,64,256]{2,1,0:T(8,128)(2,1)S(1)} %get-tuple-element.39), channel_id=1, source_target_pairs={{0,1},{1,0},{2,3},{3,2},{4,5},{5,4},{6,7},{7,6},{8,9},{9,8},{10,11... | collective-permute-start | bytes 294920 | tf_op jit(solution)/shard_map/gather/ppermute | solution.py:27
  45.4 5.4 %collective-permute-start.5 = (bf16[3,64,256]{2,1,0:T(8,128)(2,1)S(1)}, bf16[3,64,256]{2,1,0:T(8,128)(2,1)S(1)}, u32[]{:S(2)}, u32[]{:S(2)}) collective-permute-start(bf16[3,64,256]{2,1,0:T(8,128)(2,1)S(1)} %gather.3.refs_0_), channel_id=1, source_target_pairs={{0,2},{2,4},{4,6},{6,8},{8,10},{10,12},{12,14},{14,0},{1,3},{3,5},... | collective-permute-start | bytes 294920 | tf_op jit(solution)/shard_map/gather/ppermute | solution.py:31
  45.5 5.3 %collective-permute-start.6 = (bf16[3,64,256]{2,1,0:T(8,128)(2,1)S(1)}, bf16[3,64,256]{2,1,0:T(8,128)(2,1)S(1)}, u32[]{:S(2)}, u32[]{:S(2)}) collective-permute-start(bf16[3,64,256]{2,1,0:T(8,128)(2,1)S(1)} %gather.3.refs_0_), channel_id=1, source_target_pairs={{0,14},{2,0},{4,2},{6,4},{8,6},{10,8},{12,10},{14,12},{1,15},{3,1}... | collective-permute-start | bytes 294920 | tf_op jit(solution)/shard_map/gather/ppermute | solution.py:31
  50.8 5.1 %collective-permute-start.7 = (bf16[3,64,256]{2,1,0:T(8,128)(2,1)S(1)}, bf16[3,64,256]{2,1,0:T(8,128)(2,1)S(1)}, u32[]{:S(2)}, u32[]{:S(2)}) collective-permute-start(bf16[3,64,256]{2,1,0:T(8,128)(2,1)S(1)} %collective-permute-done.5.refs_1_), channel_id=1, source_target_pairs={{0,2},{2,4},{4,6},{6,8},{8,10},{10,12},{12,14},{14,0},{1,3},{3,5},... | collective-permute-start | bytes 294920 | tf_op jit(solution)/shard_map/gather/ppermute | solution.py:31
  50.8 5.1 %collective-permute-start.8 = (bf16[3,64,256]{2,1,0:T(8,128)(2,1)S(1)}, bf16[3,64,256]{2,1,0:T(8,128)(2,1)S(1)}, u32[]{:S(2)}, u32[]{:S(2)}) collective-permute-start(bf16[3,64,256]{2,1,0:T(8,128)(2,1)S(1)} %collective-permute-done.6.refs_2_), channel_id=1, source_target_pairs={{0,14},{2,0},{4,2},{6,4},{8,6},{10,8},{12,10},{14,12},{1,15},{3,1}... | collective-permute-start | bytes 294920 | tf_op jit(solution)/shard_map/gather/ppermute | solution.py:31
  55.9 4.7 %collective-permute-start.9 = (bf16[3,64,256]{2,1,0:T(8,128)(2,1)S(1)}, bf16[3,64,256]{2,1,0:T(8,128)(2,1)S(1)}, u32[]{:S(2)}, u32[]{:S(2)}) collective-permute-start(bf16[3,64,256]{2,1,0:T(8,128)(2,1)S(1)} %collective-permute-done.7.refs_3_), channel_id=1, source_target_pairs={{0,2},{2,4},{4,6},{6,8},{8,10},{10,12},{12,14},{14,0},{1,3},{3,5},... | collective-permute-start | bytes 294920 | tf_op jit(solution)/shard_map/gather/ppermute | solution.py:31
  55.9 7.9 %collective-permute-start.10 = (bf16[3,64,256]{2,1,0:T(8,128)(2,1)S(1)}, bf16[3,64,256]{2,1,0:T(8,128)(2,1)S(1)}, u32[]{:S(2)}, u32[]{:S(2)}) collective-permute-start(bf16[3,64,256]{2,1,0:T(8,128)(2,1)S(1)} %collective-permute-done.8.refs_4_), channel_id=1, source_target_pairs={{0,14},{2,0},{4,2},{6,4},{8,6},{10,8},{12,10},{14,12},{1,15},{3,1}... | collective-permute-start | bytes 294920 | tf_op jit(solution)/shard_map/gather/ppermute | solution.py:31
  60.6 4.7 %collective-permute-start.11 = (bf16[3,64,256]{2,1,0:T(8,128)(2,1)S(1)}, bf16[3,64,256]{2,1,0:T(8,128)(2,1)S(1)}, u32[]{:S(2)}, u32[]{:S(2)}) collective-permute-start(bf16[3,64,256]{2,1,0:T(8,128)(2,1)S(1)} %collective-permute-done.9.refs_5_), channel_id=1, source_target_pairs={{0,2},{2,4},{4,6},{6,8},{8,10},{10,12},{12,14},{14,0},{1,3},{3,5},... | collective-permute-start | bytes 294920 | tf_op jit(solution)/shard_map/gather/ppermute | solution.py:31
  60.6 1.1 copy-start.2
  61.7 58.2 %copy-start.1 = (bf16[3,1024,256]{2,1,0:T(8,128)(2,1)S(1)}, bf16[3,1024,256]{2,1,0:T(8,128)(2,1)}, u32[]{:S(2)}) copy-start(bf16[3,1024,256]{2,1,0:T(8,128)(2,1)} %panels_ref.7) | copy-start | bytes 4718596
  90.2 14.2 %all-to-all-start.2 = ((f32[8,24,256]{2,1,0:T(8,128)}), f32[8,24,256]{2,1,0:T(8,128)S(1)}, u32[]{:S(2)}, u32[]{:S(2)}) async-start(f32[8,24,256]{2,1,0:T(8,128)} %get-tuple-element.45), calls=%async_computation.2 | async-start | bytes 393216 | tf_op jit(solution)/shard_map/coupling/all_to_all | solution.py:269
  93.6 26.1 %collective-permute-start.12 = (bf16[3,512,256]{2,1,0:T(8,128)(2,1)S(1)}, bf16[3,512,256]{2,1,0:T(8,128)(2,1)S(1)}, u32[]{:S(2)}, u32[]{:S(2)}) collective-permute-start(bf16[3,512,256]{2,1,0:T(8,128)(2,1)S(1)} %get-tuple-element.44.own_ref), channel_id=1, source_target_pairs={{0,16},{16,0},{1,17},{17,1},{2,18},{18,2},{3,19},{19,3},{4,20},{20... | collective-permute-start | bytes 2359304 | tf_op jit(solution)/shard_map/coupling/ppermute | solution.py:27
  105.1 14.5 %all-to-all-start.3 = ((bf16[32,24,256]{2,1,0:T(8,128)(2,1)}), bf16[32,24,256]{2,1,0:T(8,128)(2,1)S(1)}, u32[]{:S(2)}, u32[]{:S(2)}) async-start(bf16[32,24,256]{2,1,0:T(8,128)(2,1)} %broadcast_in_dim.2), calls=%async_computation.3 | async-start | bytes 786432 | tf_op jit(solution)/shard_map/coupling/all_to_all | solution.py:272
  109.3 10.6 %collective-permute-start.14 = (bf16[3,512,256]{2,1,0:T(8,128)(2,1)S(1)}, bf16[3,512,256]{2,1,0:T(8,128)(2,1)}, u32[]{:S(2)}, u32[]{:S(2)}) collective-permute-start(bf16[3,512,256]{2,1,0:T(8,128)(2,1)S(1)} %get-tuple-element.44.own_ref), channel_id=1, source_target_pairs={{0,1},{1,0},{2,3},{3,2},{4,5},{5,4},{6,7},{7,6},{8,9},{9,8},{10,11... | collective-permute-start | bytes 2359304 | tf_op jit(solution)/shard_map/coupling/ppermute | solution.py:27
  119.7 5.0 %collective-permute-start.13 = (bf16[3,512,256]{2,1,0:T(8,128)(2,1)S(1)}, bf16[3,512,256]{2,1,0:T(8,128)(2,1)S(1)}, u32[]{:S(2)}, u32[]{:S(2)}) collective-permute-start(bf16[3,512,256]{2,1,0:T(8,128)(2,1)S(1)} %collective-permute-done.12.own_ref), channel_id=1, source_target_pairs={{0,1},{1,0},{2,3},{3,2},{4,5},{5,4},{6,7},{7,6},{8,9},{9,8},{10,11... | collective-permute-start | bytes 2359304 | tf_op jit(solution)/shard_map/output/ppermute | solution.py:27
